TPU v7x, 32 devices: a whole 2x2x4 slice. The times are simulated.
32 devices in a mesh: groups: 2 (over y), row: 4 (over z), col: 4 (over x, core).
Axes of the slice: x: 2, y: 2, z: 4, core: 2. Of those that a mesh axis runs over, the one named last changes fastest.
Arguments:
- features: bfloat16 [4096, 256], P(('groups', 'row', 'col')), parts along dimension 0, may hold values from -6 to 6
- adj_tiles: bfloat16 [32, 4, 2, 128, 128], P(('groups', 'row'), 'col'), parts along dimension 0, may hold values from -0.5 to 0.5
- columns: int32 [32, 4, 2], P(('groups', 'row'), 'col'), parts along dimension 0, may hold values from 0 to 3, as said below
- counts: int32 [32, 4], P(('groups', 'row'), 'col'), parts along dimension 0, may hold values from 1 to 2, as said below
- weight: bfloat16 [256, 256], replicated, may hold values from -0.375 to 0.375
- bias_term: bfloat16 [256], replicated, may hold values from -3 to 3
- cotangent: bfloat16 [4096, 256], P(('groups', 'row', 'col')), parts along dimension 0, may hold values from -6 to 6
Outputs:
- activations: bfloat16 [4096, 256], P(('groups', 'row', 'col')), parts along dimension 0
- grad_features: bfloat16 [4096, 256], P(('groups', 'row', 'col')), parts along dimension 0
- grad_weight: float32 [512, 256], P('groups'), parts along dimension 0
- grad_bias: float32 [512], P('groups'), parts along dimension 0
There are 2 independent parts, one for each index of `groups`. A program takes and returns all parts, laid end to end along the dimension named above; an argument that names none is the same for every part. Nothing has to cross between parts.
Inputs may be any that keep to these rules, and one draw needn't show every extreme that they name: The 2 tile columns of one tile row within one column block are distinct. Slots at counts and beyond hold tiles that are not part of A; some entry equals 2.
All inputs are finite; a program needn't handle non-finite values.
Results may differ from a plain program's by a relative error of at most 0.019.
Values may be sent and summed in bfloat16 or wider, within the bound.
No kernel may reach another device: no remote copies, remote signals or barrier semaphores. Data moves between devices by JAX's collectives and lax.ppermute only.
A program may use at most 128 MiB of HBM per device.

v0:
```python
import jax
import jax.numpy as jnp
from jax import lax
from jax.sharding import PartitionSpec as P


def shards(features, adj_tiles, columns, counts, weight, bias_term, cotangent):
    rows_dev, feat_width = features.shape
    tile_size = adj_tiles.shape[-1]
    slot_count = adj_tiles.shape[2]
    tile_rows = adj_tiles.shape[0]
    local_tiles = adj_tiles[:, 0]
    local_cols = columns[:, 0]
    local_counts = counts[:, 0]
    slot_ids = jnp.arange(slot_count, dtype=jnp.int32)
    active = slot_ids[None, :] < local_counts[:, None]
    gathered = lax.all_gather(features, "row", axis=0, tiled=True)
    col_tiles = gathered.shape[0] // tile_size
    feature_blocks = gathered.reshape(col_tiles, tile_size, feat_width)
    picked = feature_blocks[local_cols]
    picked = jnp.where(active[:, :, None, None], picked, jnp.zeros((), jnp.bfloat16))
    totals = jnp.einsum("tkij,tkjf->tif", local_tiles, picked, preferred_element_type=jnp.float32)
    totals = totals.reshape(tile_rows * tile_size, feat_width)
    summed = lax.psum(totals.astype(jnp.bfloat16), "col").astype(jnp.float32)
    aggregated = lax.dynamic_slice_in_dim(summed, lax.axis_index("col") * rows_dev, rows_dev, 0)
    agg_low = aggregated.astype(jnp.bfloat16)
    preact = jnp.dot(agg_low, weight, preferred_element_type=jnp.float32) + bias_term.astype(
        jnp.float32
    )
    sigmoid_value = jax.nn.sigmoid(preact)
    activations = (preact * sigmoid_value).astype(jnp.bfloat16)
    derivative = sigmoid_value * (1.0 + preact * (1.0 - sigmoid_value))
    grad_pre = (cotangent.astype(jnp.float32) * derivative).astype(jnp.bfloat16)
    grad_agg = jnp.dot(grad_pre, weight.T, preferred_element_type=jnp.float32).astype(jnp.bfloat16)
    grad_rows = lax.all_gather(grad_agg, "col", axis=0, tiled=True).reshape(
        tile_rows, tile_size, feat_width
    )
    contrib = jnp.einsum(
        "tkij,tif->tkjf", local_tiles, grad_rows, preferred_element_type=jnp.float32
    )
    contrib = jnp.where(active[:, :, None, None], contrib, jnp.float32(0.0))
    partial_value = jnp.zeros((col_tiles, tile_size, feat_width), jnp.float32)
    partial_value = partial_value.at[local_cols.reshape(-1)].add(
        contrib.reshape(-1, tile_size, feat_width)
    )
    grad_features = lax.psum_scatter(
        partial_value.reshape(col_tiles * tile_size, feat_width).astype(jnp.bfloat16),
        "row",
        scatter_dimension=0,
        tiled=True,
    ).astype(jnp.float32)
    grad_features = grad_features.astype(jnp.bfloat16)
    local_weight = jnp.dot(agg_low.T, grad_pre, preferred_element_type=jnp.float32)
    local_bias = jnp.sum(grad_pre.astype(jnp.float32), axis=0)
    grad_weight, grad_bias = lax.psum((local_weight, local_bias), ("row", "col"))
    return (activations, grad_features, grad_weight, grad_bias)


def solution(mesh):
    placed = (
        P(("groups", "row", "col"), None),
        P(("groups", "row"), "col", None, None, None),
        P(("groups", "row"), "col", None),
        P(("groups", "row"), "col"),
        P(),
        P(),
        P(("groups", "row", "col"), None),
    )
    return jax.shard_map(
        shards,
        mesh=mesh,
        in_specs=placed,
        out_specs=(
            P(("groups", "row", "col"), None),
            P(("groups", "row", "col"), None),
            P("groups", None),
            P("groups"),
        ),
        check_vma=False,
    )
```

profile of v0, /device:TPU:0, one launch (start us, length us, event | category | flops | bytes accessed | tf_op | source)
XLA Modules:
  0.0 183.2 jit_solution(9247272626871028330)
XLA Ops:
  7.2 0.0 copy-start
  7.2 0.0 copy-start.4
  7.2 0.0 all-reduce.3.cloned.1.call-start
  7.2 0.6 copy-done.4
  7.9 0.1 iota_compare_fusion
  8.0 0.0 copy-start.2
  8.0 16.0 %all_gather.6 = bf16[512,256]{1,0:T(8,128)(2,1)S(1)} all-gather(bf16[128,256]{1,0:T(8,128)(2,1)} %param.7), channel_id=1, replica_groups=mesh['groups'=2,'row'=4,'col'=4] {'row'}, dimensions={0}, use_global_device_ids=true | all-gather | bytes 327680 | tf_op jit(solution)/shard_map/all_gather | solution.py:17
  23.9 0.0 copy-done.2
  23.9 0.1 copy.14
  24.0 0.1 reshape.105
  24.1 0.6 gather_fusion
  24.7 0.0 copy-done
  24.7 1.0 fusion
  25.7 0.0 copy-start.1
  25.7 0.0 copy-start.3
  25.7 0.0 all-reduce.3.cloned.1.call-update
  25.7 0.0 all-reduce.5.cloned.1.call-start
  25.8 0.1 copy.15
  25.9 0.0 copy-start.5
  25.9 0.7 copy-done.5
  26.6 0.1 reshape_squeeze.3
  26.6 32.8 %all-reduce.3.cloned.1.call-done = bf16[512,256]{1,0:T(8,128)(2,1)} async-done(((bf16[512,256]{1,0:T(8,128)(2,1)}), bf16[512,256]{1,0:T(8,128)(2,1)}) %all-reduce.3.cloned.1.call-update) | async-done | bytes 262160 | tf_op jit(solution)/shard_map/psum | solution.py:24
  59.4 0.0 copy-done.1
  59.4 0.0 copy-done.3
  59.4 1.7 convert_reduce_fusion
  61.1 0.2 convolution_convert_fusion
  61.3 1.7 fusion.6
  63.1 0.0 all-reduce.5.cloned.1.call-update
  63.1 0.0 reduce-scatter.2.cloned.1.call-start
  63.1 5.8 %all_gather.7 = bf16[512,256]{1,0:T(8,128)(2,1)S(1)} all-gather(bf16[128,256]{1,0:T(8,128)(2,1)S(1)} %convolution_convert_fusion), channel_id=1, replica_groups=mesh['groups'=2,'row'=4,'col'=4] {'col'}, dimensions={0}, use_global_device_ids=true | all-gather | bytes 327680 | tf_op jit(solution)/shard_map/all_gather | solution.py:35
  68.9 0.3 convolution_select_fusion
  69.3 0.3 copy.17
  69.6 1.3 scatter_fusion
  71.0 0.7 convert_element_type.51
  71.7 0.0 reduce-scatter.2.cloned.1.call-update
  71.7 33.3 %psum.23 = f32[256]{0:T(256)} all-reduce(f32[256]{0:T(256)S(1)} %get-tuple-element.4), channel_id=1, replica_groups=mesh['groups'=2,'row'=4,'col'=4] {'row','col'}, use_global_device_ids=true, to_apply=%region_5.6 | all-reduce | flops 256 | bytes 2048 | tf_op jit(solution)/shard_map/psum | solution.py:55
  105.0 47.0 %all-reduce.5.cloned.1.call-done = f32[256,256]{1,0:T(8,128)} async-done(((f32[256,256]{1,0:T(8,128)}), f32[256,256]{1,0:T(8,128)}) %all-reduce.5.cloned.1.call-update) | async-done | bytes 262160 | tf_op jit(solution)/shard_map/psum | solution.py:55
  152.0 23.0 %reduce-scatter.2.cloned.1.call-done = bf16[128,256]{1,0:T(8,128)(2,1)} async-done(((bf16[512,256]{1,0:T(8,128)(2,1)}), bf16[128,256]{1,0:T(8,128)(2,1)}) %reduce-scatter.2.cloned.1.call-update) | async-done | bytes 65552 | tf_op jit(solution)/shard_map/reduce_scatter | solution.py:46
  175.0 1.7 copy.25
  (5 shorter events, 0.1 us)
Async XLA Ops:
  7.2 17.5 %copy-start = (bf16[4,1,2,128,128]{4,3,2,1,0:T(8,128)(2,1)S(1)}, bf16[4,1,2,128,128]{4,3,2,1,0:T(8,128)(2,1)}, u32[]{:S(2)}) copy-start(bf16[4,1,2,128,128]{4,3,2,1,0:T(8,128)(2,1)} %param.8) | copy-start | bytes 786436
  7.2 0.7 copy-start.4
  7.2 52.2 %all-reduce.3.cloned.1.call-start = ((), (), s32[]{:S(2)}) async-start(), calls=%async_computation.1 | async-start | bytes 524288 | tf_op jit(solution)/shard_map/psum | solution.py:24
  8.0 16.0 %copy-start.2 = (s32[4,1,2]{0,2,1:T(2,128)S(1)}, s32[4,1,2]{0,2,1:T(2,128)}, u32[]{:S(2)}) copy-start(s32[4,1,2]{0,2,1:T(2,128)} %param.9) | copy-start | bytes 100
  25.7 33.7 %copy-start.1 = (bf16[256,256]{1,0:T(8,128)(2,1)S(1)}, bf16[256,256]{1,0:T(8,128)(2,1)}, u32[]{:S(2)}) copy-start(bf16[256,256]{1,0:T(8,128)(2,1)} %param.11) | copy-start | bytes 393220
  25.7 33.7 %copy-start.3 = (bf16[128,256]{1,0:T(8,128)(2,1)S(1)}, bf16[128,256]{1,0:T(8,128)(2,1)}, u32[]{:S(2)}) copy-start(bf16[128,256]{1,0:T(8,128)(2,1)} %param.13) | copy-start | bytes 196612
  25.7 126.2 %all-reduce.5.cloned.1.call-start = ((), (), s32[]{:S(2)}) async-start(), calls=%async_computation.3 | async-start | bytes 524288 | tf_op jit(solution)/shard_map/psum | solution.py:55
  25.9 0.7 copy-start.5
  63.1 111.9 %reduce-scatter.2.cloned.1.call-start = ((), (), s32[]{:S(2)}) async-start(), calls=%async_computation.2 | async-start | bytes 327680 | tf_op jit(solution)/shard_map/reduce_scatter | solution.py:46
Sparse Core Ops, SparseCore 0:
  25.9 33.4 all-reduce.2
  63.2 88.7 all-reduce.4
  154.9 20.0 reduce-scatter.1
where the time goes:
time: 184 us; the launch traced here: 183 us
  waiting for transfers between devices  103 us (56%)
  blocking collectives  55 us (30%)
  between operations  13.8 us (8%)
  matrix products  4.98 us (3%)
  local copies, waits for them, and re-layouts  4.29 us (2%)
  other arithmetic  2.14 us (1%)
    psum x1, waiting for transfers between devices, shards(): lax.psum((local_weight, local_bias), ('row', 'col'))  47 us
    psum x1, blocking collectives, shards(): lax.psum((local_weight, local_bias), ('row', 'col'))  33.3 us
    psum x1, waiting for transfers between devices, shards(): summed = lax.psum(totals.astype(jnp.bfloat16), 'col').astype(jnp.float32)  32.8 us
    reduce_scatter x1, waiting for transfers between devices, shards(): lax.psum_scatter(partial_value.reshape(col_tiles * tile_size, feat_width)...  23 us
    all_gather x1, blocking collectives, shards(): gathered = lax.all_gather(features, 'row', axis=0, tiled=True)  16 us
    all_gather x1, blocking collectives, shards(): lax.all_gather(grad_agg, 'col', axis=0, tiled=True)  5.79 us
  transfers between devices with their start and end apart: 3, of which 3 were waited for; matrix products, arithmetic and copies ran while one was open for 2% of the time, Pallas kernels for 0%

commit v1 on v0

v1 whole, which is shorter than its diff:
```python
import jax
import jax.numpy as jnp
from jax import lax
from jax.experimental import pallas as pl
from jax.experimental.pallas import tpu as pltpu
from jax.sharding import PartitionSpec as P

BF = jnp.bfloat16
F32 = jnp.float32
LIMIT = 48 * 1024 * 1024


def dot(a, b, ca=1, cb=0):
    return lax.dot_general(a, b, (((ca,), (cb,)), ((), ())), preferred_element_type=F32)


def call(body, outs, scratch=(), smem=0, count=1):
    vm = pl.BlockSpec(memory_space=pltpu.VMEM)
    sm = pl.BlockSpec(memory_space=pltpu.SMEM)
    return pl.pallas_call(
        body,
        in_specs=[sm] * smem + [vm] * (count - smem),
        out_specs=jax.tree.map(lambda _: vm, outs),
        out_shape=outs,
        scratch_shapes=scratch,
        compiler_params=pltpu.CompilerParams(vmem_limit_bytes=LIMIT),
    )


def dense_kernel(n_row, n_col):
    def body(cols_ref, cnts_ref, tiles_ref, a_ref, at_ref):
        trows, _, slots, tile, _ = tiles_ref.shape
        r = lax.axis_index("row")
        c = lax.axis_index("col")
        a_ref[...] = jnp.zeros_like(a_ref)
        at_ref[...] = jnp.zeros_like(at_ref)

        def put(step, carry):
            t = step // slots
            k = step % slots

            @pl.when(k < cnts_ref[t, 0])
            def _():
                q = lax.rem(t - c + n_col, n_col)
                p = lax.rem(cols_ref[t, 0, k] - r + n_row, n_row)
                here = tiles_ref[t, 0, k]
                qs = pl.ds(pl.multiple_of(q * tile, tile), tile)
                ps = pl.ds(pl.multiple_of(p * tile, tile), tile)
                a_ref[qs, ps] = here
                at_ref[ps, qs] = here.T

            return carry

        lax.fori_loop(0, trows * slots, put, 0)

    return body


def forward_kernel(n_row, n_col, tile):
    def body(a_ref, *refs):
        x = jnp.concatenate([ref[...] for ref in refs[:n_row]], axis=0)
        for q, out in enumerate(refs[n_row:]):
            out[...] = dot(a_ref[q * tile : (q + 1) * tile, :], x).astype(BF)

    return body


def middle_kernel(n_col):
    def body(w_ref, b_ref, cot_ref, *refs):
        parts, (act_ref, agg_ref, pre_ref, gagg_ref) = refs[:n_col], refs[n_col:]
        total = parts[0][...].astype(F32)
        for ref in parts[1:]:
            total = total + ref[...].astype(F32)
        agg = total.astype(BF)
        agg_ref[...] = agg
        preact = dot(agg, w_ref[...]) + b_ref[...].astype(F32)
        sig = jax.nn.sigmoid(preact)
        act_ref[...] = (preact * sig).astype(BF)
        grad = cot_ref[...].astype(F32) * (sig * (1.0 + preact * (1.0 - sig)))
        grad = grad.astype(BF)
        pre_ref[...] = grad
        gagg_ref[...] = dot(grad, w_ref[...], 1, 1).astype(BF)

    return body


def weight_kernel(n_dev, rows):
    def body(agg_ref, pre_ref, out_ref):
        pre = pre_ref[...]
        local = dot(agg_ref[...], pre, 0, 0).astype(BF)
        bias = jnp.sum(pre.astype(F32), axis=0, keepdims=True)
        high = bias.astype(BF)
        low = (bias - high.astype(F32)).astype(BF)
        pad = out_ref.shape[1] - rows
        which = lax.broadcasted_iota(jnp.int32, (pad, bias.shape[1]), 0)
        tail = jnp.where(which == 0, high.astype(F32), jnp.where(which == 1, low.astype(F32), 0.0))
        tail = tail.astype(BF)
        for i in range(n_dev):
            out_ref[i, :rows, :] = local[i * rows : (i + 1) * rows, :]
            out_ref[i, rows:, :] = tail

    return body


def weight_sum_kernel(n_dev, rows):
    def body(in_ref, w_ref, b_ref):
        total = in_ref[0].astype(F32)
        for i in range(1, n_dev):
            total = total + in_ref[i].astype(F32)
        w_ref[...] = total[:rows].astype(BF)
        b_ref[...] = (total[rows : rows + 1] + total[rows + 1 : rows + 2])

    return body


def backward_kernel(n_row, n_col, tile):
    def body(at_ref, *refs):
        g = jnp.concatenate([ref[...] for ref in refs[:n_col]], axis=0)
        for p, out in enumerate(refs[n_col:]):
            out[...] = dot(at_ref[p * tile : (p + 1) * tile, :], g).astype(BF)

    return body


def sum_kernel(body_refs, out_ref):
    total = body_refs[0][...].astype(F32)
    for ref in body_refs[1:]:
        total = total + ref[...].astype(F32)
    out_ref[...] = total.astype(BF)


def shift(x, axis, n, by):
    return lax.ppermute(x, axis, [(i, (i + by) % n) for i in range(n)])


def shards(n_row, n_col, features, adj_tiles, columns, counts, weight, bias_term, cotangent):
    rows_dev, width = features.shape
    tile = adj_tiles.shape[-1]
    n_dev = n_row * n_col
    shard = jax.ShapeDtypeStruct((rows_dev, width), BF)

    xs = [features] + [shift(features, "row", n_row, -p) for p in range(1, n_row)]
    a, at = call(
        dense_kernel(n_row, n_col),
        (
            jax.ShapeDtypeStruct((n_col * tile, n_row * tile), BF),
            jax.ShapeDtypeStruct((n_row * tile, n_col * tile), BF),
        ),
        smem=2,
        count=3,
    )(columns, counts, adj_tiles)
    parts = call(forward_kernel(n_row, n_col, tile), (shard,) * n_col, count=1 + n_row)(a, *xs)
    parts = [parts[0]] + [shift(parts[q], "col", n_col, q) for q in range(1, n_col)]
    act, agg, pre, gagg = call(middle_kernel(n_col), (shard,) * 4, count=3 + n_col)(
        weight, bias_term.reshape(1, width), cotangent, *parts
    )
    gs = [gagg] + [shift(gagg, "col", n_col, -q) for q in range(1, n_col)]

    if width % n_dev == 0 and width // n_dev >= 16:
        rows = width // n_dev
        packed = call(
            weight_kernel(n_dev, rows),
            jax.ShapeDtypeStruct((n_dev, rows + 16, width), BF),
            count=2,
        )(agg, pre)
        packed = lax.all_to_all(packed, ("row", "col"), 0, 0)
        part, grad_bias = call(
            weight_sum_kernel(n_dev, rows),
            (jax.ShapeDtypeStruct((rows, width), BF), jax.ShapeDtypeStruct((1, width), F32)),
            count=1,
        )(packed)
        grad_weight = lax.all_gather(part, ("row", "col"), axis=0, tiled=True).astype(F32)
        grad_bias = grad_bias.reshape(width)
    else:
        grad_weight = jnp.dot(agg.T, pre, preferred_element_type=F32)
        grad_bias = jnp.sum(pre.astype(F32), axis=0)
        grad_weight, grad_bias = lax.psum((grad_weight, grad_bias), ("row", "col"))

    fs = call(backward_kernel(n_row, n_col, tile), (shard,) * n_row, count=1 + n_col)(at, *gs)
    fs = [fs[0]] + [shift(fs[p], "row", n_row, p) for p in range(1, n_row)]
    grad_features = call(
        lambda *refs: sum_kernel(refs[:-1], refs[-1]), shard, count=n_row
    )(*fs)
    return act, grad_features, grad_weight, grad_bias


def solution(mesh):
    n_row, n_col = mesh.shape["row"], mesh.shape["col"]
    placed = (
        P(("groups", "row", "col"), None),
        P(("groups", "row"), "col", None, None, None),
        P(("groups", "row"), "col", None),
        P(("groups", "row"), "col"),
        P(),
        P(),
        P(("groups", "row", "col"), None),
    )

    def body(*args):
        return shards(n_row, n_col, *args)

    return jax.shard_map(
        body,
        mesh=mesh,
        in_specs=placed,
        out_specs=(
            P(("groups", "row", "col"), None),
            P(("groups", "row", "col"), None),
            P("groups", None),
            P("groups"),
        ),
        check_vma=False,
    )
```

time: 184 us -> 63.3 us (0.34)
  waiting for transfers between devices: 103 us -> 16 us
  blocking collectives: 55 us -> 18.1 us
  starting transfers between devices: 0.12 us -> 20.8 us
  between operations: 13.8 us -> 0.73 us
  matrix products: 4.98 us -> 0 us
  Pallas kernels: 0 us -> 4.83 us
  local copies, waits for them, and re-layouts: 4.29 us -> 1.83 us
    psum x2 -> x0, waiting for transfers between devices: 79.7 us -> none  [the longest x1 47 us: shards(): lax.psum((local_weight, local_bias), ('row', 'col'))]
    psum x1 -> x0, blocking collectives: 33.3 us -> none  [shards(): lax.psum((local_weight, local_bias), ('row', 'col'))]
    reduce_scatter x1 -> x0, waiting for transfers between devices: 23 us -> none  [shards(): lax.psum_scatter(partial_value.reshape(col_tiles * tile_size, feat_width)...]
    ppermute x0 -> x12, starting transfers between devices: none -> 16.3 us  [shift(): return lax.ppermute(x, axis, [(i, (i + by) % n) for i in range(n)])]
    ppermute x0 -> x12, waiting for transfers between devices: none -> 16 us  [shift(): return lax.ppermute(x, axis, [(i, (i + by) % n) for i in range(n)])]
    dot_general x5 -> x0, matrix products: 4.98 us -> none  [the longest x1 1.75 us: shards(): jnp.dot(agg_low.T, grad_pre, preferred_element_type=jnp.float32)]
    pallas_call x0 -> x7, Pallas kernels: none -> 4.83 us  [the longest x1 1.22 us: shards(): call(dense_kernel(n_row, n_col), (jax.ShapeDtypeStruct((n_col * tile, n_r...]
    all_to_all x0 -> x1, starting transfers between devices: none -> 4.57 us  [shards(): packed = lax.all_to_all(packed, ('row', 'col'), 0, 0)]
  transfers between devices with their start and end apart: 3 -> 13, of which waited for: 3 -> 9; matrix products, arithmetic and copies ran while one was open for 2% -> 1% of each run, Pallas kernels for 0% -> 3%
where the time goes in v1:
time: 63.3 us; the launch traced here: 63 us
  starting transfers between devices  20.8 us (33%)
  blocking collectives  18.1 us (29%)
  waiting for transfers between devices  16 us (25%)
  Pallas kernels  4.83 us (8%)
  local copies, waits for them, and re-layouts  1.83 us (3%)
  between operations  0.73 us (1%)
  other arithmetic  0.72 us (1%)
    all_gather x1, blocking collectives, shards(): lax.all_gather(part, ('row', 'col'), axis=0, tiled=True).astype(F32)  18.1 us
    ppermute x12, starting transfers between devices, shift(): return lax.ppermute(x, axis, [(i, (i + by) % n) for i in range(n)])  16.3 us
    ppermute x12, waiting for transfers between devices, shift(): return lax.ppermute(x, axis, [(i, (i + by) % n) for i in range(n)])  16 us
    all_to_all x1, starting transfers between devices, shards(): packed = lax.all_to_all(packed, ('row', 'col'), 0, 0)  4.57 us
    unnamed x14, local copies, waits for them, and re-layouts  1.83 us
  transfers between devices with their start and end apart: 13, of which 9 were waited for; matrix products, arithmetic and copies ran while one was open for 1% of the time, Pallas kernels for 3%

profile of v1, /device:TPU:0, one launch (start us, length us, event | category | flops | bytes accessed | tf_op | source)
XLA Modules:
  0.0 63.0 jit_solution(9984109827761778875)
XLA Ops:
  0.6 0.0 copy-start.4
  0.6 5.1 %collective-permute-start = (bf16[128,256]{1,0:T(8,128)(2,1)}, bf16[128,256]{1,0:T(8,128)(2,1)S(1)}, u32[]{:S(2)}, u32[]{:S(2)}) collective-permute-start(bf16[128,256]{1,0:T(8,128)(2,1)} %refs_0_.1), channel_id=1, source_target_pairs={{0,12},{4,0},{8,4},{12,8},{1,13},{5,1},{9,5},{13,9},{2,14},{6,2},{... | collective-permute-start | bytes 196616 | tf_op jit(solution)/shard_map/ppermute | solution.py:133
  5.7 0.0 collective-permute-start.1
  5.7 1.0 %collective-permute-start.2 = (bf16[128,256]{1,0:T(8,128)(2,1)}, bf16[128,256]{1,0:T(8,128)(2,1)S(1)}, u32[]{:S(2)}, u32[]{:S(2)}) collective-permute-start(bf16[128,256]{1,0:T(8,128)(2,1)} %refs_0_.1), channel_id=1, source_target_pairs={{0,4},{4,8},{8,12},{12,0},{1,5},{5,9},{9,13},{13,1},{2,6},{6,10},{... | collective-permute-start | bytes 196616 | tf_op jit(solution)/shard_map/ppermute | solution.py:133
  6.8 0.8 %copy.11.cols_ref = s32[4,1,2]{2,1,0:T(1,128)S(1)} copy(s32[4,1,2]{0,2,1:T(2,128)} %param.9) | data formatting | bytes 64 | tf_op args[2]
  7.5 0.0 copy-done.4
  7.5 0.1 copy.12.cnts_ref
  7.6 0.0 copy-start
  7.6 0.9 %copy-done = bf16[4,1,2,128,128]{4,3,2,1,0:T(8,128)(2,1)S(1)} copy-done((bf16[4,1,2,128,128]{4,3,2,1,0:T(8,128)(2,1)S(1)}, bf16[4,1,2,128,128]{4,3,2,1,0:T(8,128)(2,1)}, u32[]{:S(2)}) %copy-start) | copy-done | bytes 262168
  8.6 0.0 copy-start.2
  8.6 1.2 %shard_map.102 = (bf16[512,512]{1,0:T(8,128)(2,1)S(1)}, bf16[512,512]{1,0:T(8,128)(2,1)S(1)}) custom-call(s32[4,1,2]{2,1,0:T(1,128)S(1)} %copy.11.cols_ref, s32[4,1]{1,0:T(4,128)S(1)} %copy.12.cnts_ref, bf16[4,1,2,128,128]{4,3,2,1,0:T(8,128)(2,1)S(1)} %copy-done), custom_call_target="tpu_custom_call" | custom-call | tf_op jit(solution)/shard_map/pallas_call | solution.py:143
  9.8 0.0 collective-permute-done.refs_1_
  9.8 2.6 %collective-permute-done.1.refs_2_ = bf16[128,256]{1,0:T(8,128)(2,1)S(1)} collective-permute-done((bf16[128,256]{1,0:T(8,128)(2,1)}, bf16[128,256]{1,0:T(8,128)(2,1)S(1)}, u32[]{:S(2)}, u32[]{:S(2)}) %collective-permute-start.1) | collective-permute-done | bytes 65568 | tf_op jit(solution)/shard_map/ppermute | solution.py:133
  12.4 0.0 collective-permute-done.2.refs_3_
  12.4 0.0 copy-done.2
  12.4 0.0 copy-start.3
  12.4 0.3 shard_map.103
  12.8 0.1 collective-permute-start.3
  12.8 0.0 copy-start.5
  12.8 1.6 %collective-permute-start.4 = (bf16[128,256]{1,0:T(8,128)(2,1)S(1)}, bf16[128,256]{1,0:T(8,128)(2,1)S(1)}, u32[]{:S(2)}, u32[]{:S(2)}) collective-permute-start(bf16[128,256]{1,0:T(8,128)(2,1)S(1)} %get-tuple-element.23), channel_id=1, source_target_pairs={{0,2},{1,3},{2,0},{3,1},{4,6},{5,7},{6,4},{7,5},{8,10},{9,11},{10,... | collective-permute-start | bytes 196616 | tf_op jit(solution)/shard_map/ppermute | solution.py:133
  14.4 1.4 %collective-permute-start.5 = (bf16[128,256]{1,0:T(8,128)(2,1)S(1)}, bf16[128,256]{1,0:T(8,128)(2,1)S(1)}, u32[]{:S(2)}, u32[]{:S(2)}) collective-permute-start(bf16[128,256]{1,0:T(8,128)(2,1)S(1)} %get-tuple-element.24), channel_id=1, source_target_pairs={{0,3},{1,0},{2,1},{3,2},{4,7},{5,4},{6,5},{7,6},{8,11},{9,8},{10,9... | collective-permute-start | bytes 196616 | tf_op jit(solution)/shard_map/ppermute | solution.py:133
  15.8 0.0 copy-done.5
  15.8 0.8 %collective-permute-done.3.refs_1_ = bf16[128,256]{1,0:T(8,128)(2,1)S(1)} collective-permute-done((bf16[128,256]{1,0:T(8,128)(2,1)S(1)}, bf16[128,256]{1,0:T(8,128)(2,1)S(1)}, u32[]{:S(2)}, u32[]{:S(2)}) %collective-permute-start.3) | collective-permute-done | bytes 65568 | tf_op jit(solution)/shard_map/ppermute | solution.py:133
  16.6 0.9 %collective-permute-done.4.refs_2_ = bf16[128,256]{1,0:T(8,128)(2,1)S(1)} collective-permute-done((bf16[128,256]{1,0:T(8,128)(2,1)S(1)}, bf16[128,256]{1,0:T(8,128)(2,1)S(1)}, u32[]{:S(2)}, u32[]{:S(2)}) %collective-permute-start.4) | collective-permute-done | bytes 65568 | tf_op jit(solution)/shard_map/ppermute | solution.py:133
  17.5 0.2 collective-permute-done.5.refs_3_
  17.7 0.0 copy-done.1
  17.7 0.0 copy-done.3
  17.7 0.8 %shard_map.104 = (bf16[128,256]{1,0:T(8,128)(2,1)}, bf16[128,256]{1,0:T(8,128)(2,1)S(1)}, bf16[128,256]{1,0:T(8,128)(2,1)S(1)}, bf16[128,256]{1,0:T(8,128)(2,1)S(1)}) custom-call(bf16[256,256]{1,0:T(8,128)(2,1)S(1)} %copy-done.1, bf16[1,256]{1,0:T(2,128)(2,1)S(1)} %reshape.14.b_ref, bf16[128,256]{1,0:T(8,128)(2,1)S(1)} %copy-done.3, ...), custom_call_target="tpu_custom_call" | custom-call | tf_op jit(solution)/shard_map/pallas_call | solution.py:154
  18.5 0.9 %shard_map.107 = bf16[16,32,256]{2,1,0:T(8,128)(2,1)} custom-call(bf16[128,256]{1,0:T(8,128)(2,1)S(1)} %get-tuple-element.32.agg_ref, bf16[128,256]{1,0:T(8,128)(2,1)S(1)} %get-tuple-element.33.pre_ref), custom_call_target="tpu_custom_call" | custom-call | tf_op jit(solution)/shard_map/pallas_call | solution.py:161
  19.4 4.6 %all-to-all-start = ((bf16[16,32,256]{2,1,0:T(8,128)(2,1)}), bf16[16,32,256]{2,1,0:T(8,128)(2,1)S(1)}, u32[]{:S(2)}, u32[]{:S(2)}) async-start(bf16[16,32,256]{2,1,0:T(8,128)(2,1)} %shard_map.107), calls=%async_computation | async-start | bytes 524288 | tf_op jit(solution)/shard_map/all_to_all | solution.py:166
  24.0 1.7 %collective-permute-start.6 = (bf16[128,256]{1,0:T(8,128)(2,1)S(1)}, bf16[128,256]{1,0:T(8,128)(2,1)S(1)}, u32[]{:S(2)}, u32[]{:S(2)}) collective-permute-start(bf16[128,256]{1,0:T(8,128)(2,1)S(1)} %get-tuple-element.27.refs_0_), channel_id=1, source_target_pairs={{0,3},{1,0},{2,1},{3,2},{4,7},{5,4},{6,5},{7,6},{8,11},{9,8},{10,9... | collective-permute-start | bytes 196616 | tf_op jit(solution)/shard_map/ppermute | solution.py:133
  25.7 0.4 collective-permute-start.7
  26.0 0.1 collective-permute-start.8
  26.2 2.8 %collective-permute-done.6.refs_1_ = bf16[128,256]{1,0:T(8,128)(2,1)S(1)} collective-permute-done((bf16[128,256]{1,0:T(8,128)(2,1)S(1)}, bf16[128,256]{1,0:T(8,128)(2,1)S(1)}, u32[]{:S(2)}, u32[]{:S(2)}) %collective-permute-start.6) | collective-permute-done | bytes 65568 | tf_op jit(solution)/shard_map/ppermute | solution.py:133
  29.0 3.1 %collective-permute-done.7.refs_2_ = bf16[128,256]{1,0:T(8,128)(2,1)S(1)} collective-permute-done((bf16[128,256]{1,0:T(8,128)(2,1)S(1)}, bf16[128,256]{1,0:T(8,128)(2,1)S(1)}, u32[]{:S(2)}, u32[]{:S(2)}) %collective-permute-start.7) | collective-permute-done | bytes 65568 | tf_op jit(solution)/shard_map/ppermute | solution.py:133
  32.0 0.0 collective-permute-done.8.refs_3_
  32.1 0.3 shard_map.105
  32.4 3.0 %collective-permute-start.10 = (bf16[128,256]{1,0:T(8,128)(2,1)S(1)}, bf16[128,256]{1,0:T(8,128)(2,1)S(1)}, u32[]{:S(2)}, u32[]{:S(2)}) collective-permute-start(bf16[128,256]{1,0:T(8,128)(2,1)S(1)} %get-tuple-element.30), channel_id=1, source_target_pairs={{0,8},{4,12},{8,0},{12,4},{1,9},{5,13},{9,1},{13,5},{2,10},{6,14},... | collective-permute-start | bytes 196616 | tf_op jit(solution)/shard_map/ppermute | solution.py:133
  35.3 1.5 %collective-permute-start.11 = (bf16[128,256]{1,0:T(8,128)(2,1)S(1)}, bf16[128,256]{1,0:T(8,128)(2,1)S(1)}, u32[]{:S(2)}, u32[]{:S(2)}) collective-permute-start(bf16[128,256]{1,0:T(8,128)(2,1)S(1)} %get-tuple-element.31), channel_id=1, source_target_pairs={{0,12},{4,0},{8,4},{12,8},{1,13},{5,1},{9,5},{13,9},{2,14},{6,2},{... | collective-permute-start | bytes 196616 | tf_op jit(solution)/shard_map/ppermute | solution.py:133
  36.9 0.5 collective-permute-start.9
  37.4 0.6 collective-permute-done.10.refs_2_
  37.9 2.0 %collective-permute-done.11.refs_3_ = bf16[128,256]{1,0:T(8,128)(2,1)S(1)} collective-permute-done((bf16[128,256]{1,0:T(8,128)(2,1)S(1)}, bf16[128,256]{1,0:T(8,128)(2,1)S(1)}, u32[]{:S(2)}, u32[]{:S(2)}) %collective-permute-start.11) | collective-permute-done | bytes 65568 | tf_op jit(solution)/shard_map/ppermute | solution.py:133
  39.9 3.0 %collective-permute-done.9.refs_1_ = bf16[128,256]{1,0:T(8,128)(2,1)S(1)} collective-permute-done((bf16[128,256]{1,0:T(8,128)(2,1)S(1)}, bf16[128,256]{1,0:T(8,128)(2,1)S(1)}, u32[]{:S(2)}, u32[]{:S(2)}) %collective-permute-start.9) | collective-permute-done | bytes 65568 | tf_op jit(solution)/shard_map/ppermute | solution.py:133
  42.9 0.7 %shard_map.106 = bf16[128,256]{1,0:T(8,128)(2,1)} custom-call(bf16[128,256]{1,0:T(8,128)(2,1)S(1)} %get-tuple-element.28.refs_0_, bf16[128,256]{1,0:T(8,128)(2,1)S(1)} %collective-permute-done.9.refs_1_, bf16[128,256]{1,0:T(8,128)(2,1)S(1)} %collective-permute-done.10.refs_2_, bf16[128,256]{1,0:T(8,128)(2,1)S(1)} %collective-permute-done.11.refs_3_), custom_call_target="tpu_custom_call" | custom-call | tf_op jit(solution)/shard_map/pallas_call | solution.py:181
  43.6 0.0 all-to-all-done.in_ref
  43.6 0.6 shard_map.108
  44.2 18.1 %all_gather.3 = bf16[256,256]{1,0:T(8,128)(2,1)S(1)} all-gather(bf16[16,256]{1,0:T(8,128)(2,1)S(1)} %get-tuple-element.34), channel_id=1, replica_groups=mesh['groups'=2,'row'=4,'col'=4] {'row','col'}, dimensions={0}, use_global_device_ids=true | all-gather | bytes 139264 | tf_op jit(solution)/shard_map/all_gather | solution.py:172
  62.2 0.7 %convert_element_type.3 = f32[256,256]{1,0:T(8,128)} convert(bf16[256,256]{1,0:T(8,128)(2,1)S(1)} %all_gather.3) | non-fusion elementwise | flops 65536 | bytes 393216 | tf_op jit(solution)/shard_map/convert_element_type | solution.py:172
  (2 shorter events, 0.0 us)
Async XLA Ops:
  0.6 6.9 %copy-start.4 = (s32[4,1]{0,1:T(1,128)S(1)}, s32[4,1]{0,1:T(1,128)}, u32[]{:S(2)}) copy-start(s32[4,1]{0,1:T(1,128)} %param.10) | copy-start | bytes 52
  0.6 9.2 %collective-permute-start = (bf16[128,256]{1,0:T(8,128)(2,1)}, bf16[128,256]{1,0:T(8,128)(2,1)S(1)}, u32[]{:S(2)}, u32[]{:S(2)}) collective-permute-start(bf16[128,256]{1,0:T(8,128)(2,1)} %refs_0_.1), channel_id=1, source_target_pairs={{0,12},{4,0},{8,4},{12,8},{1,13},{5,1},{9,5},{13,9},{2,14},{6,2},{... | collective-permute-start | bytes 196616 | tf_op jit(solution)/shard_map/ppermute | solution.py:133
  5.7 6.7 %collective-permute-start.1 = (bf16[128,256]{1,0:T(8,128)(2,1)}, bf16[128,256]{1,0:T(8,128)(2,1)S(1)}, u32[]{:S(2)}, u32[]{:S(2)}) collective-permute-start(bf16[128,256]{1,0:T(8,128)(2,1)} %refs_0_.1), channel_id=1, source_target_pairs={{0,8},{4,12},{8,0},{12,4},{1,9},{5,13},{9,1},{13,5},{2,10},{6,14},... | collective-permute-start | bytes 196616 | tf_op jit(solution)/shard_map/ppermute | solution.py:133
  5.7 6.7 %collective-permute-start.2 = (bf16[128,256]{1,0:T(8,128)(2,1)}, bf16[128,256]{1,0:T(8,128)(2,1)S(1)}, u32[]{:S(2)}, u32[]{:S(2)}) collective-permute-start(bf16[128,256]{1,0:T(8,128)(2,1)} %refs_0_.1), channel_id=1, source_target_pairs={{0,4},{4,8},{8,12},{12,0},{1,5},{5,9},{9,13},{13,1},{2,6},{6,10},{... | collective-permute-start | bytes 196616 | tf_op jit(solution)/shard_map/ppermute | solution.py:133
  7.6 1.0 %copy-start = (bf16[4,1,2,128,128]{4,3,2,1,0:T(8,128)(2,1)S(1)}, bf16[4,1,2,128,128]{4,3,2,1,0:T(8,128)(2,1)}, u32[]{:S(2)}) copy-start(bf16[4,1,2,128,128]{4,3,2,1,0:T(8,128)(2,1)} %tiles_ref.1) | copy-start | bytes 786436
  8.6 3.9 %copy-start.2 = (bf16[128,256]{1,0:T(8,128)(2,1)S(1)}, bf16[128,256]{1,0:T(8,128)(2,1)}, u32[]{:S(2)}) copy-start(bf16[128,256]{1,0:T(8,128)(2,1)} %refs_0_.1) | copy-start | bytes 196612
  12.4 5.3 %copy-start.1 = (bf16[256,256]{1,0:T(8,128)(2,1)S(1)}, bf16[256,256]{1,0:T(8,128)(2,1)}, u32[]{:S(2)}) copy-start(bf16[256,256]{1,0:T(8,128)(2,1)} %w_ref.1) | copy-start | bytes 393220
  12.4 5.2 %copy-start.3 = (bf16[128,256]{1,0:T(8,128)(2,1)S(1)}, bf16[128,256]{1,0:T(8,128)(2,1)}, u32[]{:S(2)}) copy-start(bf16[128,256]{1,0:T(8,128)(2,1)} %cot_ref.1) | copy-start | bytes 196612
  12.8 3.8 %collective-permute-start.3 = (bf16[128,256]{1,0:T(8,128)(2,1)S(1)}, bf16[128,256]{1,0:T(8,128)(2,1)S(1)}, u32[]{:S(2)}, u32[]{:S(2)}) collective-permute-start(bf16[128,256]{1,0:T(8,128)(2,1)S(1)} %get-tuple-element.22), channel_id=1, source_target_pairs={{0,1},{1,2},{2,3},{3,0},{4,5},{5,6},{6,7},{7,4},{8,9},{9,10},{10,1... | collective-permute-start | bytes 196616 | tf_op jit(solution)/shard_map/ppermute | solution.py:133
  12.8 2.9 %copy-start.5 = (bf16[256]{0:T(256)(128)(2,1)S(1)}, bf16[256]{0:T(256)(128)(2,1)}, u32[]{:S(2)}) copy-start(bf16[256]{0:T(256)(128)(2,1)} %param.12) | copy-start | bytes 1540
  12.8 4.6 %collective-permute-start.4 = (bf16[128,256]{1,0:T(8,128)(2,1)S(1)}, bf16[128,256]{1,0:T(8,128)(2,1)S(1)}, u32[]{:S(2)}, u32[]{:S(2)}) collective-permute-start(bf16[128,256]{1,0:T(8,128)(2,1)S(1)} %get-tuple-element.23), channel_id=1, source_target_pairs={{0,2},{1,3},{2,0},{3,1},{4,6},{5,7},{6,4},{7,5},{8,10},{9,11},{10,... | collective-permute-start | bytes 196616 | tf_op jit(solution)/shard_map/ppermute | solution.py:133
  14.4 3.3 %collective-permute-start.5 = (bf16[128,256]{1,0:T(8,128)(2,1)S(1)}, bf16[128,256]{1,0:T(8,128)(2,1)S(1)}, u32[]{:S(2)}, u32[]{:S(2)}) collective-permute-start(bf16[128,256]{1,0:T(8,128)(2,1)S(1)} %get-tuple-element.24), channel_id=1, source_target_pairs={{0,3},{1,0},{2,1},{3,2},{4,7},{5,4},{6,5},{7,6},{8,11},{9,8},{10,9... | collective-permute-start | bytes 196616 | tf_op jit(solution)/shard_map/ppermute | solution.py:133
  19.4 24.2 %all-to-all-start = ((bf16[16,32,256]{2,1,0:T(8,128)(2,1)}), bf16[16,32,256]{2,1,0:T(8,128)(2,1)S(1)}, u32[]{:S(2)}, u32[]{:S(2)}) async-start(bf16[16,32,256]{2,1,0:T(8,128)(2,1)} %shard_map.107), calls=%async_computation | async-start | bytes 524288 | tf_op jit(solution)/shard_map/all_to_all | solution.py:166
  24.0 5.0 %collective-permute-start.6 = (bf16[128,256]{1,0:T(8,128)(2,1)S(1)}, bf16[128,256]{1,0:T(8,128)(2,1)S(1)}, u32[]{:S(2)}, u32[]{:S(2)}) collective-permute-start(bf16[128,256]{1,0:T(8,128)(2,1)S(1)} %get-tuple-element.27.refs_0_), channel_id=1, source_target_pairs={{0,3},{1,0},{2,1},{3,2},{4,7},{5,4},{6,5},{7,6},{8,11},{9,8},{10,9... | collective-permute-start | bytes 196616 | tf_op jit(solution)/shard_map/ppermute | solution.py:133
  25.7 6.4 %collective-permute-start.7 = (bf16[128,256]{1,0:T(8,128)(2,1)S(1)}, bf16[128,256]{1,0:T(8,128)(2,1)S(1)}, u32[]{:S(2)}, u32[]{:S(2)}) collective-permute-start(bf16[128,256]{1,0:T(8,128)(2,1)S(1)} %get-tuple-element.27.refs_0_), channel_id=1, source_target_pairs={{0,2},{1,3},{2,0},{3,1},{4,6},{5,7},{6,4},{7,5},{8,10},{9,11},{10,... | collective-permute-start | bytes 196616 | tf_op jit(solution)/shard_map/ppermute | solution.py:133
  26.0 6.0 %collective-permute-start.8 = (bf16[128,256]{1,0:T(8,128)(2,1)S(1)}, bf16[128,256]{1,0:T(8,128)(2,1)S(1)}, u32[]{:S(2)}, u32[]{:S(2)}) collective-permute-start(bf16[128,256]{1,0:T(8,128)(2,1)S(1)} %get-tuple-element.27.refs_0_), channel_id=1, source_target_pairs={{0,1},{1,2},{2,3},{3,0},{4,5},{5,6},{6,7},{7,4},{8,9},{9,10},{10,1... | collective-permute-start | bytes 196616 | tf_op jit(solution)/shard_map/ppermute | solution.py:133
  32.4 5.6 %collective-permute-start.10 = (bf16[128,256]{1,0:T(8,128)(2,1)S(1)}, bf16[128,256]{1,0:T(8,128)(2,1)S(1)}, u32[]{:S(2)}, u32[]{:S(2)}) collective-permute-start(bf16[128,256]{1,0:T(8,128)(2,1)S(1)} %get-tuple-element.30), channel_id=1, source_target_pairs={{0,8},{4,12},{8,0},{12,4},{1,9},{5,13},{9,1},{13,5},{2,10},{6,14},... | collective-permute-start | bytes 196616 | tf_op jit(solution)/shard_map/ppermute | solution.py:133
  35.3 4.6 %collective-permute-start.11 = (bf16[128,256]{1,0:T(8,128)(2,1)S(1)}, bf16[128,256]{1,0:T(8,128)(2,1)S(1)}, u32[]{:S(2)}, u32[]{:S(2)}) collective-permute-start(bf16[128,256]{1,0:T(8,128)(2,1)S(1)} %get-tuple-element.31), channel_id=1, source_target_pairs={{0,12},{4,0},{8,4},{12,8},{1,13},{5,1},{9,5},{13,9},{2,14},{6,2},{... | collective-permute-start | bytes 196616 | tf_op jit(solution)/shard_map/ppermute | solution.py:133
  36.9 6.1 %collective-permute-start.9 = (bf16[128,256]{1,0:T(8,128)(2,1)S(1)}, bf16[128,256]{1,0:T(8,128)(2,1)S(1)}, u32[]{:S(2)}, u32[]{:S(2)}) collective-permute-start(bf16[128,256]{1,0:T(8,128)(2,1)S(1)} %get-tuple-element.29), channel_id=1, source_target_pairs={{0,4},{4,8},{8,12},{12,0},{1,5},{5,9},{9,13},{13,1},{2,6},{6,10},{... | collective-permute-start | bytes 196616 | tf_op jit(solution)/shard_map/ppermute | solution.py:133

commit v2 on v0

v2 whole, which is shorter than its diff:
```python
import jax
import jax.numpy as jnp
from jax import lax
from jax.experimental import pallas as pl
from jax.experimental.pallas import tpu as pltpu
from jax.sharding import PartitionSpec as P

BF = jnp.bfloat16
F32 = jnp.float32
LIMIT = 48 * 1024 * 1024
PAD = 16


def dot(a, b, ca=1, cb=0):
    return lax.dot_general(a, b, (((ca,), (cb,)), ((), ())), preferred_element_type=F32)


def call(body, outs, smem=0, count=1):
    vm = pl.BlockSpec(memory_space=pltpu.VMEM)
    sm = pl.BlockSpec(memory_space=pltpu.SMEM)
    return pl.pallas_call(
        body,
        in_specs=[sm] * smem + [vm] * (count - smem),
        out_specs=jax.tree.map(lambda _: vm, outs),
        out_shape=outs,
        compiler_params=pltpu.CompilerParams(vmem_limit_bytes=LIMIT),
    )


def shape(*dims, dtype=BF):
    return jax.ShapeDtypeStruct(dims, dtype)


def dense_kernel(n_row):
    def body(cols_ref, cnts_ref, tiles_ref, a_ref, at_ref):
        trows, _, slots, tile, _ = tiles_ref.shape
        r = lax.axis_index("row")
        a_ref[...] = jnp.zeros_like(a_ref)
        at_ref[...] = jnp.zeros_like(at_ref)

        def put(step, carry):
            t = step // slots
            k = step % slots

            @pl.when(k < cnts_ref[t, 0])
            def _():
                j = cols_ref[t, 0, k]
                p = lax.rem(j - r + n_row, n_row)
                here = tiles_ref[t, 0, k]
                ts = pl.ds(pl.multiple_of(t * tile, tile), tile)
                a_ref[ts, pl.ds(pl.multiple_of(p * tile, tile), tile)] = here
                at_ref[pl.ds(pl.multiple_of(j * tile, tile), tile), ts] = here.T

            return carry

        lax.fori_loop(0, trows * slots, put, 0)

    return body


def forward_kernel(a_ref, *refs):
    out_ref = refs[-1]
    tile = refs[0].shape[0]
    x = jnp.concatenate([ref[...] for ref in refs[:-1]], axis=0)
    for q in range(out_ref.shape[0]):
        out_ref[q] = dot(a_ref[q * tile : (q + 1) * tile, :], x).astype(BF)


def total_of(ref, first, rows):
    total = ref[0, first : first + rows, :].astype(F32)
    for i in range(1, ref.shape[0]):
        total = total + ref[i, first : first + rows, :].astype(F32)
    return total


def two_rows(line):
    high = line.astype(BF).astype(F32)
    which = lax.broadcasted_iota(jnp.int32, (PAD, line.shape[1]), 0)
    return jnp.where(which == 0, high, jnp.where(which == 1, line - high, 0.0)).astype(BF)


def middle_kernel(parts_ref, w_ref, b_ref, cot_ref, act_ref, out_ref):
    n_col, tile, width = parts_ref.shape
    piece = width // n_col
    agg = total_of(parts_ref, 0, tile).astype(BF)
    preact = dot(agg, w_ref[...]) + b_ref[...].astype(F32)
    sig = jax.nn.sigmoid(preact)
    act_ref[...] = (preact * sig).astype(BF)
    grad = cot_ref[...].astype(F32) * (sig * (1.0 + preact * (1.0 - sig)))
    grad = grad.astype(BF)
    gagg = dot(grad, w_ref[...], 1, 1).astype(BF)
    local = dot(agg, grad, 0, 0).astype(BF)
    tail = two_rows(jnp.sum(grad.astype(F32), axis=0, keepdims=True))
    for i in range(n_col):
        out_ref[i, :tile, :] = gagg
        out_ref[i, tile : tile + piece, :] = local[i * piece : (i + 1) * piece, :]
        out_ref[i, tile + piece :, :] = tail


def backward_kernel(at_ref, in_ref, out_ref):
    n_col = in_ref.shape[0]
    width = in_ref.shape[2]
    tile = at_ref.shape[0] // out_ref.shape[0]
    piece = width // n_col
    g = jnp.concatenate([in_ref[i, :tile, :] for i in range(n_col)], axis=0)
    part = total_of(in_ref, tile, piece).astype(BF)
    lines = total_of(in_ref, tile + piece, PAD)
    tail = two_rows(lines[0:1] + lines[1:2])
    for p in range(out_ref.shape[0]):
        out_ref[p, :tile, :] = dot(at_ref[p * tile : (p + 1) * tile, :], g).astype(BF)
        out_ref[p, tile : tile + piece, :] = part
        out_ref[p, tile + piece :, :] = tail


def quarter_kernel(in_ref, feat_ref, out_ref, bias_ref):
    n_col, piece, _ = out_ref.shape
    tile = feat_ref.shape[0]
    part = total_of(in_ref, tile, piece).astype(BF)
    for i in range(n_col):
        out_ref[i] = part
    feat_ref[...] = total_of(in_ref, 0, tile).astype(BF)
    lines = total_of(in_ref, tile + piece, PAD)
    bias_ref[...] = lines[0:1] + lines[1:2]


def widen_kernel(in_ref, out_ref):
    n_col, piece, _ = in_ref.shape
    for i in range(n_col):
        out_ref[i * piece : (i + 1) * piece, :] = in_ref[i].astype(F32)


def shards(n_row, n_col, features, adj_tiles, columns, counts, weight, bias_term, cotangent):
    tile, width = features.shape
    piece = width // n_col
    xs = [features]
    for p in range(1, n_row):
        xs.append(lax.ppermute(features, "row", [(i, (i - p) % n_row) for i in range(n_row)]))
    a, at = call(
        dense_kernel(n_row),
        (shape(n_col * tile, n_row * tile), shape(n_row * tile, n_col * tile)),
        smem=2,
        count=3,
    )(columns, counts, adj_tiles)
    parts = call(forward_kernel, shape(n_col, tile, width), count=1 + n_row)(a, *xs)
    parts = lax.all_to_all(parts, "col", 0, 0)
    act, packed = call(
        middle_kernel,
        (shape(tile, width), shape(n_col, tile + piece + PAD, width)),
        count=4,
    )(parts, weight, bias_term.reshape(1, width), cotangent)
    packed = lax.all_to_all(packed, "col", 0, 0)
    packed = call(backward_kernel, shape(n_row, tile + piece + PAD, width), count=2)(at, packed)
    packed = lax.all_to_all(packed, "row", 0, 0)
    grad_features, quarters, grad_bias = call(
        quarter_kernel,
        (shape(tile, width), shape(n_col, piece, width), shape(1, width, dtype=F32)),
        count=1,
    )(packed)
    quarters = lax.all_to_all(quarters, "col", 0, 0)
    grad_weight = call(widen_kernel, shape(width, width, dtype=F32), count=1)(quarters)
    return act, grad_features, grad_weight, grad_bias.reshape(width)


def solution(mesh):
    n_row, n_col = mesh.shape["row"], mesh.shape["col"]
    placed = (
        P(("groups", "row", "col"), None),
        P(("groups", "row"), "col", None, None, None),
        P(("groups", "row"), "col", None),
        P(("groups", "row"), "col"),
        P(),
        P(),
        P(("groups", "row", "col"), None),
    )

    def body(*args):
        return shards(n_row, n_col, *args)

    return jax.shard_map(
        body,
        mesh=mesh,
        in_specs=placed,
        out_specs=(
            P(("groups", "row", "col"), None),
            P(("groups", "row", "col"), None),
            P("groups", None),
            P("groups"),
        ),
        check_vma=False,
    )
```

time: 184 us -> 58.5 us (0.32)
  waiting for transfers between devices: 103 us -> 8.74 us
  blocking collectives: 55 us -> 32.6 us
  between operations: 13.8 us -> 0.7 us
  starting transfers between devices: 0.12 us -> 9.65 us
  matrix products: 4.98 us -> 0 us
  Pallas kernels: 0 us -> 4.63 us
  local copies, waits for them, and re-layouts: 4.29 us -> 1.83 us
  other arithmetic: 2.14 us -> 0 us
    psum x2 -> x0, waiting for transfers between devices: 79.7 us -> none  [the longest x1 47 us: shards(): lax.psum((local_weight, local_bias), ('row', 'col'))]
    psum x1 -> x0, blocking collectives: 33.3 us -> none  [shards(): lax.psum((local_weight, local_bias), ('row', 'col'))]
    all_to_all x0 -> x3, blocking collectives: none -> 32.6 us  [the longest x1 15.4 us: shards(): packed = lax.all_to_all(packed, 'row', 0, 0)]
    reduce_scatter x1 -> x0, waiting for transfers between devices: 23 us -> none  [shards(): lax.psum_scatter(partial_value.reshape(col_tiles * tile_size, feat_width)...]
    all_gather x2 -> x0, blocking collectives: 21.7 us -> none  [the longest x1 16 us: shards(): gathered = lax.all_gather(features, 'row', axis=0, tiled=True)]
    ppermute x0 -> x3, starting transfers between devices: none -> 6.11 us  [shards(): lax.ppermute(features, 'row', [(i, (i - p) % n_row) for i in range(n_row)])]
    all_to_all x0 -> x1, waiting for transfers between devices: none -> 5.98 us  [shards(): parts = lax.all_to_all(parts, 'col', 0, 0)]
    dot_general x5 -> x0, matrix products: 4.98 us -> none  [the longest x1 1.75 us: shards(): jnp.dot(agg_low.T, grad_pre, preferred_element_type=jnp.float32)]
  transfers between devices with their start and end apart: 3 -> 4, of which waited for: 3 -> 2; matrix products, arithmetic and copies ran while one was open for 2% -> 1% of each run, Pallas kernels for 0% -> 2%
where the time goes in v2:
time: 58.5 us; the launch traced here: 58.1 us
  blocking collectives  32.6 us (56%)
  starting transfers between devices  9.65 us (16%)
  waiting for transfers between devices  8.74 us (15%)
  Pallas kernels  4.63 us (8%)
  local copies, waits for them, and re-layouts  1.83 us (3%)
  between operations  0.7 us (1%)
    all_to_all x1, blocking collectives, shards(): packed = lax.all_to_all(packed, 'row', 0, 0)  15.4 us
    all_to_all x1, blocking collectives, shards(): packed = lax.all_to_all(packed, 'col', 0, 0)  10.1 us
    all_to_all x1, blocking collectives, shards(): quarters = lax.all_to_all(quarters, 'col', 0, 0)  7.01 us
    ppermute x3, starting transfers between devices, shards(): lax.ppermute(features, 'row', [(i, (i - p) % n_row) for i in range(n_row)])  6.11 us
    all_to_all x1, waiting for transfers between devices, shards(): parts = lax.all_to_all(parts, 'col', 0, 0)  5.98 us
    all_to_all x1, starting transfers between devices, shards(): parts = lax.all_to_all(parts, 'col', 0, 0)  3.54 us
    ppermute x3, waiting for transfers between devices, shards(): lax.ppermute(features, 'row', [(i, (i - p) % n_row) for i in range(n_row)])  2.76 us
    unnamed x14, local copies, waits for them, and re-layouts  1.83 us
  transfers between devices with their start and end apart: 4, of which 2 were waited for; matrix products, arithmetic and copies ran while one was open for 1% of the time, Pallas kernels for 2%

profile of v2, /device:TPU:0, one launch (start us, length us, event | category | flops | bytes accessed | tf_op | source)
XLA Modules:
  0.0 58.1 jit_solution(259188748955776761)
XLA Ops:
  0.6 0.0 copy-start.4
  0.6 5.1 %collective-permute-start = (bf16[128,256]{1,0:T(8,128)(2,1)}, bf16[128,256]{1,0:T(8,128)(2,1)S(1)}, u32[]{:S(2)}, u32[]{:S(2)}) collective-permute-start(bf16[128,256]{1,0:T(8,128)(2,1)} %refs_0_.1), channel_id=1, source_target_pairs={{0,12},{4,0},{8,4},{12,8},{1,13},{5,1},{9,5},{13,9},{2,14},{6,2},{... | collective-permute-start | bytes 196616 | tf_op jit(solution)/shard_map/ppermute | solution.py:137
  5.7 0.0 collective-permute-start.1
  5.7 1.0 %collective-permute-start.2 = (bf16[128,256]{1,0:T(8,128)(2,1)}, bf16[128,256]{1,0:T(8,128)(2,1)S(1)}, u32[]{:S(2)}, u32[]{:S(2)}) collective-permute-start(bf16[128,256]{1,0:T(8,128)(2,1)} %refs_0_.1), channel_id=1, source_target_pairs={{0,4},{4,8},{8,12},{12,0},{1,5},{5,9},{9,13},{13,1},{2,6},{6,10},{... | collective-permute-start | bytes 196616 | tf_op jit(solution)/shard_map/ppermute | solution.py:137
  6.8 0.8 %copy.11.cols_ref = s32[4,1,2]{2,1,0:T(1,128)S(1)} copy(s32[4,1,2]{0,2,1:T(2,128)} %param.9) | data formatting | bytes 64 | tf_op args[2]
  7.5 0.0 copy-done.4
  7.5 0.1 copy.12.cnts_ref
  7.6 0.0 copy-start
  7.6 0.9 %copy-done = bf16[4,1,2,128,128]{4,3,2,1,0:T(8,128)(2,1)S(1)} copy-done((bf16[4,1,2,128,128]{4,3,2,1,0:T(8,128)(2,1)S(1)}, bf16[4,1,2,128,128]{4,3,2,1,0:T(8,128)(2,1)}, u32[]{:S(2)}) %copy-start) | copy-done | bytes 262168
  8.6 0.0 copy-start.2
  8.6 1.1 %shard_map.102 = (bf16[512,512]{1,0:T(8,128)(2,1)S(1)}, bf16[512,512]{1,0:T(8,128)(2,1)S(1)}) custom-call(s32[4,1,2]{2,1,0:T(1,128)S(1)} %copy.11.cols_ref, s32[4,1]{1,0:T(4,128)S(1)} %copy.12.cnts_ref, bf16[4,1,2,128,128]{4,3,2,1,0:T(8,128)(2,1)S(1)} %copy-done), custom_call_target="tpu_custom_call" | custom-call | tf_op jit(solution)/shard_map/pallas_call | solution.py:138
  9.7 0.0 collective-permute-done.refs_1_
  9.7 2.8 %collective-permute-done.1.refs_2_ = bf16[128,256]{1,0:T(8,128)(2,1)S(1)} collective-permute-done((bf16[128,256]{1,0:T(8,128)(2,1)}, bf16[128,256]{1,0:T(8,128)(2,1)S(1)}, u32[]{:S(2)}, u32[]{:S(2)}) %collective-permute-start.1) | collective-permute-done | bytes 65568 | tf_op jit(solution)/shard_map/ppermute | solution.py:137
  12.4 0.0 collective-permute-done.2.refs_3_
  12.4 0.0 copy-done.2
  12.4 1.0 %shard_map.103 = bf16[4,128,256]{2,1,0:T(8,128)(2,1)} custom-call(bf16[512,512]{1,0:T(8,128)(2,1)S(1)} %get-tuple-element.11.a_ref, bf16[128,256]{1,0:T(8,128)(2,1)S(1)} %copy-done.2, bf16[128,256]{1,0:T(8,128)(2,1)S(1)} %collective-permute-done.refs_1_, bf16[128,256]{1,0:T(8,128)(2,1)S(1)} %collective-permute-done.1.refs_2_, ...), custom_call_target="tpu_custom_call" | custom-call | tf_op jit(solution)/shard_map/pallas_call | solution.py:144
  13.4 0.0 copy-start.5
  13.4 0.0 copy-start.1
  13.4 0.0 copy-start.3
  13.4 3.5 %all-to-all-start = ((bf16[4,128,256]{2,1,0:T(8,128)(2,1)}), bf16[4,128,256]{2,1,0:T(8,128)(2,1)S(1)}, u32[]{:S(2)}, u32[]{:S(2)}) async-start(bf16[4,128,256]{2,1,0:T(8,128)(2,1)} %shard_map.103), calls=%async_computation | async-start | bytes 524288 | tf_op jit(solution)/shard_map/all_to_all | solution.py:145
  17.0 0.0 copy-done.5
  17.0 6.0 %all-to-all-done.parts_ref = bf16[4,128,256]{2,1,0:T(8,128)(2,1)S(1)} async-done(((bf16[4,128,256]{2,1,0:T(8,128)(2,1)}), bf16[4,128,256]{2,1,0:T(8,128)(2,1)S(1)}, u32[]{:S(2)}, u32[]{:S(2)}) %all-to-all-start) | async-done | bytes 262176 | tf_op jit(solution)/shard_map/all_to_all | solution.py:145
  23.0 0.0 copy-done.1
  23.0 0.0 copy-done.3
  23.0 0.8 %shard_map.104 = (bf16[128,256]{1,0:T(8,128)(2,1)}, bf16[4,208,256]{2,1,0:T(8,128)(2,1)S(1)}) custom-call(bf16[4,128,256]{2,1,0:T(8,128)(2,1)S(1)} %all-to-all-done.parts_ref, bf16[256,256]{1,0:T(8,128)(2,1)S(1)} %copy-done.1, bf16[1,256]{1,0:T(2,128)(2,1)S(1)} %reshape.14.b_ref, bf16[128,256]{1,0:T(8,128)(2,1)S(1)} %copy-done.3), custom_call_target="tpu_custom_call" | custom-call | tf_op jit(solution)/shard_map/pallas_call | solution.py:146
  23.8 10.1 %all_to_all.20.in_ref = bf16[4,208,256]{2,1,0:T(8,128)(2,1)S(1)} all-to-all(bf16[4,208,256]{2,1,0:T(8,128)(2,1)S(1)} %get-tuple-element.14), channel_id=1, replica_groups=mesh['groups'=2,'row'=4,'col'=4] {'col'}, dimensions={0} | all-to-all | bytes 851968 | tf_op jit(solution)/shard_map/all_to_all | solution.py:151
  34.0 0.3 shard_map.105
  34.3 15.4 %all_to_all.21.in_ref = bf16[4,208,256]{2,1,0:T(8,128)(2,1)S(1)} all-to-all(bf16[4,208,256]{2,1,0:T(8,128)(2,1)S(1)} %shard_map.105), channel_id=1, replica_groups=mesh['groups'=2,'row'=4,'col'=4] {'row'}, dimensions={0} | all-to-all | bytes 851968 | tf_op jit(solution)/shard_map/all_to_all | solution.py:153
  49.8 0.7 %shard_map.106 = (bf16[128,256]{1,0:T(8,128)(2,1)}, bf16[4,64,256]{2,1,0:T(8,128)(2,1)S(1)}, f32[1,256]{1,0:T(1,128)}) custom-call(bf16[4,208,256]{2,1,0:T(8,128)(2,1)S(1)} %all_to_all.21.in_ref), custom_call_target="tpu_custom_call" | custom-call | tf_op jit(solution)/shard_map/pallas_call | solution.py:154
  50.4 7.0 %all_to_all.22.in_ref = bf16[4,64,256]{2,1,0:T(8,128)(2,1)S(1)} all-to-all(bf16[4,64,256]{2,1,0:T(8,128)(2,1)S(1)} %get-tuple-element.16), channel_id=1, replica_groups=mesh['groups'=2,'row'=4,'col'=4] {'col'}, dimensions={0} | all-to-all | bytes 262144 | tf_op jit(solution)/shard_map/all_to_all | solution.py:159
  57.4 0.7 %shard_map.107 = f32[256,256]{1,0:T(8,128)} custom-call(bf16[4,64,256]{2,1,0:T(8,128)(2,1)S(1)} %all_to_all.22.in_ref), custom_call_target="tpu_custom_call" | custom-call | tf_op jit(solution)/shard_map/pallas_call | solution.py:160
  (1 shorter events, 0.0 us)
Async XLA Ops:
  0.6 6.9 %copy-start.4 = (s32[4,1]{0,1:T(1,128)S(1)}, s32[4,1]{0,1:T(1,128)}, u32[]{:S(2)}) copy-start(s32[4,1]{0,1:T(1,128)} %param.10) | copy-start | bytes 52
  0.6 9.0 %collective-permute-start = (bf16[128,256]{1,0:T(8,128)(2,1)}, bf16[128,256]{1,0:T(8,128)(2,1)S(1)}, u32[]{:S(2)}, u32[]{:S(2)}) collective-permute-start(bf16[128,256]{1,0:T(8,128)(2,1)} %refs_0_.1), channel_id=1, source_target_pairs={{0,12},{4,0},{8,4},{12,8},{1,13},{5,1},{9,5},{13,9},{2,14},{6,2},{... | collective-permute-start | bytes 196616 | tf_op jit(solution)/shard_map/ppermute | solution.py:137
  5.7 6.7 %collective-permute-start.1 = (bf16[128,256]{1,0:T(8,128)(2,1)}, bf16[128,256]{1,0:T(8,128)(2,1)S(1)}, u32[]{:S(2)}, u32[]{:S(2)}) collective-permute-start(bf16[128,256]{1,0:T(8,128)(2,1)} %refs_0_.1), channel_id=1, source_target_pairs={{0,8},{4,12},{8,0},{12,4},{1,9},{5,13},{9,1},{13,5},{2,10},{6,14},... | collective-permute-start | bytes 196616 | tf_op jit(solution)/shard_map/ppermute | solution.py:137
  5.7 6.7 %collective-permute-start.2 = (bf16[128,256]{1,0:T(8,128)(2,1)}, bf16[128,256]{1,0:T(8,128)(2,1)S(1)}, u32[]{:S(2)}, u32[]{:S(2)}) collective-permute-start(bf16[128,256]{1,0:T(8,128)(2,1)} %refs_0_.1), channel_id=1, source_target_pairs={{0,4},{4,8},{8,12},{12,0},{1,5},{5,9},{9,13},{13,1},{2,6},{6,10},{... | collective-permute-start | bytes 196616 | tf_op jit(solution)/shard_map/ppermute | solution.py:137
  7.6 1.0 %copy-start = (bf16[4,1,2,128,128]{4,3,2,1,0:T(8,128)(2,1)S(1)}, bf16[4,1,2,128,128]{4,3,2,1,0:T(8,128)(2,1)}, u32[]{:S(2)}) copy-start(bf16[4,1,2,128,128]{4,3,2,1,0:T(8,128)(2,1)} %tiles_ref.1) | copy-start | bytes 786436
  8.6 3.9 %copy-start.2 = (bf16[128,256]{1,0:T(8,128)(2,1)S(1)}, bf16[128,256]{1,0:T(8,128)(2,1)}, u32[]{:S(2)}) copy-start(bf16[128,256]{1,0:T(8,128)(2,1)} %refs_0_.1) | copy-start | bytes 196612
  13.4 3.6 %copy-start.5 = (bf16[256]{0:T(256)(128)(2,1)S(1)}, bf16[256]{0:T(256)(128)(2,1)}, u32[]{:S(2)}) copy-start(bf16[256]{0:T(256)(128)(2,1)} %param.12) | copy-start | bytes 1540
  13.4 9.6 %copy-start.1 = (bf16[256,256]{1,0:T(8,128)(2,1)S(1)}, bf16[256,256]{1,0:T(8,128)(2,1)}, u32[]{:S(2)}) copy-start(bf16[256,256]{1,0:T(8,128)(2,1)} %w_ref.1) | copy-start | bytes 393220
  13.4 9.6 %copy-start.3 = (bf16[128,256]{1,0:T(8,128)(2,1)S(1)}, bf16[128,256]{1,0:T(8,128)(2,1)}, u32[]{:S(2)}) copy-start(bf16[128,256]{1,0:T(8,128)(2,1)} %cot_ref.1) | copy-start | bytes 196612
  13.4 9.5 %all-to-all-start = ((bf16[4,128,256]{2,1,0:T(8,128)(2,1)}), bf16[4,128,256]{2,1,0:T(8,128)(2,1)S(1)}, u32[]{:S(2)}, u32[]{:S(2)}) async-start(bf16[4,128,256]{2,1,0:T(8,128)(2,1)} %shard_map.103), calls=%async_computation | async-start | bytes 524288 | tf_op jit(solution)/shard_map/all_to_all | solution.py:145

commit v3 on v0

v3 whole, which is shorter than its diff:
```python
import jax
import jax.numpy as jnp
from jax import lax
from jax.experimental import pallas as pl
from jax.experimental.pallas import tpu as pltpu
from jax.sharding import PartitionSpec as P

BF = jnp.bfloat16
F32 = jnp.float32
LIMIT = 48 * 1024 * 1024
PAD = 16


def dot(a, b, ca=1, cb=0):
    return lax.dot_general(a, b, (((ca,), (cb,)), ((), ())), preferred_element_type=F32)


def call(body, outs, smem=0, count=1, scratch=()):
    vm = pl.BlockSpec(memory_space=pltpu.VMEM)
    sm = pl.BlockSpec(memory_space=pltpu.SMEM)
    return pl.pallas_call(
        body,
        in_specs=[sm] * smem + [vm] * (count - smem),
        out_specs=jax.tree.map(lambda _: vm, outs),
        out_shape=outs,
        scratch_shapes=scratch,
        compiler_params=pltpu.CompilerParams(vmem_limit_bytes=LIMIT),
    )


def shape(*dims, dtype=BF):
    return jax.ShapeDtypeStruct(dims, dtype)


def dense_kernel(cols_ref, cnts_ref, tiles_ref, a_ref, at_ref):
    trows, _, slots, tile, _ = tiles_ref.shape
    r = lax.axis_index("row")
    c = lax.axis_index("col")
    a_ref[...] = jnp.zeros_like(a_ref)
    at_ref[...] = jnp.zeros_like(at_ref)

    def put(step, carry):
        t = step // slots
        k = step % slots

        @pl.when(k < cnts_ref[0, t])
        def _():
            q = jnp.bitwise_xor(t, c)
            p = jnp.bitwise_xor(cols_ref[0, k, t], r)
            here = tiles_ref[t, 0, k]
            qs = pl.ds(pl.multiple_of(q * tile, tile), tile)
            ps = pl.ds(pl.multiple_of(p * tile, tile), tile)
            a_ref[qs, ps] = here
            at_ref[ps, qs] = here.T

        return carry

    lax.fori_loop(0, trows * slots, put, 0)


def forward_kernel(n_row):
    def body(a_ref, *refs):
        tile = refs[0].shape[0]
        x = jnp.concatenate([ref[...] for ref in refs[:n_row]], axis=0)
        for q, out in enumerate(refs[n_row:]):
            out[...] = dot(a_ref[q * tile : (q + 1) * tile, :], x).astype(BF)

    return body


def total_of(refs, first, rows):
    total = refs[0][first : first + rows, :].astype(F32)
    for ref in refs[1:]:
        total = total + ref[first : first + rows, :].astype(F32)
    return total


def two_rows(line):
    high = line.astype(BF).astype(F32)
    which = lax.broadcasted_iota(jnp.int32, (PAD, line.shape[1]), 0)
    return jnp.where(which == 0, high, jnp.where(which == 1, line - high, 0.0)).astype(BF)


def middle_kernel(n_col):
    def body(w_ref, b_ref, cot_ref, *refs):
        parts, act_ref, outs, local_ref = refs[:n_col], refs[n_col], refs[n_col + 1 : -1], refs[-1]
        tile, width = cot_ref.shape
        piece = width // n_col
        c = lax.axis_index("col")
        agg = total_of(parts, 0, tile).astype(BF)
        preact = dot(agg, w_ref[...]) + b_ref[...].astype(F32)
        sig = jax.nn.sigmoid(preact)
        act_ref[...] = (preact * sig).astype(BF)
        grad = cot_ref[...].astype(F32) * (sig * (1.0 + preact * (1.0 - sig)))
        grad = grad.astype(BF)
        gagg = dot(grad, w_ref[...], 1, 1).astype(BF)
        local_ref[...] = dot(agg, grad, 0, 0)
        tail = two_rows(jnp.sum(grad.astype(F32), axis=0, keepdims=True))
        for q, out in enumerate(outs):
            first = pl.multiple_of(jnp.bitwise_xor(c, q) * piece, piece)
            out[:tile, :] = gagg
            out[tile : tile + piece, :] = local_ref[pl.ds(first, piece), :].astype(BF)
            out[tile + piece :, :] = tail

    return body


def backward_kernel(n_col):
    def body(at_ref, *refs):
        ins, outs = refs[:n_col], refs[n_col:]
        tile = at_ref.shape[0] // len(outs)
        piece = ins[0].shape[0] - tile - PAD
        g = jnp.concatenate([ref[:tile, :] for ref in ins], axis=0)
        part = total_of(ins, tile, piece).astype(BF)
        lines = total_of(ins, tile + piece, PAD)
        tail = two_rows(lines[0:1] + lines[1:2])
        for p, out in enumerate(outs):
            out[:tile, :] = dot(at_ref[p * tile : (p + 1) * tile, :], g).astype(BF)
            out[tile : tile + piece, :] = part
            out[tile + piece :, :] = tail

    return body


def quarter_kernel(*refs):
    ins, (feat_ref, out_ref, bias_ref) = refs[:-3], refs[-3:]
    tile, piece = feat_ref.shape[0], out_ref.shape[0]
    out_ref[...] = total_of(ins, tile, piece).astype(BF)
    feat_ref[...] = total_of(ins, 0, tile).astype(BF)
    lines = total_of(ins, tile + piece, PAD)
    bias_ref[...] = lines[0:1] + lines[1:2]


def widen_kernel(*refs):
    ins, out_ref = refs[:-1], refs[-1]
    piece = ins[0].shape[0]
    c = lax.axis_index("col")
    for q, ref in enumerate(ins):
        first = pl.multiple_of(jnp.bitwise_xor(c, q) * piece, piece)
        out_ref[pl.ds(first, piece), :] = ref[...].astype(F32)


def swap(x, axis, n, by):
    return lax.ppermute(x, axis, [(i, i ^ by) for i in range(n)])


def deal(xs, axis):
    n = len(xs)
    got = {by: swap(xs[by], axis, n, by) for by in [*range(2, n), 1]}
    return [xs[0]] + [got[by] for by in range(1, n)]


def spread(x, axis, n):
    return deal([x] * n, axis)


def shards(n_row, n_col, features, adj_tiles, columns, counts, weight, bias_term, cotangent):
    tile, width = features.shape
    piece = width // n_col
    message = shape(tile + piece + PAD, width)
    xs = spread(features, "row", n_row)
    a, at = call(
        dense_kernel,
        (shape(n_col * tile, n_row * tile), shape(n_row * tile, n_col * tile)),
        smem=2,
        count=3,
    )(columns.transpose(1, 2, 0), counts.T, adj_tiles)
    parts = call(forward_kernel(n_row), (shape(tile, width),) * n_col, count=1 + n_row)(a, *xs)
    act, *packed = call(
        middle_kernel(n_col),
        (shape(tile, width),) + (message,) * n_col,
        count=3 + n_col,
        scratch=[pltpu.VMEM((width, width), F32)],
    )(weight, bias_term.reshape(1, width), cotangent, *deal(parts, "col"))
    packed = call(backward_kernel(n_col), (message,) * n_row, count=1 + n_col)(
        at, *deal(packed, "col")
    )
    grad_features, quarter, grad_bias = call(
        quarter_kernel,
        (shape(tile, width), shape(piece, width), shape(1, width, dtype=F32)),
        count=n_row,
    )(*deal(packed, "row"))
    grad_weight = call(widen_kernel, shape(width, width, dtype=F32), count=n_col)(
        *spread(quarter, "col", n_col)
    )
    return act, grad_features, grad_weight, grad_bias.reshape(width)


def solution(mesh):
    n_row, n_col = mesh.shape["row"], mesh.shape["col"]
    placed = (
        P(("groups", "row", "col"), None),
        P(("groups", "row"), "col", None, None, None),
        P(("groups", "row"), "col", None),
        P(("groups", "row"), "col"),
        P(),
        P(),
        P(("groups", "row", "col"), None),
    )

    def body(*args):
        return shards(n_row, n_col, *args)

    return jax.shard_map(
        body,
        mesh=mesh,
        in_specs=placed,
        out_specs=(
            P(("groups", "row", "col"), None),
            P(("groups", "row", "col"), None),
            P("groups", None),
            P("groups"),
        ),
        check_vma=False,
    )
```

time: 184 us -> 44.6 us (0.24)
  waiting for transfers between devices: 103 us -> 23.3 us
  blocking collectives: 55 us -> 0 us
  starting transfers between devices: 0.12 us -> 14.9 us
  between operations: 13.8 us -> 0.7 us
  matrix products: 4.98 us -> 0 us
  Pallas kernels: 0 us -> 3.88 us
  local copies, waits for them, and re-layouts: 4.29 us -> 1.65 us
  other arithmetic: 2.14 us -> 0 us
    psum x2 -> x0, waiting for transfers between devices: 79.7 us -> none  [the longest x1 47 us: shards(): lax.psum((local_weight, local_bias), ('row', 'col'))]
    psum x1 -> x0, blocking collectives: 33.3 us -> none  [shards(): lax.psum((local_weight, local_bias), ('row', 'col'))]
    ppermute x0 -> x15, waiting for transfers between devices: none -> 23.3 us  [swap(): return lax.ppermute(x, axis, [(i, i ^ by) for i in range(n)])]
    reduce_scatter x1 -> x0, waiting for transfers between devices: 23 us -> none  [shards(): lax.psum_scatter(partial_value.reshape(col_tiles * tile_size, feat_width)...]
    all_gather x2 -> x0, blocking collectives: 21.7 us -> none  [the longest x1 16 us: shards(): gathered = lax.all_gather(features, 'row', axis=0, tiled=True)]
    ppermute x0 -> x15, starting transfers between devices: none -> 14.9 us  [swap(): return lax.ppermute(x, axis, [(i, i ^ by) for i in range(n)])]
    dot_general x5 -> x0, matrix products: 4.98 us -> none  [the longest x1 1.75 us: shards(): jnp.dot(agg_low.T, grad_pre, preferred_element_type=jnp.float32)]
    pallas_call x0 -> x6, Pallas kernels: none -> 3.88 us  [the longest x1 1.04 us: shards(): call(dense_kernel, (shape(n_col * tile, n_row * tile), shape(n_row * tile...]
  transfers between devices with their start and end apart: 3 -> 15, of which waited for: 3 -> 10; matrix products, arithmetic and copies ran while one was open for 2% -> 0% of each run, Pallas kernels for 0% -> 2%
where the time goes in v3:
time: 44.6 us; the launch traced here: 44.4 us
  waiting for transfers between devices  23.3 us (52%)
  starting transfers between devices  14.9 us (33%)
  Pallas kernels  3.88 us (9%)
  local copies, waits for them, and re-layouts  1.65 us (4%)
  between operations  0.7 us (2%)
    ppermute x15, waiting for transfers between devices, swap(): return lax.ppermute(x, axis, [(i, i ^ by) for i in range(n)])  23.3 us
    ppermute x15, starting transfers between devices, swap(): return lax.ppermute(x, axis, [(i, i ^ by) for i in range(n)])  14.9 us
    unnamed x14, local copies, waits for them, and re-layouts  1.65 us
    pallas_call x1, Pallas kernels, shards(): call(dense_kernel, (shape(n_col * tile, n_row * tile), shape(n_row * tile...  1.04 us
  transfers between devices with their start and end apart: 15, of which 10 were waited for; matrix products, arithmetic and copies ran while one was open for 0% of the time, Pallas kernels for 2%

profile of v3, /device:TPU:0, one launch (start us, length us, event | category | flops | bytes accessed | tf_op | source)
XLA Modules:
  0.0 44.4 jit_solution(3421396031620042262)
XLA Ops:
  0.6 3.1 %collective-permute-start = (bf16[128,256]{1,0:T(8,128)(2,1)}, bf16[128,256]{1,0:T(8,128)(2,1)S(1)}, u32[]{:S(2)}, u32[]{:S(2)}) collective-permute-start(bf16[128,256]{1,0:T(8,128)(2,1)} %refs_0_.1), channel_id=1, source_target_pairs={{0,4},{4,0},{8,12},{12,8},{1,5},{5,1},{9,13},{13,9},{2,6},{6,2},{1... | collective-permute-start | bytes 196616 | tf_op jit(solution)/shard_map/ppermute | solution.py:144
  3.7 2.6 %collective-permute-start.1 = (bf16[128,256]{1,0:T(8,128)(2,1)}, bf16[128,256]{1,0:T(8,128)(2,1)S(1)}, u32[]{:S(2)}, u32[]{:S(2)}) collective-permute-start(bf16[128,256]{1,0:T(8,128)(2,1)} %refs_0_.1), channel_id=1, source_target_pairs={{0,8},{4,12},{8,0},{12,4},{1,9},{5,13},{9,1},{13,5},{2,10},{6,14},... | collective-permute-start | bytes 196616 | tf_op jit(solution)/shard_map/ppermute | solution.py:144
  6.3 0.0 collective-permute-start.2
  6.3 0.0 copy-start.4
  6.3 0.0 copy-start.5
  6.3 0.7 %copy-done.4 = s32[4,1,2]{0,2,1:T(2,128)S(1)} copy-done((s32[4,1,2]{0,2,1:T(2,128)S(1)}, s32[4,1,2]{0,2,1:T(2,128)}, u32[]{:S(2)}) %copy-start.4) | copy-done | bytes 56
  7.0 0.0 copy-done.5
  7.0 0.0 copy-start
  7.0 0.9 %copy-done = bf16[4,1,2,128,128]{4,3,2,1,0:T(8,128)(2,1)S(1)} copy-done((bf16[4,1,2,128,128]{4,3,2,1,0:T(8,128)(2,1)S(1)}, bf16[4,1,2,128,128]{4,3,2,1,0:T(8,128)(2,1)}, u32[]{:S(2)}) %copy-start) | copy-done | bytes 262168
  7.9 0.0 copy-start.2
  7.9 1.0 %shard_map.102 = (bf16[512,512]{1,0:T(8,128)(2,1)S(1)}, bf16[512,512]{1,0:T(8,128)(2,1)S(1)}) custom-call(s32[1,2,4]{2,1,0:T(2,128)S(1)} %bitcast.3, s32[1,4]{1,0:T(1,128)S(1)} %bitcast.4, bf16[4,1,2,128,128]{4,3,2,1,0:T(8,128)(2,1)S(1)} %copy-done), custom_call_target="tpu_custom_call" | custom-call | tf_op jit(solution)/shard_map/pallas_call | solution.py:162
  9.0 0.0 collective-permute-done.refs_1_
  9.0 2.2 %collective-permute-done.1.refs_2_ = bf16[128,256]{1,0:T(8,128)(2,1)S(1)} collective-permute-done((bf16[128,256]{1,0:T(8,128)(2,1)}, bf16[128,256]{1,0:T(8,128)(2,1)S(1)}, u32[]{:S(2)}, u32[]{:S(2)}) %collective-permute-start.1) | collective-permute-done | bytes 65568 | tf_op jit(solution)/shard_map/ppermute | solution.py:144
  11.2 1.4 %collective-permute-done.2.refs_3_ = bf16[128,256]{1,0:T(8,128)(2,1)S(1)} collective-permute-done((bf16[128,256]{1,0:T(8,128)(2,1)}, bf16[128,256]{1,0:T(8,128)(2,1)S(1)}, u32[]{:S(2)}, u32[]{:S(2)}) %collective-permute-start.2) | collective-permute-done | bytes 65568 | tf_op jit(solution)/shard_map/ppermute | solution.py:144
  12.6 0.0 copy-done.2
  12.6 0.3 shard_map.103
  12.9 0.1 collective-permute-start.3
  13.0 0.0 copy-start.6
  13.0 1.6 %collective-permute-start.4 = (bf16[128,256]{1,0:T(8,128)(2,1)S(1)}, bf16[128,256]{1,0:T(8,128)(2,1)S(1)}, u32[]{:S(2)}, u32[]{:S(2)}) collective-permute-start(bf16[128,256]{1,0:T(8,128)(2,1)S(1)} %get-tuple-element.25), channel_id=1, source_target_pairs={{0,2},{1,3},{2,0},{3,1},{4,6},{5,7},{6,4},{7,5},{8,10},{9,11},{10,... | collective-permute-start | bytes 196616 | tf_op jit(solution)/shard_map/ppermute | solution.py:144
  14.6 0.3 collective-permute-start.5
  14.9 0.0 copy-done.6
  14.9 0.0 collective-permute-done.3.refs_1_
  14.9 2.6 %collective-permute-done.4.refs_2_ = bf16[128,256]{1,0:T(8,128)(2,1)S(1)} collective-permute-done((bf16[128,256]{1,0:T(8,128)(2,1)S(1)}, bf16[128,256]{1,0:T(8,128)(2,1)S(1)}, u32[]{:S(2)}, u32[]{:S(2)}) %collective-permute-start.4) | collective-permute-done | bytes 65568 | tf_op jit(solution)/shard_map/ppermute | solution.py:144
  17.5 1.1 %collective-permute-done.5.refs_3_ = bf16[128,256]{1,0:T(8,128)(2,1)S(1)} collective-permute-done((bf16[128,256]{1,0:T(8,128)(2,1)S(1)}, bf16[128,256]{1,0:T(8,128)(2,1)S(1)}, u32[]{:S(2)}, u32[]{:S(2)}) %collective-permute-start.5) | collective-permute-done | bytes 65568 | tf_op jit(solution)/shard_map/ppermute | solution.py:144
  18.6 0.0 copy-done.1
  18.6 0.0 copy-done.3
  18.6 0.8 %shard_map.104 = (bf16[128,256]{1,0:T(8,128)(2,1)}, bf16[208,256]{1,0:T(8,128)(2,1)S(1)}, bf16[208,256]{1,0:T(8,128)(2,1)S(1)}, bf16[208,256]{1,0:T(8,128)(2,1)S(1)}, bf16[208,256]{1,0:T(8,128)(2,1)S(1)}) custom-call(bf16[256,256]{1,0:T(8,128)(2,1)S(1)} %copy-done.1, bf16[1,256]{1,0:T(2,128)(2,1)S(1)} %reshape.14.b_ref, bf16[128,256]{1,0:T(8,128)(2,1)S(1)} %copy-done.3, ...), custom_call_target="tpu_custom_call" | custom-call | tf_op jit(solution)/shard_map/pallas_call | solution.py:169
  19.5 0.2 collective-permute-start.6
  19.6 1.4 %collective-permute-start.7 = (bf16[208,256]{1,0:T(8,128)(2,1)S(1)}, bf16[208,256]{1,0:T(8,128)(2,1)S(1)}, u32[]{:S(2)}, u32[]{:S(2)}) collective-permute-start(bf16[208,256]{1,0:T(8,128)(2,1)S(1)} %get-tuple-element.31), channel_id=1, source_target_pairs={{0,2},{1,3},{2,0},{3,1},{4,6},{5,7},{6,4},{7,5},{8,10},{9,11},{10,... | collective-permute-start | bytes 319496 | tf_op jit(solution)/shard_map/ppermute | solution.py:144
  21.1 0.3 collective-permute-start.8
  21.3 0.0 collective-permute-done.6.refs_1_
  21.3 4.1 %collective-permute-done.7.refs_2_ = bf16[208,256]{1,0:T(8,128)(2,1)S(1)} collective-permute-done((bf16[208,256]{1,0:T(8,128)(2,1)S(1)}, bf16[208,256]{1,0:T(8,128)(2,1)S(1)}, u32[]{:S(2)}, u32[]{:S(2)}) %collective-permute-start.7) | collective-permute-done | bytes 106528 | tf_op jit(solution)/shard_map/ppermute | solution.py:144
  25.4 1.1 %collective-permute-done.8.refs_3_ = bf16[208,256]{1,0:T(8,128)(2,1)S(1)} collective-permute-done((bf16[208,256]{1,0:T(8,128)(2,1)S(1)}, bf16[208,256]{1,0:T(8,128)(2,1)S(1)}, u32[]{:S(2)}, u32[]{:S(2)}) %collective-permute-start.8) | collective-permute-done | bytes 106528 | tf_op jit(solution)/shard_map/ppermute | solution.py:144
  26.6 0.3 shard_map.105
  26.9 1.7 %collective-permute-start.10 = (bf16[208,256]{1,0:T(8,128)(2,1)S(1)}, bf16[208,256]{1,0:T(8,128)(2,1)S(1)}, u32[]{:S(2)}, u32[]{:S(2)}) collective-permute-start(bf16[208,256]{1,0:T(8,128)(2,1)S(1)} %get-tuple-element.35), channel_id=1, source_target_pairs={{0,8},{4,12},{8,0},{12,4},{1,9},{5,13},{9,1},{13,5},{2,10},{6,14},... | collective-permute-start | bytes 319496 | tf_op jit(solution)/shard_map/ppermute | solution.py:144
  28.6 0.7 %collective-permute-start.11 = (bf16[208,256]{1,0:T(8,128)(2,1)S(1)}, bf16[208,256]{1,0:T(8,128)(2,1)S(1)}, u32[]{:S(2)}, u32[]{:S(2)}) collective-permute-start(bf16[208,256]{1,0:T(8,128)(2,1)S(1)} %get-tuple-element.36), channel_id=1, source_target_pairs={{0,12},{4,8},{8,4},{12,0},{1,13},{5,9},{9,5},{13,1},{2,14},{6,10},... | collective-permute-start | bytes 319496 | tf_op jit(solution)/shard_map/ppermute | solution.py:144
  29.2 1.3 %collective-permute-start.9 = (bf16[208,256]{1,0:T(8,128)(2,1)S(1)}, bf16[208,256]{1,0:T(8,128)(2,1)S(1)}, u32[]{:S(2)}, u32[]{:S(2)}) collective-permute-start(bf16[208,256]{1,0:T(8,128)(2,1)S(1)} %get-tuple-element.34), channel_id=1, source_target_pairs={{0,4},{4,0},{8,12},{12,8},{1,5},{5,1},{9,13},{13,9},{2,6},{6,2},{1... | collective-permute-start | bytes 319496 | tf_op jit(solution)/shard_map/ppermute | solution.py:144
  30.5 6.6 %collective-permute-done.10.refs_2_ = bf16[208,256]{1,0:T(8,128)(2,1)S(1)} collective-permute-done((bf16[208,256]{1,0:T(8,128)(2,1)S(1)}, bf16[208,256]{1,0:T(8,128)(2,1)S(1)}, u32[]{:S(2)}, u32[]{:S(2)}) %collective-permute-start.10) | collective-permute-done | bytes 106528 | tf_op jit(solution)/shard_map/ppermute | solution.py:144
  37.1 0.0 collective-permute-done.11.refs_3_
  37.1 1.3 %collective-permute-done.9.refs_1_ = bf16[208,256]{1,0:T(8,128)(2,1)S(1)} collective-permute-done((bf16[208,256]{1,0:T(8,128)(2,1)S(1)}, bf16[208,256]{1,0:T(8,128)(2,1)S(1)}, u32[]{:S(2)}, u32[]{:S(2)}) %collective-permute-start.9) | collective-permute-done | bytes 106528 | tf_op jit(solution)/shard_map/ppermute | solution.py:144
  38.4 0.7 %shard_map.106 = (bf16[128,256]{1,0:T(8,128)(2,1)}, bf16[64,256]{1,0:T(8,128)(2,1)S(1)}, f32[1,256]{1,0:T(1,128)}) custom-call(bf16[208,256]{1,0:T(8,128)(2,1)S(1)} %get-tuple-element.33.refs_0_, bf16[208,256]{1,0:T(8,128)(2,1)S(1)} %collective-permute-done.9.refs_1_, bf16[208,256]{1,0:T(8,128)(2,1)S(1)} %collective-permute-done.10.refs_2_, ...), custom_call_target="tpu_custom_call" | custom-call | tf_op jit(solution)/shard_map/pallas_call | solution.py:178
  39.1 0.0 collective-permute-start.12
  39.1 1.3 %collective-permute-start.13 = (bf16[64,256]{1,0:T(8,128)(2,1)S(1)}, bf16[64,256]{1,0:T(8,128)(2,1)S(1)}, u32[]{:S(2)}, u32[]{:S(2)}) collective-permute-start(bf16[64,256]{1,0:T(8,128)(2,1)S(1)} %get-tuple-element.38.refs_0_), channel_id=1, source_target_pairs={{0,2},{1,3},{2,0},{3,1},{4,6},{5,7},{6,4},{7,5},{8,10},{9,11},{10,... | collective-permute-start | bytes 98312 | tf_op jit(solution)/shard_map/ppermute | solution.py:144
  40.4 0.5 %collective-permute-start.14 = (bf16[64,256]{1,0:T(8,128)(2,1)S(1)}, bf16[64,256]{1,0:T(8,128)(2,1)S(1)}, u32[]{:S(2)}, u32[]{:S(2)}) collective-permute-start(bf16[64,256]{1,0:T(8,128)(2,1)S(1)} %get-tuple-element.38.refs_0_), channel_id=1, source_target_pairs={{0,3},{1,2},{2,1},{3,0},{4,7},{5,6},{6,5},{7,4},{8,11},{9,10},{10,... | collective-permute-start | bytes 98312 | tf_op jit(solution)/shard_map/ppermute | solution.py:144
  40.9 0.0 collective-permute-done.12.refs_1_
  40.9 2.1 %collective-permute-done.13.refs_2_ = bf16[64,256]{1,0:T(8,128)(2,1)S(1)} collective-permute-done((bf16[64,256]{1,0:T(8,128)(2,1)S(1)}, bf16[64,256]{1,0:T(8,128)(2,1)S(1)}, u32[]{:S(2)}, u32[]{:S(2)}) %collective-permute-start.13) | collective-permute-done | bytes 32800 | tf_op jit(solution)/shard_map/ppermute | solution.py:144
  43.0 0.7 %collective-permute-done.14.refs_3_ = bf16[64,256]{1,0:T(8,128)(2,1)S(1)} collective-permute-done((bf16[64,256]{1,0:T(8,128)(2,1)S(1)}, bf16[64,256]{1,0:T(8,128)(2,1)S(1)}, u32[]{:S(2)}, u32[]{:S(2)}) %collective-permute-start.14) | collective-permute-done | bytes 32800 | tf_op jit(solution)/shard_map/ppermute | solution.py:144
  43.7 0.7 %shard_map.107 = f32[256,256]{1,0:T(8,128)} custom-call(bf16[64,256]{1,0:T(8,128)(2,1)S(1)} %get-tuple-element.38.refs_0_, bf16[64,256]{1,0:T(8,128)(2,1)S(1)} %collective-permute-done.12.refs_1_, bf16[64,256]{1,0:T(8,128)(2,1)S(1)} %collective-permute-done.13.refs_2_, bf16[64,256]{1,0:T(8,128)(2,1)S(1)} %collective-permute-done.14.refs_3_), custom_call_target="tpu_custom_call" | custom-call | tf_op jit(solution)/shard_map/pallas_call | solution.py:183
  (3 shorter events, 0.0 us)
Async XLA Ops:
  0.6 8.4 %collective-permute-start = (bf16[128,256]{1,0:T(8,128)(2,1)}, bf16[128,256]{1,0:T(8,128)(2,1)S(1)}, u32[]{:S(2)}, u32[]{:S(2)}) collective-permute-start(bf16[128,256]{1,0:T(8,128)(2,1)} %refs_0_.1), channel_id=1, source_target_pairs={{0,4},{4,0},{8,12},{12,8},{1,5},{5,1},{9,13},{13,9},{2,6},{6,2},{1... | collective-permute-start | bytes 196616 | tf_op jit(solution)/shard_map/ppermute | solution.py:144
  3.7 7.5 %collective-permute-start.1 = (bf16[128,256]{1,0:T(8,128)(2,1)}, bf16[128,256]{1,0:T(8,128)(2,1)S(1)}, u32[]{:S(2)}, u32[]{:S(2)}) collective-permute-start(bf16[128,256]{1,0:T(8,128)(2,1)} %refs_0_.1), channel_id=1, source_target_pairs={{0,8},{4,12},{8,0},{12,4},{1,9},{5,13},{9,1},{13,5},{2,10},{6,14},... | collective-permute-start | bytes 196616 | tf_op jit(solution)/shard_map/ppermute | solution.py:144
  6.3 6.3 %collective-permute-start.2 = (bf16[128,256]{1,0:T(8,128)(2,1)}, bf16[128,256]{1,0:T(8,128)(2,1)S(1)}, u32[]{:S(2)}, u32[]{:S(2)}) collective-permute-start(bf16[128,256]{1,0:T(8,128)(2,1)} %refs_0_.1), channel_id=1, source_target_pairs={{0,12},{4,8},{8,4},{12,0},{1,13},{5,9},{9,5},{13,1},{2,14},{6,10},... | collective-permute-start | bytes 196616 | tf_op jit(solution)/shard_map/ppermute | solution.py:144
  6.3 0.7 %copy-start.4 = (s32[4,1,2]{0,2,1:T(2,128)S(1)}, s32[4,1,2]{0,2,1:T(2,128)}, u32[]{:S(2)}) copy-start(s32[4,1,2]{0,2,1:T(2,128)} %param.9) | copy-start | bytes 100
  6.3 0.7 %copy-start.5 = (s32[4,1]{0,1:T(1,128)S(1)}, s32[4,1]{0,1:T(1,128)}, u32[]{:S(2)}) copy-start(s32[4,1]{0,1:T(1,128)} %param.10) | copy-start | bytes 52
  7.0 1.0 %copy-start = (bf16[4,1,2,128,128]{4,3,2,1,0:T(8,128)(2,1)S(1)}, bf16[4,1,2,128,128]{4,3,2,1,0:T(8,128)(2,1)}, u32[]{:S(2)}) copy-start(bf16[4,1,2,128,128]{4,3,2,1,0:T(8,128)(2,1)} %tiles_ref.1) | copy-start | bytes 786436
  7.9 4.7 %copy-start.2 = (bf16[128,256]{1,0:T(8,128)(2,1)S(1)}, bf16[128,256]{1,0:T(8,128)(2,1)}, u32[]{:S(2)}) copy-start(bf16[128,256]{1,0:T(8,128)(2,1)} %refs_0_.1) | copy-start | bytes 196612
  12.6 6.0 %copy-start.1 = (bf16[256,256]{1,0:T(8,128)(2,1)S(1)}, bf16[256,256]{1,0:T(8,128)(2,1)}, u32[]{:S(2)}) copy-start(bf16[256,256]{1,0:T(8,128)(2,1)} %w_ref.1) | copy-start | bytes 393220
  12.6 6.0 %copy-start.3 = (bf16[128,256]{1,0:T(8,128)(2,1)S(1)}, bf16[128,256]{1,0:T(8,128)(2,1)}, u32[]{:S(2)}) copy-start(bf16[128,256]{1,0:T(8,128)(2,1)} %cot_ref.1) | copy-start | bytes 196612
  12.9 2.0 %collective-permute-start.3 = (bf16[128,256]{1,0:T(8,128)(2,1)S(1)}, bf16[128,256]{1,0:T(8,128)(2,1)S(1)}, u32[]{:S(2)}, u32[]{:S(2)}) collective-permute-start(bf16[128,256]{1,0:T(8,128)(2,1)S(1)} %get-tuple-element.24), channel_id=1, source_target_pairs={{0,1},{1,0},{2,3},{3,2},{4,5},{5,4},{6,7},{7,6},{8,9},{9,8},{10,11... | collective-permute-start | bytes 196616 | tf_op jit(solution)/shard_map/ppermute | solution.py:144
  13.0 1.9 %copy-start.6 = (bf16[256]{0:T(256)(128)(2,1)S(1)}, bf16[256]{0:T(256)(128)(2,1)}, u32[]{:S(2)}) copy-start(bf16[256]{0:T(256)(128)(2,1)} %param.12) | copy-start | bytes 1540
  13.0 4.5 %collective-permute-start.4 = (bf16[128,256]{1,0:T(8,128)(2,1)S(1)}, bf16[128,256]{1,0:T(8,128)(2,1)S(1)}, u32[]{:S(2)}, u32[]{:S(2)}) collective-permute-start(bf16[128,256]{1,0:T(8,128)(2,1)S(1)} %get-tuple-element.25), channel_id=1, source_target_pairs={{0,2},{1,3},{2,0},{3,1},{4,6},{5,7},{6,4},{7,5},{8,10},{9,11},{10,... | collective-permute-start | bytes 196616 | tf_op jit(solution)/shard_map/ppermute | solution.py:144
  14.6 4.1 %collective-permute-start.5 = (bf16[128,256]{1,0:T(8,128)(2,1)S(1)}, bf16[128,256]{1,0:T(8,128)(2,1)S(1)}, u32[]{:S(2)}, u32[]{:S(2)}) collective-permute-start(bf16[128,256]{1,0:T(8,128)(2,1)S(1)} %get-tuple-element.26), channel_id=1, source_target_pairs={{0,3},{1,2},{2,1},{3,0},{4,7},{5,6},{6,5},{7,4},{8,11},{9,10},{10,... | collective-permute-start | bytes 196616 | tf_op jit(solution)/shard_map/ppermute | solution.py:144
  19.5 1.9 %collective-permute-start.6 = (bf16[208,256]{1,0:T(8,128)(2,1)S(1)}, bf16[208,256]{1,0:T(8,128)(2,1)S(1)}, u32[]{:S(2)}, u32[]{:S(2)}) collective-permute-start(bf16[208,256]{1,0:T(8,128)(2,1)S(1)} %get-tuple-element.30), channel_id=1, source_target_pairs={{0,1},{1,0},{2,3},{3,2},{4,5},{5,4},{6,7},{7,6},{8,9},{9,8},{10,11... | collective-permute-start | bytes 319496 | tf_op jit(solution)/shard_map/ppermute | solution.py:144
  19.6 5.8 %collective-permute-start.7 = (bf16[208,256]{1,0:T(8,128)(2,1)S(1)}, bf16[208,256]{1,0:T(8,128)(2,1)S(1)}, u32[]{:S(2)}, u32[]{:S(2)}) collective-permute-start(bf16[208,256]{1,0:T(8,128)(2,1)S(1)} %get-tuple-element.31), channel_id=1, source_target_pairs={{0,2},{1,3},{2,0},{3,1},{4,6},{5,7},{6,4},{7,5},{8,10},{9,11},{10,... | collective-permute-start | bytes 319496 | tf_op jit(solution)/shard_map/ppermute | solution.py:144
  21.1 5.5 %collective-permute-start.8 = (bf16[208,256]{1,0:T(8,128)(2,1)S(1)}, bf16[208,256]{1,0:T(8,128)(2,1)S(1)}, u32[]{:S(2)}, u32[]{:S(2)}) collective-permute-start(bf16[208,256]{1,0:T(8,128)(2,1)S(1)} %get-tuple-element.32), channel_id=1, source_target_pairs={{0,3},{1,2},{2,1},{3,0},{4,7},{5,6},{6,5},{7,4},{8,11},{9,10},{10,... | collective-permute-start | bytes 319496 | tf_op jit(solution)/shard_map/ppermute | solution.py:144
  26.9 10.2 %collective-permute-start.10 = (bf16[208,256]{1,0:T(8,128)(2,1)S(1)}, bf16[208,256]{1,0:T(8,128)(2,1)S(1)}, u32[]{:S(2)}, u32[]{:S(2)}) collective-permute-start(bf16[208,256]{1,0:T(8,128)(2,1)S(1)} %get-tuple-element.35), channel_id=1, source_target_pairs={{0,8},{4,12},{8,0},{12,4},{1,9},{5,13},{9,1},{13,5},{2,10},{6,14},... | collective-permute-start | bytes 319496 | tf_op jit(solution)/shard_map/ppermute | solution.py:144
  28.6 8.6 %collective-permute-start.11 = (bf16[208,256]{1,0:T(8,128)(2,1)S(1)}, bf16[208,256]{1,0:T(8,128)(2,1)S(1)}, u32[]{:S(2)}, u32[]{:S(2)}) collective-permute-start(bf16[208,256]{1,0:T(8,128)(2,1)S(1)} %get-tuple-element.36), channel_id=1, source_target_pairs={{0,12},{4,8},{8,4},{12,0},{1,13},{5,9},{9,5},{13,1},{2,14},{6,10},... | collective-permute-start | bytes 319496 | tf_op jit(solution)/shard_map/ppermute | solution.py:144
  29.2 9.2 %collective-permute-start.9 = (bf16[208,256]{1,0:T(8,128)(2,1)S(1)}, bf16[208,256]{1,0:T(8,128)(2,1)S(1)}, u32[]{:S(2)}, u32[]{:S(2)}) collective-permute-start(bf16[208,256]{1,0:T(8,128)(2,1)S(1)} %get-tuple-element.34), channel_id=1, source_target_pairs={{0,4},{4,0},{8,12},{12,8},{1,5},{5,1},{9,13},{13,9},{2,6},{6,2},{1... | collective-permute-start | bytes 319496 | tf_op jit(solution)/shard_map/ppermute | solution.py:144
  39.1 1.9 %collective-permute-start.12 = (bf16[64,256]{1,0:T(8,128)(2,1)S(1)}, bf16[64,256]{1,0:T(8,128)(2,1)S(1)}, u32[]{:S(2)}, u32[]{:S(2)}) collective-permute-start(bf16[64,256]{1,0:T(8,128)(2,1)S(1)} %get-tuple-element.38.refs_0_), channel_id=1, source_target_pairs={{0,1},{1,0},{2,3},{3,2},{4,5},{5,4},{6,7},{7,6},{8,9},{9,8},{10,11... | collective-permute-start | bytes 98312 | tf_op jit(solution)/shard_map/ppermute | solution.py:144
  39.1 3.9 %collective-permute-start.13 = (bf16[64,256]{1,0:T(8,128)(2,1)S(1)}, bf16[64,256]{1,0:T(8,128)(2,1)S(1)}, u32[]{:S(2)}, u32[]{:S(2)}) collective-permute-start(bf16[64,256]{1,0:T(8,128)(2,1)S(1)} %get-tuple-element.38.refs_0_), channel_id=1, source_target_pairs={{0,2},{1,3},{2,0},{3,1},{4,6},{5,7},{6,4},{7,5},{8,10},{9,11},{10,... | collective-permute-start | bytes 98312 | tf_op jit(solution)/shard_map/ppermute | solution.py:144
  40.4 3.3 %collective-permute-start.14 = (bf16[64,256]{1,0:T(8,128)(2,1)S(1)}, bf16[64,256]{1,0:T(8,128)(2,1)S(1)}, u32[]{:S(2)}, u32[]{:S(2)}) collective-permute-start(bf16[64,256]{1,0:T(8,128)(2,1)S(1)} %get-tuple-element.38.refs_0_), channel_id=1, source_target_pairs={{0,3},{1,2},{2,1},{3,0},{4,7},{5,6},{6,5},{7,4},{8,11},{9,10},{10,... | collective-permute-start | bytes 98312 | tf_op jit(solution)/shard_map/ppermute | solution.py:144

commit v4 on v3

v4 whole, which is shorter than its diff:
```python
import jax
import jax.numpy as jnp
from jax import lax
from jax.experimental import pallas as pl
from jax.experimental.pallas import tpu as pltpu
from jax.sharding import PartitionSpec as P

BF = jnp.bfloat16
F32 = jnp.float32
LIMIT = 48 * 1024 * 1024
PAD = 16


def dot(a, b, ca=1, cb=0):
    return lax.dot_general(a, b, (((ca,), (cb,)), ((), ())), preferred_element_type=F32)


def call(body, outs, smem=0, count=1, scratch=()):
    vm = pl.BlockSpec(memory_space=pltpu.VMEM)
    sm = pl.BlockSpec(memory_space=pltpu.SMEM)
    return pl.pallas_call(
        body,
        in_specs=[sm] * smem + [vm] * (count - smem),
        out_specs=jax.tree.map(lambda _: vm, outs),
        out_shape=outs,
        scratch_shapes=scratch,
        compiler_params=pltpu.CompilerParams(vmem_limit_bytes=LIMIT),
    )


def shape(*dims, dtype=BF):
    return jax.ShapeDtypeStruct(dims, dtype)


def own_piece(c, n_chip):
    return lax.rem(c, 2) * n_chip + lax.div(c, 2)


def dense_kernel(n_chip):
    def body(cols_ref, cnts_ref, tiles_ref, a_ref, at_ref):
        trows, _, slots, tile, _ = tiles_ref.shape
        r = lax.axis_index("row")
        c = lax.axis_index("col")
        a_ref[...] = jnp.zeros_like(a_ref)
        at_ref[...] = jnp.zeros_like(at_ref)

        def put(step, carry):
            t = step // slots
            k = step % slots

            @pl.when(k < cnts_ref[0, t])
            def _():
                q = own_piece(jnp.bitwise_xor(t, c), n_chip)
                p = jnp.bitwise_xor(cols_ref[0, k, t], r)
                here = tiles_ref[t, 0, k]
                qs = pl.ds(pl.multiple_of(q * tile, tile), tile)
                ps = pl.ds(pl.multiple_of(p * tile, tile), tile)
                a_ref[qs, ps] = here
                at_ref[ps, qs] = here.T

            return carry

        lax.fori_loop(0, trows * slots, put, 0)

    return body


def forward_kernel(n_row):
    def body(a_ref, *refs):
        ins, (keep_ref, send_ref) = refs[:n_row], refs[-2:]
        half = keep_ref.shape[0]
        x = jnp.concatenate([ref[...] for ref in ins], axis=0)
        send_ref[...] = dot(a_ref[half:, :], x).astype(BF)
        keep_ref[...] = dot(a_ref[:half, :], x)

    return body


def chip_kernel(keep_ref, got_ref, out_ref):
    out_ref[...] = (keep_ref[...] + got_ref[...].astype(F32)).astype(BF)


def two_rows(line):
    high = line.astype(BF).astype(F32)
    which = lax.broadcasted_iota(jnp.int32, (PAD, line.shape[1]), 0)
    return jnp.where(which == 0, high, jnp.where(which == 1, line - high, 0.0)).astype(BF)


def middle_kernel(n_chip):
    def body(w_ref, b_ref, *refs):
        cots, sums = refs[:n_chip], refs[n_chip : 2 * n_chip]
        act_ref, keep_ref, piece_ref, line_ref, send_ref, local_ref = refs[2 * n_chip :]
        tile, width = cots[0].shape
        rows = n_chip * tile
        piece = piece_ref.shape[0]
        c = lax.axis_index("col")
        blocks = []
        for u in range(n_chip):
            total = sums[0][u * tile : (u + 1) * tile, :].astype(F32)
            for v in range(1, n_chip):
                total = total + sums[v][(u ^ v) * tile : ((u ^ v) + 1) * tile, :].astype(F32)
            blocks.append(total.astype(BF))
        agg = jnp.concatenate(blocks, axis=0)
        cot = jnp.concatenate([ref[...] for ref in cots], axis=0).astype(F32)
        preact = dot(agg, w_ref[...]) + b_ref[...].astype(F32)
        sig = jax.nn.sigmoid(preact)
        act_ref[...] = (preact[:tile] * sig[:tile]).astype(BF)
        grad = (cot * (sig * (1.0 + preact * (1.0 - sig)))).astype(BF)
        gagg = dot(grad, w_ref[...], 1, 1).astype(BF)
        keep_ref[...] = gagg
        send_ref[:rows, :] = gagg
        local_ref[...] = dot(agg, grad, 0, 0)
        mine = pl.multiple_of(own_piece(c, n_chip) * piece, piece)
        other = pl.multiple_of(own_piece(jnp.bitwise_xor(c, 1), n_chip) * piece, piece)
        piece_ref[...] = local_ref[pl.ds(mine, piece), :]
        send_ref[rows : rows + piece, :] = local_ref[pl.ds(other, piece), :].astype(BF)
        line = jnp.sum(grad.astype(F32), axis=0, keepdims=True)
        line_ref[...] = line
        send_ref[rows + piece :, :] = two_rows(line)

    return body


def backward_kernel(at_ref, keep_ref, got_ref, piece_ref, line_ref, *outs):
    outs, part_ref = outs[:-1], outs[-1]
    rows, piece = keep_ref.shape[0], piece_ref.shape[0]
    tile = at_ref.shape[0] // len(outs)
    part_ref[:piece, :] = (piece_ref[...] + got_ref[rows : rows + piece, :].astype(F32)).astype(BF)
    lines = got_ref[rows + piece :, :].astype(F32)
    part_ref[piece:, :] = two_rows(line_ref[...] + lines[0:1] + lines[1:2])
    g = jnp.concatenate([keep_ref[...], got_ref[:rows, :]], axis=0)
    for p, out in enumerate(outs):
        out[...] = dot(at_ref[p * tile : (p + 1) * tile, :], g).astype(BF)


def total_of(refs):
    total = refs[0][...].astype(F32)
    for ref in refs[1:]:
        total = total + ref[...].astype(F32)
    return total


def piece_kernel(*refs):
    ins, (piece_ref, line_ref) = refs[:-2], refs[-2:]
    piece = piece_ref.shape[0]
    total = total_of(ins)
    piece_ref[...] = total[:piece].astype(BF)
    line_ref[...] = total[piece : piece + 1] + total[piece + 1 : piece + 2]


def last_kernel(n_row, n_col):
    def body(act_ref, line_ref, *refs):
        feats, pieces = refs[:n_row], refs[n_row : n_row + n_col]
        act_out, feat_out, weight_out, bias_out = refs[n_row + n_col :]
        piece = pieces[0].shape[0]
        c = lax.axis_index("col")
        act_out[...] = act_ref[...]
        bias_out[...] = line_ref[...]
        feat_out[...] = total_of(feats).astype(BF)
        for q, ref in enumerate(pieces):
            first = own_piece(jnp.bitwise_xor(c, q), n_col // 2) * piece
            weight_out[pl.ds(pl.multiple_of(first, piece), piece), :] = ref[...].astype(F32)

    return body


def swap(x, axis, n, by):
    return lax.ppermute(x, axis, [(i, i ^ by) for i in range(n)])


def deal(xs, axis):
    n = len(xs)
    got = {by: swap(xs[by], axis, n, by) for by in [*range(2, n), 1]}
    return [xs[0]] + [got[by] for by in range(1, n)]


def spread(x, axis, n):
    return deal([x] * n, axis)


def shards(n_row, n_col, features, adj_tiles, columns, counts, weight, bias_term, cotangent):
    tile, width = features.shape
    n_chip = n_col // 2
    piece = width // n_col
    half = n_chip * tile
    xs = spread(features, "row", n_row)
    cots = [cotangent] + [swap(cotangent, "col", n_col, 2 * v) for v in range(1, n_chip)]
    a, at = call(
        dense_kernel(n_chip),
        (shape(n_col * tile, n_row * tile), shape(n_row * tile, n_col * tile)),
        smem=2,
        count=3,
    )(columns.transpose(1, 2, 0), counts.T, adj_tiles)
    keep, send = call(
        forward_kernel(n_row),
        (shape(half, width, dtype=F32), shape(half, width)),
        count=n_row + n_chip,
    )(a, *xs, *cots[1:])
    chip = call(chip_kernel, shape(half, width), count=2)(keep, swap(send, "col", n_col, 1))
    sums = [chip] + [swap(chip, "col", n_col, 2 * v) for v in range(1, n_chip)]
    act, keep, mine, line, send = call(
        middle_kernel(n_chip),
        (
            shape(tile, width),
            shape(half, width),
            shape(piece, width, dtype=F32),
            shape(1, width, dtype=F32),
            shape(half + piece + PAD, width),
        ),
        count=2 + 2 * n_chip,
        scratch=[pltpu.VMEM((width, width), F32)],
    )(weight, bias_term.reshape(1, width), *cots, *sums)
    *feats, part = call(
        backward_kernel, (shape(tile, width),) * n_row + (shape(piece + PAD, width),), count=5
    )(at, keep, swap(send, "col", n_col, 1), mine, line)
    whole, line = call(
        piece_kernel, (shape(piece, width), shape(1, width, dtype=F32)), count=n_row
    )(*spread(part, "row", n_row))
    act, grad_features, grad_weight, grad_bias = call(
        last_kernel(n_row, n_col),
        (
            shape(tile, width),
            shape(tile, width),
            shape(width, width, dtype=F32),
            shape(1, width, dtype=F32),
        ),
        count=2 + n_row + n_col,
    )(act, line, *deal(feats, "row"), *spread(whole, "col", n_col))
    return act, grad_features, grad_weight, grad_bias.reshape(width)


def solution(mesh):
    n_row, n_col = mesh.shape["row"], mesh.shape["col"]
    placed = (
        P(("groups", "row", "col"), None),
        P(("groups", "row"), "col", None, None, None),
        P(("groups", "row"), "col", None),
        P(("groups", "row"), "col"),
        P(),
        P(),
        P(("groups", "row", "col"), None),
    )

    def body(*args):
        return shards(n_row, n_col, *args)

    return jax.shard_map(
        body,
        mesh=mesh,
        in_specs=placed,
        out_specs=(
            P(("groups", "row", "col"), None),
            P(("groups", "row", "col"), None),
            P("groups", None),
            P("groups"),
        ),
        check_vma=False,
    )
```

time: 44.6 us -> 39.1 us (0.88)
  waiting for transfers between devices: 23.3 us -> 15.2 us
  starting transfers between devices: 14.9 us -> 18 us
  Pallas kernels: 3.88 us -> 3.06 us
    ppermute x15 -> x16, waiting for transfers between devices: 23.3 us -> 15.2 us  [swap(): return lax.ppermute(x, axis, [(i, i ^ by) for i in range(n)])]
    ppermute x15 -> x16, starting transfers between devices: 14.9 us -> 18 us  [swap(): return lax.ppermute(x, axis, [(i, i ^ by) for i in range(n)])]
    pallas_call x6 -> x7, Pallas kernels: 3.88 us -> 3.06 us  [the longest x1 1.18 us: shards(): call(dense_kernel(n_chip), (shape(n_col * tile, n_row * tile), shape(n_ro...]
  transfers between devices with their start and end apart: 15 -> 16, of which waited for: 10 -> 9; matrix products, arithmetic and copies ran while one was open for 0% -> 0% of each run, Pallas kernels for 2% -> 3%
where the time goes in v4:
time: 39.1 us; the launch traced here: 38.6 us
  starting transfers between devices  18 us (46%)
  waiting for transfers between devices  15.2 us (39%)
  Pallas kernels  3.06 us (8%)
  local copies, waits for them, and re-layouts  1.67 us (4%)
  between operations  0.74 us (2%)
    ppermute x16, starting transfers between devices, swap(): return lax.ppermute(x, axis, [(i, i ^ by) for i in range(n)])  18 us
    ppermute x16, waiting for transfers between devices, swap(): return lax.ppermute(x, axis, [(i, i ^ by) for i in range(n)])  15.2 us
    unnamed x14, local copies, waits for them, and re-layouts  1.66 us
    pallas_call x1, Pallas kernels, shards(): call(dense_kernel(n_chip), (shape(n_col * tile, n_row * tile), shape(n_ro...  1.18 us
  transfers between devices with their start and end apart: 16, of which 9 were waited for; matrix products, arithmetic and copies ran while one was open for 0% of the time, Pallas kernels for 3%

profile of v4, /device:TPU:0, one launch (start us, length us, event | category | flops | bytes accessed | tf_op | source)
XLA Modules:
  0.0 38.6 jit_solution(12984121815087985080)
XLA Ops:
  0.6 3.0 %collective-permute-start = (bf16[128,256]{1,0:T(8,128)(2,1)}, bf16[128,256]{1,0:T(8,128)(2,1)S(1)}, u32[]{:S(2)}, u32[]{:S(2)}) collective-permute-start(bf16[128,256]{1,0:T(8,128)(2,1)} %refs_0_.3), channel_id=1, source_target_pairs={{0,2},{1,3},{2,0},{3,1},{4,6},{5,7},{6,4},{7,5},{8,10},{9,11},{10,... | collective-permute-start | bytes 196616 | tf_op jit(solution)/shard_map/ppermute | solution.py:168
  3.6 1.6 %collective-permute-start.1 = (bf16[128,256]{1,0:T(8,128)(2,1)}, bf16[128,256]{1,0:T(8,128)(2,1)S(1)}, u32[]{:S(2)}, u32[]{:S(2)}) collective-permute-start(bf16[128,256]{1,0:T(8,128)(2,1)} %refs_0_.2), channel_id=1, source_target_pairs={{0,4},{4,0},{8,12},{12,8},{1,5},{5,1},{9,13},{13,9},{2,6},{6,2},{1... | collective-permute-start | bytes 196616 | tf_op jit(solution)/shard_map/ppermute | solution.py:168
  5.2 2.6 %collective-permute-start.2 = (bf16[128,256]{1,0:T(8,128)(2,1)}, bf16[128,256]{1,0:T(8,128)(2,1)S(1)}, u32[]{:S(2)}, u32[]{:S(2)}) collective-permute-start(bf16[128,256]{1,0:T(8,128)(2,1)} %refs_0_.2), channel_id=1, source_target_pairs={{0,8},{4,12},{8,0},{12,4},{1,9},{5,13},{9,1},{13,5},{2,10},{6,14},... | collective-permute-start | bytes 196616 | tf_op jit(solution)/shard_map/ppermute | solution.py:168
  7.8 0.2 collective-permute-start.3
  8.0 0.0 copy-start.5
  8.0 0.7 %copy-done.4 = s32[4,1,2]{0,2,1:T(2,128)S(1)} copy-done((s32[4,1,2]{0,2,1:T(2,128)S(1)}, s32[4,1,2]{0,2,1:T(2,128)}, u32[]{:S(2)}) %copy-start.4) | copy-done | bytes 56
  8.7 0.0 copy-done.5
  8.7 0.0 copy-start
  8.7 0.9 %copy-done = bf16[4,1,2,128,128]{4,3,2,1,0:T(8,128)(2,1)S(1)} copy-done((bf16[4,1,2,128,128]{4,3,2,1,0:T(8,128)(2,1)S(1)}, bf16[4,1,2,128,128]{4,3,2,1,0:T(8,128)(2,1)}, u32[]{:S(2)}) %copy-start) | copy-done | bytes 262168
  9.7 0.0 copy-start.2
  9.7 1.2 %shard_map.102 = (bf16[512,512]{1,0:T(8,128)(2,1)S(1)}, bf16[512,512]{1,0:T(8,128)(2,1)S(1)}) custom-call(s32[1,2,4]{2,1,0:T(2,128)S(1)} %bitcast.3, s32[1,4]{1,0:T(1,128)S(1)} %bitcast.4, bf16[4,1,2,128,128]{4,3,2,1,0:T(8,128)(2,1)S(1)} %copy-done), custom_call_target="tpu_custom_call" | custom-call | tf_op jit(solution)/shard_map/pallas_call | solution.py:188
  10.8 0.0 collective-permute-done.refs_4_.refs_1_
  10.9 0.0 collective-permute-done.1.refs_1_
  10.9 1.6 %collective-permute-done.2.refs_2_ = bf16[128,256]{1,0:T(8,128)(2,1)S(1)} collective-permute-done((bf16[128,256]{1,0:T(8,128)(2,1)}, bf16[128,256]{1,0:T(8,128)(2,1)S(1)}, u32[]{:S(2)}, u32[]{:S(2)}) %collective-permute-start.2) | collective-permute-done | bytes 65568 | tf_op jit(solution)/shard_map/ppermute | solution.py:168
  12.4 1.7 %collective-permute-done.3.refs_3_ = bf16[128,256]{1,0:T(8,128)(2,1)S(1)} collective-permute-done((bf16[128,256]{1,0:T(8,128)(2,1)}, bf16[128,256]{1,0:T(8,128)(2,1)S(1)}, u32[]{:S(2)}, u32[]{:S(2)}) %collective-permute-start.3) | collective-permute-done | bytes 65568 | tf_op jit(solution)/shard_map/ppermute | solution.py:168
  14.1 0.0 copy-done.2
  14.1 0.3 shard_map.103
  14.4 0.1 collective-permute-start.4
  14.5 1.3 %collective-permute-done.4.got_ref = bf16[256,256]{1,0:T(8,128)(2,1)S(1)} collective-permute-done((bf16[256,256]{1,0:T(8,128)(2,1)S(1)}, bf16[256,256]{1,0:T(8,128)(2,1)S(1)}, u32[]{:S(2)}, u32[]{:S(2)}) %collective-permute-start.4) | collective-permute-done | bytes 131104 | tf_op jit(solution)/shard_map/ppermute | solution.py:168
  15.8 0.0 copy-start.6
  15.8 0.6 %collective-permute-start.5 = (bf16[256,256]{1,0:T(8,128)(2,1)S(1)}, bf16[256,256]{1,0:T(8,128)(2,1)S(1)}, u32[]{:S(2)}, u32[]{:S(2)}) collective-permute-start(bf16[256,256]{1,0:T(8,128)(2,1)S(1)} %shard_map.104.refs_2_), channel_id=1, source_target_pairs={{0,2},{1,3},{2,0},{3,1},{4,6},{5,7},{6,4},{7,5},{8,10},{9,11},{10,... | collective-permute-start | bytes 393224 | tf_op jit(solution)/shard_map/ppermute | solution.py:168
  16.4 0.0 copy-done.6
  16.5 5.0 %collective-permute-done.5.refs_3_ = bf16[256,256]{1,0:T(8,128)(2,1)S(1)} collective-permute-done((bf16[256,256]{1,0:T(8,128)(2,1)S(1)}, bf16[256,256]{1,0:T(8,128)(2,1)S(1)}, u32[]{:S(2)}, u32[]{:S(2)}) %collective-permute-start.5) | collective-permute-done | bytes 131104 | tf_op jit(solution)/shard_map/ppermute | solution.py:168
  21.4 0.0 copy-done.1
  21.5 0.0 copy-done.3
  21.5 0.4 %shard_map.105 = (bf16[128,256]{1,0:T(8,128)(2,1)S(1)}, bf16[256,256]{1,0:T(8,128)(2,1)S(1)}, f32[64,256]{1,0:T(8,128)S(1)}, f32[1,256]{1,0:T(1,128)S(1)}, bf16[336,256]{1,0:T(8,128)(2,1)S(1)}) custom-call(bf16[256,256]{1,0:T(8,128)(2,1)S(1)} %copy-done.1, bf16[1,256]{1,0:T(2,128)(2,1)S(1)} %reshape.14.b_ref, bf16[128,256]{1,0:T(8,128)(2,1)S(1)} %copy-done.3, ...), custom_call_target="tpu_custom_call" | custom-call | tf_op jit(solution)/shard_map/pallas_call | solution.py:201
  21.9 0.1 collective-permute-start.6
  22.0 1.4 %collective-permute-done.6.got_ref = bf16[336,256]{1,0:T(8,128)(2,1)S(1)} collective-permute-done((bf16[336,256]{1,0:T(8,128)(2,1)S(1)}, bf16[336,256]{1,0:T(8,128)(2,1)S(1)}, u32[]{:S(2)}, u32[]{:S(2)}) %collective-permute-start.6) | collective-permute-done | bytes 172064 | tf_op jit(solution)/shard_map/ppermute | solution.py:168
  23.4 0.3 shard_map.106
  23.7 0.1 collective-permute-start.7
  23.8 2.0 %collective-permute-start.10 = (bf16[128,256]{1,0:T(8,128)(2,1)S(1)}, bf16[128,256]{1,0:T(8,128)(2,1)S(1)}, u32[]{:S(2)}, u32[]{:S(2)}) collective-permute-start(bf16[128,256]{1,0:T(8,128)(2,1)S(1)} %get-tuple-element.36), channel_id=1, source_target_pairs={{0,4},{4,0},{8,12},{12,8},{1,5},{5,1},{9,13},{13,9},{2,6},{6,2},{1... | collective-permute-start | bytes 196616 | tf_op jit(solution)/shard_map/ppermute | solution.py:168
  25.8 1.3 %collective-permute-start.8 = (bf16[80,256]{1,0:T(8,128)(2,1)S(1)}, bf16[80,256]{1,0:T(8,128)(2,1)S(1)}, u32[]{:S(2)}, u32[]{:S(2)}) collective-permute-start(bf16[80,256]{1,0:T(8,128)(2,1)S(1)} %get-tuple-element.33.refs_0_), channel_id=1, source_target_pairs={{0,8},{4,12},{8,0},{12,4},{1,9},{5,13},{9,1},{13,5},{2,10},{6,14},... | collective-permute-start | bytes 122888 | tf_op jit(solution)/shard_map/ppermute | solution.py:168
  27.1 1.1 %collective-permute-start.9 = (bf16[80,256]{1,0:T(8,128)(2,1)S(1)}, bf16[80,256]{1,0:T(8,128)(2,1)S(1)}, u32[]{:S(2)}, u32[]{:S(2)}) collective-permute-start(bf16[80,256]{1,0:T(8,128)(2,1)S(1)} %get-tuple-element.33.refs_0_), channel_id=1, source_target_pairs={{0,12},{4,8},{8,4},{12,0},{1,13},{5,9},{9,5},{13,1},{2,14},{6,10},... | collective-permute-start | bytes 122888 | tf_op jit(solution)/shard_map/ppermute | solution.py:168
  28.2 1.1 %collective-permute-start.11 = (bf16[128,256]{1,0:T(8,128)(2,1)S(1)}, bf16[128,256]{1,0:T(8,128)(2,1)S(1)}, u32[]{:S(2)}, u32[]{:S(2)}) collective-permute-start(bf16[128,256]{1,0:T(8,128)(2,1)S(1)} %get-tuple-element.37), channel_id=1, source_target_pairs={{0,8},{4,12},{8,0},{12,4},{1,9},{5,13},{9,1},{13,5},{2,10},{6,14},... | collective-permute-start | bytes 196616 | tf_op jit(solution)/shard_map/ppermute | solution.py:168
  29.3 0.0 collective-permute-done.7.refs_1_
  29.3 2.3 %collective-permute-start.12 = (bf16[128,256]{1,0:T(8,128)(2,1)S(1)}, bf16[128,256]{1,0:T(8,128)(2,1)S(1)}, u32[]{:S(2)}, u32[]{:S(2)}) collective-permute-start(bf16[128,256]{1,0:T(8,128)(2,1)S(1)} %get-tuple-element.38), channel_id=1, source_target_pairs={{0,12},{4,8},{8,4},{12,0},{1,13},{5,9},{9,5},{13,1},{2,14},{6,10},... | collective-permute-start | bytes 196616 | tf_op jit(solution)/shard_map/ppermute | solution.py:168
  31.6 0.8 %collective-permute-done.8.refs_2_ = bf16[80,256]{1,0:T(8,128)(2,1)S(1)} collective-permute-done((bf16[80,256]{1,0:T(8,128)(2,1)S(1)}, bf16[80,256]{1,0:T(8,128)(2,1)S(1)}, u32[]{:S(2)}, u32[]{:S(2)}) %collective-permute-start.8) | collective-permute-done | bytes 40992 | tf_op jit(solution)/shard_map/ppermute | solution.py:168
  32.4 1.0 %collective-permute-done.9.refs_3_ = bf16[80,256]{1,0:T(8,128)(2,1)S(1)} collective-permute-done((bf16[80,256]{1,0:T(8,128)(2,1)S(1)}, bf16[80,256]{1,0:T(8,128)(2,1)S(1)}, u32[]{:S(2)}, u32[]{:S(2)}) %collective-permute-start.9) | collective-permute-done | bytes 40992 | tf_op jit(solution)/shard_map/ppermute | solution.py:168
  33.5 0.1 collective-permute-start.13
  33.5 0.6 %collective-permute-start.14 = (bf16[64,256]{1,0:T(8,128)(2,1)S(1)}, bf16[64,256]{1,0:T(8,128)(2,1)S(1)}, u32[]{:S(2)}, u32[]{:S(2)}) collective-permute-start(bf16[64,256]{1,0:T(8,128)(2,1)S(1)} %get-tuple-element.39.refs_4_), channel_id=1, source_target_pairs={{0,2},{1,3},{2,0},{3,1},{4,6},{5,7},{6,4},{7,5},{8,10},{9,11},{10,... | collective-permute-start | bytes 98312 | tf_op jit(solution)/shard_map/ppermute | solution.py:168
  34.1 0.0 collective-permute-done.10.refs_1_
  34.1 1.3 %collective-permute-start.15 = (bf16[64,256]{1,0:T(8,128)(2,1)S(1)}, bf16[64,256]{1,0:T(8,128)(2,1)S(1)}, u32[]{:S(2)}, u32[]{:S(2)}) collective-permute-start(bf16[64,256]{1,0:T(8,128)(2,1)S(1)} %get-tuple-element.39.refs_4_), channel_id=1, source_target_pairs={{0,3},{1,2},{2,1},{3,0},{4,7},{5,6},{6,5},{7,4},{8,11},{9,10},{10,... | collective-permute-start | bytes 98312 | tf_op jit(solution)/shard_map/ppermute | solution.py:168
  35.4 1.8 %collective-permute-done.11.refs_2_ = bf16[128,256]{1,0:T(8,128)(2,1)S(1)} collective-permute-done((bf16[128,256]{1,0:T(8,128)(2,1)S(1)}, bf16[128,256]{1,0:T(8,128)(2,1)S(1)}, u32[]{:S(2)}, u32[]{:S(2)}) %collective-permute-start.11) | collective-permute-done | bytes 65568 | tf_op jit(solution)/shard_map/ppermute | solution.py:168
  37.2 0.0 collective-permute-done.12.refs_3_
  37.2 0.0 collective-permute-done.13.refs_5_
  37.2 0.6 %collective-permute-done.14.refs_6_ = bf16[64,256]{1,0:T(8,128)(2,1)S(1)} collective-permute-done((bf16[64,256]{1,0:T(8,128)(2,1)S(1)}, bf16[64,256]{1,0:T(8,128)(2,1)S(1)}, u32[]{:S(2)}, u32[]{:S(2)}) %collective-permute-start.14) | collective-permute-done | bytes 32800 | tf_op jit(solution)/shard_map/ppermute | solution.py:168
  37.8 0.0 collective-permute-done.15.refs_7_
  37.8 0.8 %shard_map.108 = (bf16[128,256]{1,0:T(8,128)(2,1)}, bf16[128,256]{1,0:T(8,128)(2,1)}, f32[256,256]{1,0:T(8,128)}, f32[1,256]{1,0:T(1,128)}) custom-call(bf16[128,256]{1,0:T(8,128)(2,1)S(1)} %get-tuple-element.27.act_ref, f32[1,256]{1,0:T(1,128)S(1)} %get-tuple-element.34.line_ref, bf16[128,256]{1,0:T(8,128)(2,1)S(1)} %get-tuple-element.35.refs_0_, ...), custom_call_target="tpu_custom_call" | custom-call | tf_op jit(solution)/shard_map/pallas_call | solution.py:219
  (6 shorter events, 0.1 us)
Async XLA Ops:
  0.6 10.2 %collective-permute-start = (bf16[128,256]{1,0:T(8,128)(2,1)}, bf16[128,256]{1,0:T(8,128)(2,1)S(1)}, u32[]{:S(2)}, u32[]{:S(2)}) collective-permute-start(bf16[128,256]{1,0:T(8,128)(2,1)} %refs_0_.3), channel_id=1, source_target_pairs={{0,2},{1,3},{2,0},{3,1},{4,6},{5,7},{6,4},{7,5},{8,10},{9,11},{10,... | collective-permute-start | bytes 196616 | tf_op jit(solution)/shard_map/ppermute | solution.py:168
  3.6 7.2 %collective-permute-start.1 = (bf16[128,256]{1,0:T(8,128)(2,1)}, bf16[128,256]{1,0:T(8,128)(2,1)S(1)}, u32[]{:S(2)}, u32[]{:S(2)}) collective-permute-start(bf16[128,256]{1,0:T(8,128)(2,1)} %refs_0_.2), channel_id=1, source_target_pairs={{0,4},{4,0},{8,12},{12,8},{1,5},{5,1},{9,13},{13,9},{2,6},{6,2},{1... | collective-permute-start | bytes 196616 | tf_op jit(solution)/shard_map/ppermute | solution.py:168
  5.2 7.2 %collective-permute-start.2 = (bf16[128,256]{1,0:T(8,128)(2,1)}, bf16[128,256]{1,0:T(8,128)(2,1)S(1)}, u32[]{:S(2)}, u32[]{:S(2)}) collective-permute-start(bf16[128,256]{1,0:T(8,128)(2,1)} %refs_0_.2), channel_id=1, source_target_pairs={{0,8},{4,12},{8,0},{12,4},{1,9},{5,13},{9,1},{13,5},{2,10},{6,14},... | collective-permute-start | bytes 196616 | tf_op jit(solution)/shard_map/ppermute | solution.py:168
  7.8 6.3 %collective-permute-start.3 = (bf16[128,256]{1,0:T(8,128)(2,1)}, bf16[128,256]{1,0:T(8,128)(2,1)S(1)}, u32[]{:S(2)}, u32[]{:S(2)}) collective-permute-start(bf16[128,256]{1,0:T(8,128)(2,1)} %refs_0_.2), channel_id=1, source_target_pairs={{0,12},{4,8},{8,4},{12,0},{1,13},{5,9},{9,5},{13,1},{2,14},{6,10},... | collective-permute-start | bytes 196616 | tf_op jit(solution)/shard_map/ppermute | solution.py:168
  8.0 0.7 %copy-start.4 = (s32[4,1,2]{0,2,1:T(2,128)S(1)}, s32[4,1,2]{0,2,1:T(2,128)}, u32[]{:S(2)}) copy-start(s32[4,1,2]{0,2,1:T(2,128)} %param.9) | copy-start | bytes 100
  8.0 0.7 %copy-start.5 = (s32[4,1]{0,1:T(1,128)S(1)}, s32[4,1]{0,1:T(1,128)}, u32[]{:S(2)}) copy-start(s32[4,1]{0,1:T(1,128)} %param.10) | copy-start | bytes 52
  8.7 1.0 %copy-start = (bf16[4,1,2,128,128]{4,3,2,1,0:T(8,128)(2,1)S(1)}, bf16[4,1,2,128,128]{4,3,2,1,0:T(8,128)(2,1)}, u32[]{:S(2)}) copy-start(bf16[4,1,2,128,128]{4,3,2,1,0:T(8,128)(2,1)} %tiles_ref.1) | copy-start | bytes 786436
  9.7 4.4 %copy-start.2 = (bf16[128,256]{1,0:T(8,128)(2,1)S(1)}, bf16[128,256]{1,0:T(8,128)(2,1)}, u32[]{:S(2)}) copy-start(bf16[128,256]{1,0:T(8,128)(2,1)} %refs_0_.2) | copy-start | bytes 196612
  14.4 1.4 %collective-permute-start.4 = (bf16[256,256]{1,0:T(8,128)(2,1)S(1)}, bf16[256,256]{1,0:T(8,128)(2,1)S(1)}, u32[]{:S(2)}, u32[]{:S(2)}) collective-permute-start(bf16[256,256]{1,0:T(8,128)(2,1)S(1)} %get-tuple-element.26), channel_id=1, source_target_pairs={{0,1},{1,0},{2,3},{3,2},{4,5},{5,4},{6,7},{7,6},{8,9},{9,8},{10,11... | collective-permute-start | bytes 393224 | tf_op jit(solution)/shard_map/ppermute | solution.py:168
  15.8 0.7 %copy-start.6 = (bf16[256]{0:T(256)(128)(2,1)S(1)}, bf16[256]{0:T(256)(128)(2,1)}, u32[]{:S(2)}) copy-start(bf16[256]{0:T(256)(128)(2,1)} %param.12) | copy-start | bytes 1540
  15.8 5.7 %copy-start.1 = (bf16[256,256]{1,0:T(8,128)(2,1)S(1)}, bf16[256,256]{1,0:T(8,128)(2,1)}, u32[]{:S(2)}) copy-start(bf16[256,256]{1,0:T(8,128)(2,1)} %w_ref.1) | copy-start | bytes 393220
  15.8 5.7 %copy-start.3 = (bf16[128,256]{1,0:T(8,128)(2,1)S(1)}, bf16[128,256]{1,0:T(8,128)(2,1)}, u32[]{:S(2)}) copy-start(bf16[128,256]{1,0:T(8,128)(2,1)} %refs_0_.3) | copy-start | bytes 196612
  15.8 5.6 %collective-permute-start.5 = (bf16[256,256]{1,0:T(8,128)(2,1)S(1)}, bf16[256,256]{1,0:T(8,128)(2,1)S(1)}, u32[]{:S(2)}, u32[]{:S(2)}) collective-permute-start(bf16[256,256]{1,0:T(8,128)(2,1)S(1)} %shard_map.104.refs_2_), channel_id=1, source_target_pairs={{0,2},{1,3},{2,0},{3,1},{4,6},{5,7},{6,4},{7,5},{8,10},{9,11},{10,... | collective-permute-start | bytes 393224 | tf_op jit(solution)/shard_map/ppermute | solution.py:168
  21.9 1.5 %collective-permute-start.6 = (bf16[336,256]{1,0:T(8,128)(2,1)S(1)}, bf16[336,256]{1,0:T(8,128)(2,1)S(1)}, u32[]{:S(2)}, u32[]{:S(2)}) collective-permute-start(bf16[336,256]{1,0:T(8,128)(2,1)S(1)} %get-tuple-element.30), channel_id=1, source_target_pairs={{0,1},{1,0},{2,3},{3,2},{4,5},{5,4},{6,7},{7,6},{8,9},{9,8},{10,11... | collective-permute-start | bytes 516104 | tf_op jit(solution)/shard_map/ppermute | solution.py:168
  23.7 5.6 %collective-permute-start.7 = (bf16[80,256]{1,0:T(8,128)(2,1)S(1)}, bf16[80,256]{1,0:T(8,128)(2,1)S(1)}, u32[]{:S(2)}, u32[]{:S(2)}) collective-permute-start(bf16[80,256]{1,0:T(8,128)(2,1)S(1)} %get-tuple-element.33.refs_0_), channel_id=1, source_target_pairs={{0,4},{4,0},{8,12},{12,8},{1,5},{5,1},{9,13},{13,9},{2,6},{6,2},{1... | collective-permute-start | bytes 122888 | tf_op jit(solution)/shard_map/ppermute | solution.py:168
  23.8 10.4 %collective-permute-start.10 = (bf16[128,256]{1,0:T(8,128)(2,1)S(1)}, bf16[128,256]{1,0:T(8,128)(2,1)S(1)}, u32[]{:S(2)}, u32[]{:S(2)}) collective-permute-start(bf16[128,256]{1,0:T(8,128)(2,1)S(1)} %get-tuple-element.36), channel_id=1, source_target_pairs={{0,4},{4,0},{8,12},{12,8},{1,5},{5,1},{9,13},{13,9},{2,6},{6,2},{1... | collective-permute-start | bytes 196616 | tf_op jit(solution)/shard_map/ppermute | solution.py:168
  25.8 6.6 %collective-permute-start.8 = (bf16[80,256]{1,0:T(8,128)(2,1)S(1)}, bf16[80,256]{1,0:T(8,128)(2,1)S(1)}, u32[]{:S(2)}, u32[]{:S(2)}) collective-permute-start(bf16[80,256]{1,0:T(8,128)(2,1)S(1)} %get-tuple-element.33.refs_0_), channel_id=1, source_target_pairs={{0,8},{4,12},{8,0},{12,4},{1,9},{5,13},{9,1},{13,5},{2,10},{6,14},... | collective-permute-start | bytes 122888 | tf_op jit(solution)/shard_map/ppermute | solution.py:168
  27.1 6.3 %collective-permute-start.9 = (bf16[80,256]{1,0:T(8,128)(2,1)S(1)}, bf16[80,256]{1,0:T(8,128)(2,1)S(1)}, u32[]{:S(2)}, u32[]{:S(2)}) collective-permute-start(bf16[80,256]{1,0:T(8,128)(2,1)S(1)} %get-tuple-element.33.refs_0_), channel_id=1, source_target_pairs={{0,12},{4,8},{8,4},{12,0},{1,13},{5,9},{9,5},{13,1},{2,14},{6,10},... | collective-permute-start | bytes 122888 | tf_op jit(solution)/shard_map/ppermute | solution.py:168
  28.2 9.0 %collective-permute-start.11 = (bf16[128,256]{1,0:T(8,128)(2,1)S(1)}, bf16[128,256]{1,0:T(8,128)(2,1)S(1)}, u32[]{:S(2)}, u32[]{:S(2)}) collective-permute-start(bf16[128,256]{1,0:T(8,128)(2,1)S(1)} %get-tuple-element.37), channel_id=1, source_target_pairs={{0,8},{4,12},{8,0},{12,4},{1,9},{5,13},{9,1},{13,5},{2,10},{6,14},... | collective-permute-start | bytes 196616 | tf_op jit(solution)/shard_map/ppermute | solution.py:168
  29.3 7.9 %collective-permute-start.12 = (bf16[128,256]{1,0:T(8,128)(2,1)S(1)}, bf16[128,256]{1,0:T(8,128)(2,1)S(1)}, u32[]{:S(2)}, u32[]{:S(2)}) collective-permute-start(bf16[128,256]{1,0:T(8,128)(2,1)S(1)} %get-tuple-element.38), channel_id=1, source_target_pairs={{0,12},{4,8},{8,4},{12,0},{1,13},{5,9},{9,5},{13,1},{2,14},{6,10},... | collective-permute-start | bytes 196616 | tf_op jit(solution)/shard_map/ppermute | solution.py:168
  33.5 3.8 %collective-permute-start.13 = (bf16[64,256]{1,0:T(8,128)(2,1)S(1)}, bf16[64,256]{1,0:T(8,128)(2,1)S(1)}, u32[]{:S(2)}, u32[]{:S(2)}) collective-permute-start(bf16[64,256]{1,0:T(8,128)(2,1)S(1)} %get-tuple-element.39.refs_4_), channel_id=1, source_target_pairs={{0,1},{1,0},{2,3},{3,2},{4,5},{5,4},{6,7},{7,6},{8,9},{9,8},{10,11... | collective-permute-start | bytes 98312 | tf_op jit(solution)/shard_map/ppermute | solution.py:168
  33.5 4.3 %collective-permute-start.14 = (bf16[64,256]{1,0:T(8,128)(2,1)S(1)}, bf16[64,256]{1,0:T(8,128)(2,1)S(1)}, u32[]{:S(2)}, u32[]{:S(2)}) collective-permute-start(bf16[64,256]{1,0:T(8,128)(2,1)S(1)} %get-tuple-element.39.refs_4_), channel_id=1, source_target_pairs={{0,2},{1,3},{2,0},{3,1},{4,6},{5,7},{6,4},{7,5},{8,10},{9,11},{10,... | collective-permute-start | bytes 98312 | tf_op jit(solution)/shard_map/ppermute | solution.py:168
  34.1 3.7 %collective-permute-start.15 = (bf16[64,256]{1,0:T(8,128)(2,1)S(1)}, bf16[64,256]{1,0:T(8,128)(2,1)S(1)}, u32[]{:S(2)}, u32[]{:S(2)}) collective-permute-start(bf16[64,256]{1,0:T(8,128)(2,1)S(1)} %get-tuple-element.39.refs_4_), channel_id=1, source_target_pairs={{0,3},{1,2},{2,1},{3,0},{4,7},{5,6},{6,5},{7,4},{8,11},{9,10},{10,... | collective-permute-start | bytes 98312 | tf_op jit(solution)/shard_map/ppermute | solution.py:168

commit v5 on v4

--- a/solution.py
+++ b/solution.py
@@ -65,11 +65,13 @@
     return body
 
 
-def forward_kernel(n_row):
+def forward_kernel(n_row, n_cot):
     def body(a_ref, *refs):
-        ins, (keep_ref, send_ref) = refs[:n_row], refs[-2:]
+        ins, (keep_ref, send_ref, *outs) = refs[:n_row], refs[n_row + n_cot :]
+        for ref, out in zip(refs[n_row:], outs):
+            out[...] = ref[...]
         half = keep_ref.shape[0]
-        x = jnp.concatenate([ref[...] for ref in ins], axis=0)
+        x = jnp.concatenate([ref[...] for ref in ins[::-1]], axis=0)
         send_ref[...] = dot(a_ref[half:, :], x).astype(BF)
         keep_ref[...] = dot(a_ref[:half, :], x)
 
@@ -121,13 +123,17 @@
     return body
 
 
-def backward_kernel(at_ref, keep_ref, got_ref, piece_ref, line_ref, *outs):
-    outs, part_ref = outs[:-1], outs[-1]
-    rows, piece = keep_ref.shape[0], piece_ref.shape[0]
-    tile = at_ref.shape[0] // len(outs)
+def part_kernel(got_ref, piece_ref, line_ref, part_ref):
+    piece = piece_ref.shape[0]
+    rows = got_ref.shape[0] - piece - PAD
     part_ref[:piece, :] = (piece_ref[...] + got_ref[rows : rows + piece, :].astype(F32)).astype(BF)
     lines = got_ref[rows + piece :, :].astype(F32)
     part_ref[piece:, :] = two_rows(line_ref[...] + lines[0:1] + lines[1:2])
+
+
+def backward_kernel(at_ref, keep_ref, got_ref, *outs):
+    rows = keep_ref.shape[0]
+    tile = at_ref.shape[0] // len(outs)
     g = jnp.concatenate([keep_ref[...], got_ref[:rows, :]], axis=0)
     for p, out in enumerate(outs):
         out[...] = dot(at_ref[p * tile : (p + 1) * tile, :], g).astype(BF)
@@ -191,11 +197,11 @@
         smem=2,
         count=3,
     )(columns.transpose(1, 2, 0), counts.T, adj_tiles)
-    keep, send = call(
-        forward_kernel(n_row),
-        (shape(half, width, dtype=F32), shape(half, width)),
+    keep, send, *cots[1:] = call(
+        forward_kernel(n_row, n_chip - 1),
+        (shape(half, width, dtype=F32), shape(half, width)) + (shape(tile, width),) * (n_chip - 1),
         count=n_row + n_chip,
-    )(a, *xs, *cots[1:])
+    )(a, *xs[::-1], *cots[1:])
     chip = call(chip_kernel, shape(half, width), count=2)(keep, swap(send, "col", n_col, 1))
     sums = [chip] + [swap(chip, "col", n_col, 2 * v) for v in range(1, n_chip)]
     act, keep, mine, line, send = call(
@@ -210,12 +216,12 @@
         count=2 + 2 * n_chip,
         scratch=[pltpu.VMEM((width, width), F32)],
     )(weight, bias_term.reshape(1, width), *cots, *sums)
-    *feats, part = call(
-        backward_kernel, (shape(tile, width),) * n_row + (shape(piece + PAD, width),), count=5
-    )(at, keep, swap(send, "col", n_col, 1), mine, line)
+    got = swap(send, "col", n_col, 1)
+    part = call(part_kernel, shape(piece + PAD, width), count=3)(got, mine, line)
+    feats = call(backward_kernel, (shape(tile, width),) * n_row, count=3)(at, keep, got)
     whole, line = call(
         piece_kernel, (shape(piece, width), shape(1, width, dtype=F32)), count=n_row
-    )(*spread(part, "row", n_row))
+    )(*spread(part, "row", n_row)[::-1])
     act, grad_features, grad_weight, grad_bias = call(
         last_kernel(n_row, n_col),
         (
@@ -225,7 +231,7 @@
             shape(1, width, dtype=F32),
         ),
         count=2 + n_row + n_col,
-    )(act, line, *deal(feats, "row"), *spread(whole, "col", n_col))
+    )(act, line, *deal(feats, "row")[::-1], *spread(whole, "col", n_col))
     return act, grad_features, grad_weight, grad_bias.reshape(width)
 
 

time: 39.1 us -> 37.9 us (0.969)
  waiting for transfers between devices: 15.2 us -> 12.2 us
  starting transfers between devices: 18 us -> 19.9 us
    ppermute x16, waiting for transfers between devices: 15.2 us -> 12.2 us  [swap(): return lax.ppermute(x, axis, [(i, i ^ by) for i in range(n)])]
    ppermute x16, starting transfers between devices: 18 us -> 19.9 us  [swap(): return lax.ppermute(x, axis, [(i, i ^ by) for i in range(n)])]
  transfers between devices with their start and end apart: 16 -> 16, of which waited for: 9 -> 9; matrix products, arithmetic and copies ran while one was open for 0% -> 0% of each run, Pallas kernels for 3% -> 4%
where the time goes in v5:
time: 37.9 us; the launch traced here: 37.7 us
  starting transfers between devices  19.9 us (53%)
  waiting for transfers between devices  12.2 us (32%)
  Pallas kernels  3.14 us (8%)
  local copies, waits for them, and re-layouts  1.65 us (4%)
  between operations  0.72 us (2%)
    ppermute x16, starting transfers between devices, swap(): return lax.ppermute(x, axis, [(i, i ^ by) for i in range(n)])  19.9 us
    ppermute x16, waiting for transfers between devices, swap(): return lax.ppermute(x, axis, [(i, i ^ by) for i in range(n)])  12.2 us
    unnamed x14, local copies, waits for them, and re-layouts  1.64 us
    pallas_call x1, Pallas kernels, shards(): call(dense_kernel(n_chip), (shape(n_col * tile, n_row * tile), shape(n_ro...  1.25 us
    pallas_call x1, Pallas kernels, shards(): call(last_kernel(n_row, n_col), (shape(tile, width), shape(tile, width),...  0.78 us
  transfers between devices with their start and end apart: 16, of which 9 were waited for; matrix products, arithmetic and copies ran while one was open for 0% of the time, Pallas kernels for 4%

profile of v5, /device:TPU:0, one launch (start us, length us, event | category | flops | bytes accessed | tf_op | source)
XLA Modules:
  0.0 37.7 jit_solution(1481532893764268113)
XLA Ops:
  0.6 5.1 %collective-permute-start = (bf16[128,256]{1,0:T(8,128)(2,1)}, bf16[128,256]{1,0:T(8,128)(2,1)S(1)}, u32[]{:S(2)}, u32[]{:S(2)}) collective-permute-start(bf16[128,256]{1,0:T(8,128)(2,1)} %refs_3_.1), channel_id=1, source_target_pairs={{0,12},{4,8},{8,4},{12,0},{1,13},{5,9},{9,5},{13,1},{2,14},{6,10},... | collective-permute-start | bytes 196616 | tf_op jit(solution)/shard_map/ppermute | solution.py:174
  5.7 0.0 collective-permute-start.1
  5.7 0.6 %collective-permute-start.2 = (bf16[128,256]{1,0:T(8,128)(2,1)}, bf16[128,256]{1,0:T(8,128)(2,1)S(1)}, u32[]{:S(2)}, u32[]{:S(2)}) collective-permute-start(bf16[128,256]{1,0:T(8,128)(2,1)} %refs_3_.1), channel_id=1, source_target_pairs={{0,4},{4,0},{8,12},{12,8},{1,5},{5,1},{9,13},{13,9},{2,6},{6,2},{1... | collective-permute-start | bytes 196616 | tf_op jit(solution)/shard_map/ppermute | solution.py:174
  6.4 1.6 %collective-permute-start.3 = (bf16[128,256]{1,0:T(8,128)(2,1)}, bf16[128,256]{1,0:T(8,128)(2,1)S(1)}, u32[]{:S(2)}, u32[]{:S(2)}) collective-permute-start(bf16[128,256]{1,0:T(8,128)(2,1)} %refs_0_.1), channel_id=1, source_target_pairs={{0,2},{1,3},{2,0},{3,1},{4,6},{5,7},{6,4},{7,5},{8,10},{9,11},{10,... | collective-permute-start | bytes 196616 | tf_op jit(solution)/shard_map/ppermute | solution.py:174
  8.0 0.0 copy-start.4
  8.0 0.0 copy-start.5
  8.0 0.7 %copy-done.4 = s32[4,1,2]{0,2,1:T(2,128)S(1)} copy-done((s32[4,1,2]{0,2,1:T(2,128)S(1)}, s32[4,1,2]{0,2,1:T(2,128)}, u32[]{:S(2)}) %copy-start.4) | copy-done | bytes 56
  8.7 0.0 copy-done.5
  8.7 0.0 copy-start
  8.7 0.9 %copy-done = bf16[4,1,2,128,128]{4,3,2,1,0:T(8,128)(2,1)S(1)} copy-done((bf16[4,1,2,128,128]{4,3,2,1,0:T(8,128)(2,1)S(1)}, bf16[4,1,2,128,128]{4,3,2,1,0:T(8,128)(2,1)}, u32[]{:S(2)}) %copy-start) | copy-done | bytes 262168
  9.7 0.0 copy-start.2
  9.7 1.2 %shard_map.102 = (bf16[512,512]{1,0:T(8,128)(2,1)S(1)}, bf16[512,512]{1,0:T(8,128)(2,1)S(1)}) custom-call(s32[1,2,4]{2,1,0:T(2,128)S(1)} %bitcast.3, s32[1,4]{1,0:T(1,128)S(1)} %bitcast.4, bf16[4,1,2,128,128]{4,3,2,1,0:T(8,128)(2,1)S(1)} %copy-done), custom_call_target="tpu_custom_call" | custom-call | tf_op jit(solution)/shard_map/pallas_call | solution.py:194
  10.9 0.0 collective-permute-done.refs_0_
  10.9 0.6 %collective-permute-done.1.refs_1_ = bf16[128,256]{1,0:T(8,128)(2,1)S(1)} collective-permute-done((bf16[128,256]{1,0:T(8,128)(2,1)}, bf16[128,256]{1,0:T(8,128)(2,1)S(1)}, u32[]{:S(2)}, u32[]{:S(2)}) %collective-permute-start.1) | collective-permute-done | bytes 65568 | tf_op jit(solution)/shard_map/ppermute | solution.py:174
  11.6 0.0 collective-permute-done.2.refs_2_
  11.6 0.0 collective-permute-done.3.refs_4_
  11.6 0.0 copy-done.2
  11.6 0.3 shard_map.103
  11.9 0.1 collective-permute-start.4
  12.0 1.3 %collective-permute-done.4.got_ref = bf16[256,256]{1,0:T(8,128)(2,1)S(1)} collective-permute-done((bf16[256,256]{1,0:T(8,128)(2,1)S(1)}, bf16[256,256]{1,0:T(8,128)(2,1)S(1)}, u32[]{:S(2)}, u32[]{:S(2)}) %collective-permute-start.4) | collective-permute-done | bytes 131104 | tf_op jit(solution)/shard_map/ppermute | solution.py:174
  13.3 1.6 %collective-permute-start.5 = (bf16[256,256]{1,0:T(8,128)(2,1)S(1)}, bf16[256,256]{1,0:T(8,128)(2,1)S(1)}, u32[]{:S(2)}, u32[]{:S(2)}) collective-permute-start(bf16[256,256]{1,0:T(8,128)(2,1)S(1)} %shard_map.104.refs_2_), channel_id=1, source_target_pairs={{0,2},{1,3},{2,0},{3,1},{4,6},{5,7},{6,4},{7,5},{8,10},{9,11},{10,... | collective-permute-start | bytes 393224 | tf_op jit(solution)/shard_map/ppermute | solution.py:174
  14.9 0.0 copy-done.6
  14.9 4.1 %collective-permute-done.5.refs_3_ = bf16[256,256]{1,0:T(8,128)(2,1)S(1)} collective-permute-done((bf16[256,256]{1,0:T(8,128)(2,1)S(1)}, bf16[256,256]{1,0:T(8,128)(2,1)S(1)}, u32[]{:S(2)}, u32[]{:S(2)}) %collective-permute-start.5) | collective-permute-done | bytes 131104 | tf_op jit(solution)/shard_map/ppermute | solution.py:174
  18.9 0.0 copy-done.1
  18.9 0.0 copy-done.3
  19.0 0.4 %shard_map.105 = (bf16[128,256]{1,0:T(8,128)(2,1)S(1)}, bf16[256,256]{1,0:T(8,128)(2,1)S(1)}, f32[64,256]{1,0:T(8,128)S(1)}, f32[1,256]{1,0:T(1,128)S(1)}, bf16[336,256]{1,0:T(8,128)(2,1)S(1)}) custom-call(bf16[256,256]{1,0:T(8,128)(2,1)S(1)} %copy-done.1, bf16[1,256]{1,0:T(2,128)(2,1)S(1)} %reshape.14.b_ref, bf16[128,256]{1,0:T(8,128)(2,1)S(1)} %copy-done.3, ...), custom_call_target="tpu_custom_call" | custom-call | tf_op jit(solution)/shard_map/pallas_call | solution.py:207
  19.4 0.1 collective-permute-start.6
  19.5 1.4 %collective-permute-done.6.got_ref = bf16[336,256]{1,0:T(8,128)(2,1)S(1)} collective-permute-done((bf16[336,256]{1,0:T(8,128)(2,1)S(1)}, bf16[336,256]{1,0:T(8,128)(2,1)S(1)}, u32[]{:S(2)}, u32[]{:S(2)}) %collective-permute-start.6) | collective-permute-done | bytes 172064 | tf_op jit(solution)/shard_map/ppermute | solution.py:174
  20.9 3.1 %collective-permute-start.7 = (bf16[80,256]{1,0:T(8,128)(2,1)S(1)}, bf16[80,256]{1,0:T(8,128)(2,1)S(1)}, u32[]{:S(2)}, u32[]{:S(2)}) collective-permute-start(bf16[80,256]{1,0:T(8,128)(2,1)S(1)} %shard_map.106.refs_3_), channel_id=1, source_target_pairs={{0,12},{4,8},{8,4},{12,0},{1,13},{5,9},{9,5},{13,1},{2,14},{6,10},... | collective-permute-start | bytes 122888 | tf_op jit(solution)/shard_map/ppermute | solution.py:174
  24.0 0.3 shard_map.108
  24.3 0.9 %collective-permute-start.10 = (bf16[128,256]{1,0:T(8,128)(2,1)S(1)}, bf16[128,256]{1,0:T(8,128)(2,1)S(1)}, u32[]{:S(2)}, u32[]{:S(2)}) collective-permute-start(bf16[128,256]{1,0:T(8,128)(2,1)S(1)} %get-tuple-element.35), channel_id=1, source_target_pairs={{0,12},{4,8},{8,4},{12,0},{1,13},{5,9},{9,5},{13,1},{2,14},{6,10},... | collective-permute-start | bytes 196616 | tf_op jit(solution)/shard_map/ppermute | solution.py:174
  25.2 0.0 collective-permute-start.8
  25.2 3.6 %collective-permute-start.9 = (bf16[80,256]{1,0:T(8,128)(2,1)S(1)}, bf16[80,256]{1,0:T(8,128)(2,1)S(1)}, u32[]{:S(2)}, u32[]{:S(2)}) collective-permute-start(bf16[80,256]{1,0:T(8,128)(2,1)S(1)} %shard_map.106.refs_3_), channel_id=1, source_target_pairs={{0,4},{4,0},{8,12},{12,8},{1,5},{5,1},{9,13},{13,9},{2,6},{6,2},{1... | collective-permute-start | bytes 122888 | tf_op jit(solution)/shard_map/ppermute | solution.py:174
  28.8 0.0 collective-permute-start.11
  28.8 0.0 collective-permute-done.7.refs_0_
  28.8 1.3 %collective-permute-start.12 = (bf16[128,256]{1,0:T(8,128)(2,1)S(1)}, bf16[128,256]{1,0:T(8,128)(2,1)S(1)}, u32[]{:S(2)}, u32[]{:S(2)}) collective-permute-start(bf16[128,256]{1,0:T(8,128)(2,1)S(1)} %get-tuple-element.37), channel_id=1, source_target_pairs={{0,4},{4,0},{8,12},{12,8},{1,5},{5,1},{9,13},{13,9},{2,6},{6,2},{1... | collective-permute-start | bytes 196616 | tf_op jit(solution)/shard_map/ppermute | solution.py:174
  30.1 1.6 %collective-permute-done.8.refs_1_ = bf16[80,256]{1,0:T(8,128)(2,1)S(1)} collective-permute-done((bf16[80,256]{1,0:T(8,128)(2,1)S(1)}, bf16[80,256]{1,0:T(8,128)(2,1)S(1)}, u32[]{:S(2)}, u32[]{:S(2)}) %collective-permute-start.8) | collective-permute-done | bytes 40992 | tf_op jit(solution)/shard_map/ppermute | solution.py:174
  31.8 0.1 collective-permute-done.9.refs_2_
  31.9 0.1 collective-permute-start.13
  32.0 1.6 %collective-permute-start.14 = (bf16[64,256]{1,0:T(8,128)(2,1)S(1)}, bf16[64,256]{1,0:T(8,128)(2,1)S(1)}, u32[]{:S(2)}, u32[]{:S(2)}) collective-permute-start(bf16[64,256]{1,0:T(8,128)(2,1)S(1)} %get-tuple-element.39.refs_4_), channel_id=1, source_target_pairs={{0,2},{1,3},{2,0},{3,1},{4,6},{5,7},{6,4},{7,5},{8,10},{9,11},{10,... | collective-permute-start | bytes 98312 | tf_op jit(solution)/shard_map/ppermute | solution.py:174
  33.6 0.0 collective-permute-done.10.refs_0_
  33.6 0.3 collective-permute-start.15
  33.9 0.5 %collective-permute-done.11.refs_1_ = bf16[128,256]{1,0:T(8,128)(2,1)S(1)} collective-permute-done((bf16[128,256]{1,0:T(8,128)(2,1)S(1)}, bf16[128,256]{1,0:T(8,128)(2,1)S(1)}, u32[]{:S(2)}, u32[]{:S(2)}) %collective-permute-start.11) | collective-permute-done | bytes 65568 | tf_op jit(solution)/shard_map/ppermute | solution.py:174
  34.4 0.0 collective-permute-done.12.refs_2_
  34.4 0.0 collective-permute-done.13.refs_5_
  34.4 1.6 %collective-permute-done.14.refs_6_ = bf16[64,256]{1,0:T(8,128)(2,1)S(1)} collective-permute-done((bf16[64,256]{1,0:T(8,128)(2,1)S(1)}, bf16[64,256]{1,0:T(8,128)(2,1)S(1)}, u32[]{:S(2)}, u32[]{:S(2)}) %collective-permute-start.14) | collective-permute-done | bytes 32800 | tf_op jit(solution)/shard_map/ppermute | solution.py:174
  36.0 0.9 %collective-permute-done.15.refs_7_ = bf16[64,256]{1,0:T(8,128)(2,1)S(1)} collective-permute-done((bf16[64,256]{1,0:T(8,128)(2,1)S(1)}, bf16[64,256]{1,0:T(8,128)(2,1)S(1)}, u32[]{:S(2)}, u32[]{:S(2)}) %collective-permute-start.15) | collective-permute-done | bytes 32800 | tf_op jit(solution)/shard_map/ppermute | solution.py:174
  36.9 0.8 %shard_map.109 = (bf16[128,256]{1,0:T(8,128)(2,1)}, bf16[128,256]{1,0:T(8,128)(2,1)}, f32[256,256]{1,0:T(8,128)}, f32[1,256]{1,0:T(1,128)}) custom-call(bf16[128,256]{1,0:T(8,128)(2,1)S(1)} %get-tuple-element.28.act_ref, f32[1,256]{1,0:T(1,128)S(1)} %get-tuple-element.32.line_ref, bf16[128,256]{1,0:T(8,128)(2,1)S(1)} %collective-permute-done.10.refs_0_, ...), custom_call_target="tpu_custom_call" | custom-call | tf_op jit(solution)/shard_map/pallas_call | solution.py:225
  (7 shorter events, 0.1 us)
Async XLA Ops:
  0.6 10.3 %collective-permute-start = (bf16[128,256]{1,0:T(8,128)(2,1)}, bf16[128,256]{1,0:T(8,128)(2,1)S(1)}, u32[]{:S(2)}, u32[]{:S(2)}) collective-permute-start(bf16[128,256]{1,0:T(8,128)(2,1)} %refs_3_.1), channel_id=1, source_target_pairs={{0,12},{4,8},{8,4},{12,0},{1,13},{5,9},{9,5},{13,1},{2,14},{6,10},... | collective-permute-start | bytes 196616 | tf_op jit(solution)/shard_map/ppermute | solution.py:174
  5.7 5.8 %collective-permute-start.1 = (bf16[128,256]{1,0:T(8,128)(2,1)}, bf16[128,256]{1,0:T(8,128)(2,1)S(1)}, u32[]{:S(2)}, u32[]{:S(2)}) collective-permute-start(bf16[128,256]{1,0:T(8,128)(2,1)} %refs_3_.1), channel_id=1, source_target_pairs={{0,8},{4,12},{8,0},{12,4},{1,9},{5,13},{9,1},{13,5},{2,10},{6,14},... | collective-permute-start | bytes 196616 | tf_op jit(solution)/shard_map/ppermute | solution.py:174
  5.7 5.8 %collective-permute-start.2 = (bf16[128,256]{1,0:T(8,128)(2,1)}, bf16[128,256]{1,0:T(8,128)(2,1)S(1)}, u32[]{:S(2)}, u32[]{:S(2)}) collective-permute-start(bf16[128,256]{1,0:T(8,128)(2,1)} %refs_3_.1), channel_id=1, source_target_pairs={{0,4},{4,0},{8,12},{12,8},{1,5},{5,1},{9,13},{13,9},{2,6},{6,2},{1... | collective-permute-start | bytes 196616 | tf_op jit(solution)/shard_map/ppermute | solution.py:174
  6.4 5.2 %collective-permute-start.3 = (bf16[128,256]{1,0:T(8,128)(2,1)}, bf16[128,256]{1,0:T(8,128)(2,1)S(1)}, u32[]{:S(2)}, u32[]{:S(2)}) collective-permute-start(bf16[128,256]{1,0:T(8,128)(2,1)} %refs_0_.1), channel_id=1, source_target_pairs={{0,2},{1,3},{2,0},{3,1},{4,6},{5,7},{6,4},{7,5},{8,10},{9,11},{10,... | collective-permute-start | bytes 196616 | tf_op jit(solution)/shard_map/ppermute | solution.py:174
  8.0 0.7 %copy-start.4 = (s32[4,1,2]{0,2,1:T(2,128)S(1)}, s32[4,1,2]{0,2,1:T(2,128)}, u32[]{:S(2)}) copy-start(s32[4,1,2]{0,2,1:T(2,128)} %param.9) | copy-start | bytes 100
  8.0 0.7 %copy-start.5 = (s32[4,1]{0,1:T(1,128)S(1)}, s32[4,1]{0,1:T(1,128)}, u32[]{:S(2)}) copy-start(s32[4,1]{0,1:T(1,128)} %param.10) | copy-start | bytes 52
  8.7 1.0 %copy-start = (bf16[4,1,2,128,128]{4,3,2,1,0:T(8,128)(2,1)S(1)}, bf16[4,1,2,128,128]{4,3,2,1,0:T(8,128)(2,1)}, u32[]{:S(2)}) copy-start(bf16[4,1,2,128,128]{4,3,2,1,0:T(8,128)(2,1)} %tiles_ref.1) | copy-start | bytes 786436
  9.7 1.9 %copy-start.2 = (bf16[128,256]{1,0:T(8,128)(2,1)S(1)}, bf16[128,256]{1,0:T(8,128)(2,1)}, u32[]{:S(2)}) copy-start(bf16[128,256]{1,0:T(8,128)(2,1)} %refs_3_.1) | copy-start | bytes 196612
  11.9 1.4 %collective-permute-start.4 = (bf16[256,256]{1,0:T(8,128)(2,1)S(1)}, bf16[256,256]{1,0:T(8,128)(2,1)S(1)}, u32[]{:S(2)}, u32[]{:S(2)}) collective-permute-start(bf16[256,256]{1,0:T(8,128)(2,1)S(1)} %get-tuple-element.27), channel_id=1, source_target_pairs={{0,1},{1,0},{2,3},{3,2},{4,5},{5,4},{6,7},{7,6},{8,9},{9,8},{10,11... | collective-permute-start | bytes 393224 | tf_op jit(solution)/shard_map/ppermute | solution.py:174
  13.3 1.6 %copy-start.6 = (bf16[256]{0:T(256)(128)(2,1)S(1)}, bf16[256]{0:T(256)(128)(2,1)}, u32[]{:S(2)}) copy-start(bf16[256]{0:T(256)(128)(2,1)} %param.12) | copy-start | bytes 1540
  13.3 5.7 %copy-start.1 = (bf16[256,256]{1,0:T(8,128)(2,1)S(1)}, bf16[256,256]{1,0:T(8,128)(2,1)}, u32[]{:S(2)}) copy-start(bf16[256,256]{1,0:T(8,128)(2,1)} %w_ref.1) | copy-start | bytes 393220
  13.3 5.7 %copy-start.3 = (bf16[128,256]{1,0:T(8,128)(2,1)S(1)}, bf16[128,256]{1,0:T(8,128)(2,1)}, u32[]{:S(2)}) copy-start(bf16[128,256]{1,0:T(8,128)(2,1)} %refs_0_.1) | copy-start | bytes 196612
  13.3 5.6 %collective-permute-start.5 = (bf16[256,256]{1,0:T(8,128)(2,1)S(1)}, bf16[256,256]{1,0:T(8,128)(2,1)S(1)}, u32[]{:S(2)}, u32[]{:S(2)}) collective-permute-start(bf16[256,256]{1,0:T(8,128)(2,1)S(1)} %shard_map.104.refs_2_), channel_id=1, source_target_pairs={{0,2},{1,3},{2,0},{3,1},{4,6},{5,7},{6,4},{7,5},{8,10},{9,11},{10,... | collective-permute-start | bytes 393224 | tf_op jit(solution)/shard_map/ppermute | solution.py:174
  19.4 1.5 %collective-permute-start.6 = (bf16[336,256]{1,0:T(8,128)(2,1)S(1)}, bf16[336,256]{1,0:T(8,128)(2,1)S(1)}, u32[]{:S(2)}, u32[]{:S(2)}) collective-permute-start(bf16[336,256]{1,0:T(8,128)(2,1)S(1)} %get-tuple-element.29), channel_id=1, source_target_pairs={{0,1},{1,0},{2,3},{3,2},{4,5},{5,4},{6,7},{7,6},{8,9},{9,8},{10,11... | collective-permute-start | bytes 516104 | tf_op jit(solution)/shard_map/ppermute | solution.py:174
  20.9 7.9 %collective-permute-start.7 = (bf16[80,256]{1,0:T(8,128)(2,1)S(1)}, bf16[80,256]{1,0:T(8,128)(2,1)S(1)}, u32[]{:S(2)}, u32[]{:S(2)}) collective-permute-start(bf16[80,256]{1,0:T(8,128)(2,1)S(1)} %shard_map.106.refs_3_), channel_id=1, source_target_pairs={{0,12},{4,8},{8,4},{12,0},{1,13},{5,9},{9,5},{13,1},{2,14},{6,10},... | collective-permute-start | bytes 122888 | tf_op jit(solution)/shard_map/ppermute | solution.py:174
  24.3 9.3 %collective-permute-start.10 = (bf16[128,256]{1,0:T(8,128)(2,1)S(1)}, bf16[128,256]{1,0:T(8,128)(2,1)S(1)}, u32[]{:S(2)}, u32[]{:S(2)}) collective-permute-start(bf16[128,256]{1,0:T(8,128)(2,1)S(1)} %get-tuple-element.35), channel_id=1, source_target_pairs={{0,12},{4,8},{8,4},{12,0},{1,13},{5,9},{9,5},{13,1},{2,14},{6,10},... | collective-permute-start | bytes 196616 | tf_op jit(solution)/shard_map/ppermute | solution.py:174
  25.2 6.6 %collective-permute-start.8 = (bf16[80,256]{1,0:T(8,128)(2,1)S(1)}, bf16[80,256]{1,0:T(8,128)(2,1)S(1)}, u32[]{:S(2)}, u32[]{:S(2)}) collective-permute-start(bf16[80,256]{1,0:T(8,128)(2,1)S(1)} %shard_map.106.refs_3_), channel_id=1, source_target_pairs={{0,8},{4,12},{8,0},{12,4},{1,9},{5,13},{9,1},{13,5},{2,10},{6,14},... | collective-permute-start | bytes 122888 | tf_op jit(solution)/shard_map/ppermute | solution.py:174
  25.2 6.7 %collective-permute-start.9 = (bf16[80,256]{1,0:T(8,128)(2,1)S(1)}, bf16[80,256]{1,0:T(8,128)(2,1)S(1)}, u32[]{:S(2)}, u32[]{:S(2)}) collective-permute-start(bf16[80,256]{1,0:T(8,128)(2,1)S(1)} %shard_map.106.refs_3_), channel_id=1, source_target_pairs={{0,4},{4,0},{8,12},{12,8},{1,5},{5,1},{9,13},{13,9},{2,6},{6,2},{1... | collective-permute-start | bytes 122888 | tf_op jit(solution)/shard_map/ppermute | solution.py:174
  28.8 5.6 %collective-permute-start.11 = (bf16[128,256]{1,0:T(8,128)(2,1)S(1)}, bf16[128,256]{1,0:T(8,128)(2,1)S(1)}, u32[]{:S(2)}, u32[]{:S(2)}) collective-permute-start(bf16[128,256]{1,0:T(8,128)(2,1)S(1)} %get-tuple-element.36), channel_id=1, source_target_pairs={{0,8},{4,12},{8,0},{12,4},{1,9},{5,13},{9,1},{13,5},{2,10},{6,14},... | collective-permute-start | bytes 196616 | tf_op jit(solution)/shard_map/ppermute | solution.py:174
  28.8 5.6 %collective-permute-start.12 = (bf16[128,256]{1,0:T(8,128)(2,1)S(1)}, bf16[128,256]{1,0:T(8,128)(2,1)S(1)}, u32[]{:S(2)}, u32[]{:S(2)}) collective-permute-start(bf16[128,256]{1,0:T(8,128)(2,1)S(1)} %get-tuple-element.37), channel_id=1, source_target_pairs={{0,4},{4,0},{8,12},{12,8},{1,5},{5,1},{9,13},{13,9},{2,6},{6,2},{1... | collective-permute-start | bytes 196616 | tf_op jit(solution)/shard_map/ppermute | solution.py:174
  31.9 2.4 %collective-permute-start.13 = (bf16[64,256]{1,0:T(8,128)(2,1)S(1)}, bf16[64,256]{1,0:T(8,128)(2,1)S(1)}, u32[]{:S(2)}, u32[]{:S(2)}) collective-permute-start(bf16[64,256]{1,0:T(8,128)(2,1)S(1)} %get-tuple-element.39.refs_4_), channel_id=1, source_target_pairs={{0,1},{1,0},{2,3},{3,2},{4,5},{5,4},{6,7},{7,6},{8,9},{9,8},{10,11... | collective-permute-start | bytes 98312 | tf_op jit(solution)/shard_map/ppermute | solution.py:174
  32.0 4.0 %collective-permute-start.14 = (bf16[64,256]{1,0:T(8,128)(2,1)S(1)}, bf16[64,256]{1,0:T(8,128)(2,1)S(1)}, u32[]{:S(2)}, u32[]{:S(2)}) collective-permute-start(bf16[64,256]{1,0:T(8,128)(2,1)S(1)} %get-tuple-element.39.refs_4_), channel_id=1, source_target_pairs={{0,2},{1,3},{2,0},{3,1},{4,6},{5,7},{6,4},{7,5},{8,10},{9,11},{10,... | collective-permute-start | bytes 98312 | tf_op jit(solution)/shard_map/ppermute | solution.py:174
  33.6 3.3 %collective-permute-start.15 = (bf16[64,256]{1,0:T(8,128)(2,1)S(1)}, bf16[64,256]{1,0:T(8,128)(2,1)S(1)}, u32[]{:S(2)}, u32[]{:S(2)}) collective-permute-start(bf16[64,256]{1,0:T(8,128)(2,1)S(1)} %get-tuple-element.39.refs_4_), channel_id=1, source_target_pairs={{0,3},{1,2},{2,1},{3,0},{4,7},{5,6},{6,5},{7,4},{8,11},{9,10},{10,... | collective-permute-start | bytes 98312 | tf_op jit(solution)/shard_map/ppermute | solution.py:174

commit v6 on v5

--- a/solution.py
+++ b/solution.py
@@ -32,7 +32,7 @@
     return jax.ShapeDtypeStruct(dims, dtype)
 
 
-def own_piece(c, n_chip):
+def place_of(c, n_chip):
     return lax.rem(c, 2) * n_chip + lax.div(c, 2)
 
 
@@ -50,7 +50,7 @@
 
             @pl.when(k < cnts_ref[0, t])
             def _():
-                q = own_piece(jnp.bitwise_xor(t, c), n_chip)
+                q = place_of(jnp.bitwise_xor(t, c), n_chip)
                 p = jnp.bitwise_xor(cols_ref[0, k, t], r)
                 here = tiles_ref[t, 0, k]
                 qs = pl.ds(pl.multiple_of(q * tile, tile), tile)
@@ -90,12 +90,12 @@
 
 def middle_kernel(n_chip):
     def body(w_ref, b_ref, *refs):
-        cots, sums = refs[:n_chip], refs[n_chip : 2 * n_chip]
-        act_ref, keep_ref, piece_ref, line_ref, send_ref, local_ref = refs[2 * n_chip :]
+        sums, cots = refs[:n_chip], refs[n_chip : 2 * n_chip]
+        act_ref, keep_ref, part_ref, send_ref, agg_ref, grad_ref, local_ref = refs[2 * n_chip :]
         tile, width = cots[0].shape
-        rows = n_chip * tile
-        piece = piece_ref.shape[0]
+        rows, piece = n_chip * tile, width // 2
         c = lax.axis_index("col")
+        chip, core = lax.div(c, 2), lax.rem(c, 2)
         blocks = []
         for u in range(n_chip):
             total = sums[0][u * tile : (u + 1) * tile, :].astype(F32)
@@ -111,63 +111,70 @@
         gagg = dot(grad, w_ref[...], 1, 1).astype(BF)
         keep_ref[...] = gagg
         send_ref[:rows, :] = gagg
-        local_ref[...] = dot(agg, grad, 0, 0)
-        mine = pl.multiple_of(own_piece(c, n_chip) * piece, piece)
-        other = pl.multiple_of(own_piece(jnp.bitwise_xor(c, 1), n_chip) * piece, piece)
-        piece_ref[...] = local_ref[pl.ds(mine, piece), :]
+        for u in range(n_chip):
+            here = pl.ds(pl.multiple_of(jnp.bitwise_xor(chip, u) * tile, tile), tile)
+            agg_ref[here, :] = blocks[u]
+            grad_ref[here, :] = grad[u * tile : (u + 1) * tile, :]
+        grad = grad_ref[...]
+        local_ref[...] = dot(agg_ref[...], grad, 0, 0)
+        mine = pl.multiple_of(core * piece, piece)
+        other = pl.multiple_of((1 - core) * piece, piece)
+        lines = two_rows(jnp.sum(grad.astype(F32), axis=0, keepdims=True))
+        part_ref[:piece, :] = local_ref[pl.ds(mine, piece), :].astype(BF)
+        part_ref[piece:, :] = lines
         send_ref[rows : rows + piece, :] = local_ref[pl.ds(other, piece), :].astype(BF)
-        line = jnp.sum(grad.astype(F32), axis=0, keepdims=True)
-        line_ref[...] = line
-        send_ref[rows + piece :, :] = two_rows(line)
+        send_ref[rows + piece :, :] = lines
 
     return body
 
 
-def part_kernel(got_ref, piece_ref, line_ref, part_ref):
-    piece = piece_ref.shape[0]
-    rows = got_ref.shape[0] - piece - PAD
-    part_ref[:piece, :] = (piece_ref[...] + got_ref[rows : rows + piece, :].astype(F32)).astype(BF)
-    lines = got_ref[rows + piece :, :].astype(F32)
-    part_ref[piece:, :] = two_rows(line_ref[...] + lines[0:1] + lines[1:2])
-
-
-def backward_kernel(at_ref, keep_ref, got_ref, *outs):
-    rows = keep_ref.shape[0]
-    tile = at_ref.shape[0] // len(outs)
+def sum_lines(refs, first):
+    total = refs[0][first : first + PAD, :].astype(F32)
+    for ref in refs[1:]:
+        total = total + ref[first : first + PAD, :].astype(F32)
+    return total[0:1] + total[1:2]
+
+
+def backward_kernel(at_ref, keep_ref, got_ref, part_ref, *outs):
+    rows, tile = keep_ref.shape[0], outs[0].shape[0] - PAD
+    piece = part_ref.shape[0] - PAD
+    mine, other = part_ref[...].astype(F32), got_ref[rows:, :].astype(F32)
+    total = mine + other
+    outs[1][tile + PAD :, :] = total[:piece].astype(BF)
+    lines = two_rows(total[piece : piece + 1] + total[piece + 1 : piece + 2])
     g = jnp.concatenate([keep_ref[...], got_ref[:rows, :]], axis=0)
     for p, out in enumerate(outs):
-        out[...] = dot(at_ref[p * tile : (p + 1) * tile, :], g).astype(BF)
-
-
-def total_of(refs):
-    total = refs[0][...].astype(F32)
-    for ref in refs[1:]:
-        total = total + ref[...].astype(F32)
-    return total
-
-
-def piece_kernel(*refs):
-    ins, (piece_ref, line_ref) = refs[:-2], refs[-2:]
-    piece = piece_ref.shape[0]
-    total = total_of(ins)
-    piece_ref[...] = total[:piece].astype(BF)
-    line_ref[...] = total[piece : piece + 1] + total[piece + 1 : piece + 2]
-
-
-def last_kernel(n_row, n_col):
-    def body(act_ref, line_ref, *refs):
-        feats, pieces = refs[:n_row], refs[n_row : n_row + n_col]
-        act_out, feat_out, weight_out, bias_out = refs[n_row + n_col :]
-        piece = pieces[0].shape[0]
-        c = lax.axis_index("col")
-        act_out[...] = act_ref[...]
-        bias_out[...] = line_ref[...]
-        feat_out[...] = total_of(feats).astype(BF)
-        for q, ref in enumerate(pieces):
-            first = own_piece(jnp.bitwise_xor(c, q), n_col // 2) * piece
-            weight_out[pl.ds(pl.multiple_of(first, piece), piece), :] = ref[...].astype(F32)
-
-    return body
+        out[:tile, :] = dot(at_ref[p * tile : (p + 1) * tile, :], g).astype(BF)
+        out[tile : tile + PAD, :] = lines
+
+
+def pair_kernel(a_ref, b_ref, out_ref):
+    first = a_ref.shape[0] - out_ref.shape[0]
+    out_ref[...] = (a_ref[first:, :].astype(F32) + b_ref[first:, :].astype(F32)).astype(BF)
+
+
+def sum_kernel(a_ref, b_ref, *refs):
+    feats, (part_ref, feat_ref, line_ref) = refs[:-3], refs[-3:]
+    part_ref[...] = (a_ref[...].astype(F32) + b_ref[...].astype(F32)).astype(BF)
+    tile = feat_ref.shape[0]
+    total = feats[0][:tile, :].astype(F32)
+    for ref in feats[1:]:
+        total = total + ref[:tile, :].astype(F32)
+    feat_ref[...] = total.astype(BF)
+    line_ref[...] = sum_lines(feats, tile)
+
+
+def last_kernel(act_ref, feat_ref, line_ref, mine_ref, got_ref, *outs):
+    act_out, feat_out, weight_out, bias_out = outs
+    piece = mine_ref.shape[0]
+    core = lax.rem(lax.axis_index("col"), 2)
+    act_out[...] = act_ref[...]
+    feat_out[...] = feat_ref[...]
+    bias_out[...] = line_ref[...]
+    mine = pl.multiple_of(core * piece, piece)
+    other = pl.multiple_of((1 - core) * piece, piece)
+    weight_out[pl.ds(mine, piece), :] = mine_ref[...].astype(F32)
+    weight_out[pl.ds(other, piece), :] = got_ref[...].astype(F32)
 
 
 def swap(x, axis, n, by):
@@ -176,7 +183,7 @@
 
 def deal(xs, axis):
     n = len(xs)
-    got = {by: swap(xs[by], axis, n, by) for by in [*range(2, n), 1]}
+    got = {by: swap(xs[by], axis, n, by) for by in range(1, n)}
     return [xs[0]] + [got[by] for by in range(1, n)]
 
 
@@ -187,7 +194,7 @@
 def shards(n_row, n_col, features, adj_tiles, columns, counts, weight, bias_term, cotangent):
     tile, width = features.shape
     n_chip = n_col // 2
-    piece = width // n_col
+    piece = width // 2
     half = n_chip * tile
     xs = spread(features, "row", n_row)
     cots = [cotangent] + [swap(cotangent, "col", n_col, 2 * v) for v in range(1, n_chip)]
@@ -204,34 +211,41 @@
     )(a, *xs[::-1], *cots[1:])
     chip = call(chip_kernel, shape(half, width), count=2)(keep, swap(send, "col", n_col, 1))
     sums = [chip] + [swap(chip, "col", n_col, 2 * v) for v in range(1, n_chip)]
-    act, keep, mine, line, send = call(
+    act, keep, part, send = call(
         middle_kernel(n_chip),
         (
             shape(tile, width),
             shape(half, width),
-            shape(piece, width, dtype=F32),
-            shape(1, width, dtype=F32),
+            shape(piece + PAD, width),
             shape(half + piece + PAD, width),
         ),
         count=2 + 2 * n_chip,
-        scratch=[pltpu.VMEM((width, width), F32)],
-    )(weight, bias_term.reshape(1, width), *cots, *sums)
-    got = swap(send, "col", n_col, 1)
-    part = call(part_kernel, shape(piece + PAD, width), count=3)(got, mine, line)
-    feats = call(backward_kernel, (shape(tile, width),) * n_row, count=3)(at, keep, got)
-    whole, line = call(
-        piece_kernel, (shape(piece, width), shape(1, width, dtype=F32)), count=n_row
-    )(*spread(part, "row", n_row)[::-1])
+        scratch=[
+            pltpu.VMEM((half, width), BF),
+            pltpu.VMEM((half, width), BF),
+            pltpu.VMEM((width, width), F32),
+        ],
+    )(weight, bias_term.reshape(1, width), *sums, *cots)
+    messages = [shape(tile + PAD, width)] * n_row
+    messages[1] = shape(tile + PAD + piece, width)
+    sent = call(backward_kernel, tuple(messages), count=4)(
+        at, keep, swap(send, "col", n_col, 1), part
+    )
+    feats = deal(sent, "row")
+    part = call(pair_kernel, shape(piece, width), count=2)(sent[1], feats[1])
+    by = 2
+    while 2 * by < n_row:
+        part = call(pair_kernel, shape(piece, width), count=2)(part, swap(part, "row", n_row, by))
+        by *= 2
+    line = shape(1, width, dtype=F32)
+    part, grad_features, grad_bias = call(
+        sum_kernel, (shape(piece, width), shape(tile, width), line), count=2 + n_row
+    )(part, swap(part, "row", n_row, by), *feats)
     act, grad_features, grad_weight, grad_bias = call(
-        last_kernel(n_row, n_col),
-        (
-            shape(tile, width),
-            shape(tile, width),
-            shape(width, width, dtype=F32),
-            shape(1, width, dtype=F32),
-        ),
-        count=2 + n_row + n_col,
-    )(act, line, *deal(feats, "row")[::-1], *spread(whole, "col", n_col))
+        last_kernel,
+        (shape(tile, width), shape(tile, width), shape(width, width, dtype=F32), line),
+        count=5,
+    )(act, grad_features, grad_bias, part, swap(part, "col", n_col, 1))
     return act, grad_features, grad_weight, grad_bias.reshape(width)
 
 

time: 37.9 us -> 37.7 us (level)
  waiting for transfers between devices: 12.2 us -> 16.6 us
  starting transfers between devices: 19.9 us -> 15.6 us
    ppermute x16 -> x12, starting transfers between devices: 19.9 us -> 15.6 us  [swap(): return lax.ppermute(x, axis, [(i, i ^ by) for i in range(n)])]
    ppermute x16 -> x12, waiting for transfers between devices: 12.2 us -> 16.6 us  [swap(): return lax.ppermute(x, axis, [(i, i ^ by) for i in range(n)])]
  transfers between devices with their start and end apart: 16 -> 12, of which waited for: 9 -> 9; matrix products, arithmetic and copies ran while one was open for 0% -> 0% of each run, Pallas kernels for 4% -> 3%
where the time goes in v6:
time: 37.7 us; the launch traced here: 37.5 us
  waiting for transfers between devices  16.6 us (44%)
  starting transfers between devices  15.6 us (41%)
  Pallas kernels  3.05 us (8%)
  local copies, waits for them, and re-layouts  1.65 us (4%)
  between operations  0.72 us (2%)
    ppermute x12, waiting for transfers between devices, swap(): return lax.ppermute(x, axis, [(i, i ^ by) for i in range(n)])  16.6 us
    ppermute x12, starting transfers between devices, swap(): return lax.ppermute(x, axis, [(i, i ^ by) for i in range(n)])  15.6 us
    unnamed x14, local copies, waits for them, and re-layouts  1.64 us
    pallas_call x1, Pallas kernels, shards(): call(dense_kernel(n_chip), (shape(n_col * tile, n_row * tile), shape(n_ro...  1.05 us
    pallas_call x1, Pallas kernels, shards(): call(last_kernel, (shape(tile, width), shape(tile, width), shape(width, w...  0.78 us
  transfers between devices with their start and end apart: 12, of which 9 were waited for; matrix products, arithmetic and copies ran while one was open for 0% of the time, Pallas kernels for 3%

profile of v6, /device:TPU:0, one launch (start us, length us, event | category | flops | bytes accessed | tf_op | source)
XLA Modules:
  0.0 37.5 jit_solution(173137225768896578)
XLA Ops:
  0.6 5.1 %collective-permute-start = (bf16[128,256]{1,0:T(8,128)(2,1)}, bf16[128,256]{1,0:T(8,128)(2,1)S(1)}, u32[]{:S(2)}, u32[]{:S(2)}) collective-permute-start(bf16[128,256]{1,0:T(8,128)(2,1)} %refs_3_.1), channel_id=1, source_target_pairs={{0,12},{4,8},{8,4},{12,0},{1,13},{5,9},{9,5},{13,1},{2,14},{6,10},... | collective-permute-start | bytes 196616 | tf_op jit(solution)/shard_map/ppermute | solution.py:181
  5.7 0.0 collective-permute-start.1
  5.7 0.6 %collective-permute-start.2 = (bf16[128,256]{1,0:T(8,128)(2,1)}, bf16[128,256]{1,0:T(8,128)(2,1)S(1)}, u32[]{:S(2)}, u32[]{:S(2)}) collective-permute-start(bf16[128,256]{1,0:T(8,128)(2,1)} %refs_3_.1), channel_id=1, source_target_pairs={{0,4},{4,0},{8,12},{12,8},{1,5},{5,1},{9,13},{13,9},{2,6},{6,2},{1... | collective-permute-start | bytes 196616 | tf_op jit(solution)/shard_map/ppermute | solution.py:181
  6.4 1.6 %collective-permute-start.3 = (bf16[128,256]{1,0:T(8,128)(2,1)}, bf16[128,256]{1,0:T(8,128)(2,1)S(1)}, u32[]{:S(2)}, u32[]{:S(2)}) collective-permute-start(bf16[128,256]{1,0:T(8,128)(2,1)} %refs_2_.1), channel_id=1, source_target_pairs={{0,2},{1,3},{2,0},{3,1},{4,6},{5,7},{6,4},{7,5},{8,10},{9,11},{10,... | collective-permute-start | bytes 196616 | tf_op jit(solution)/shard_map/ppermute | solution.py:181
  8.0 0.0 copy-start.4
  8.0 0.0 copy-start.5
  8.0 0.7 %copy-done.4 = s32[4,1,2]{0,2,1:T(2,128)S(1)} copy-done((s32[4,1,2]{0,2,1:T(2,128)S(1)}, s32[4,1,2]{0,2,1:T(2,128)}, u32[]{:S(2)}) %copy-start.4) | copy-done | bytes 56
  8.7 0.0 copy-done.5
  8.7 0.0 copy-start
  8.7 0.9 %copy-done = bf16[4,1,2,128,128]{4,3,2,1,0:T(8,128)(2,1)S(1)} copy-done((bf16[4,1,2,128,128]{4,3,2,1,0:T(8,128)(2,1)S(1)}, bf16[4,1,2,128,128]{4,3,2,1,0:T(8,128)(2,1)}, u32[]{:S(2)}) %copy-start) | copy-done | bytes 262168
  9.7 0.0 copy-start.2
  9.7 1.0 %shard_map.102 = (bf16[512,512]{1,0:T(8,128)(2,1)S(1)}, bf16[512,512]{1,0:T(8,128)(2,1)S(1)}) custom-call(s32[1,2,4]{2,1,0:T(2,128)S(1)} %bitcast.3, s32[1,4]{1,0:T(1,128)S(1)} %bitcast.4, bf16[4,1,2,128,128]{4,3,2,1,0:T(8,128)(2,1)S(1)} %copy-done), custom_call_target="tpu_custom_call" | custom-call | tf_op jit(solution)/shard_map/pallas_call | solution.py:201
  10.7 0.0 collective-permute-done.refs_0_
  10.7 0.8 %collective-permute-done.1.refs_1_ = bf16[128,256]{1,0:T(8,128)(2,1)S(1)} collective-permute-done((bf16[128,256]{1,0:T(8,128)(2,1)}, bf16[128,256]{1,0:T(8,128)(2,1)S(1)}, u32[]{:S(2)}, u32[]{:S(2)}) %collective-permute-start.1) | collective-permute-done | bytes 65568 | tf_op jit(solution)/shard_map/ppermute | solution.py:181
  11.6 0.0 collective-permute-done.2.refs_2_
  11.6 0.0 collective-permute-done.3.refs_4_
  11.6 0.0 copy-done.2
  11.6 0.3 shard_map.103
  11.9 0.1 collective-permute-start.4
  12.0 1.3 %collective-permute-done.4.got_ref = bf16[256,256]{1,0:T(8,128)(2,1)S(1)} collective-permute-done((bf16[256,256]{1,0:T(8,128)(2,1)S(1)}, bf16[256,256]{1,0:T(8,128)(2,1)S(1)}, u32[]{:S(2)}, u32[]{:S(2)}) %collective-permute-start.4) | collective-permute-done | bytes 131104 | tf_op jit(solution)/shard_map/ppermute | solution.py:181
  13.3 0.0 copy-start.6
  13.3 0.0 copy-start.1
  13.3 0.0 copy-start.3
  13.3 1.6 %collective-permute-start.5 = (bf16[256,256]{1,0:T(8,128)(2,1)S(1)}, bf16[256,256]{1,0:T(8,128)(2,1)S(1)}, u32[]{:S(2)}, u32[]{:S(2)}) collective-permute-start(bf16[256,256]{1,0:T(8,128)(2,1)S(1)} %shard_map.104.refs_0_), channel_id=1, source_target_pairs={{0,2},{1,3},{2,0},{3,1},{4,6},{5,7},{6,4},{7,5},{8,10},{9,11},{10,... | collective-permute-start | bytes 393224 | tf_op jit(solution)/shard_map/ppermute | solution.py:181
  14.9 0.0 copy-done.6
  14.9 4.1 %collective-permute-done.5.refs_1_ = bf16[256,256]{1,0:T(8,128)(2,1)S(1)} collective-permute-done((bf16[256,256]{1,0:T(8,128)(2,1)S(1)}, bf16[256,256]{1,0:T(8,128)(2,1)S(1)}, u32[]{:S(2)}, u32[]{:S(2)}) %collective-permute-start.5) | collective-permute-done | bytes 131104 | tf_op jit(solution)/shard_map/ppermute | solution.py:181
  19.0 0.0 copy-done.1
  19.0 0.0 copy-done.3
  19.0 0.5 %shard_map.105 = (bf16[128,256]{1,0:T(8,128)(2,1)S(1)}, bf16[256,256]{1,0:T(8,128)(2,1)S(1)}, bf16[144,256]{1,0:T(8,128)(2,1)S(1)}, bf16[400,256]{1,0:T(8,128)(2,1)S(1)}) custom-call(bf16[256,256]{1,0:T(8,128)(2,1)S(1)} %copy-done.1, bf16[1,256]{1,0:T(2,128)(2,1)S(1)} %reshape.14.b_ref, bf16[256,256]{1,0:T(8,128)(2,1)S(1)} %shard_map.104.refs_0_, ...), custom_call_target="tpu_custom_call" | custom-call | tf_op jit(solution)/shard_map/pallas_call | solution.py:214
  19.5 0.1 collective-permute-start.6
  19.5 1.4 %collective-permute-done.6.got_ref = bf16[400,256]{1,0:T(8,128)(2,1)S(1)} collective-permute-done((bf16[400,256]{1,0:T(8,128)(2,1)S(1)}, bf16[400,256]{1,0:T(8,128)(2,1)S(1)}, u32[]{:S(2)}, u32[]{:S(2)}) %collective-permute-start.6) | collective-permute-done | bytes 204832 | tf_op jit(solution)/shard_map/ppermute | solution.py:181
  21.0 0.3 shard_map.106
  21.3 1.1 %collective-permute-start.7 = (bf16[272,256]{1,0:T(8,128)(2,1)S(1)}, bf16[272,256]{1,0:T(8,128)(2,1)S(1)}, u32[]{:S(2)}, u32[]{:S(2)}) collective-permute-start(bf16[272,256]{1,0:T(8,128)(2,1)S(1)} %get-tuple-element.33.a_ref), channel_id=1, source_target_pairs={{0,4},{4,0},{8,12},{12,8},{1,5},{5,1},{9,13},{13,9},{2,6},{6,2},{1... | collective-permute-start | bytes 417800 | tf_op jit(solution)/shard_map/ppermute | solution.py:181
  22.4 2.0 %collective-permute-start.10 = (bf16[144,256]{1,0:T(8,128)(2,1)S(1)}, bf16[144,256]{1,0:T(8,128)(2,1)S(1)}, u32[]{:S(2)}, u32[]{:S(2)}) collective-permute-start(bf16[144,256]{1,0:T(8,128)(2,1)S(1)} %get-tuple-element.36), channel_id=1, source_target_pairs={{0,12},{4,8},{8,4},{12,0},{1,13},{5,9},{9,5},{13,1},{2,14},{6,10},... | collective-permute-start | bytes 221192 | tf_op jit(solution)/shard_map/ppermute | solution.py:181
  24.5 0.5 %collective-permute-start.9 = (bf16[144,256]{1,0:T(8,128)(2,1)S(1)}, bf16[144,256]{1,0:T(8,128)(2,1)S(1)}, u32[]{:S(2)}, u32[]{:S(2)}) collective-permute-start(bf16[144,256]{1,0:T(8,128)(2,1)S(1)} %get-tuple-element.35), channel_id=1, source_target_pairs={{0,8},{4,12},{8,0},{12,4},{1,9},{5,13},{9,1},{13,5},{2,10},{6,14},... | collective-permute-start | bytes 221192 | tf_op jit(solution)/shard_map/ppermute | solution.py:181
  25.0 2.1 %collective-permute-done.7.b_ref.refs_1_ = bf16[272,256]{1,0:T(8,128)(2,1)S(1)} collective-permute-done((bf16[272,256]{1,0:T(8,128)(2,1)S(1)}, bf16[272,256]{1,0:T(8,128)(2,1)S(1)}, u32[]{:S(2)}, u32[]{:S(2)}) %collective-permute-start.7) | collective-permute-done | bytes 139296 | tf_op jit(solution)/shard_map/ppermute | solution.py:181
  27.1 2.7 %collective-permute-start.8 = (bf16[128,256]{1,0:T(8,128)(2,1)S(1)}, bf16[128,256]{1,0:T(8,128)(2,1)S(1)}, u32[]{:S(2)}, u32[]{:S(2)}) collective-permute-start(bf16[128,256]{1,0:T(8,128)(2,1)S(1)} %shard_map.107.a_ref), channel_id=1, source_target_pairs={{0,8},{4,12},{8,0},{12,4},{1,9},{5,13},{9,1},{13,5},{2,10},{6,14},... | collective-permute-start | bytes 196616 | tf_op jit(solution)/shard_map/ppermute | solution.py:181
  29.8 0.7 %collective-permute-done.10.refs_3_ = bf16[144,256]{1,0:T(8,128)(2,1)S(1)} collective-permute-done((bf16[144,256]{1,0:T(8,128)(2,1)S(1)}, bf16[144,256]{1,0:T(8,128)(2,1)S(1)}, u32[]{:S(2)}, u32[]{:S(2)}) %collective-permute-start.10) | collective-permute-done | bytes 73760 | tf_op jit(solution)/shard_map/ppermute | solution.py:181
  30.6 4.0 %collective-permute-done.9.refs_2_ = bf16[144,256]{1,0:T(8,128)(2,1)S(1)} collective-permute-done((bf16[144,256]{1,0:T(8,128)(2,1)S(1)}, bf16[144,256]{1,0:T(8,128)(2,1)S(1)}, u32[]{:S(2)}, u32[]{:S(2)}) %collective-permute-start.9) | collective-permute-done | bytes 73760 | tf_op jit(solution)/shard_map/ppermute | solution.py:181
  34.6 0.8 %collective-permute-done.8.b_ref = bf16[128,256]{1,0:T(8,128)(2,1)S(1)} collective-permute-done((bf16[128,256]{1,0:T(8,128)(2,1)S(1)}, bf16[128,256]{1,0:T(8,128)(2,1)S(1)}, u32[]{:S(2)}, u32[]{:S(2)}) %collective-permute-start.8) | collective-permute-done | bytes 65568 | tf_op jit(solution)/shard_map/ppermute | solution.py:181
  35.4 0.1 shard_map.108
  35.4 0.1 collective-permute-start.11
  35.5 1.2 %collective-permute-done.11.got_ref = bf16[128,256]{1,0:T(8,128)(2,1)S(1)} collective-permute-done((bf16[128,256]{1,0:T(8,128)(2,1)S(1)}, bf16[128,256]{1,0:T(8,128)(2,1)S(1)}, u32[]{:S(2)}, u32[]{:S(2)}) %collective-permute-start.11) | collective-permute-done | bytes 65568 | tf_op jit(solution)/shard_map/ppermute | solution.py:181
  36.8 0.8 %shard_map.109 = (bf16[128,256]{1,0:T(8,128)(2,1)}, bf16[128,256]{1,0:T(8,128)(2,1)}, f32[256,256]{1,0:T(8,128)}, f32[1,256]{1,0:T(1,128)}) custom-call(bf16[128,256]{1,0:T(8,128)(2,1)S(1)} %get-tuple-element.28.act_ref, bf16[128,256]{1,0:T(8,128)(2,1)S(1)} %get-tuple-element.37.feat_ref, f32[1,256]{1,0:T(1,128)S(1)} %get-tuple-element.38.line_ref, ...), custom_call_target="tpu_custom_call" | custom-call | tf_op jit(solution)/shard_map/pallas_call | solution.py:244
  (3 shorter events, 0.1 us)
Async XLA Ops:
  0.6 10.1 %collective-permute-start = (bf16[128,256]{1,0:T(8,128)(2,1)}, bf16[128,256]{1,0:T(8,128)(2,1)S(1)}, u32[]{:S(2)}, u32[]{:S(2)}) collective-permute-start(bf16[128,256]{1,0:T(8,128)(2,1)} %refs_3_.1), channel_id=1, source_target_pairs={{0,12},{4,8},{8,4},{12,0},{1,13},{5,9},{9,5},{13,1},{2,14},{6,10},... | collective-permute-start | bytes 196616 | tf_op jit(solution)/shard_map/ppermute | solution.py:181
  5.7 5.8 %collective-permute-start.1 = (bf16[128,256]{1,0:T(8,128)(2,1)}, bf16[128,256]{1,0:T(8,128)(2,1)S(1)}, u32[]{:S(2)}, u32[]{:S(2)}) collective-permute-start(bf16[128,256]{1,0:T(8,128)(2,1)} %refs_3_.1), channel_id=1, source_target_pairs={{0,8},{4,12},{8,0},{12,4},{1,9},{5,13},{9,1},{13,5},{2,10},{6,14},... | collective-permute-start | bytes 196616 | tf_op jit(solution)/shard_map/ppermute | solution.py:181
  5.7 5.8 %collective-permute-start.2 = (bf16[128,256]{1,0:T(8,128)(2,1)}, bf16[128,256]{1,0:T(8,128)(2,1)S(1)}, u32[]{:S(2)}, u32[]{:S(2)}) collective-permute-start(bf16[128,256]{1,0:T(8,128)(2,1)} %refs_3_.1), channel_id=1, source_target_pairs={{0,4},{4,0},{8,12},{12,8},{1,5},{5,1},{9,13},{13,9},{2,6},{6,2},{1... | collective-permute-start | bytes 196616 | tf_op jit(solution)/shard_map/ppermute | solution.py:181
  6.4 5.2 %collective-permute-start.3 = (bf16[128,256]{1,0:T(8,128)(2,1)}, bf16[128,256]{1,0:T(8,128)(2,1)S(1)}, u32[]{:S(2)}, u32[]{:S(2)}) collective-permute-start(bf16[128,256]{1,0:T(8,128)(2,1)} %refs_2_.1), channel_id=1, source_target_pairs={{0,2},{1,3},{2,0},{3,1},{4,6},{5,7},{6,4},{7,5},{8,10},{9,11},{10,... | collective-permute-start | bytes 196616 | tf_op jit(solution)/shard_map/ppermute | solution.py:181
  8.0 0.7 %copy-start.4 = (s32[4,1,2]{0,2,1:T(2,128)S(1)}, s32[4,1,2]{0,2,1:T(2,128)}, u32[]{:S(2)}) copy-start(s32[4,1,2]{0,2,1:T(2,128)} %param.9) | copy-start | bytes 100
  8.0 0.7 %copy-start.5 = (s32[4,1]{0,1:T(1,128)S(1)}, s32[4,1]{0,1:T(1,128)}, u32[]{:S(2)}) copy-start(s32[4,1]{0,1:T(1,128)} %param.10) | copy-start | bytes 52
  8.7 1.0 %copy-start = (bf16[4,1,2,128,128]{4,3,2,1,0:T(8,128)(2,1)S(1)}, bf16[4,1,2,128,128]{4,3,2,1,0:T(8,128)(2,1)}, u32[]{:S(2)}) copy-start(bf16[4,1,2,128,128]{4,3,2,1,0:T(8,128)(2,1)} %tiles_ref.1) | copy-start | bytes 786436
  9.7 1.9 %copy-start.2 = (bf16[128,256]{1,0:T(8,128)(2,1)S(1)}, bf16[128,256]{1,0:T(8,128)(2,1)}, u32[]{:S(2)}) copy-start(bf16[128,256]{1,0:T(8,128)(2,1)} %refs_3_.1) | copy-start | bytes 196612
  11.9 1.4 %collective-permute-start.4 = (bf16[256,256]{1,0:T(8,128)(2,1)S(1)}, bf16[256,256]{1,0:T(8,128)(2,1)S(1)}, u32[]{:S(2)}, u32[]{:S(2)}) collective-permute-start(bf16[256,256]{1,0:T(8,128)(2,1)S(1)} %get-tuple-element.26), channel_id=1, source_target_pairs={{0,1},{1,0},{2,3},{3,2},{4,5},{5,4},{6,7},{7,6},{8,9},{9,8},{10,11... | collective-permute-start | bytes 393224 | tf_op jit(solution)/shard_map/ppermute | solution.py:181
  13.3 1.6 %copy-start.6 = (bf16[256]{0:T(256)(128)(2,1)S(1)}, bf16[256]{0:T(256)(128)(2,1)}, u32[]{:S(2)}) copy-start(bf16[256]{0:T(256)(128)(2,1)} %param.12) | copy-start | bytes 1540
  13.3 5.7 %copy-start.1 = (bf16[256,256]{1,0:T(8,128)(2,1)S(1)}, bf16[256,256]{1,0:T(8,128)(2,1)}, u32[]{:S(2)}) copy-start(bf16[256,256]{1,0:T(8,128)(2,1)} %w_ref.1) | copy-start | bytes 393220
  13.3 5.7 %copy-start.3 = (bf16[128,256]{1,0:T(8,128)(2,1)S(1)}, bf16[128,256]{1,0:T(8,128)(2,1)}, u32[]{:S(2)}) copy-start(bf16[128,256]{1,0:T(8,128)(2,1)} %refs_2_.1) | copy-start | bytes 196612
  13.3 5.6 %collective-permute-start.5 = (bf16[256,256]{1,0:T(8,128)(2,1)S(1)}, bf16[256,256]{1,0:T(8,128)(2,1)S(1)}, u32[]{:S(2)}, u32[]{:S(2)}) collective-permute-start(bf16[256,256]{1,0:T(8,128)(2,1)S(1)} %shard_map.104.refs_0_), channel_id=1, source_target_pairs={{0,2},{1,3},{2,0},{3,1},{4,6},{5,7},{6,4},{7,5},{8,10},{9,11},{10,... | collective-permute-start | bytes 393224 | tf_op jit(solution)/shard_map/ppermute | solution.py:181
  19.5 1.5 %collective-permute-start.6 = (bf16[400,256]{1,0:T(8,128)(2,1)S(1)}, bf16[400,256]{1,0:T(8,128)(2,1)S(1)}, u32[]{:S(2)}, u32[]{:S(2)}) collective-permute-start(bf16[400,256]{1,0:T(8,128)(2,1)S(1)} %get-tuple-element.31), channel_id=1, source_target_pairs={{0,1},{1,0},{2,3},{3,2},{4,5},{5,4},{6,7},{7,6},{8,9},{9,8},{10,11... | collective-permute-start | bytes 614408 | tf_op jit(solution)/shard_map/ppermute | solution.py:181
  21.3 5.8 %collective-permute-start.7 = (bf16[272,256]{1,0:T(8,128)(2,1)S(1)}, bf16[272,256]{1,0:T(8,128)(2,1)S(1)}, u32[]{:S(2)}, u32[]{:S(2)}) collective-permute-start(bf16[272,256]{1,0:T(8,128)(2,1)S(1)} %get-tuple-element.33.a_ref), channel_id=1, source_target_pairs={{0,4},{4,0},{8,12},{12,8},{1,5},{5,1},{9,13},{13,9},{2,6},{6,2},{1... | collective-permute-start | bytes 417800 | tf_op jit(solution)/shard_map/ppermute | solution.py:181
  22.4 8.1 %collective-permute-start.10 = (bf16[144,256]{1,0:T(8,128)(2,1)S(1)}, bf16[144,256]{1,0:T(8,128)(2,1)S(1)}, u32[]{:S(2)}, u32[]{:S(2)}) collective-permute-start(bf16[144,256]{1,0:T(8,128)(2,1)S(1)} %get-tuple-element.36), channel_id=1, source_target_pairs={{0,12},{4,8},{8,4},{12,0},{1,13},{5,9},{9,5},{13,1},{2,14},{6,10},... | collective-permute-start | bytes 221192 | tf_op jit(solution)/shard_map/ppermute | solution.py:181
  24.5 10.1 %collective-permute-start.9 = (bf16[144,256]{1,0:T(8,128)(2,1)S(1)}, bf16[144,256]{1,0:T(8,128)(2,1)S(1)}, u32[]{:S(2)}, u32[]{:S(2)}) collective-permute-start(bf16[144,256]{1,0:T(8,128)(2,1)S(1)} %get-tuple-element.35), channel_id=1, source_target_pairs={{0,8},{4,12},{8,0},{12,4},{1,9},{5,13},{9,1},{13,5},{2,10},{6,14},... | collective-permute-start | bytes 221192 | tf_op jit(solution)/shard_map/ppermute | solution.py:181
  27.1 8.3 %collective-permute-start.8 = (bf16[128,256]{1,0:T(8,128)(2,1)S(1)}, bf16[128,256]{1,0:T(8,128)(2,1)S(1)}, u32[]{:S(2)}, u32[]{:S(2)}) collective-permute-start(bf16[128,256]{1,0:T(8,128)(2,1)S(1)} %shard_map.107.a_ref), channel_id=1, source_target_pairs={{0,8},{4,12},{8,0},{12,4},{1,9},{5,13},{9,1},{13,5},{2,10},{6,14},... | collective-permute-start | bytes 196616 | tf_op jit(solution)/shard_map/ppermute | solution.py:181
  35.4 1.3 %collective-permute-start.11 = (bf16[128,256]{1,0:T(8,128)(2,1)S(1)}, bf16[128,256]{1,0:T(8,128)(2,1)S(1)}, u32[]{:S(2)}, u32[]{:S(2)}) collective-permute-start(bf16[128,256]{1,0:T(8,128)(2,1)S(1)} %get-tuple-element.39.mine_ref), channel_id=1, source_target_pairs={{0,1},{1,0},{2,3},{3,2},{4,5},{5,4},{6,7},{7,6},{8,9},{9,8},{10,11... | collective-permute-start | bytes 196616 | tf_op jit(solution)/shard_map/ppermute | solution.py:181

commit v7 on v6

--- a/solution.py
+++ b/solution.py
@@ -36,7 +36,15 @@
     return lax.rem(c, 2) * n_chip + lax.div(c, 2)
 
 
-def dense_kernel(n_chip):
+def reversed_bits(p, n):
+    total, bit = 0, 1
+    while bit < n:
+        total = 2 * total + lax.rem(lax.div(p, bit), 2)
+        bit *= 2
+    return total
+
+
+def dense_kernel(n_chip, n_row):
     def body(cols_ref, cnts_ref, tiles_ref, a_ref, at_ref):
         trows, _, slots, tile, _ = tiles_ref.shape
         r = lax.axis_index("row")
@@ -56,7 +64,8 @@
                 qs = pl.ds(pl.multiple_of(q * tile, tile), tile)
                 ps = pl.ds(pl.multiple_of(p * tile, tile), tile)
                 a_ref[qs, ps] = here
-                at_ref[ps, qs] = here.T
+                rs = pl.ds(pl.multiple_of(reversed_bits(p, n_row) * tile, tile), tile)
+                at_ref[rs, qs] = here.T
 
             return carry
 
@@ -109,7 +118,7 @@
         act_ref[...] = (preact[:tile] * sig[:tile]).astype(BF)
         grad = (cot * (sig * (1.0 + preact * (1.0 - sig)))).astype(BF)
         gagg = dot(grad, w_ref[...], 1, 1).astype(BF)
-        keep_ref[...] = gagg
+        keep_ref[:rows, :] = gagg
         send_ref[:rows, :] = gagg
         for u in range(n_chip):
             here = pl.ds(pl.multiple_of(jnp.bitwise_xor(chip, u) * tile, tile), tile)
@@ -120,57 +129,51 @@
         mine = pl.multiple_of(core * piece, piece)
         other = pl.multiple_of((1 - core) * piece, piece)
         lines = two_rows(jnp.sum(grad.astype(F32), axis=0, keepdims=True))
-        part_ref[:piece, :] = local_ref[pl.ds(mine, piece), :].astype(BF)
-        part_ref[piece:, :] = lines
-        send_ref[rows : rows + piece, :] = local_ref[pl.ds(other, piece), :].astype(BF)
-        send_ref[rows + piece :, :] = lines
+        part_ref[...] = local_ref[pl.ds(mine, piece), :].astype(BF)
+        keep_ref[rows:, :] = lines
+        send_ref[rows : rows + PAD, :] = lines
+        send_ref[rows + PAD :, :] = local_ref[pl.ds(other, piece), :].astype(BF)
 
     return body
 
 
-def sum_lines(refs, first):
-    total = refs[0][first : first + PAD, :].astype(F32)
-    for ref in refs[1:]:
-        total = total + ref[first : first + PAD, :].astype(F32)
-    return total[0:1] + total[1:2]
-
-
-def backward_kernel(at_ref, keep_ref, got_ref, part_ref, *outs):
-    rows, tile = keep_ref.shape[0], outs[0].shape[0] - PAD
-    piece = part_ref.shape[0] - PAD
-    mine, other = part_ref[...].astype(F32), got_ref[rows:, :].astype(F32)
-    total = mine + other
-    outs[1][tile + PAD :, :] = total[:piece].astype(BF)
-    lines = two_rows(total[piece : piece + 1] + total[piece + 1 : piece + 2])
-    g = jnp.concatenate([keep_ref[...], got_ref[:rows, :]], axis=0)
-    for p, out in enumerate(outs):
-        out[:tile, :] = dot(at_ref[p * tile : (p + 1) * tile, :], g).astype(BF)
-        out[tile : tile + PAD, :] = lines
-
-
-def pair_kernel(a_ref, b_ref, out_ref):
-    first = a_ref.shape[0] - out_ref.shape[0]
-    out_ref[...] = (a_ref[first:, :].astype(F32) + b_ref[first:, :].astype(F32)).astype(BF)
-
-
-def sum_kernel(a_ref, b_ref, *refs):
-    feats, (part_ref, feat_ref, line_ref) = refs[:-3], refs[-3:]
-    part_ref[...] = (a_ref[...].astype(F32) + b_ref[...].astype(F32)).astype(BF)
-    tile = feat_ref.shape[0]
-    total = feats[0][:tile, :].astype(F32)
-    for ref in feats[1:]:
-        total = total + ref[:tile, :].astype(F32)
-    feat_ref[...] = total.astype(BF)
-    line_ref[...] = sum_lines(feats, tile)
-
-
-def last_kernel(act_ref, feat_ref, line_ref, mine_ref, got_ref, *outs):
+def line_of(rows):
+    rows = rows.astype(F32)
+    return rows[0:1] + rows[1:2]
+
+
+def part_kernel(part_ref, got_ref, out_ref):
+    piece = out_ref.shape[0]
+    first = got_ref.shape[0] - piece
+    out_ref[...] = (part_ref[...].astype(F32) + got_ref[first:, :].astype(F32)).astype(BF)
+
+
+def backward_kernel(at_ref, mine_ref, got_ref, keep_ref, send_ref):
+    rows, half = mine_ref.shape[0] - PAD, keep_ref.shape[0] - PAD
+    g = jnp.concatenate([mine_ref[:rows, :], got_ref[:rows, :]], axis=0)
+    send_ref[:half, :] = dot(at_ref[half:, :], g).astype(BF)
+    keep_ref[:half, :] = dot(at_ref[:half, :], g)
+    line = two_rows(line_of(mine_ref[rows:, :]) + line_of(got_ref[rows : rows + PAD, :]))
+    send_ref[half:, :] = line
+    keep_ref[half:, :] = line.astype(F32)
+
+
+def halve_kernel(in_ref, got_ref, keep_ref, send_ref):
+    half, rows = keep_ref.shape[0] - PAD, in_ref.shape[0] - PAD
+    send_ref[:half, :] = (in_ref[half:rows, :] + got_ref[half:rows, :].astype(F32)).astype(BF)
+    keep_ref[:half, :] = in_ref[:half, :] + got_ref[:half, :].astype(F32)
+    line = two_rows(line_of(in_ref[rows:, :]) + line_of(got_ref[rows:, :]))
+    send_ref[half:, :] = line
+    keep_ref[half:, :] = line.astype(F32)
+
+
+def last_kernel(act_ref, feat_ref, more_ref, mine_ref, got_ref, *outs):
     act_out, feat_out, weight_out, bias_out = outs
-    piece = mine_ref.shape[0]
+    tile, piece = act_ref.shape[0], mine_ref.shape[0]
     core = lax.rem(lax.axis_index("col"), 2)
     act_out[...] = act_ref[...]
-    feat_out[...] = feat_ref[...]
-    bias_out[...] = line_ref[...]
+    feat_out[...] = (feat_ref[:tile, :] + more_ref[:tile, :].astype(F32)).astype(BF)
+    bias_out[...] = line_of(feat_ref[tile:, :]) + line_of(more_ref[tile:, :])
     mine = pl.multiple_of(core * piece, piece)
     other = pl.multiple_of((1 - core) * piece, piece)
     weight_out[pl.ds(mine, piece), :] = mine_ref[...].astype(F32)
@@ -199,7 +202,7 @@
     xs = spread(features, "row", n_row)
     cots = [cotangent] + [swap(cotangent, "col", n_col, 2 * v) for v in range(1, n_chip)]
     a, at = call(
-        dense_kernel(n_chip),
+        dense_kernel(n_chip, n_row),
         (shape(n_col * tile, n_row * tile), shape(n_row * tile, n_col * tile)),
         smem=2,
         count=3,
@@ -215,9 +218,9 @@
         middle_kernel(n_chip),
         (
             shape(tile, width),
-            shape(half, width),
-            shape(piece + PAD, width),
-            shape(half + piece + PAD, width),
+            shape(half + PAD, width),
+            shape(piece, width),
+            shape(half + PAD + piece, width),
         ),
         count=2 + 2 * n_chip,
         scratch=[
@@ -226,26 +229,34 @@
             pltpu.VMEM((width, width), F32),
         ],
     )(weight, bias_term.reshape(1, width), *sums, *cots)
-    messages = [shape(tile + PAD, width)] * n_row
-    messages[1] = shape(tile + PAD + piece, width)
-    sent = call(backward_kernel, tuple(messages), count=4)(
-        at, keep, swap(send, "col", n_col, 1), part
-    )
-    feats = deal(sent, "row")
-    part = call(pair_kernel, shape(piece, width), count=2)(sent[1], feats[1])
-    by = 2
-    while 2 * by < n_row:
-        part = call(pair_kernel, shape(piece, width), count=2)(part, swap(part, "row", n_row, by))
+    got = swap(send, "col", n_col, 1)
+    part = call(part_kernel, shape(piece, width), count=2)(part, got)
+    rows = n_row * tile // 2
+    feats, send = call(
+        backward_kernel, (shape(rows + PAD, width, dtype=F32), shape(rows + PAD, width)), count=3
+    )(at, keep, got)
+    by = 1
+    while by < n_row:
+        part = call(part_kernel, shape(piece, width), count=2)(
+            part, swap(part, "row", n_row, by)
+        )
+        got = swap(send, "row", n_row, by)
         by *= 2
-    line = shape(1, width, dtype=F32)
-    part, grad_features, grad_bias = call(
-        sum_kernel, (shape(piece, width), shape(tile, width), line), count=2 + n_row
-    )(part, swap(part, "row", n_row, by), *feats)
+        if by < n_row:
+            rows //= 2
+            feats, send = call(
+                halve_kernel, (shape(rows + PAD, width, dtype=F32), shape(rows + PAD, width)), count=2
+            )(feats, got)
     act, grad_features, grad_weight, grad_bias = call(
         last_kernel,
-        (shape(tile, width), shape(tile, width), shape(width, width, dtype=F32), line),
+        (
+            shape(tile, width),
+            shape(tile, width),
+            shape(width, width, dtype=F32),
+            shape(1, width, dtype=F32),
+        ),
         count=5,
-    )(act, grad_features, grad_bias, part, swap(part, "col", n_col, 1))
+    )(act, feats, got, part, swap(part, "col", n_col, 1))
     return act, grad_features, grad_weight, grad_bias.reshape(width)
 
 

time: 37.7 us -> 38.5 us (1.021)
  waiting for transfers between devices: 16.6 us -> 18.6 us
  starting transfers between devices: 15.6 us -> 14.4 us
    ppermute x12, waiting for transfers between devices: 16.6 us -> 18.6 us  [swap(): return lax.ppermute(x, axis, [(i, i ^ by) for i in range(n)])]
    ppermute x12, starting transfers between devices: 15.6 us -> 14.4 us  [swap(): return lax.ppermute(x, axis, [(i, i ^ by) for i in range(n)])]
    pallas_call x5 -> x7, Pallas kernels: 1.94 us -> 1.95 us  [the longest x1 1.05 us: shards(): call(dense_kernel(n_chip, n_row), (shape(n_col * tile, n_row * tile), sha...]
  transfers between devices with their start and end apart: 12 -> 12, of which waited for: 9 -> 8; matrix products, arithmetic and copies ran while one was open for 0% -> 0% of each run, Pallas kernels for 3% -> 3%
where the time goes in v7:
time: 38.5 us; the launch traced here: 38.4 us
  waiting for transfers between devices  18.6 us (48%)
  starting transfers between devices  14.4 us (37%)
  Pallas kernels  3.05 us (8%)
  local copies, waits for them, and re-layouts  1.65 us (4%)
  between operations  0.72 us (2%)
    ppermute x12, waiting for transfers between devices, swap(): return lax.ppermute(x, axis, [(i, i ^ by) for i in range(n)])  18.6 us
    ppermute x12, starting transfers between devices, swap(): return lax.ppermute(x, axis, [(i, i ^ by) for i in range(n)])  14.4 us
    unnamed x14, local copies, waits for them, and re-layouts  1.64 us
    pallas_call x1, Pallas kernels, shards(): call(dense_kernel(n_chip, n_row), (shape(n_col * tile, n_row * tile), sha...  1.05 us
    pallas_call x1, Pallas kernels, shards(): call(last_kernel, (shape(tile, width), shape(tile, width), shape(width, w...  0.78 us
  transfers between devices with their start and end apart: 12, of which 8 were waited for; matrix products, arithmetic and copies ran while one was open for 0% of the time, Pallas kernels for 3%

profile of v7, /device:TPU:0, one launch (start us, length us, event | category | flops | bytes accessed | tf_op | source)
XLA Modules:
  0.0 38.4 jit_solution(16509701622286853833)
XLA Ops:
  0.6 5.1 %collective-permute-start = (bf16[128,256]{1,0:T(8,128)(2,1)}, bf16[128,256]{1,0:T(8,128)(2,1)S(1)}, u32[]{:S(2)}, u32[]{:S(2)}) collective-permute-start(bf16[128,256]{1,0:T(8,128)(2,1)} %refs_3_.1), channel_id=1, source_target_pairs={{0,12},{4,8},{8,4},{12,0},{1,13},{5,9},{9,5},{13,1},{2,14},{6,10},... | collective-permute-start | bytes 196616 | tf_op jit(solution)/shard_map/ppermute | solution.py:184
  5.7 0.0 collective-permute-start.1
  5.7 0.6 %collective-permute-start.2 = (bf16[128,256]{1,0:T(8,128)(2,1)}, bf16[128,256]{1,0:T(8,128)(2,1)S(1)}, u32[]{:S(2)}, u32[]{:S(2)}) collective-permute-start(bf16[128,256]{1,0:T(8,128)(2,1)} %refs_3_.1), channel_id=1, source_target_pairs={{0,4},{4,0},{8,12},{12,8},{1,5},{5,1},{9,13},{13,9},{2,6},{6,2},{1... | collective-permute-start | bytes 196616 | tf_op jit(solution)/shard_map/ppermute | solution.py:184
  6.4 1.6 %collective-permute-start.3 = (bf16[128,256]{1,0:T(8,128)(2,1)}, bf16[128,256]{1,0:T(8,128)(2,1)S(1)}, u32[]{:S(2)}, u32[]{:S(2)}) collective-permute-start(bf16[128,256]{1,0:T(8,128)(2,1)} %refs_2_.1), channel_id=1, source_target_pairs={{0,2},{1,3},{2,0},{3,1},{4,6},{5,7},{6,4},{7,5},{8,10},{9,11},{10,... | collective-permute-start | bytes 196616 | tf_op jit(solution)/shard_map/ppermute | solution.py:184
  8.0 0.0 copy-start.4
  8.0 0.0 copy-start.5
  8.0 0.7 %copy-done.4 = s32[4,1,2]{0,2,1:T(2,128)S(1)} copy-done((s32[4,1,2]{0,2,1:T(2,128)S(1)}, s32[4,1,2]{0,2,1:T(2,128)}, u32[]{:S(2)}) %copy-start.4) | copy-done | bytes 56
  8.7 0.0 copy-done.5
  8.7 0.0 copy-start
  8.7 0.9 %copy-done = bf16[4,1,2,128,128]{4,3,2,1,0:T(8,128)(2,1)S(1)} copy-done((bf16[4,1,2,128,128]{4,3,2,1,0:T(8,128)(2,1)S(1)}, bf16[4,1,2,128,128]{4,3,2,1,0:T(8,128)(2,1)}, u32[]{:S(2)}) %copy-start) | copy-done | bytes 262168
  9.7 0.0 copy-start.2
  9.7 1.0 %shard_map.102 = (bf16[512,512]{1,0:T(8,128)(2,1)S(1)}, bf16[512,512]{1,0:T(8,128)(2,1)S(1)}) custom-call(s32[1,2,4]{2,1,0:T(2,128)S(1)} %bitcast.3, s32[1,4]{1,0:T(1,128)S(1)} %bitcast.4, bf16[4,1,2,128,128]{4,3,2,1,0:T(8,128)(2,1)S(1)} %copy-done), custom_call_target="tpu_custom_call" | custom-call | tf_op jit(solution)/shard_map/pallas_call | solution.py:204
  10.7 0.0 collective-permute-done.refs_0_
  10.7 0.8 %collective-permute-done.1.refs_1_ = bf16[128,256]{1,0:T(8,128)(2,1)S(1)} collective-permute-done((bf16[128,256]{1,0:T(8,128)(2,1)}, bf16[128,256]{1,0:T(8,128)(2,1)S(1)}, u32[]{:S(2)}, u32[]{:S(2)}) %collective-permute-start.1) | collective-permute-done | bytes 65568 | tf_op jit(solution)/shard_map/ppermute | solution.py:184
  11.6 0.0 collective-permute-done.2.refs_2_
  11.6 0.0 collective-permute-done.3.refs_4_
  11.6 0.0 copy-done.2
  11.6 0.3 shard_map.103
  11.9 0.1 collective-permute-start.4
  12.0 1.3 %collective-permute-done.4.got_ref = bf16[256,256]{1,0:T(8,128)(2,1)S(1)} collective-permute-done((bf16[256,256]{1,0:T(8,128)(2,1)S(1)}, bf16[256,256]{1,0:T(8,128)(2,1)S(1)}, u32[]{:S(2)}, u32[]{:S(2)}) %collective-permute-start.4) | collective-permute-done | bytes 131104 | tf_op jit(solution)/shard_map/ppermute | solution.py:184
  13.3 0.0 copy-start.6
  13.3 0.0 copy-start.1
  13.3 0.0 copy-start.3
  13.3 1.6 %collective-permute-start.5 = (bf16[256,256]{1,0:T(8,128)(2,1)S(1)}, bf16[256,256]{1,0:T(8,128)(2,1)S(1)}, u32[]{:S(2)}, u32[]{:S(2)}) collective-permute-start(bf16[256,256]{1,0:T(8,128)(2,1)S(1)} %shard_map.104.refs_0_), channel_id=1, source_target_pairs={{0,2},{1,3},{2,0},{3,1},{4,6},{5,7},{6,4},{7,5},{8,10},{9,11},{10,... | collective-permute-start | bytes 393224 | tf_op jit(solution)/shard_map/ppermute | solution.py:184
  14.9 0.0 copy-done.6
  14.9 4.1 %collective-permute-done.5.refs_1_ = bf16[256,256]{1,0:T(8,128)(2,1)S(1)} collective-permute-done((bf16[256,256]{1,0:T(8,128)(2,1)S(1)}, bf16[256,256]{1,0:T(8,128)(2,1)S(1)}, u32[]{:S(2)}, u32[]{:S(2)}) %collective-permute-start.5) | collective-permute-done | bytes 131104 | tf_op jit(solution)/shard_map/ppermute | solution.py:184
  18.9 0.0 copy-done.1
  18.9 0.0 copy-done.3
  19.0 0.5 %shard_map.105 = (bf16[128,256]{1,0:T(8,128)(2,1)S(1)}, bf16[272,256]{1,0:T(8,128)(2,1)S(1)}, bf16[128,256]{1,0:T(8,128)(2,1)S(1)}, bf16[400,256]{1,0:T(8,128)(2,1)S(1)}) custom-call(bf16[256,256]{1,0:T(8,128)(2,1)S(1)} %copy-done.1, bf16[1,256]{1,0:T(2,128)(2,1)S(1)} %reshape.14.b_ref, bf16[256,256]{1,0:T(8,128)(2,1)S(1)} %shard_map.104.refs_0_, ...), custom_call_target="tpu_custom_call" | custom-call | tf_op jit(solution)/shard_map/pallas_call | solution.py:217
  19.5 0.1 collective-permute-start.6
  19.5 1.4 %collective-permute-done.6.got_ref = bf16[400,256]{1,0:T(8,128)(2,1)S(1)} collective-permute-done((bf16[400,256]{1,0:T(8,128)(2,1)S(1)}, bf16[400,256]{1,0:T(8,128)(2,1)S(1)}, u32[]{:S(2)}, u32[]{:S(2)}) %collective-permute-start.6) | collective-permute-done | bytes 204832 | tf_op jit(solution)/shard_map/ppermute | solution.py:184
  21.0 0.3 shard_map.106
  21.3 1.1 %collective-permute-start.7 = (bf16[272,256]{1,0:T(8,128)(2,1)S(1)}, bf16[272,256]{1,0:T(8,128)(2,1)S(1)}, u32[]{:S(2)}, u32[]{:S(2)}) collective-permute-start(bf16[272,256]{1,0:T(8,128)(2,1)S(1)} %get-tuple-element.30), channel_id=1, source_target_pairs={{0,4},{4,0},{8,12},{12,8},{1,5},{5,1},{9,13},{13,9},{2,6},{6,2},{1... | collective-permute-start | bytes 417800 | tf_op jit(solution)/shard_map/ppermute | solution.py:184
  22.5 1.0 %collective-permute-start.9 = (bf16[128,256]{1,0:T(8,128)(2,1)S(1)}, bf16[128,256]{1,0:T(8,128)(2,1)S(1)}, u32[]{:S(2)}, u32[]{:S(2)}) collective-permute-start(bf16[128,256]{1,0:T(8,128)(2,1)S(1)} %shard_map.108.part_ref), channel_id=1, source_target_pairs={{0,4},{4,0},{8,12},{12,8},{1,5},{5,1},{9,13},{13,9},{2,6},{6,2},{1... | collective-permute-start | bytes 196616 | tf_op jit(solution)/shard_map/ppermute | solution.py:184
  23.5 5.0 %collective-permute-done.9.got_ref = bf16[128,256]{1,0:T(8,128)(2,1)S(1)} collective-permute-done((bf16[128,256]{1,0:T(8,128)(2,1)S(1)}, bf16[128,256]{1,0:T(8,128)(2,1)S(1)}, u32[]{:S(2)}, u32[]{:S(2)}) %collective-permute-start.9) | collective-permute-done | bytes 65568 | tf_op jit(solution)/shard_map/ppermute | solution.py:184
  28.5 1.9 %collective-permute-start.10 = (bf16[128,256]{1,0:T(8,128)(2,1)S(1)}, bf16[128,256]{1,0:T(8,128)(2,1)S(1)}, u32[]{:S(2)}, u32[]{:S(2)}) collective-permute-start(bf16[128,256]{1,0:T(8,128)(2,1)S(1)} %shard_map.109.part_ref), channel_id=1, source_target_pairs={{0,8},{4,12},{8,0},{12,4},{1,9},{5,13},{9,1},{13,5},{2,10},{6,14},... | collective-permute-start | bytes 196616 | tf_op jit(solution)/shard_map/ppermute | solution.py:184
  30.4 0.0 collective-permute-done.7.got_ref
  30.5 1.1 %collective-permute-start.8 = (bf16[144,256]{1,0:T(8,128)(2,1)S(1)}, bf16[144,256]{1,0:T(8,128)(2,1)S(1)}, u32[]{:S(2)}, u32[]{:S(2)}) collective-permute-start(bf16[144,256]{1,0:T(8,128)(2,1)S(1)} %get-tuple-element.32), channel_id=1, source_target_pairs={{0,8},{4,12},{8,0},{12,4},{1,9},{5,13},{9,1},{13,5},{2,10},{6,14},... | collective-permute-start | bytes 221192 | tf_op jit(solution)/shard_map/ppermute | solution.py:184
  31.6 4.0 %collective-permute-done.10.got_ref = bf16[128,256]{1,0:T(8,128)(2,1)S(1)} collective-permute-done((bf16[128,256]{1,0:T(8,128)(2,1)S(1)}, bf16[128,256]{1,0:T(8,128)(2,1)S(1)}, u32[]{:S(2)}, u32[]{:S(2)}) %collective-permute-start.10) | collective-permute-done | bytes 65568 | tf_op jit(solution)/shard_map/ppermute | solution.py:184
  35.6 0.1 collective-permute-start.11
  35.7 1.2 %collective-permute-done.11.got_ref = bf16[128,256]{1,0:T(8,128)(2,1)S(1)} collective-permute-done((bf16[128,256]{1,0:T(8,128)(2,1)S(1)}, bf16[128,256]{1,0:T(8,128)(2,1)S(1)}, u32[]{:S(2)}, u32[]{:S(2)}) %collective-permute-start.11) | collective-permute-done | bytes 65568 | tf_op jit(solution)/shard_map/ppermute | solution.py:184
  36.9 0.7 %collective-permute-done.8.more_ref = bf16[144,256]{1,0:T(8,128)(2,1)S(1)} collective-permute-done((bf16[144,256]{1,0:T(8,128)(2,1)S(1)}, bf16[144,256]{1,0:T(8,128)(2,1)S(1)}, u32[]{:S(2)}, u32[]{:S(2)}) %collective-permute-start.8) | collective-permute-done | bytes 73760 | tf_op jit(solution)/shard_map/ppermute | solution.py:184
  37.6 0.8 %shard_map.111 = (bf16[128,256]{1,0:T(8,128)(2,1)}, bf16[128,256]{1,0:T(8,128)(2,1)}, f32[256,256]{1,0:T(8,128)}, f32[1,256]{1,0:T(1,128)}) custom-call(bf16[128,256]{1,0:T(8,128)(2,1)S(1)} %get-tuple-element.25.act_ref, f32[144,256]{1,0:T(8,128)S(1)} %get-tuple-element.31.feat_ref, bf16[144,256]{1,0:T(8,128)(2,1)S(1)} %collective-permute-done.8.more_ref, ...), custom_call_target="tpu_custom_call" | custom-call | tf_op jit(solution)/shard_map/pallas_call | solution.py:250
  (6 shorter events, 0.1 us)
Async XLA Ops:
  0.6 10.1 %collective-permute-start = (bf16[128,256]{1,0:T(8,128)(2,1)}, bf16[128,256]{1,0:T(8,128)(2,1)S(1)}, u32[]{:S(2)}, u32[]{:S(2)}) collective-permute-start(bf16[128,256]{1,0:T(8,128)(2,1)} %refs_3_.1), channel_id=1, source_target_pairs={{0,12},{4,8},{8,4},{12,0},{1,13},{5,9},{9,5},{13,1},{2,14},{6,10},... | collective-permute-start | bytes 196616 | tf_op jit(solution)/shard_map/ppermute | solution.py:184
  5.7 5.8 %collective-permute-start.1 = (bf16[128,256]{1,0:T(8,128)(2,1)}, bf16[128,256]{1,0:T(8,128)(2,1)S(1)}, u32[]{:S(2)}, u32[]{:S(2)}) collective-permute-start(bf16[128,256]{1,0:T(8,128)(2,1)} %refs_3_.1), channel_id=1, source_target_pairs={{0,8},{4,12},{8,0},{12,4},{1,9},{5,13},{9,1},{13,5},{2,10},{6,14},... | collective-permute-start | bytes 196616 | tf_op jit(solution)/shard_map/ppermute | solution.py:184
  5.7 5.8 %collective-permute-start.2 = (bf16[128,256]{1,0:T(8,128)(2,1)}, bf16[128,256]{1,0:T(8,128)(2,1)S(1)}, u32[]{:S(2)}, u32[]{:S(2)}) collective-permute-start(bf16[128,256]{1,0:T(8,128)(2,1)} %refs_3_.1), channel_id=1, source_target_pairs={{0,4},{4,0},{8,12},{12,8},{1,5},{5,1},{9,13},{13,9},{2,6},{6,2},{1... | collective-permute-start | bytes 196616 | tf_op jit(solution)/shard_map/ppermute | solution.py:184
  6.4 5.2 %collective-permute-start.3 = (bf16[128,256]{1,0:T(8,128)(2,1)}, bf16[128,256]{1,0:T(8,128)(2,1)S(1)}, u32[]{:S(2)}, u32[]{:S(2)}) collective-permute-start(bf16[128,256]{1,0:T(8,128)(2,1)} %refs_2_.1), channel_id=1, source_target_pairs={{0,2},{1,3},{2,0},{3,1},{4,6},{5,7},{6,4},{7,5},{8,10},{9,11},{10,... | collective-permute-start | bytes 196616 | tf_op jit(solution)/shard_map/ppermute | solution.py:184
  8.0 0.7 %copy-start.4 = (s32[4,1,2]{0,2,1:T(2,128)S(1)}, s32[4,1,2]{0,2,1:T(2,128)}, u32[]{:S(2)}) copy-start(s32[4,1,2]{0,2,1:T(2,128)} %param.9) | copy-start | bytes 100
  8.0 0.7 %copy-start.5 = (s32[4,1]{0,1:T(1,128)S(1)}, s32[4,1]{0,1:T(1,128)}, u32[]{:S(2)}) copy-start(s32[4,1]{0,1:T(1,128)} %param.10) | copy-start | bytes 52
  8.7 1.0 %copy-start = (bf16[4,1,2,128,128]{4,3,2,1,0:T(8,128)(2,1)S(1)}, bf16[4,1,2,128,128]{4,3,2,1,0:T(8,128)(2,1)}, u32[]{:S(2)}) copy-start(bf16[4,1,2,128,128]{4,3,2,1,0:T(8,128)(2,1)} %tiles_ref.1) | copy-start | bytes 786436
  9.7 1.9 %copy-start.2 = (bf16[128,256]{1,0:T(8,128)(2,1)S(1)}, bf16[128,256]{1,0:T(8,128)(2,1)}, u32[]{:S(2)}) copy-start(bf16[128,256]{1,0:T(8,128)(2,1)} %refs_3_.1) | copy-start | bytes 196612
  11.9 1.4 %collective-permute-start.4 = (bf16[256,256]{1,0:T(8,128)(2,1)S(1)}, bf16[256,256]{1,0:T(8,128)(2,1)S(1)}, u32[]{:S(2)}, u32[]{:S(2)}) collective-permute-start(bf16[256,256]{1,0:T(8,128)(2,1)S(1)} %get-tuple-element.23), channel_id=1, source_target_pairs={{0,1},{1,0},{2,3},{3,2},{4,5},{5,4},{6,7},{7,6},{8,9},{9,8},{10,11... | collective-permute-start | bytes 393224 | tf_op jit(solution)/shard_map/ppermute | solution.py:184
  13.3 1.6 %copy-start.6 = (bf16[256]{0:T(256)(128)(2,1)S(1)}, bf16[256]{0:T(256)(128)(2,1)}, u32[]{:S(2)}) copy-start(bf16[256]{0:T(256)(128)(2,1)} %param.12) | copy-start | bytes 1540
  13.3 5.7 %copy-start.1 = (bf16[256,256]{1,0:T(8,128)(2,1)S(1)}, bf16[256,256]{1,0:T(8,128)(2,1)}, u32[]{:S(2)}) copy-start(bf16[256,256]{1,0:T(8,128)(2,1)} %w_ref.1) | copy-start | bytes 393220
  13.3 5.7 %copy-start.3 = (bf16[128,256]{1,0:T(8,128)(2,1)S(1)}, bf16[128,256]{1,0:T(8,128)(2,1)}, u32[]{:S(2)}) copy-start(bf16[128,256]{1,0:T(8,128)(2,1)} %refs_2_.1) | copy-start | bytes 196612
  13.3 5.6 %collective-permute-start.5 = (bf16[256,256]{1,0:T(8,128)(2,1)S(1)}, bf16[256,256]{1,0:T(8,128)(2,1)S(1)}, u32[]{:S(2)}, u32[]{:S(2)}) collective-permute-start(bf16[256,256]{1,0:T(8,128)(2,1)S(1)} %shard_map.104.refs_0_), channel_id=1, source_target_pairs={{0,2},{1,3},{2,0},{3,1},{4,6},{5,7},{6,4},{7,5},{8,10},{9,11},{10,... | collective-permute-start | bytes 393224 | tf_op jit(solution)/shard_map/ppermute | solution.py:184
  19.5 1.5 %collective-permute-start.6 = (bf16[400,256]{1,0:T(8,128)(2,1)S(1)}, bf16[400,256]{1,0:T(8,128)(2,1)S(1)}, u32[]{:S(2)}, u32[]{:S(2)}) collective-permute-start(bf16[400,256]{1,0:T(8,128)(2,1)S(1)} %get-tuple-element.28), channel_id=1, source_target_pairs={{0,1},{1,0},{2,3},{3,2},{4,5},{5,4},{6,7},{7,6},{8,9},{9,8},{10,11... | collective-permute-start | bytes 614408 | tf_op jit(solution)/shard_map/ppermute | solution.py:184
  21.3 9.1 %collective-permute-start.7 = (bf16[272,256]{1,0:T(8,128)(2,1)S(1)}, bf16[272,256]{1,0:T(8,128)(2,1)S(1)}, u32[]{:S(2)}, u32[]{:S(2)}) collective-permute-start(bf16[272,256]{1,0:T(8,128)(2,1)S(1)} %get-tuple-element.30), channel_id=1, source_target_pairs={{0,4},{4,0},{8,12},{12,8},{1,5},{5,1},{9,13},{13,9},{2,6},{6,2},{1... | collective-permute-start | bytes 417800 | tf_op jit(solution)/shard_map/ppermute | solution.py:184
  22.5 6.0 %collective-permute-start.9 = (bf16[128,256]{1,0:T(8,128)(2,1)S(1)}, bf16[128,256]{1,0:T(8,128)(2,1)S(1)}, u32[]{:S(2)}, u32[]{:S(2)}) collective-permute-start(bf16[128,256]{1,0:T(8,128)(2,1)S(1)} %shard_map.108.part_ref), channel_id=1, source_target_pairs={{0,4},{4,0},{8,12},{12,8},{1,5},{5,1},{9,13},{13,9},{2,6},{6,2},{1... | collective-permute-start | bytes 196616 | tf_op jit(solution)/shard_map/ppermute | solution.py:184
  28.5 7.1 %collective-permute-start.10 = (bf16[128,256]{1,0:T(8,128)(2,1)S(1)}, bf16[128,256]{1,0:T(8,128)(2,1)S(1)}, u32[]{:S(2)}, u32[]{:S(2)}) collective-permute-start(bf16[128,256]{1,0:T(8,128)(2,1)S(1)} %shard_map.109.part_ref), channel_id=1, source_target_pairs={{0,8},{4,12},{8,0},{12,4},{1,9},{5,13},{9,1},{13,5},{2,10},{6,14},... | collective-permute-start | bytes 196616 | tf_op jit(solution)/shard_map/ppermute | solution.py:184
  30.5 7.1 %collective-permute-start.8 = (bf16[144,256]{1,0:T(8,128)(2,1)S(1)}, bf16[144,256]{1,0:T(8,128)(2,1)S(1)}, u32[]{:S(2)}, u32[]{:S(2)}) collective-permute-start(bf16[144,256]{1,0:T(8,128)(2,1)S(1)} %get-tuple-element.32), channel_id=1, source_target_pairs={{0,8},{4,12},{8,0},{12,4},{1,9},{5,13},{9,1},{13,5},{2,10},{6,14},... | collective-permute-start | bytes 221192 | tf_op jit(solution)/shard_map/ppermute | solution.py:184
  35.6 1.3 %collective-permute-start.11 = (bf16[128,256]{1,0:T(8,128)(2,1)S(1)}, bf16[128,256]{1,0:T(8,128)(2,1)S(1)}, u32[]{:S(2)}, u32[]{:S(2)}) collective-permute-start(bf16[128,256]{1,0:T(8,128)(2,1)S(1)} %shard_map.110.mine_ref), channel_id=1, source_target_pairs={{0,1},{1,0},{2,3},{3,2},{4,5},{5,4},{6,7},{7,6},{8,9},{9,8},{10,11... | collective-permute-start | bytes 196616 | tf_op jit(solution)/shard_map/ppermute | solution.py:184

commit v8 on v7

--- a/solution.py
+++ b/solution.py
@@ -118,7 +118,7 @@
         act_ref[...] = (preact[:tile] * sig[:tile]).astype(BF)
         grad = (cot * (sig * (1.0 + preact * (1.0 - sig)))).astype(BF)
         gagg = dot(grad, w_ref[...], 1, 1).astype(BF)
-        keep_ref[:rows, :] = gagg
+        keep_ref[...] = gagg
         send_ref[:rows, :] = gagg
         for u in range(n_chip):
             here = pl.ds(pl.multiple_of(jnp.bitwise_xor(chip, u) * tile, tile), tile)
@@ -129,51 +129,54 @@
         mine = pl.multiple_of(core * piece, piece)
         other = pl.multiple_of((1 - core) * piece, piece)
         lines = two_rows(jnp.sum(grad.astype(F32), axis=0, keepdims=True))
-        part_ref[...] = local_ref[pl.ds(mine, piece), :].astype(BF)
-        keep_ref[rows:, :] = lines
-        send_ref[rows : rows + PAD, :] = lines
-        send_ref[rows + PAD :, :] = local_ref[pl.ds(other, piece), :].astype(BF)
+        part_ref[:piece, :] = local_ref[pl.ds(mine, piece), :].astype(BF)
+        part_ref[piece:, :] = lines
+        send_ref[rows : rows + piece, :] = local_ref[pl.ds(other, piece), :].astype(BF)
+        send_ref[rows + piece :, :] = lines
 
     return body
 
 
-def line_of(rows):
-    rows = rows.astype(F32)
-    return rows[0:1] + rows[1:2]
+def add_parts(a, b):
+    piece = a.shape[0] - PAD
+    a, b = a.astype(F32), b.astype(F32)
+    total = a + b
+    line = total[piece : piece + 1] + total[piece + 1 : piece + 2]
+    return jnp.concatenate([total[:piece].astype(BF), two_rows(line)], axis=0)
 
 
 def part_kernel(part_ref, got_ref, out_ref):
+    first = got_ref.shape[0] - part_ref.shape[0]
+    out_ref[...] = add_parts(part_ref[...], got_ref[first:, :])
+
+
+def last_part_kernel(part_ref, got_ref, out_ref, line_ref):
     piece = out_ref.shape[0]
-    first = got_ref.shape[0] - piece
-    out_ref[...] = (part_ref[...].astype(F32) + got_ref[first:, :].astype(F32)).astype(BF)
+    total = part_ref[...].astype(F32) + got_ref[...].astype(F32)
+    out_ref[...] = total[:piece].astype(BF)
+    line_ref[...] = total[piece : piece + 1] + total[piece + 1 : piece + 2]
 
 
 def backward_kernel(at_ref, mine_ref, got_ref, keep_ref, send_ref):
-    rows, half = mine_ref.shape[0] - PAD, keep_ref.shape[0] - PAD
-    g = jnp.concatenate([mine_ref[:rows, :], got_ref[:rows, :]], axis=0)
-    send_ref[:half, :] = dot(at_ref[half:, :], g).astype(BF)
-    keep_ref[:half, :] = dot(at_ref[:half, :], g)
-    line = two_rows(line_of(mine_ref[rows:, :]) + line_of(got_ref[rows : rows + PAD, :]))
-    send_ref[half:, :] = line
-    keep_ref[half:, :] = line.astype(F32)
+    rows, half = mine_ref.shape[0], keep_ref.shape[0]
+    g = jnp.concatenate([mine_ref[...], got_ref[:rows, :]], axis=0)
+    send_ref[...] = dot(at_ref[half:, :], g).astype(BF)
+    keep_ref[...] = dot(at_ref[:half, :], g)
 
 
 def halve_kernel(in_ref, got_ref, keep_ref, send_ref):
-    half, rows = keep_ref.shape[0] - PAD, in_ref.shape[0] - PAD
-    send_ref[:half, :] = (in_ref[half:rows, :] + got_ref[half:rows, :].astype(F32)).astype(BF)
-    keep_ref[:half, :] = in_ref[:half, :] + got_ref[:half, :].astype(F32)
-    line = two_rows(line_of(in_ref[rows:, :]) + line_of(got_ref[rows:, :]))
-    send_ref[half:, :] = line
-    keep_ref[half:, :] = line.astype(F32)
-
-
-def last_kernel(act_ref, feat_ref, more_ref, mine_ref, got_ref, *outs):
+    half = keep_ref.shape[0]
+    send_ref[...] = (in_ref[half:, :] + got_ref[half:, :].astype(F32)).astype(BF)
+    keep_ref[...] = in_ref[:half, :] + got_ref[:half, :].astype(F32)
+
+
+def last_kernel(act_ref, feat_ref, more_ref, line_ref, mine_ref, got_ref, *outs):
     act_out, feat_out, weight_out, bias_out = outs
-    tile, piece = act_ref.shape[0], mine_ref.shape[0]
+    piece = mine_ref.shape[0]
     core = lax.rem(lax.axis_index("col"), 2)
     act_out[...] = act_ref[...]
-    feat_out[...] = (feat_ref[:tile, :] + more_ref[:tile, :].astype(F32)).astype(BF)
-    bias_out[...] = line_of(feat_ref[tile:, :]) + line_of(more_ref[tile:, :])
+    feat_out[...] = (feat_ref[...] + more_ref[...].astype(F32)).astype(BF)
+    bias_out[...] = line_ref[...]
     mine = pl.multiple_of(core * piece, piece)
     other = pl.multiple_of((1 - core) * piece, piece)
     weight_out[pl.ds(mine, piece), :] = mine_ref[...].astype(F32)
@@ -218,9 +221,9 @@
         middle_kernel(n_chip),
         (
             shape(tile, width),
-            shape(half + PAD, width),
-            shape(piece, width),
-            shape(half + PAD + piece, width),
+            shape(half, width),
+            shape(piece + PAD, width),
+            shape(half + piece + PAD, width),
         ),
         count=2 + 2 * n_chip,
         scratch=[
@@ -230,23 +233,25 @@
         ],
     )(weight, bias_term.reshape(1, width), *sums, *cots)
     got = swap(send, "col", n_col, 1)
-    part = call(part_kernel, shape(piece, width), count=2)(part, got)
+    part = call(part_kernel, shape(piece + PAD, width), count=2)(part, got)
     rows = n_row * tile // 2
     feats, send = call(
-        backward_kernel, (shape(rows + PAD, width, dtype=F32), shape(rows + PAD, width)), count=3
+        backward_kernel, (shape(rows, width, dtype=F32), shape(rows, width)), count=3
     )(at, keep, got)
     by = 1
     while by < n_row:
-        part = call(part_kernel, shape(piece, width), count=2)(
-            part, swap(part, "row", n_row, by)
-        )
+        other = swap(part, "row", n_row, by)
         got = swap(send, "row", n_row, by)
         by *= 2
         if by < n_row:
+            part = call(part_kernel, shape(piece + PAD, width), count=2)(part, other)
             rows //= 2
             feats, send = call(
-                halve_kernel, (shape(rows + PAD, width, dtype=F32), shape(rows + PAD, width)), count=2
+                halve_kernel, (shape(rows, width, dtype=F32), shape(rows, width)), count=2
             )(feats, got)
+    part, grad_bias = call(
+        last_part_kernel, (shape(piece, width), shape(1, width, dtype=F32)), count=2
+    )(part, other)
     act, grad_features, grad_weight, grad_bias = call(
         last_kernel,
         (
@@ -255,8 +260,8 @@
             shape(width, width, dtype=F32),
             shape(1, width, dtype=F32),
         ),
-        count=5,
-    )(act, feats, got, part, swap(part, "col", n_col, 1))
+        count=6,
+    )(act, feats, got, grad_bias, part, swap(part, "col", n_col, 1))
     return act, grad_features, grad_weight, grad_bias.reshape(width)
 
 

time: 38.5 us -> 36 us (0.935)
  waiting for transfers between devices: 18.6 us -> 15.4 us
  starting transfers between devices: 14.4 us -> 14.9 us
    ppermute x12, waiting for transfers between devices: 18.6 us -> 15.4 us  [swap(): return lax.ppermute(x, axis, [(i, i ^ by) for i in range(n)])]
    ppermute x12, starting transfers between devices: 14.4 us -> 14.9 us  [swap(): return lax.ppermute(x, axis, [(i, i ^ by) for i in range(n)])]
  transfers between devices with their start and end apart: 12 -> 12, of which waited for: 8 -> 8; matrix products, arithmetic and copies ran while one was open for 0% -> 0% of each run, Pallas kernels for 3% -> 4%
where the time goes in v8:
time: 36 us; the launch traced here: 35.8 us
  waiting for transfers between devices  15.4 us (43%)
  starting transfers between devices  14.9 us (41%)
  Pallas kernels  3.07 us (9%)
  local copies, waits for them, and re-layouts  1.65 us (5%)
  between operations  0.73 us (2%)
    ppermute x12, waiting for transfers between devices, swap(): return lax.ppermute(x, axis, [(i, i ^ by) for i in range(n)])  15.4 us
    ppermute x12, starting transfers between devices, swap(): return lax.ppermute(x, axis, [(i, i ^ by) for i in range(n)])  14.9 us
    unnamed x14, local copies, waits for them, and re-layouts  1.64 us
    pallas_call x1, Pallas kernels, shards(): call(dense_kernel(n_chip, n_row), (shape(n_col * tile, n_row * tile), sha...  1.05 us
    pallas_call x1, Pallas kernels, shards(): call(last_kernel, (shape(tile, width), shape(tile, width), shape(width, w...  0.79 us
  transfers between devices with their start and end apart: 12, of which 8 were waited for; matrix products, arithmetic and copies ran while one was open for 0% of the time, Pallas kernels for 4%

profile of v8, /device:TPU:0, one launch (start us, length us, event | category | flops | bytes accessed | tf_op | source)
XLA Modules:
  0.0 35.8 jit_solution(13699663570255396035)
XLA Ops:
  0.6 5.1 %collective-permute-start = (bf16[128,256]{1,0:T(8,128)(2,1)}, bf16[128,256]{1,0:T(8,128)(2,1)S(1)}, u32[]{:S(2)}, u32[]{:S(2)}) collective-permute-start(bf16[128,256]{1,0:T(8,128)(2,1)} %refs_3_.1), channel_id=1, source_target_pairs={{0,12},{4,8},{8,4},{12,0},{1,13},{5,9},{9,5},{13,1},{2,14},{6,10},... | collective-permute-start | bytes 196616 | tf_op jit(solution)/shard_map/ppermute | solution.py:187
  5.7 0.0 collective-permute-start.1
  5.7 0.6 %collective-permute-start.2 = (bf16[128,256]{1,0:T(8,128)(2,1)}, bf16[128,256]{1,0:T(8,128)(2,1)S(1)}, u32[]{:S(2)}, u32[]{:S(2)}) collective-permute-start(bf16[128,256]{1,0:T(8,128)(2,1)} %refs_3_.1), channel_id=1, source_target_pairs={{0,4},{4,0},{8,12},{12,8},{1,5},{5,1},{9,13},{13,9},{2,6},{6,2},{1... | collective-permute-start | bytes 196616 | tf_op jit(solution)/shard_map/ppermute | solution.py:187
  6.4 1.6 %collective-permute-start.3 = (bf16[128,256]{1,0:T(8,128)(2,1)}, bf16[128,256]{1,0:T(8,128)(2,1)S(1)}, u32[]{:S(2)}, u32[]{:S(2)}) collective-permute-start(bf16[128,256]{1,0:T(8,128)(2,1)} %refs_2_.1), channel_id=1, source_target_pairs={{0,2},{1,3},{2,0},{3,1},{4,6},{5,7},{6,4},{7,5},{8,10},{9,11},{10,... | collective-permute-start | bytes 196616 | tf_op jit(solution)/shard_map/ppermute | solution.py:187
  8.0 0.0 copy-start.4
  8.0 0.0 copy-start.5
  8.0 0.7 %copy-done.4 = s32[4,1,2]{0,2,1:T(2,128)S(1)} copy-done((s32[4,1,2]{0,2,1:T(2,128)S(1)}, s32[4,1,2]{0,2,1:T(2,128)}, u32[]{:S(2)}) %copy-start.4) | copy-done | bytes 56
  8.7 0.0 copy-done.5
  8.7 0.0 copy-start
  8.7 0.9 %copy-done = bf16[4,1,2,128,128]{4,3,2,1,0:T(8,128)(2,1)S(1)} copy-done((bf16[4,1,2,128,128]{4,3,2,1,0:T(8,128)(2,1)S(1)}, bf16[4,1,2,128,128]{4,3,2,1,0:T(8,128)(2,1)}, u32[]{:S(2)}) %copy-start) | copy-done | bytes 262168
  9.7 0.0 copy-start.2
  9.7 1.0 %shard_map.102 = (bf16[512,512]{1,0:T(8,128)(2,1)S(1)}, bf16[512,512]{1,0:T(8,128)(2,1)S(1)}) custom-call(s32[1,2,4]{2,1,0:T(2,128)S(1)} %bitcast.3, s32[1,4]{1,0:T(1,128)S(1)} %bitcast.4, bf16[4,1,2,128,128]{4,3,2,1,0:T(8,128)(2,1)S(1)} %copy-done), custom_call_target="tpu_custom_call" | custom-call | tf_op jit(solution)/shard_map/pallas_call | solution.py:207
  10.7 0.0 collective-permute-done.refs_0_
  10.7 0.8 %collective-permute-done.1.refs_1_ = bf16[128,256]{1,0:T(8,128)(2,1)S(1)} collective-permute-done((bf16[128,256]{1,0:T(8,128)(2,1)}, bf16[128,256]{1,0:T(8,128)(2,1)S(1)}, u32[]{:S(2)}, u32[]{:S(2)}) %collective-permute-start.1) | collective-permute-done | bytes 65568 | tf_op jit(solution)/shard_map/ppermute | solution.py:187
  11.6 0.0 collective-permute-done.2.refs_2_
  11.6 0.0 collective-permute-done.3.refs_4_
  11.6 0.0 copy-done.2
  11.6 0.3 shard_map.103
  11.9 0.1 collective-permute-start.4
  12.0 1.3 %collective-permute-done.4.got_ref = bf16[256,256]{1,0:T(8,128)(2,1)S(1)} collective-permute-done((bf16[256,256]{1,0:T(8,128)(2,1)S(1)}, bf16[256,256]{1,0:T(8,128)(2,1)S(1)}, u32[]{:S(2)}, u32[]{:S(2)}) %collective-permute-start.4) | collective-permute-done | bytes 131104 | tf_op jit(solution)/shard_map/ppermute | solution.py:187
  13.3 0.0 copy-start.6
  13.3 0.0 copy-start.1
  13.3 0.0 copy-start.3
  13.3 1.6 %collective-permute-start.5 = (bf16[256,256]{1,0:T(8,128)(2,1)S(1)}, bf16[256,256]{1,0:T(8,128)(2,1)S(1)}, u32[]{:S(2)}, u32[]{:S(2)}) collective-permute-start(bf16[256,256]{1,0:T(8,128)(2,1)S(1)} %shard_map.104.refs_0_), channel_id=1, source_target_pairs={{0,2},{1,3},{2,0},{3,1},{4,6},{5,7},{6,4},{7,5},{8,10},{9,11},{10,... | collective-permute-start | bytes 393224 | tf_op jit(solution)/shard_map/ppermute | solution.py:187
  14.9 0.0 copy-done.6
  14.9 4.1 %collective-permute-done.5.refs_1_ = bf16[256,256]{1,0:T(8,128)(2,1)S(1)} collective-permute-done((bf16[256,256]{1,0:T(8,128)(2,1)S(1)}, bf16[256,256]{1,0:T(8,128)(2,1)S(1)}, u32[]{:S(2)}, u32[]{:S(2)}) %collective-permute-start.5) | collective-permute-done | bytes 131104 | tf_op jit(solution)/shard_map/ppermute | solution.py:187
  19.0 0.0 copy-done.1
  19.0 0.0 copy-done.3
  19.0 0.5 %shard_map.105 = (bf16[128,256]{1,0:T(8,128)(2,1)S(1)}, bf16[256,256]{1,0:T(8,128)(2,1)S(1)}, bf16[144,256]{1,0:T(8,128)(2,1)S(1)}, bf16[400,256]{1,0:T(8,128)(2,1)S(1)}) custom-call(bf16[256,256]{1,0:T(8,128)(2,1)S(1)} %copy-done.1, bf16[1,256]{1,0:T(2,128)(2,1)S(1)} %reshape.14.b_ref, bf16[256,256]{1,0:T(8,128)(2,1)S(1)} %shard_map.104.refs_0_, ...), custom_call_target="tpu_custom_call" | custom-call | tf_op jit(solution)/shard_map/pallas_call | solution.py:220
  19.5 0.1 collective-permute-start.6
  19.5 1.4 %collective-permute-done.6.got_ref = bf16[400,256]{1,0:T(8,128)(2,1)S(1)} collective-permute-done((bf16[400,256]{1,0:T(8,128)(2,1)S(1)}, bf16[400,256]{1,0:T(8,128)(2,1)S(1)}, u32[]{:S(2)}, u32[]{:S(2)}) %collective-permute-start.6) | collective-permute-done | bytes 204832 | tf_op jit(solution)/shard_map/ppermute | solution.py:187
  21.0 1.1 %collective-permute-start.9 = (bf16[144,256]{1,0:T(8,128)(2,1)S(1)}, bf16[144,256]{1,0:T(8,128)(2,1)S(1)}, u32[]{:S(2)}, u32[]{:S(2)}) collective-permute-start(bf16[144,256]{1,0:T(8,128)(2,1)S(1)} %shard_map.108.part_ref), channel_id=1, source_target_pairs={{0,4},{4,0},{8,12},{12,8},{1,5},{5,1},{9,13},{13,9},{2,6},{6,2},{1... | collective-permute-start | bytes 221192 | tf_op jit(solution)/shard_map/ppermute | solution.py:187
  22.2 0.3 shard_map.106
  22.5 1.0 %collective-permute-start.7 = (bf16[256,256]{1,0:T(8,128)(2,1)S(1)}, bf16[256,256]{1,0:T(8,128)(2,1)S(1)}, u32[]{:S(2)}, u32[]{:S(2)}) collective-permute-start(bf16[256,256]{1,0:T(8,128)(2,1)S(1)} %get-tuple-element.32), channel_id=1, source_target_pairs={{0,4},{4,0},{8,12},{12,8},{1,5},{5,1},{9,13},{13,9},{2,6},{6,2},{1... | collective-permute-start | bytes 393224 | tf_op jit(solution)/shard_map/ppermute | solution.py:187
  23.5 2.4 %collective-permute-done.9.got_ref = bf16[144,256]{1,0:T(8,128)(2,1)S(1)} collective-permute-done((bf16[144,256]{1,0:T(8,128)(2,1)S(1)}, bf16[144,256]{1,0:T(8,128)(2,1)S(1)}, u32[]{:S(2)}, u32[]{:S(2)}) %collective-permute-start.9) | collective-permute-done | bytes 73760 | tf_op jit(solution)/shard_map/ppermute | solution.py:187
  25.9 1.5 %collective-permute-start.10 = (bf16[144,256]{1,0:T(8,128)(2,1)S(1)}, bf16[144,256]{1,0:T(8,128)(2,1)S(1)}, u32[]{:S(2)}, u32[]{:S(2)}) collective-permute-start(bf16[144,256]{1,0:T(8,128)(2,1)S(1)} %shard_map.109.part_ref), channel_id=1, source_target_pairs={{0,8},{4,12},{8,0},{12,4},{1,9},{5,13},{9,1},{13,5},{2,10},{6,14},... | collective-permute-start | bytes 221192 | tf_op jit(solution)/shard_map/ppermute | solution.py:187
  27.4 1.6 %collective-permute-done.7.got_ref = bf16[256,256]{1,0:T(8,128)(2,1)S(1)} collective-permute-done((bf16[256,256]{1,0:T(8,128)(2,1)S(1)}, bf16[256,256]{1,0:T(8,128)(2,1)S(1)}, u32[]{:S(2)}, u32[]{:S(2)}) %collective-permute-start.7) | collective-permute-done | bytes 131104 | tf_op jit(solution)/shard_map/ppermute | solution.py:187
  29.1 2.1 %collective-permute-start.8 = (bf16[128,256]{1,0:T(8,128)(2,1)S(1)}, bf16[128,256]{1,0:T(8,128)(2,1)S(1)}, u32[]{:S(2)}, u32[]{:S(2)}) collective-permute-start(bf16[128,256]{1,0:T(8,128)(2,1)S(1)} %get-tuple-element.34), channel_id=1, source_target_pairs={{0,8},{4,12},{8,0},{12,4},{1,9},{5,13},{9,1},{13,5},{2,10},{6,14},... | collective-permute-start | bytes 196616 | tf_op jit(solution)/shard_map/ppermute | solution.py:187
  31.2 1.6 %collective-permute-done.10.got_ref = bf16[144,256]{1,0:T(8,128)(2,1)S(1)} collective-permute-done((bf16[144,256]{1,0:T(8,128)(2,1)S(1)}, bf16[144,256]{1,0:T(8,128)(2,1)S(1)}, u32[]{:S(2)}, u32[]{:S(2)}) %collective-permute-start.10) | collective-permute-done | bytes 73760 | tf_op jit(solution)/shard_map/ppermute | solution.py:187
  32.9 0.1 collective-permute-start.11
  32.9 2.1 %collective-permute-done.8.more_ref = bf16[128,256]{1,0:T(8,128)(2,1)S(1)} collective-permute-done((bf16[128,256]{1,0:T(8,128)(2,1)S(1)}, bf16[128,256]{1,0:T(8,128)(2,1)S(1)}, u32[]{:S(2)}, u32[]{:S(2)}) %collective-permute-start.8) | collective-permute-done | bytes 65568 | tf_op jit(solution)/shard_map/ppermute | solution.py:187
  35.0 0.0 collective-permute-done.11.got_ref
  35.0 0.8 %shard_map.111 = (bf16[128,256]{1,0:T(8,128)(2,1)}, bf16[128,256]{1,0:T(8,128)(2,1)}, f32[256,256]{1,0:T(8,128)}, f32[1,256]{1,0:T(1,128)}) custom-call(bf16[128,256]{1,0:T(8,128)(2,1)S(1)} %get-tuple-element.27.act_ref, f32[128,256]{1,0:T(8,128)S(1)} %get-tuple-element.33.feat_ref, bf16[128,256]{1,0:T(8,128)(2,1)S(1)} %collective-permute-done.8.more_ref, ...), custom_call_target="tpu_custom_call" | custom-call | tf_op jit(solution)/shard_map/pallas_call | solution.py:255
  (6 shorter events, 0.1 us)
Async XLA Ops:
  0.6 10.1 %collective-permute-start = (bf16[128,256]{1,0:T(8,128)(2,1)}, bf16[128,256]{1,0:T(8,128)(2,1)S(1)}, u32[]{:S(2)}, u32[]{:S(2)}) collective-permute-start(bf16[128,256]{1,0:T(8,128)(2,1)} %refs_3_.1), channel_id=1, source_target_pairs={{0,12},{4,8},{8,4},{12,0},{1,13},{5,9},{9,5},{13,1},{2,14},{6,10},... | collective-permute-start | bytes 196616 | tf_op jit(solution)/shard_map/ppermute | solution.py:187
  5.7 5.8 %collective-permute-start.1 = (bf16[128,256]{1,0:T(8,128)(2,1)}, bf16[128,256]{1,0:T(8,128)(2,1)S(1)}, u32[]{:S(2)}, u32[]{:S(2)}) collective-permute-start(bf16[128,256]{1,0:T(8,128)(2,1)} %refs_3_.1), channel_id=1, source_target_pairs={{0,8},{4,12},{8,0},{12,4},{1,9},{5,13},{9,1},{13,5},{2,10},{6,14},... | collective-permute-start | bytes 196616 | tf_op jit(solution)/shard_map/ppermute | solution.py:187
  5.7 5.8 %collective-permute-start.2 = (bf16[128,256]{1,0:T(8,128)(2,1)}, bf16[128,256]{1,0:T(8,128)(2,1)S(1)}, u32[]{:S(2)}, u32[]{:S(2)}) collective-permute-start(bf16[128,256]{1,0:T(8,128)(2,1)} %refs_3_.1), channel_id=1, source_target_pairs={{0,4},{4,0},{8,12},{12,8},{1,5},{5,1},{9,13},{13,9},{2,6},{6,2},{1... | collective-permute-start | bytes 196616 | tf_op jit(solution)/shard_map/ppermute | solution.py:187
  6.4 5.2 %collective-permute-start.3 = (bf16[128,256]{1,0:T(8,128)(2,1)}, bf16[128,256]{1,0:T(8,128)(2,1)S(1)}, u32[]{:S(2)}, u32[]{:S(2)}) collective-permute-start(bf16[128,256]{1,0:T(8,128)(2,1)} %refs_2_.1), channel_id=1, source_target_pairs={{0,2},{1,3},{2,0},{3,1},{4,6},{5,7},{6,4},{7,5},{8,10},{9,11},{10,... | collective-permute-start | bytes 196616 | tf_op jit(solution)/shard_map/ppermute | solution.py:187
  8.0 0.7 %copy-start.4 = (s32[4,1,2]{0,2,1:T(2,128)S(1)}, s32[4,1,2]{0,2,1:T(2,128)}, u32[]{:S(2)}) copy-start(s32[4,1,2]{0,2,1:T(2,128)} %param.9) | copy-start | bytes 100
  8.0 0.7 %copy-start.5 = (s32[4,1]{0,1:T(1,128)S(1)}, s32[4,1]{0,1:T(1,128)}, u32[]{:S(2)}) copy-start(s32[4,1]{0,1:T(1,128)} %param.10) | copy-start | bytes 52
  8.7 1.0 %copy-start = (bf16[4,1,2,128,128]{4,3,2,1,0:T(8,128)(2,1)S(1)}, bf16[4,1,2,128,128]{4,3,2,1,0:T(8,128)(2,1)}, u32[]{:S(2)}) copy-start(bf16[4,1,2,128,128]{4,3,2,1,0:T(8,128)(2,1)} %tiles_ref.1) | copy-start | bytes 786436
  9.7 1.9 %copy-start.2 = (bf16[128,256]{1,0:T(8,128)(2,1)S(1)}, bf16[128,256]{1,0:T(8,128)(2,1)}, u32[]{:S(2)}) copy-start(bf16[128,256]{1,0:T(8,128)(2,1)} %refs_3_.1) | copy-start | bytes 196612
  11.9 1.4 %collective-permute-start.4 = (bf16[256,256]{1,0:T(8,128)(2,1)S(1)}, bf16[256,256]{1,0:T(8,128)(2,1)S(1)}, u32[]{:S(2)}, u32[]{:S(2)}) collective-permute-start(bf16[256,256]{1,0:T(8,128)(2,1)S(1)} %get-tuple-element.25), channel_id=1, source_target_pairs={{0,1},{1,0},{2,3},{3,2},{4,5},{5,4},{6,7},{7,6},{8,9},{9,8},{10,11... | collective-permute-start | bytes 393224 | tf_op jit(solution)/shard_map/ppermute | solution.py:187
  13.3 1.6 %copy-start.6 = (bf16[256]{0:T(256)(128)(2,1)S(1)}, bf16[256]{0:T(256)(128)(2,1)}, u32[]{:S(2)}) copy-start(bf16[256]{0:T(256)(128)(2,1)} %param.12) | copy-start | bytes 1540
  13.3 5.7 %copy-start.1 = (bf16[256,256]{1,0:T(8,128)(2,1)S(1)}, bf16[256,256]{1,0:T(8,128)(2,1)}, u32[]{:S(2)}) copy-start(bf16[256,256]{1,0:T(8,128)(2,1)} %w_ref.1) | copy-start | bytes 393220
  13.3 5.7 %copy-start.3 = (bf16[128,256]{1,0:T(8,128)(2,1)S(1)}, bf16[128,256]{1,0:T(8,128)(2,1)}, u32[]{:S(2)}) copy-start(bf16[128,256]{1,0:T(8,128)(2,1)} %refs_2_.1) | copy-start | bytes 196612
  13.3 5.6 %collective-permute-start.5 = (bf16[256,256]{1,0:T(8,128)(2,1)S(1)}, bf16[256,256]{1,0:T(8,128)(2,1)S(1)}, u32[]{:S(2)}, u32[]{:S(2)}) collective-permute-start(bf16[256,256]{1,0:T(8,128)(2,1)S(1)} %shard_map.104.refs_0_), channel_id=1, source_target_pairs={{0,2},{1,3},{2,0},{3,1},{4,6},{5,7},{6,4},{7,5},{8,10},{9,11},{10,... | collective-permute-start | bytes 393224 | tf_op jit(solution)/shard_map/ppermute | solution.py:187
  19.5 1.5 %collective-permute-start.6 = (bf16[400,256]{1,0:T(8,128)(2,1)S(1)}, bf16[400,256]{1,0:T(8,128)(2,1)S(1)}, u32[]{:S(2)}, u32[]{:S(2)}) collective-permute-start(bf16[400,256]{1,0:T(8,128)(2,1)S(1)} %get-tuple-element.30), channel_id=1, source_target_pairs={{0,1},{1,0},{2,3},{3,2},{4,5},{5,4},{6,7},{7,6},{8,9},{9,8},{10,11... | collective-permute-start | bytes 614408 | tf_op jit(solution)/shard_map/ppermute | solution.py:187
  21.0 4.9 %collective-permute-start.9 = (bf16[144,256]{1,0:T(8,128)(2,1)S(1)}, bf16[144,256]{1,0:T(8,128)(2,1)S(1)}, u32[]{:S(2)}, u32[]{:S(2)}) collective-permute-start(bf16[144,256]{1,0:T(8,128)(2,1)S(1)} %shard_map.108.part_ref), channel_id=1, source_target_pairs={{0,4},{4,0},{8,12},{12,8},{1,5},{5,1},{9,13},{13,9},{2,6},{6,2},{1... | collective-permute-start | bytes 221192 | tf_op jit(solution)/shard_map/ppermute | solution.py:187
  22.5 6.6 %collective-permute-start.7 = (bf16[256,256]{1,0:T(8,128)(2,1)S(1)}, bf16[256,256]{1,0:T(8,128)(2,1)S(1)}, u32[]{:S(2)}, u32[]{:S(2)}) collective-permute-start(bf16[256,256]{1,0:T(8,128)(2,1)S(1)} %get-tuple-element.32), channel_id=1, source_target_pairs={{0,4},{4,0},{8,12},{12,8},{1,5},{5,1},{9,13},{13,9},{2,6},{6,2},{1... | collective-permute-start | bytes 393224 | tf_op jit(solution)/shard_map/ppermute | solution.py:187
  25.9 6.9 %collective-permute-start.10 = (bf16[144,256]{1,0:T(8,128)(2,1)S(1)}, bf16[144,256]{1,0:T(8,128)(2,1)S(1)}, u32[]{:S(2)}, u32[]{:S(2)}) collective-permute-start(bf16[144,256]{1,0:T(8,128)(2,1)S(1)} %shard_map.109.part_ref), channel_id=1, source_target_pairs={{0,8},{4,12},{8,0},{12,4},{1,9},{5,13},{9,1},{13,5},{2,10},{6,14},... | collective-permute-start | bytes 221192 | tf_op jit(solution)/shard_map/ppermute | solution.py:187
  29.1 5.9 %collective-permute-start.8 = (bf16[128,256]{1,0:T(8,128)(2,1)S(1)}, bf16[128,256]{1,0:T(8,128)(2,1)S(1)}, u32[]{:S(2)}, u32[]{:S(2)}) collective-permute-start(bf16[128,256]{1,0:T(8,128)(2,1)S(1)} %get-tuple-element.34), channel_id=1, source_target_pairs={{0,8},{4,12},{8,0},{12,4},{1,9},{5,13},{9,1},{13,5},{2,10},{6,14},... | collective-permute-start | bytes 196616 | tf_op jit(solution)/shard_map/ppermute | solution.py:187
  32.9 2.1 %collective-permute-start.11 = (bf16[128,256]{1,0:T(8,128)(2,1)S(1)}, bf16[128,256]{1,0:T(8,128)(2,1)S(1)}, u32[]{:S(2)}, u32[]{:S(2)}) collective-permute-start(bf16[128,256]{1,0:T(8,128)(2,1)S(1)} %get-tuple-element.37.mine_ref), channel_id=1, source_target_pairs={{0,1},{1,0},{2,3},{3,2},{4,5},{5,4},{6,7},{7,6},{8,9},{9,8},{10,11... | collective-permute-start | bytes 196616 | tf_op jit(solution)/shard_map/ppermute | solution.py:187

commit v9 on v8

--- a/solution.py
+++ b/solution.py
@@ -64,7 +64,8 @@
                 qs = pl.ds(pl.multiple_of(q * tile, tile), tile)
                 ps = pl.ds(pl.multiple_of(p * tile, tile), tile)
                 a_ref[qs, ps] = here
-                rs = pl.ds(pl.multiple_of(reversed_bits(p, n_row) * tile, tile), tile)
+                turned = jnp.where(lax.rem(c, 2) == 0, reversed_bits(p, n_row), p)
+                rs = pl.ds(pl.multiple_of(turned * tile, tile), tile)
                 at_ref[rs, qs] = here.T
 
             return carry
@@ -185,6 +186,15 @@
 
 def swap(x, axis, n, by):
     return lax.ppermute(x, axis, [(i, i ^ by) for i in range(n)])
+
+
+def step(x, n_row, n_col, by):
+    pairs = []
+    for i in range(n_row):
+        for j in range(n_col):
+            bit = by if j % 2 == 0 else n_row // 2 // by
+            pairs.append((i * n_col + j, (i ^ bit) * n_col + j))
+    return lax.ppermute(x, ("row", "col"), pairs)
 
 
 def deal(xs, axis):
@@ -240,8 +250,8 @@
     )(at, keep, got)
     by = 1
     while by < n_row:
-        other = swap(part, "row", n_row, by)
-        got = swap(send, "row", n_row, by)
+        other = step(part, n_row, n_col, by)
+        got = step(send, n_row, n_col, by)
         by *= 2
         if by < n_row:
             part = call(part_kernel, shape(piece + PAD, width), count=2)(part, other)

time: 36 us -> 36.3 us (level)
  waiting for transfers between devices: 15.4 us -> 16 us
    ppermute x0 -> x4, waiting for transfers between devices: none -> 8.32 us  [step(): return lax.ppermute(x, ('row', 'col'), pairs)]
    ppermute x12 -> x8, waiting for transfers between devices: 15.4 us -> 7.67 us  [swap(): return lax.ppermute(x, axis, [(i, i ^ by) for i in range(n)])]
    ppermute x12 -> x8, starting transfers between devices: 14.9 us -> 9.16 us  [swap(): return lax.ppermute(x, axis, [(i, i ^ by) for i in range(n)])]
    ppermute x0 -> x4, starting transfers between devices: none -> 5.5 us  [step(): return lax.ppermute(x, ('row', 'col'), pairs)]
where the time goes in v9:
time: 36.3 us; the launch traced here: 36.1 us
  waiting for transfers between devices  16 us (44%)
  starting transfers between devices  14.7 us (40%)
  Pallas kernels  3.07 us (8%)
  local copies, waits for them, and re-layouts  1.65 us (5%)
  between operations  0.73 us (2%)
    ppermute x8, starting transfers between devices, swap(): return lax.ppermute(x, axis, [(i, i ^ by) for i in range(n)])  9.16 us
    ppermute x4, waiting for transfers between devices, step(): return lax.ppermute(x, ('row', 'col'), pairs)  8.32 us
    ppermute x8, waiting for transfers between devices, swap(): return lax.ppermute(x, axis, [(i, i ^ by) for i in range(n)])  7.67 us
    ppermute x4, starting transfers between devices, step(): return lax.ppermute(x, ('row', 'col'), pairs)  5.5 us
    unnamed x14, local copies, waits for them, and re-layouts  1.64 us
    pallas_call x1, Pallas kernels, shards(): call(dense_kernel(n_chip, n_row), (shape(n_col * tile, n_row * tile), sha...  1.05 us
    pallas_call x1, Pallas kernels, shards(): call(last_kernel, (shape(tile, width), shape(tile, width), shape(width, w...  0.79 us
  transfers between devices with their start and end apart: 12, of which 8 were waited for; matrix products, arithmetic and copies ran while one was open for 0% of the time, Pallas kernels for 4%

profile of v9, /device:TPU:0, one launch (start us, length us, event | category | flops | bytes accessed | tf_op | source)
XLA Modules:
  0.0 36.1 jit_solution(16010530192816578573)
XLA Ops:
  0.6 5.1 %collective-permute-start = (bf16[128,256]{1,0:T(8,128)(2,1)}, bf16[128,256]{1,0:T(8,128)(2,1)S(1)}, u32[]{:S(2)}, u32[]{:S(2)}) collective-permute-start(bf16[128,256]{1,0:T(8,128)(2,1)} %refs_3_.1), channel_id=1, source_target_pairs={{0,12},{4,8},{8,4},{12,0},{1,13},{5,9},{9,5},{13,1},{2,14},{6,10},... | collective-permute-start | bytes 196616 | tf_op jit(solution)/shard_map/ppermute | solution.py:188
  5.7 0.0 collective-permute-start.1
  5.7 0.6 %collective-permute-start.2 = (bf16[128,256]{1,0:T(8,128)(2,1)}, bf16[128,256]{1,0:T(8,128)(2,1)S(1)}, u32[]{:S(2)}, u32[]{:S(2)}) collective-permute-start(bf16[128,256]{1,0:T(8,128)(2,1)} %refs_3_.1), channel_id=1, source_target_pairs={{0,4},{4,0},{8,12},{12,8},{1,5},{5,1},{9,13},{13,9},{2,6},{6,2},{1... | collective-permute-start | bytes 196616 | tf_op jit(solution)/shard_map/ppermute | solution.py:188
  6.4 1.6 %collective-permute-start.3 = (bf16[128,256]{1,0:T(8,128)(2,1)}, bf16[128,256]{1,0:T(8,128)(2,1)S(1)}, u32[]{:S(2)}, u32[]{:S(2)}) collective-permute-start(bf16[128,256]{1,0:T(8,128)(2,1)} %refs_2_.1), channel_id=1, source_target_pairs={{0,2},{1,3},{2,0},{3,1},{4,6},{5,7},{6,4},{7,5},{8,10},{9,11},{10,... | collective-permute-start | bytes 196616 | tf_op jit(solution)/shard_map/ppermute | solution.py:188
  8.0 0.0 copy-start.4
  8.0 0.0 copy-start.5
  8.0 0.7 %copy-done.4 = s32[4,1,2]{0,2,1:T(2,128)S(1)} copy-done((s32[4,1,2]{0,2,1:T(2,128)S(1)}, s32[4,1,2]{0,2,1:T(2,128)}, u32[]{:S(2)}) %copy-start.4) | copy-done | bytes 56
  8.7 0.0 copy-done.5
  8.7 0.0 copy-start
  8.7 0.9 %copy-done = bf16[4,1,2,128,128]{4,3,2,1,0:T(8,128)(2,1)S(1)} copy-done((bf16[4,1,2,128,128]{4,3,2,1,0:T(8,128)(2,1)S(1)}, bf16[4,1,2,128,128]{4,3,2,1,0:T(8,128)(2,1)}, u32[]{:S(2)}) %copy-start) | copy-done | bytes 262168
  9.7 0.0 copy-start.2
  9.7 1.0 %shard_map.102 = (bf16[512,512]{1,0:T(8,128)(2,1)S(1)}, bf16[512,512]{1,0:T(8,128)(2,1)S(1)}) custom-call(s32[1,2,4]{2,1,0:T(2,128)S(1)} %bitcast.3, s32[1,4]{1,0:T(1,128)S(1)} %bitcast.4, bf16[4,1,2,128,128]{4,3,2,1,0:T(8,128)(2,1)S(1)} %copy-done), custom_call_target="tpu_custom_call" | custom-call | tf_op jit(solution)/shard_map/pallas_call | solution.py:217
  10.7 0.0 collective-permute-done.refs_0_
  10.7 0.8 %collective-permute-done.1.refs_1_ = bf16[128,256]{1,0:T(8,128)(2,1)S(1)} collective-permute-done((bf16[128,256]{1,0:T(8,128)(2,1)}, bf16[128,256]{1,0:T(8,128)(2,1)S(1)}, u32[]{:S(2)}, u32[]{:S(2)}) %collective-permute-start.1) | collective-permute-done | bytes 65568 | tf_op jit(solution)/shard_map/ppermute | solution.py:188
  11.6 0.0 collective-permute-done.2.refs_2_
  11.6 0.0 collective-permute-done.3.refs_4_
  11.6 0.0 copy-done.2
  11.6 0.3 shard_map.103
  11.9 0.1 collective-permute-start.4
  12.0 1.3 %collective-permute-done.4.got_ref = bf16[256,256]{1,0:T(8,128)(2,1)S(1)} collective-permute-done((bf16[256,256]{1,0:T(8,128)(2,1)S(1)}, bf16[256,256]{1,0:T(8,128)(2,1)S(1)}, u32[]{:S(2)}, u32[]{:S(2)}) %collective-permute-start.4) | collective-permute-done | bytes 131104 | tf_op jit(solution)/shard_map/ppermute | solution.py:188
  13.3 0.0 copy-start.6
  13.3 0.0 copy-start.1
  13.3 0.0 copy-start.3
  13.3 1.6 %collective-permute-start.5 = (bf16[256,256]{1,0:T(8,128)(2,1)S(1)}, bf16[256,256]{1,0:T(8,128)(2,1)S(1)}, u32[]{:S(2)}, u32[]{:S(2)}) collective-permute-start(bf16[256,256]{1,0:T(8,128)(2,1)S(1)} %shard_map.104.refs_0_), channel_id=1, source_target_pairs={{0,2},{1,3},{2,0},{3,1},{4,6},{5,7},{6,4},{7,5},{8,10},{9,11},{10,... | collective-permute-start | bytes 393224 | tf_op jit(solution)/shard_map/ppermute | solution.py:188
  14.9 0.0 copy-done.6
  14.9 4.1 %collective-permute-done.5.refs_1_ = bf16[256,256]{1,0:T(8,128)(2,1)S(1)} collective-permute-done((bf16[256,256]{1,0:T(8,128)(2,1)S(1)}, bf16[256,256]{1,0:T(8,128)(2,1)S(1)}, u32[]{:S(2)}, u32[]{:S(2)}) %collective-permute-start.5) | collective-permute-done | bytes 131104 | tf_op jit(solution)/shard_map/ppermute | solution.py:188
  19.0 0.0 copy-done.1
  19.0 0.0 copy-done.3
  19.0 0.5 %shard_map.105 = (bf16[128,256]{1,0:T(8,128)(2,1)S(1)}, bf16[256,256]{1,0:T(8,128)(2,1)S(1)}, bf16[144,256]{1,0:T(8,128)(2,1)S(1)}, bf16[400,256]{1,0:T(8,128)(2,1)S(1)}) custom-call(bf16[256,256]{1,0:T(8,128)(2,1)S(1)} %copy-done.1, bf16[1,256]{1,0:T(2,128)(2,1)S(1)} %reshape.14.b_ref, bf16[256,256]{1,0:T(8,128)(2,1)S(1)} %shard_map.104.refs_0_, ...), custom_call_target="tpu_custom_call" | custom-call | tf_op jit(solution)/shard_map/pallas_call | solution.py:230
  19.5 0.1 collective-permute-start.6
  19.5 1.4 %collective-permute-done.6.got_ref = bf16[400,256]{1,0:T(8,128)(2,1)S(1)} collective-permute-done((bf16[400,256]{1,0:T(8,128)(2,1)S(1)}, bf16[400,256]{1,0:T(8,128)(2,1)S(1)}, u32[]{:S(2)}, u32[]{:S(2)}) %collective-permute-start.6) | collective-permute-done | bytes 204832 | tf_op jit(solution)/shard_map/ppermute | solution.py:188
  21.0 1.1 %collective-permute-start.9 = (bf16[144,256]{1,0:T(8,128)(2,1)S(1)}, bf16[144,256]{1,0:T(8,128)(2,1)S(1)}, u32[]{:S(2)}, u32[]{:S(2)}) collective-permute-start(bf16[144,256]{1,0:T(8,128)(2,1)S(1)} %shard_map.108.part_ref), channel_id=1, source_target_pairs={{0,4},{1,9},{2,6},{3,11},{4,0},{5,13},{6,2},{7,15},{8,12},{9,1},{1... | collective-permute-start | bytes 221192 | tf_op jit(solution)/shard_map/ppermute | solution.py:197
  22.2 0.3 shard_map.106
  22.5 1.0 %collective-permute-start.7 = (bf16[256,256]{1,0:T(8,128)(2,1)S(1)}, bf16[256,256]{1,0:T(8,128)(2,1)S(1)}, u32[]{:S(2)}, u32[]{:S(2)}) collective-permute-start(bf16[256,256]{1,0:T(8,128)(2,1)S(1)} %get-tuple-element.32), channel_id=1, source_target_pairs={{0,4},{1,9},{2,6},{3,11},{4,0},{5,13},{6,2},{7,15},{8,12},{9,1},{1... | collective-permute-start | bytes 393224 | tf_op jit(solution)/shard_map/ppermute | solution.py:197
  23.5 2.7 %collective-permute-done.9.got_ref = bf16[144,256]{1,0:T(8,128)(2,1)S(1)} collective-permute-done((bf16[144,256]{1,0:T(8,128)(2,1)S(1)}, bf16[144,256]{1,0:T(8,128)(2,1)S(1)}, u32[]{:S(2)}, u32[]{:S(2)}) %collective-permute-start.9) | collective-permute-done | bytes 73760 | tf_op jit(solution)/shard_map/ppermute | solution.py:197
  26.3 1.2 %collective-permute-start.10 = (bf16[144,256]{1,0:T(8,128)(2,1)S(1)}, bf16[144,256]{1,0:T(8,128)(2,1)S(1)}, u32[]{:S(2)}, u32[]{:S(2)}) collective-permute-start(bf16[144,256]{1,0:T(8,128)(2,1)S(1)} %shard_map.109.part_ref), channel_id=1, source_target_pairs={{0,8},{1,5},{2,10},{3,7},{4,12},{5,1},{6,14},{7,3},{8,0},{9,13},{1... | collective-permute-start | bytes 221192 | tf_op jit(solution)/shard_map/ppermute | solution.py:197
  27.5 1.9 %collective-permute-done.7.got_ref = bf16[256,256]{1,0:T(8,128)(2,1)S(1)} collective-permute-done((bf16[256,256]{1,0:T(8,128)(2,1)S(1)}, bf16[256,256]{1,0:T(8,128)(2,1)S(1)}, u32[]{:S(2)}, u32[]{:S(2)}) %collective-permute-start.7) | collective-permute-done | bytes 131104 | tf_op jit(solution)/shard_map/ppermute | solution.py:197
  29.4 2.1 %collective-permute-start.8 = (bf16[128,256]{1,0:T(8,128)(2,1)S(1)}, bf16[128,256]{1,0:T(8,128)(2,1)S(1)}, u32[]{:S(2)}, u32[]{:S(2)}) collective-permute-start(bf16[128,256]{1,0:T(8,128)(2,1)S(1)} %get-tuple-element.34), channel_id=1, source_target_pairs={{0,8},{1,5},{2,10},{3,7},{4,12},{5,1},{6,14},{7,3},{8,0},{9,13},{1... | collective-permute-start | bytes 196616 | tf_op jit(solution)/shard_map/ppermute | solution.py:197
  31.5 1.0 %collective-permute-done.10.got_ref = bf16[144,256]{1,0:T(8,128)(2,1)S(1)} collective-permute-done((bf16[144,256]{1,0:T(8,128)(2,1)S(1)}, bf16[144,256]{1,0:T(8,128)(2,1)S(1)}, u32[]{:S(2)}, u32[]{:S(2)}) %collective-permute-start.10) | collective-permute-done | bytes 73760 | tf_op jit(solution)/shard_map/ppermute | solution.py:197
  32.5 0.1 collective-permute-start.11
  32.6 2.7 %collective-permute-done.8.more_ref = bf16[128,256]{1,0:T(8,128)(2,1)S(1)} collective-permute-done((bf16[128,256]{1,0:T(8,128)(2,1)S(1)}, bf16[128,256]{1,0:T(8,128)(2,1)S(1)}, u32[]{:S(2)}, u32[]{:S(2)}) %collective-permute-start.8) | collective-permute-done | bytes 65568 | tf_op jit(solution)/shard_map/ppermute | solution.py:197
  35.3 0.0 collective-permute-done.11.got_ref
  35.3 0.8 %shard_map.111 = (bf16[128,256]{1,0:T(8,128)(2,1)}, bf16[128,256]{1,0:T(8,128)(2,1)}, f32[256,256]{1,0:T(8,128)}, f32[1,256]{1,0:T(1,128)}) custom-call(bf16[128,256]{1,0:T(8,128)(2,1)S(1)} %get-tuple-element.27.act_ref, f32[128,256]{1,0:T(8,128)S(1)} %get-tuple-element.33.feat_ref, bf16[128,256]{1,0:T(8,128)(2,1)S(1)} %collective-permute-done.8.more_ref, ...), custom_call_target="tpu_custom_call" | custom-call | tf_op jit(solution)/shard_map/pallas_call | solution.py:265
  (6 shorter events, 0.1 us)
Async XLA Ops:
  0.6 10.1 %collective-permute-start = (bf16[128,256]{1,0:T(8,128)(2,1)}, bf16[128,256]{1,0:T(8,128)(2,1)S(1)}, u32[]{:S(2)}, u32[]{:S(2)}) collective-permute-start(bf16[128,256]{1,0:T(8,128)(2,1)} %refs_3_.1), channel_id=1, source_target_pairs={{0,12},{4,8},{8,4},{12,0},{1,13},{5,9},{9,5},{13,1},{2,14},{6,10},... | collective-permute-start | bytes 196616 | tf_op jit(solution)/shard_map/ppermute | solution.py:188
  5.7 5.8 %collective-permute-start.1 = (bf16[128,256]{1,0:T(8,128)(2,1)}, bf16[128,256]{1,0:T(8,128)(2,1)S(1)}, u32[]{:S(2)}, u32[]{:S(2)}) collective-permute-start(bf16[128,256]{1,0:T(8,128)(2,1)} %refs_3_.1), channel_id=1, source_target_pairs={{0,8},{4,12},{8,0},{12,4},{1,9},{5,13},{9,1},{13,5},{2,10},{6,14},... | collective-permute-start | bytes 196616 | tf_op jit(solution)/shard_map/ppermute | solution.py:188
  5.7 5.8 %collective-permute-start.2 = (bf16[128,256]{1,0:T(8,128)(2,1)}, bf16[128,256]{1,0:T(8,128)(2,1)S(1)}, u32[]{:S(2)}, u32[]{:S(2)}) collective-permute-start(bf16[128,256]{1,0:T(8,128)(2,1)} %refs_3_.1), channel_id=1, source_target_pairs={{0,4},{4,0},{8,12},{12,8},{1,5},{5,1},{9,13},{13,9},{2,6},{6,2},{1... | collective-permute-start | bytes 196616 | tf_op jit(solution)/shard_map/ppermute | solution.py:188
  6.4 5.2 %collective-permute-start.3 = (bf16[128,256]{1,0:T(8,128)(2,1)}, bf16[128,256]{1,0:T(8,128)(2,1)S(1)}, u32[]{:S(2)}, u32[]{:S(2)}) collective-permute-start(bf16[128,256]{1,0:T(8,128)(2,1)} %refs_2_.1), channel_id=1, source_target_pairs={{0,2},{1,3},{2,0},{3,1},{4,6},{5,7},{6,4},{7,5},{8,10},{9,11},{10,... | collective-permute-start | bytes 196616 | tf_op jit(solution)/shard_map/ppermute | solution.py:188
  8.0 0.7 %copy-start.4 = (s32[4,1,2]{0,2,1:T(2,128)S(1)}, s32[4,1,2]{0,2,1:T(2,128)}, u32[]{:S(2)}) copy-start(s32[4,1,2]{0,2,1:T(2,128)} %param.9) | copy-start | bytes 100
  8.0 0.7 %copy-start.5 = (s32[4,1]{0,1:T(1,128)S(1)}, s32[4,1]{0,1:T(1,128)}, u32[]{:S(2)}) copy-start(s32[4,1]{0,1:T(1,128)} %param.10) | copy-start | bytes 52
  8.7 1.0 %copy-start = (bf16[4,1,2,128,128]{4,3,2,1,0:T(8,128)(2,1)S(1)}, bf16[4,1,2,128,128]{4,3,2,1,0:T(8,128)(2,1)}, u32[]{:S(2)}) copy-start(bf16[4,1,2,128,128]{4,3,2,1,0:T(8,128)(2,1)} %tiles_ref.1) | copy-start | bytes 786436
  9.7 1.9 %copy-start.2 = (bf16[128,256]{1,0:T(8,128)(2,1)S(1)}, bf16[128,256]{1,0:T(8,128)(2,1)}, u32[]{:S(2)}) copy-start(bf16[128,256]{1,0:T(8,128)(2,1)} %refs_3_.1) | copy-start | bytes 196612
  11.9 1.4 %collective-permute-start.4 = (bf16[256,256]{1,0:T(8,128)(2,1)S(1)}, bf16[256,256]{1,0:T(8,128)(2,1)S(1)}, u32[]{:S(2)}, u32[]{:S(2)}) collective-permute-start(bf16[256,256]{1,0:T(8,128)(2,1)S(1)} %get-tuple-element.25), channel_id=1, source_target_pairs={{0,1},{1,0},{2,3},{3,2},{4,5},{5,4},{6,7},{7,6},{8,9},{9,8},{10,11... | collective-permute-start | bytes 393224 | tf_op jit(solution)/shard_map/ppermute | solution.py:188
  13.3 1.6 %copy-start.6 = (bf16[256]{0:T(256)(128)(2,1)S(1)}, bf16[256]{0:T(256)(128)(2,1)}, u32[]{:S(2)}) copy-start(bf16[256]{0:T(256)(128)(2,1)} %param.12) | copy-start | bytes 1540
  13.3 5.7 %copy-start.1 = (bf16[256,256]{1,0:T(8,128)(2,1)S(1)}, bf16[256,256]{1,0:T(8,128)(2,1)}, u32[]{:S(2)}) copy-start(bf16[256,256]{1,0:T(8,128)(2,1)} %w_ref.1) | copy-start | bytes 393220
  13.3 5.7 %copy-start.3 = (bf16[128,256]{1,0:T(8,128)(2,1)S(1)}, bf16[128,256]{1,0:T(8,128)(2,1)}, u32[]{:S(2)}) copy-start(bf16[128,256]{1,0:T(8,128)(2,1)} %refs_2_.1) | copy-start | bytes 196612
  13.3 5.6 %collective-permute-start.5 = (bf16[256,256]{1,0:T(8,128)(2,1)S(1)}, bf16[256,256]{1,0:T(8,128)(2,1)S(1)}, u32[]{:S(2)}, u32[]{:S(2)}) collective-permute-start(bf16[256,256]{1,0:T(8,128)(2,1)S(1)} %shard_map.104.refs_0_), channel_id=1, source_target_pairs={{0,2},{1,3},{2,0},{3,1},{4,6},{5,7},{6,4},{7,5},{8,10},{9,11},{10,... | collective-permute-start | bytes 393224 | tf_op jit(solution)/shard_map/ppermute | solution.py:188
  19.5 1.5 %collective-permute-start.6 = (bf16[400,256]{1,0:T(8,128)(2,1)S(1)}, bf16[400,256]{1,0:T(8,128)(2,1)S(1)}, u32[]{:S(2)}, u32[]{:S(2)}) collective-permute-start(bf16[400,256]{1,0:T(8,128)(2,1)S(1)} %get-tuple-element.30), channel_id=1, source_target_pairs={{0,1},{1,0},{2,3},{3,2},{4,5},{5,4},{6,7},{7,6},{8,9},{9,8},{10,11... | collective-permute-start | bytes 614408 | tf_op jit(solution)/shard_map/ppermute | solution.py:188
  21.0 5.2 %collective-permute-start.9 = (bf16[144,256]{1,0:T(8,128)(2,1)S(1)}, bf16[144,256]{1,0:T(8,128)(2,1)S(1)}, u32[]{:S(2)}, u32[]{:S(2)}) collective-permute-start(bf16[144,256]{1,0:T(8,128)(2,1)S(1)} %shard_map.108.part_ref), channel_id=1, source_target_pairs={{0,4},{1,9},{2,6},{3,11},{4,0},{5,13},{6,2},{7,15},{8,12},{9,1},{1... | collective-permute-start | bytes 221192 | tf_op jit(solution)/shard_map/ppermute | solution.py:197
  22.5 6.9 %collective-permute-start.7 = (bf16[256,256]{1,0:T(8,128)(2,1)S(1)}, bf16[256,256]{1,0:T(8,128)(2,1)S(1)}, u32[]{:S(2)}, u32[]{:S(2)}) collective-permute-start(bf16[256,256]{1,0:T(8,128)(2,1)S(1)} %get-tuple-element.32), channel_id=1, source_target_pairs={{0,4},{1,9},{2,6},{3,11},{4,0},{5,13},{6,2},{7,15},{8,12},{9,1},{1... | collective-permute-start | bytes 393224 | tf_op jit(solution)/shard_map/ppermute | solution.py:197
  26.3 6.2 %collective-permute-start.10 = (bf16[144,256]{1,0:T(8,128)(2,1)S(1)}, bf16[144,256]{1,0:T(8,128)(2,1)S(1)}, u32[]{:S(2)}, u32[]{:S(2)}) collective-permute-start(bf16[144,256]{1,0:T(8,128)(2,1)S(1)} %shard_map.109.part_ref), channel_id=1, source_target_pairs={{0,8},{1,5},{2,10},{3,7},{4,12},{5,1},{6,14},{7,3},{8,0},{9,13},{1... | collective-permute-start | bytes 221192 | tf_op jit(solution)/shard_map/ppermute | solution.py:197
  29.4 5.9 %collective-permute-start.8 = (bf16[128,256]{1,0:T(8,128)(2,1)S(1)}, bf16[128,256]{1,0:T(8,128)(2,1)S(1)}, u32[]{:S(2)}, u32[]{:S(2)}) collective-permute-start(bf16[128,256]{1,0:T(8,128)(2,1)S(1)} %get-tuple-element.34), channel_id=1, source_target_pairs={{0,8},{1,5},{2,10},{3,7},{4,12},{5,1},{6,14},{7,3},{8,0},{9,13},{1... | collective-permute-start | bytes 196616 | tf_op jit(solution)/shard_map/ppermute | solution.py:197
  32.5 2.8 %collective-permute-start.11 = (bf16[128,256]{1,0:T(8,128)(2,1)S(1)}, bf16[128,256]{1,0:T(8,128)(2,1)S(1)}, u32[]{:S(2)}, u32[]{:S(2)}) collective-permute-start(bf16[128,256]{1,0:T(8,128)(2,1)S(1)} %get-tuple-element.37.mine_ref), channel_id=1, source_target_pairs={{0,1},{1,0},{2,3},{3,2},{4,5},{5,4},{6,7},{7,6},{8,9},{9,8},{10,11... | collective-permute-start | bytes 196616 | tf_op jit(solution)/shard_map/ppermute | solution.py:188

commit v10 on v7

--- a/solution.py
+++ b/solution.py
@@ -64,7 +64,8 @@
                 qs = pl.ds(pl.multiple_of(q * tile, tile), tile)
                 ps = pl.ds(pl.multiple_of(p * tile, tile), tile)
                 a_ref[qs, ps] = here
-                rs = pl.ds(pl.multiple_of(reversed_bits(p, n_row) * tile, tile), tile)
+                turned = jnp.where(lax.rem(c, 2) == 0, reversed_bits(p, n_row), p)
+                rs = pl.ds(pl.multiple_of(turned * tile, tile), tile)
                 at_ref[rs, qs] = here.T
 
             return carry
@@ -137,8 +138,8 @@
     return body
 
 
-def line_of(rows):
-    rows = rows.astype(F32)
+def line_of(ref):
+    rows = ref[ref.shape[0] - PAD :, :].astype(F32)
     return rows[0:1] + rows[1:2]
 
 
@@ -148,32 +149,42 @@
     out_ref[...] = (part_ref[...].astype(F32) + got_ref[first:, :].astype(F32)).astype(BF)
 
 
-def backward_kernel(at_ref, mine_ref, got_ref, keep_ref, send_ref):
-    rows, half = mine_ref.shape[0] - PAD, keep_ref.shape[0] - PAD
+def backward_kernel(at_ref, mine_ref, got_ref, keep_ref, stay_ref, pass_ref):
+    rows, first, size = mine_ref.shape[0] - PAD, keep_ref.shape[0], stay_ref.shape[0]
     g = jnp.concatenate([mine_ref[:rows, :], got_ref[:rows, :]], axis=0)
-    send_ref[:half, :] = dot(at_ref[half:, :], g).astype(BF)
-    keep_ref[:half, :] = dot(at_ref[:half, :], g)
-    line = two_rows(line_of(mine_ref[rows:, :]) + line_of(got_ref[rows : rows + PAD, :]))
-    send_ref[half:, :] = line
-    keep_ref[half:, :] = line.astype(F32)
-
-
-def halve_kernel(in_ref, got_ref, keep_ref, send_ref):
-    half, rows = keep_ref.shape[0] - PAD, in_ref.shape[0] - PAD
-    send_ref[:half, :] = (in_ref[half:rows, :] + got_ref[half:rows, :].astype(F32)).astype(BF)
-    keep_ref[:half, :] = in_ref[:half, :] + got_ref[:half, :].astype(F32)
-    line = two_rows(line_of(in_ref[rows:, :]) + line_of(got_ref[rows:, :]))
-    send_ref[half:, :] = line
-    keep_ref[half:, :] = line.astype(F32)
-
-
-def last_kernel(act_ref, feat_ref, more_ref, mine_ref, got_ref, *outs):
-    act_out, feat_out, weight_out, bias_out = outs
-    tile, piece = act_ref.shape[0], mine_ref.shape[0]
+    pass_ref[:size, :] = dot(at_ref[first + size :, :], g).astype(BF)
+    other = got_ref[rows : rows + PAD, :].astype(F32)
+    pass_ref[size:, :] = two_rows(line_of(mine_ref) + (other[0:1] + other[1:2]))
+    stay_ref[...] = dot(at_ref[first : first + size, :], g).astype(BF)
+    keep_ref[...] = dot(at_ref[:first, :], g)
+
+
+def sum_of(refs, firsts, rows):
+    total = None
+    for ref, first in zip(refs, firsts):
+        term = ref[first : first + rows, :].astype(F32)
+        total = term if total is None else total + term
+    return total
+
+
+def range_kernel(firsts, with_line):
+    def body(sent_ref, got_ref, *refs):
+        out_ref = refs[-1]
+        size = out_ref.shape[0] - PAD * with_line
+        out_ref[:size, :] = sum_of(refs[:-1], firsts, size).astype(BF)
+        if with_line:
+            out_ref[size:, :] = two_rows(line_of(sent_ref) + line_of(got_ref))
+
+    return body
+
+
+def last_kernel(act_ref, sent_ref, line_ref, mine_ref, got_ref, *refs):
+    terms, (act_out, feat_out, weight_out, bias_out) = refs[:-4], refs[-4:]
+    piece = mine_ref.shape[0]
     core = lax.rem(lax.axis_index("col"), 2)
     act_out[...] = act_ref[...]
-    feat_out[...] = (feat_ref[:tile, :] + more_ref[:tile, :].astype(F32)).astype(BF)
-    bias_out[...] = line_of(feat_ref[tile:, :]) + line_of(more_ref[tile:, :])
+    feat_out[...] = sum_of(terms, [0] * len(terms), feat_out.shape[0]).astype(BF)
+    bias_out[...] = line_of(sent_ref) + line_of(line_ref)
     mine = pl.multiple_of(core * piece, piece)
     other = pl.multiple_of((1 - core) * piece, piece)
     weight_out[pl.ds(mine, piece), :] = mine_ref[...].astype(F32)
@@ -182,6 +193,15 @@
 
 def swap(x, axis, n, by):
     return lax.ppermute(x, axis, [(i, i ^ by) for i in range(n)])
+
+
+def step(x, n_row, n_col, by):
+    pairs = []
+    for i in range(n_row):
+        for j in range(n_col):
+            bit = by if j % 2 == 0 else n_row // 2 // by
+            pairs.append((i * n_col + j, (i ^ bit) * n_col + j))
+    return lax.ppermute(x, ("row", "col"), pairs)
 
 
 def deal(xs, axis):
@@ -231,22 +251,36 @@
     )(weight, bias_term.reshape(1, width), *sums, *cots)
     got = swap(send, "col", n_col, 1)
     part = call(part_kernel, shape(piece, width), count=2)(part, got)
-    rows = n_row * tile // 2
-    feats, send = call(
-        backward_kernel, (shape(rows + PAD, width, dtype=F32), shape(rows + PAD, width)), count=3
+    live = n_row * tile // 2
+    size = live // 2
+    keep, *sends = call(
+        backward_kernel,
+        (shape(live, width, dtype=F32), shape(size, width), shape(size + PAD, width)),
+        count=3,
     )(at, keep, got)
-    by = 1
-    while by < n_row:
-        part = call(part_kernel, shape(piece, width), count=2)(
-            part, swap(part, "row", n_row, by)
-        )
-        got = swap(send, "row", n_row, by)
+    terms, by = [(keep, 0, live)], 1
+    while True:
+        other = step(part, n_row, n_col, by)
+        sent, gots = sends[-1], [step(x, n_row, n_col, by) for x in reversed(sends)][::-1]
+        terms += [(x, i * size, size) for i, x in enumerate(gots)]
+        part = call(part_kernel, shape(piece, width), count=2)(part, other)
         by *= 2
-        if by < n_row:
-            rows //= 2
-            feats, send = call(
-                halve_kernel, (shape(rows + PAD, width, dtype=F32), shape(rows + PAD, width)), count=2
-            )(feats, got)
+        if by == n_row:
+            break
+        live //= 2
+        size = live if live == tile else live // 2
+        sends = []
+        for first in range(live, 2 * live, size):
+            over = [(x, first - at) for x, at, rows in terms if at <= first < at + rows]
+            last = first + size == 2 * live
+            sends.append(
+                call(
+                    range_kernel([at for _, at in over], last),
+                    shape(size + PAD * last, width),
+                    count=2 + len(over),
+                )(sent, gots[-1], *[x for x, _ in over])
+            )
+        terms = [(x, at, rows) for x, at, rows in terms if at < live]
     act, grad_features, grad_weight, grad_bias = call(
         last_kernel,
         (
@@ -255,8 +289,8 @@
             shape(width, width, dtype=F32),
             shape(1, width, dtype=F32),
         ),
-        count=5,
-    )(act, feats, got, part, swap(part, "col", n_col, 1))
+        count=5 + len(terms),
+    )(act, sent, gots[-1], part, swap(part, "col", n_col, 1), *[x for x, _, _ in terms])
     return act, grad_features, grad_weight, grad_bias.reshape(width)
 
 

time: 38.5 us -> 35.7 us (0.927)
  waiting for transfers between devices: 18.6 us -> 13.9 us
  starting transfers between devices: 14.4 us -> 16.2 us
    ppermute x12 -> x8, waiting for transfers between devices: 18.6 us -> 7.67 us  [swap(): return lax.ppermute(x, axis, [(i, i ^ by) for i in range(n)])]
    ppermute x0 -> x5, starting transfers between devices: none -> 7.02 us  [step(): return lax.ppermute(x, ('row', 'col'), pairs)]
    ppermute x0 -> x5, waiting for transfers between devices: none -> 6.28 us  [step(): return lax.ppermute(x, ('row', 'col'), pairs)]
    ppermute x12 -> x8, starting transfers between devices: 14.4 us -> 9.16 us  [swap(): return lax.ppermute(x, axis, [(i, i ^ by) for i in range(n)])]
  transfers between devices with their start and end apart: 12 -> 13, of which waited for: 8 -> 9; matrix products, arithmetic and copies ran while one was open for 0% -> 0% of each run, Pallas kernels for 3% -> 4%
where the time goes in v10:
time: 35.7 us; the launch traced here: 35.6 us
  starting transfers between devices  16.2 us (45%)
  waiting for transfers between devices  13.9 us (39%)
  Pallas kernels  3.05 us (9%)
  local copies, waits for them, and re-layouts  1.65 us (5%)
  between operations  0.73 us (2%)
    ppermute x8, starting transfers between devices, swap(): return lax.ppermute(x, axis, [(i, i ^ by) for i in range(n)])  9.16 us
    ppermute x8, waiting for transfers between devices, swap(): return lax.ppermute(x, axis, [(i, i ^ by) for i in range(n)])  7.67 us
    ppermute x5, starting transfers between devices, step(): return lax.ppermute(x, ('row', 'col'), pairs)  7.02 us
    ppermute x5, waiting for transfers between devices, step(): return lax.ppermute(x, ('row', 'col'), pairs)  6.28 us
    unnamed x14, local copies, waits for them, and re-layouts  1.64 us
    pallas_call x1, Pallas kernels, shards(): call(dense_kernel(n_chip, n_row), (shape(n_col * tile, n_row * tile), sha...  1.05 us
    pallas_call x1, Pallas kernels, shards(): call(last_kernel, (shape(tile, width), shape(tile, width), shape(width, w...  0.77 us
  transfers between devices with their start and end apart: 13, of which 9 were waited for; matrix products, arithmetic and copies ran while one was open for 0% of the time, Pallas kernels for 4%

profile of v10, /device:TPU:0, one launch (start us, length us, event | category | flops | bytes accessed | tf_op | source)
XLA Modules:
  0.0 35.6 jit_solution(10659469277266559670)
XLA Ops:
  0.6 5.1 %collective-permute-start = (bf16[128,256]{1,0:T(8,128)(2,1)}, bf16[128,256]{1,0:T(8,128)(2,1)S(1)}, u32[]{:S(2)}, u32[]{:S(2)}) collective-permute-start(bf16[128,256]{1,0:T(8,128)(2,1)} %refs_3_.1), channel_id=1, source_target_pairs={{0,12},{4,8},{8,4},{12,0},{1,13},{5,9},{9,5},{13,1},{2,14},{6,10},... | collective-permute-start | bytes 196616 | tf_op jit(solution)/shard_map/ppermute | solution.py:195
  5.7 0.0 collective-permute-start.1
  5.7 0.6 %collective-permute-start.2 = (bf16[128,256]{1,0:T(8,128)(2,1)}, bf16[128,256]{1,0:T(8,128)(2,1)S(1)}, u32[]{:S(2)}, u32[]{:S(2)}) collective-permute-start(bf16[128,256]{1,0:T(8,128)(2,1)} %refs_3_.1), channel_id=1, source_target_pairs={{0,4},{4,0},{8,12},{12,8},{1,5},{5,1},{9,13},{13,9},{2,6},{6,2},{1... | collective-permute-start | bytes 196616 | tf_op jit(solution)/shard_map/ppermute | solution.py:195
  6.4 1.6 %collective-permute-start.3 = (bf16[128,256]{1,0:T(8,128)(2,1)}, bf16[128,256]{1,0:T(8,128)(2,1)S(1)}, u32[]{:S(2)}, u32[]{:S(2)}) collective-permute-start(bf16[128,256]{1,0:T(8,128)(2,1)} %refs_2_.1), channel_id=1, source_target_pairs={{0,2},{1,3},{2,0},{3,1},{4,6},{5,7},{6,4},{7,5},{8,10},{9,11},{10,... | collective-permute-start | bytes 196616 | tf_op jit(solution)/shard_map/ppermute | solution.py:195
  8.0 0.0 copy-start.4
  8.0 0.0 copy-start.5
  8.0 0.7 %copy-done.4 = s32[4,1,2]{0,2,1:T(2,128)S(1)} copy-done((s32[4,1,2]{0,2,1:T(2,128)S(1)}, s32[4,1,2]{0,2,1:T(2,128)}, u32[]{:S(2)}) %copy-start.4) | copy-done | bytes 56
  8.7 0.0 copy-done.5
  8.7 0.0 copy-start
  8.7 0.9 %copy-done = bf16[4,1,2,128,128]{4,3,2,1,0:T(8,128)(2,1)S(1)} copy-done((bf16[4,1,2,128,128]{4,3,2,1,0:T(8,128)(2,1)S(1)}, bf16[4,1,2,128,128]{4,3,2,1,0:T(8,128)(2,1)}, u32[]{:S(2)}) %copy-start) | copy-done | bytes 262168
  9.7 0.0 copy-start.2
  9.7 1.0 %shard_map.102 = (bf16[512,512]{1,0:T(8,128)(2,1)S(1)}, bf16[512,512]{1,0:T(8,128)(2,1)S(1)}) custom-call(s32[1,2,4]{2,1,0:T(2,128)S(1)} %bitcast.3, s32[1,4]{1,0:T(1,128)S(1)} %bitcast.4, bf16[4,1,2,128,128]{4,3,2,1,0:T(8,128)(2,1)S(1)} %copy-done), custom_call_target="tpu_custom_call" | custom-call | tf_op jit(solution)/shard_map/pallas_call | solution.py:224
  10.7 0.0 collective-permute-done.refs_0_
  10.7 0.8 %collective-permute-done.1.refs_1_ = bf16[128,256]{1,0:T(8,128)(2,1)S(1)} collective-permute-done((bf16[128,256]{1,0:T(8,128)(2,1)}, bf16[128,256]{1,0:T(8,128)(2,1)S(1)}, u32[]{:S(2)}, u32[]{:S(2)}) %collective-permute-start.1) | collective-permute-done | bytes 65568 | tf_op jit(solution)/shard_map/ppermute | solution.py:195
  11.6 0.0 collective-permute-done.2.refs_2_
  11.6 0.0 collective-permute-done.3.refs_4_
  11.6 0.0 copy-done.2
  11.6 0.3 shard_map.103
  11.9 0.1 collective-permute-start.4
  12.0 1.3 %collective-permute-done.4.got_ref = bf16[256,256]{1,0:T(8,128)(2,1)S(1)} collective-permute-done((bf16[256,256]{1,0:T(8,128)(2,1)S(1)}, bf16[256,256]{1,0:T(8,128)(2,1)S(1)}, u32[]{:S(2)}, u32[]{:S(2)}) %collective-permute-start.4) | collective-permute-done | bytes 131104 | tf_op jit(solution)/shard_map/ppermute | solution.py:195
  13.3 0.0 copy-start.6
  13.3 0.0 copy-start.1
  13.3 0.0 copy-start.3
  13.3 1.6 %collective-permute-start.5 = (bf16[256,256]{1,0:T(8,128)(2,1)S(1)}, bf16[256,256]{1,0:T(8,128)(2,1)S(1)}, u32[]{:S(2)}, u32[]{:S(2)}) collective-permute-start(bf16[256,256]{1,0:T(8,128)(2,1)S(1)} %shard_map.104.refs_0_), channel_id=1, source_target_pairs={{0,2},{1,3},{2,0},{3,1},{4,6},{5,7},{6,4},{7,5},{8,10},{9,11},{10,... | collective-permute-start | bytes 393224 | tf_op jit(solution)/shard_map/ppermute | solution.py:195
  14.9 0.0 copy-done.6
  14.9 4.1 %collective-permute-done.5.refs_1_ = bf16[256,256]{1,0:T(8,128)(2,1)S(1)} collective-permute-done((bf16[256,256]{1,0:T(8,128)(2,1)S(1)}, bf16[256,256]{1,0:T(8,128)(2,1)S(1)}, u32[]{:S(2)}, u32[]{:S(2)}) %collective-permute-start.5) | collective-permute-done | bytes 131104 | tf_op jit(solution)/shard_map/ppermute | solution.py:195
  18.9 0.0 copy-done.1
  18.9 0.0 copy-done.3
  19.0 0.5 %shard_map.105 = (bf16[128,256]{1,0:T(8,128)(2,1)S(1)}, bf16[272,256]{1,0:T(8,128)(2,1)S(1)}, bf16[128,256]{1,0:T(8,128)(2,1)S(1)}, bf16[400,256]{1,0:T(8,128)(2,1)S(1)}) custom-call(bf16[256,256]{1,0:T(8,128)(2,1)S(1)} %copy-done.1, bf16[1,256]{1,0:T(2,128)(2,1)S(1)} %reshape.14.b_ref, bf16[256,256]{1,0:T(8,128)(2,1)S(1)} %shard_map.104.refs_0_, ...), custom_call_target="tpu_custom_call" | custom-call | tf_op jit(solution)/shard_map/pallas_call | solution.py:237
  19.5 0.1 collective-permute-start.6
  19.5 1.4 %collective-permute-done.6.got_ref = bf16[400,256]{1,0:T(8,128)(2,1)S(1)} collective-permute-done((bf16[400,256]{1,0:T(8,128)(2,1)S(1)}, bf16[400,256]{1,0:T(8,128)(2,1)S(1)}, u32[]{:S(2)}, u32[]{:S(2)}) %collective-permute-start.6) | collective-permute-done | bytes 204832 | tf_op jit(solution)/shard_map/ppermute | solution.py:195
  21.0 1.1 %collective-permute-start.9 = (bf16[128,256]{1,0:T(8,128)(2,1)S(1)}, bf16[128,256]{1,0:T(8,128)(2,1)S(1)}, u32[]{:S(2)}, u32[]{:S(2)}) collective-permute-start(bf16[128,256]{1,0:T(8,128)(2,1)S(1)} %shard_map.108.part_ref), channel_id=1, source_target_pairs={{0,4},{1,9},{2,6},{3,11},{4,0},{5,13},{6,2},{7,15},{8,12},{9,1},{1... | collective-permute-start | bytes 196616 | tf_op jit(solution)/shard_map/ppermute | solution.py:204
  22.2 0.3 shard_map.106
  22.5 1.0 %collective-permute-start.7 = (bf16[144,256]{1,0:T(8,128)(2,1)S(1)}, bf16[144,256]{1,0:T(8,128)(2,1)S(1)}, u32[]{:S(2)}, u32[]{:S(2)}) collective-permute-start(bf16[144,256]{1,0:T(8,128)(2,1)S(1)} %get-tuple-element.28.sent_ref), channel_id=1, source_target_pairs={{0,4},{1,9},{2,6},{3,11},{4,0},{5,13},{6,2},{7,15},{8,12},{9,1},{1... | collective-permute-start | bytes 221192 | tf_op jit(solution)/shard_map/ppermute | solution.py:204
  23.5 2.6 %collective-permute-done.9.got_ref = bf16[128,256]{1,0:T(8,128)(2,1)S(1)} collective-permute-done((bf16[128,256]{1,0:T(8,128)(2,1)S(1)}, bf16[128,256]{1,0:T(8,128)(2,1)S(1)}, u32[]{:S(2)}, u32[]{:S(2)}) %collective-permute-start.9) | collective-permute-done | bytes 65568 | tf_op jit(solution)/shard_map/ppermute | solution.py:204
  26.1 1.2 %collective-permute-start.10 = (bf16[128,256]{1,0:T(8,128)(2,1)S(1)}, bf16[128,256]{1,0:T(8,128)(2,1)S(1)}, u32[]{:S(2)}, u32[]{:S(2)}) collective-permute-start(bf16[128,256]{1,0:T(8,128)(2,1)S(1)} %shard_map.109.part_ref), channel_id=1, source_target_pairs={{0,8},{1,5},{2,10},{3,7},{4,12},{5,1},{6,14},{7,3},{8,0},{9,13},{1... | collective-permute-start | bytes 196616 | tf_op jit(solution)/shard_map/ppermute | solution.py:204
  27.3 0.4 %collective-permute-done.7.got_ref.refs_1_ = bf16[144,256]{1,0:T(8,128)(2,1)S(1)} collective-permute-done((bf16[144,256]{1,0:T(8,128)(2,1)S(1)}, bf16[144,256]{1,0:T(8,128)(2,1)S(1)}, u32[]{:S(2)}, u32[]{:S(2)}) %collective-permute-start.7) | collective-permute-done | bytes 73760 | tf_op jit(solution)/shard_map/ppermute | solution.py:204
  27.7 2.4 %collective-permute-start.8 = (bf16[144,256]{1,0:T(8,128)(2,1)S(1)}, bf16[144,256]{1,0:T(8,128)(2,1)S(1)}, u32[]{:S(2)}, u32[]{:S(2)}) collective-permute-start(bf16[144,256]{1,0:T(8,128)(2,1)S(1)} %shard_map.107.sent_ref), channel_id=1, source_target_pairs={{0,8},{1,5},{2,10},{3,7},{4,12},{5,1},{6,14},{7,3},{8,0},{9,13},{1... | collective-permute-start | bytes 221192 | tf_op jit(solution)/shard_map/ppermute | solution.py:204
  30.1 1.2 %collective-permute-start.12 = (bf16[128,256]{1,0:T(8,128)(2,1)S(1)}, bf16[128,256]{1,0:T(8,128)(2,1)S(1)}, u32[]{:S(2)}, u32[]{:S(2)}) collective-permute-start(bf16[128,256]{1,0:T(8,128)(2,1)S(1)} %get-tuple-element.31), channel_id=1, source_target_pairs={{0,4},{1,9},{2,6},{3,11},{4,0},{5,13},{6,2},{7,15},{8,12},{9,1},{1... | collective-permute-start | bytes 196616 | tf_op jit(solution)/shard_map/ppermute | solution.py:204
  31.3 0.7 %collective-permute-done.10.got_ref = bf16[128,256]{1,0:T(8,128)(2,1)S(1)} collective-permute-done((bf16[128,256]{1,0:T(8,128)(2,1)S(1)}, bf16[128,256]{1,0:T(8,128)(2,1)S(1)}, u32[]{:S(2)}, u32[]{:S(2)}) %collective-permute-start.10) | collective-permute-done | bytes 65568 | tf_op jit(solution)/shard_map/ppermute | solution.py:204
  32.0 0.1 collective-permute-start.11
  32.1 2.4 %collective-permute-done.12.refs_1_ = bf16[128,256]{1,0:T(8,128)(2,1)S(1)} collective-permute-done((bf16[128,256]{1,0:T(8,128)(2,1)S(1)}, bf16[128,256]{1,0:T(8,128)(2,1)S(1)}, u32[]{:S(2)}, u32[]{:S(2)}) %collective-permute-start.12) | collective-permute-done | bytes 65568 | tf_op jit(solution)/shard_map/ppermute | solution.py:204
  34.5 0.3 collective-permute-done.8.line_ref.refs_2_
  34.8 0.0 collective-permute-done.11.got_ref
  34.8 0.8 %shard_map.111 = (bf16[128,256]{1,0:T(8,128)(2,1)}, bf16[128,256]{1,0:T(8,128)(2,1)}, f32[256,256]{1,0:T(8,128)}, f32[1,256]{1,0:T(1,128)}) custom-call(bf16[128,256]{1,0:T(8,128)(2,1)S(1)} %get-tuple-element.24.act_ref, bf16[144,256]{1,0:T(8,128)(2,1)S(1)} %shard_map.107.sent_ref, bf16[144,256]{1,0:T(8,128)(2,1)S(1)} %collective-permute-done.8.line_ref.refs_2_, ...), custom_call_target="tpu_custom_call" | custom-call | tf_op jit(solution)/shard_map/pallas_call | solution.py:284
  (6 shorter events, 0.1 us)
Async XLA Ops:
  0.6 10.1 %collective-permute-start = (bf16[128,256]{1,0:T(8,128)(2,1)}, bf16[128,256]{1,0:T(8,128)(2,1)S(1)}, u32[]{:S(2)}, u32[]{:S(2)}) collective-permute-start(bf16[128,256]{1,0:T(8,128)(2,1)} %refs_3_.1), channel_id=1, source_target_pairs={{0,12},{4,8},{8,4},{12,0},{1,13},{5,9},{9,5},{13,1},{2,14},{6,10},... | collective-permute-start | bytes 196616 | tf_op jit(solution)/shard_map/ppermute | solution.py:195
  5.7 5.8 %collective-permute-start.1 = (bf16[128,256]{1,0:T(8,128)(2,1)}, bf16[128,256]{1,0:T(8,128)(2,1)S(1)}, u32[]{:S(2)}, u32[]{:S(2)}) collective-permute-start(bf16[128,256]{1,0:T(8,128)(2,1)} %refs_3_.1), channel_id=1, source_target_pairs={{0,8},{4,12},{8,0},{12,4},{1,9},{5,13},{9,1},{13,5},{2,10},{6,14},... | collective-permute-start | bytes 196616 | tf_op jit(solution)/shard_map/ppermute | solution.py:195
  5.7 5.8 %collective-permute-start.2 = (bf16[128,256]{1,0:T(8,128)(2,1)}, bf16[128,256]{1,0:T(8,128)(2,1)S(1)}, u32[]{:S(2)}, u32[]{:S(2)}) collective-permute-start(bf16[128,256]{1,0:T(8,128)(2,1)} %refs_3_.1), channel_id=1, source_target_pairs={{0,4},{4,0},{8,12},{12,8},{1,5},{5,1},{9,13},{13,9},{2,6},{6,2},{1... | collective-permute-start | bytes 196616 | tf_op jit(solution)/shard_map/ppermute | solution.py:195
  6.4 5.2 %collective-permute-start.3 = (bf16[128,256]{1,0:T(8,128)(2,1)}, bf16[128,256]{1,0:T(8,128)(2,1)S(1)}, u32[]{:S(2)}, u32[]{:S(2)}) collective-permute-start(bf16[128,256]{1,0:T(8,128)(2,1)} %refs_2_.1), channel_id=1, source_target_pairs={{0,2},{1,3},{2,0},{3,1},{4,6},{5,7},{6,4},{7,5},{8,10},{9,11},{10,... | collective-permute-start | bytes 196616 | tf_op jit(solution)/shard_map/ppermute | solution.py:195
  8.0 0.7 %copy-start.4 = (s32[4,1,2]{0,2,1:T(2,128)S(1)}, s32[4,1,2]{0,2,1:T(2,128)}, u32[]{:S(2)}) copy-start(s32[4,1,2]{0,2,1:T(2,128)} %param.9) | copy-start | bytes 100
  8.0 0.7 %copy-start.5 = (s32[4,1]{0,1:T(1,128)S(1)}, s32[4,1]{0,1:T(1,128)}, u32[]{:S(2)}) copy-start(s32[4,1]{0,1:T(1,128)} %param.10) | copy-start | bytes 52
  8.7 1.0 %copy-start = (bf16[4,1,2,128,128]{4,3,2,1,0:T(8,128)(2,1)S(1)}, bf16[4,1,2,128,128]{4,3,2,1,0:T(8,128)(2,1)}, u32[]{:S(2)}) copy-start(bf16[4,1,2,128,128]{4,3,2,1,0:T(8,128)(2,1)} %tiles_ref.1) | copy-start | bytes 786436
  9.7 1.9 %copy-start.2 = (bf16[128,256]{1,0:T(8,128)(2,1)S(1)}, bf16[128,256]{1,0:T(8,128)(2,1)}, u32[]{:S(2)}) copy-start(bf16[128,256]{1,0:T(8,128)(2,1)} %refs_3_.1) | copy-start | bytes 196612
  11.9 1.4 %collective-permute-start.4 = (bf16[256,256]{1,0:T(8,128)(2,1)S(1)}, bf16[256,256]{1,0:T(8,128)(2,1)S(1)}, u32[]{:S(2)}, u32[]{:S(2)}) collective-permute-start(bf16[256,256]{1,0:T(8,128)(2,1)S(1)} %get-tuple-element.22), channel_id=1, source_target_pairs={{0,1},{1,0},{2,3},{3,2},{4,5},{5,4},{6,7},{7,6},{8,9},{9,8},{10,11... | collective-permute-start | bytes 393224 | tf_op jit(solution)/shard_map/ppermute | solution.py:195
  13.3 1.6 %copy-start.6 = (bf16[256]{0:T(256)(128)(2,1)S(1)}, bf16[256]{0:T(256)(128)(2,1)}, u32[]{:S(2)}) copy-start(bf16[256]{0:T(256)(128)(2,1)} %param.12) | copy-start | bytes 1540
  13.3 5.7 %copy-start.1 = (bf16[256,256]{1,0:T(8,128)(2,1)S(1)}, bf16[256,256]{1,0:T(8,128)(2,1)}, u32[]{:S(2)}) copy-start(bf16[256,256]{1,0:T(8,128)(2,1)} %w_ref.1) | copy-start | bytes 393220
  13.3 5.7 %copy-start.3 = (bf16[128,256]{1,0:T(8,128)(2,1)S(1)}, bf16[128,256]{1,0:T(8,128)(2,1)}, u32[]{:S(2)}) copy-start(bf16[128,256]{1,0:T(8,128)(2,1)} %refs_2_.1) | copy-start | bytes 196612
  13.3 5.6 %collective-permute-start.5 = (bf16[256,256]{1,0:T(8,128)(2,1)S(1)}, bf16[256,256]{1,0:T(8,128)(2,1)S(1)}, u32[]{:S(2)}, u32[]{:S(2)}) collective-permute-start(bf16[256,256]{1,0:T(8,128)(2,1)S(1)} %shard_map.104.refs_0_), channel_id=1, source_target_pairs={{0,2},{1,3},{2,0},{3,1},{4,6},{5,7},{6,4},{7,5},{8,10},{9,11},{10,... | collective-permute-start | bytes 393224 | tf_op jit(solution)/shard_map/ppermute | solution.py:195
  19.5 1.5 %collective-permute-start.6 = (bf16[400,256]{1,0:T(8,128)(2,1)S(1)}, bf16[400,256]{1,0:T(8,128)(2,1)S(1)}, u32[]{:S(2)}, u32[]{:S(2)}) collective-permute-start(bf16[400,256]{1,0:T(8,128)(2,1)S(1)} %get-tuple-element.27), channel_id=1, source_target_pairs={{0,1},{1,0},{2,3},{3,2},{4,5},{5,4},{6,7},{7,6},{8,9},{9,8},{10,11... | collective-permute-start | bytes 614408 | tf_op jit(solution)/shard_map/ppermute | solution.py:195
  21.0 5.0 %collective-permute-start.9 = (bf16[128,256]{1,0:T(8,128)(2,1)S(1)}, bf16[128,256]{1,0:T(8,128)(2,1)S(1)}, u32[]{:S(2)}, u32[]{:S(2)}) collective-permute-start(bf16[128,256]{1,0:T(8,128)(2,1)S(1)} %shard_map.108.part_ref), channel_id=1, source_target_pairs={{0,4},{1,9},{2,6},{3,11},{4,0},{5,13},{6,2},{7,15},{8,12},{9,1},{1... | collective-permute-start | bytes 196616 | tf_op jit(solution)/shard_map/ppermute | solution.py:204
  22.5 5.2 %collective-permute-start.7 = (bf16[144,256]{1,0:T(8,128)(2,1)S(1)}, bf16[144,256]{1,0:T(8,128)(2,1)S(1)}, u32[]{:S(2)}, u32[]{:S(2)}) collective-permute-start(bf16[144,256]{1,0:T(8,128)(2,1)S(1)} %get-tuple-element.28.sent_ref), channel_id=1, source_target_pairs={{0,4},{1,9},{2,6},{3,11},{4,0},{5,13},{6,2},{7,15},{8,12},{9,1},{1... | collective-permute-start | bytes 221192 | tf_op jit(solution)/shard_map/ppermute | solution.py:204
  26.1 5.9 %collective-permute-start.10 = (bf16[128,256]{1,0:T(8,128)(2,1)S(1)}, bf16[128,256]{1,0:T(8,128)(2,1)S(1)}, u32[]{:S(2)}, u32[]{:S(2)}) collective-permute-start(bf16[128,256]{1,0:T(8,128)(2,1)S(1)} %shard_map.109.part_ref), channel_id=1, source_target_pairs={{0,8},{1,5},{2,10},{3,7},{4,12},{5,1},{6,14},{7,3},{8,0},{9,13},{1... | collective-permute-start | bytes 196616 | tf_op jit(solution)/shard_map/ppermute | solution.py:204
  27.7 7.1 %collective-permute-start.8 = (bf16[144,256]{1,0:T(8,128)(2,1)S(1)}, bf16[144,256]{1,0:T(8,128)(2,1)S(1)}, u32[]{:S(2)}, u32[]{:S(2)}) collective-permute-start(bf16[144,256]{1,0:T(8,128)(2,1)S(1)} %shard_map.107.sent_ref), channel_id=1, source_target_pairs={{0,8},{1,5},{2,10},{3,7},{4,12},{5,1},{6,14},{7,3},{8,0},{9,13},{1... | collective-permute-start | bytes 221192 | tf_op jit(solution)/shard_map/ppermute | solution.py:204
  30.1 4.4 %collective-permute-start.12 = (bf16[128,256]{1,0:T(8,128)(2,1)S(1)}, bf16[128,256]{1,0:T(8,128)(2,1)S(1)}, u32[]{:S(2)}, u32[]{:S(2)}) collective-permute-start(bf16[128,256]{1,0:T(8,128)(2,1)S(1)} %get-tuple-element.31), channel_id=1, source_target_pairs={{0,4},{1,9},{2,6},{3,11},{4,0},{5,13},{6,2},{7,15},{8,12},{9,1},{1... | collective-permute-start | bytes 196616 | tf_op jit(solution)/shard_map/ppermute | solution.py:204
  32.0 2.7 %collective-permute-start.11 = (bf16[128,256]{1,0:T(8,128)(2,1)S(1)}, bf16[128,256]{1,0:T(8,128)(2,1)S(1)}, u32[]{:S(2)}, u32[]{:S(2)}) collective-permute-start(bf16[128,256]{1,0:T(8,128)(2,1)S(1)} %shard_map.110.mine_ref), channel_id=1, source_target_pairs={{0,1},{1,0},{2,3},{3,2},{4,5},{5,4},{6,7},{7,6},{8,9},{9,8},{10,11... | collective-permute-start | bytes 196616 | tf_op jit(solution)/shard_map/ppermute | solution.py:195

commit v11 on v10

--- a/solution.py
+++ b/solution.py
@@ -44,13 +44,12 @@
     return total
 
 
-def dense_kernel(n_chip, n_row):
-    def body(cols_ref, cnts_ref, tiles_ref, a_ref, at_ref):
+def dense_kernel(n_chip):
+    def body(cols_ref, cnts_ref, tiles_ref, a_ref):
         trows, _, slots, tile, _ = tiles_ref.shape
         r = lax.axis_index("row")
         c = lax.axis_index("col")
         a_ref[...] = jnp.zeros_like(a_ref)
-        at_ref[...] = jnp.zeros_like(at_ref)
 
         def put(step, carry):
             t = step // slots
@@ -60,17 +59,29 @@
             def _():
                 q = place_of(jnp.bitwise_xor(t, c), n_chip)
                 p = jnp.bitwise_xor(cols_ref[0, k, t], r)
-                here = tiles_ref[t, 0, k]
                 qs = pl.ds(pl.multiple_of(q * tile, tile), tile)
                 ps = pl.ds(pl.multiple_of(p * tile, tile), tile)
-                a_ref[qs, ps] = here
-                turned = jnp.where(lax.rem(c, 2) == 0, reversed_bits(p, n_row), p)
-                rs = pl.ds(pl.multiple_of(turned * tile, tile), tile)
-                at_ref[rs, qs] = here.T
+                a_ref[qs, ps] = tiles_ref[t, 0, k]
 
             return carry
 
         lax.fori_loop(0, trows * slots, put, 0)
+
+    return body
+
+
+def transpose_kernel(n_row):
+    def body(a_ref, at_ref):
+        tile = at_ref.shape[0] // n_row
+        core = lax.rem(lax.axis_index("col"), 2)
+
+        def turn(p, carry):
+            place = jnp.where(core == 0, reversed_bits(p, n_row), p)
+            here = a_ref[:, pl.ds(pl.multiple_of(p * tile, tile), tile)]
+            at_ref[pl.ds(pl.multiple_of(place * tile, tile), tile), :] = here.T
+            return carry
+
+        lax.fori_loop(0, n_row, turn, 0)
 
     return body
 
@@ -101,7 +112,7 @@
 def middle_kernel(n_chip):
     def body(w_ref, b_ref, *refs):
         sums, cots = refs[:n_chip], refs[n_chip : 2 * n_chip]
-        act_ref, keep_ref, part_ref, send_ref, agg_ref, grad_ref, local_ref = refs[2 * n_chip :]
+        act_ref, keep_ref, part_ref, send_ref, agg_ref, grad_ref, local_ref = refs[2 * n_chip + 1 :]
         tile, width = cots[0].shape
         rows, piece = n_chip * tile, width // 2
         c = lax.axis_index("col")
@@ -221,12 +232,14 @@
     half = n_chip * tile
     xs = spread(features, "row", n_row)
     cots = [cotangent] + [swap(cotangent, "col", n_col, 2 * v) for v in range(1, n_chip)]
-    a, at = call(
-        dense_kernel(n_chip, n_row),
-        (shape(n_col * tile, n_row * tile), shape(n_row * tile, n_col * tile)),
+    columns, counts = columns.transpose(1, 2, 0), counts.T
+    a = call(
+        dense_kernel(n_chip),
+        shape(n_col * tile, n_row * tile),
+        count=3,
         smem=2,
-        count=3,
-    )(columns.transpose(1, 2, 0), counts.T, adj_tiles)
+    )(columns, counts, adj_tiles)
+    at = call(transpose_kernel(n_row), shape(n_row * tile, n_col * tile), count=1)(a)
     keep, send, *cots[1:] = call(
         forward_kernel(n_row, n_chip - 1),
         (shape(half, width, dtype=F32), shape(half, width)) + (shape(tile, width),) * (n_chip - 1),
@@ -242,13 +255,13 @@
             shape(piece, width),
             shape(half + PAD + piece, width),
         ),
-        count=2 + 2 * n_chip,
+        count=3 + 2 * n_chip,
         scratch=[
             pltpu.VMEM((half, width), BF),
             pltpu.VMEM((half, width), BF),
             pltpu.VMEM((width, width), F32),
         ],
-    )(weight, bias_term.reshape(1, width), *sums, *cots)
+    )(weight, bias_term.reshape(1, width), *sums, *cots, at)
     got = swap(send, "col", n_col, 1)
     part = call(part_kernel, shape(piece, width), count=2)(part, got)
     live = n_row * tile // 2

time: 35.7 us -> 35.8 us (level)
    pallas_call x1 -> x2, Pallas kernels: 1.05 us -> 1.16 us  [the longest x1 0.81 us: shards(): call(dense_kernel(n_chip), shape(n_col * tile, n_row * tile), count=3, sm...]
where the time goes in v11:
time: 35.8 us; the launch traced here: 35.6 us
  starting transfers between devices  16.2 us (45%)
  waiting for transfers between devices  13.8 us (39%)
  Pallas kernels  3.17 us (9%)
  local copies, waits for them, and re-layouts  1.66 us (5%)
  between operations  0.77 us (2%)
    ppermute x8, starting transfers between devices, swap(): return lax.ppermute(x, axis, [(i, i ^ by) for i in range(n)])  9.16 us
    ppermute x8, waiting for transfers between devices, swap(): return lax.ppermute(x, axis, [(i, i ^ by) for i in range(n)])  7.54 us
    ppermute x5, starting transfers between devices, step(): return lax.ppermute(x, ('row', 'col'), pairs)  7.02 us
    ppermute x5, waiting for transfers between devices, step(): return lax.ppermute(x, ('row', 'col'), pairs)  6.29 us
    unnamed x14, local copies, waits for them, and re-layouts  1.65 us
    pallas_call x1, Pallas kernels, shards(): call(dense_kernel(n_chip), shape(n_col * tile, n_row * tile), count=3, sm...  0.81 us
    pallas_call x1, Pallas kernels, shards(): call(last_kernel, (shape(tile, width), shape(tile, width), shape(width, w...  0.77 us
  transfers between devices with their start and end apart: 13, of which 9 were waited for; matrix products, arithmetic and copies ran while one was open for 0% of the time, Pallas kernels for 4%

profile of v11, /device:TPU:0, one launch (start us, length us, event | category | flops | bytes accessed | tf_op | source)
XLA Modules:
  0.0 35.6 jit_solution(2613687727433244571)
XLA Ops:
  0.6 5.1 %collective-permute-start = (bf16[128,256]{1,0:T(8,128)(2,1)}, bf16[128,256]{1,0:T(8,128)(2,1)S(1)}, u32[]{:S(2)}, u32[]{:S(2)}) collective-permute-start(bf16[128,256]{1,0:T(8,128)(2,1)} %refs_3_.1), channel_id=1, source_target_pairs={{0,12},{4,8},{8,4},{12,0},{1,13},{5,9},{9,5},{13,1},{2,14},{6,10},... | collective-permute-start | bytes 196616 | tf_op jit(solution)/shard_map/ppermute | solution.py:206
  5.7 0.0 collective-permute-start.1
  5.7 0.6 %collective-permute-start.2 = (bf16[128,256]{1,0:T(8,128)(2,1)}, bf16[128,256]{1,0:T(8,128)(2,1)S(1)}, u32[]{:S(2)}, u32[]{:S(2)}) collective-permute-start(bf16[128,256]{1,0:T(8,128)(2,1)} %refs_3_.1), channel_id=1, source_target_pairs={{0,4},{4,0},{8,12},{12,8},{1,5},{5,1},{9,13},{13,9},{2,6},{6,2},{1... | collective-permute-start | bytes 196616 | tf_op jit(solution)/shard_map/ppermute | solution.py:206
  6.4 1.6 %collective-permute-start.3 = (bf16[128,256]{1,0:T(8,128)(2,1)}, bf16[128,256]{1,0:T(8,128)(2,1)S(1)}, u32[]{:S(2)}, u32[]{:S(2)}) collective-permute-start(bf16[128,256]{1,0:T(8,128)(2,1)} %refs_2_.1), channel_id=1, source_target_pairs={{0,2},{1,3},{2,0},{3,1},{4,6},{5,7},{6,4},{7,5},{8,10},{9,11},{10,... | collective-permute-start | bytes 196616 | tf_op jit(solution)/shard_map/ppermute | solution.py:206
  8.0 0.0 copy-start.4
  8.0 0.0 copy-start.5
  8.0 0.7 %copy-done.4 = s32[4,1,2]{0,2,1:T(2,128)S(1)} copy-done((s32[4,1,2]{0,2,1:T(2,128)S(1)}, s32[4,1,2]{0,2,1:T(2,128)}, u32[]{:S(2)}) %copy-start.4) | copy-done | bytes 56
  8.7 0.0 copy-done.5
  8.7 0.0 copy-start
  8.7 0.9 %copy-done = bf16[4,1,2,128,128]{4,3,2,1,0:T(8,128)(2,1)S(1)} copy-done((bf16[4,1,2,128,128]{4,3,2,1,0:T(8,128)(2,1)S(1)}, bf16[4,1,2,128,128]{4,3,2,1,0:T(8,128)(2,1)}, u32[]{:S(2)}) %copy-start) | copy-done | bytes 262168
  9.7 0.0 copy-start.3
  9.7 0.8 %shard_map.102.a_ref = bf16[512,512]{1,0:T(8,128)(2,1)S(1)} custom-call(s32[1,2,4]{2,1,0:T(2,128)S(1)} %bitcast.3, s32[1,4]{1,0:T(1,128)S(1)} %bitcast.4, bf16[4,1,2,128,128]{4,3,2,1,0:T(8,128)(2,1)S(1)} %copy-done), custom_call_target="tpu_custom_call" | custom-call | tf_op jit(solution)/shard_map/pallas_call | solution.py:236
  10.5 0.0 collective-permute-done.refs_0_
  10.5 1.1 %collective-permute-done.1.refs_1_ = bf16[128,256]{1,0:T(8,128)(2,1)S(1)} collective-permute-done((bf16[128,256]{1,0:T(8,128)(2,1)}, bf16[128,256]{1,0:T(8,128)(2,1)S(1)}, u32[]{:S(2)}, u32[]{:S(2)}) %collective-permute-start.1) | collective-permute-done | bytes 65568 | tf_op jit(solution)/shard_map/ppermute | solution.py:206
  11.6 0.0 collective-permute-done.2.refs_2_
  11.6 0.0 collective-permute-done.3.refs_4_
  11.6 0.0 copy-done.3
  11.6 0.3 shard_map.103
  11.9 0.1 collective-permute-start.4
  12.0 1.3 %collective-permute-done.4.got_ref = bf16[256,256]{1,0:T(8,128)(2,1)S(1)} collective-permute-done((bf16[256,256]{1,0:T(8,128)(2,1)S(1)}, bf16[256,256]{1,0:T(8,128)(2,1)S(1)}, u32[]{:S(2)}, u32[]{:S(2)}) %collective-permute-start.4) | collective-permute-done | bytes 131104 | tf_op jit(solution)/shard_map/ppermute | solution.py:206
  13.3 0.0 copy-start.6
  13.3 0.0 copy-start.1
  13.3 0.0 copy-start.2
  13.4 1.6 %collective-permute-start.5 = (bf16[256,256]{1,0:T(8,128)(2,1)S(1)}, bf16[256,256]{1,0:T(8,128)(2,1)S(1)}, u32[]{:S(2)}, u32[]{:S(2)}) collective-permute-start(bf16[256,256]{1,0:T(8,128)(2,1)S(1)} %shard_map.104.refs_0_), channel_id=1, source_target_pairs={{0,2},{1,3},{2,0},{3,1},{4,6},{5,7},{6,4},{7,5},{8,10},{9,11},{10,... | collective-permute-start | bytes 393224 | tf_op jit(solution)/shard_map/ppermute | solution.py:206
  14.9 0.3 shard_map.105.refs_4_.at_ref
  15.3 0.0 copy-done.6
  15.3 3.7 %collective-permute-done.5.refs_1_ = bf16[256,256]{1,0:T(8,128)(2,1)S(1)} collective-permute-done((bf16[256,256]{1,0:T(8,128)(2,1)S(1)}, bf16[256,256]{1,0:T(8,128)(2,1)S(1)}, u32[]{:S(2)}, u32[]{:S(2)}) %collective-permute-start.5) | collective-permute-done | bytes 131104 | tf_op jit(solution)/shard_map/ppermute | solution.py:206
  19.0 0.0 copy-done.1
  19.0 0.0 copy-done.2
  19.0 0.5 %shard_map.106 = (bf16[128,256]{1,0:T(8,128)(2,1)S(1)}, bf16[272,256]{1,0:T(8,128)(2,1)S(1)}, bf16[128,256]{1,0:T(8,128)(2,1)S(1)}, bf16[400,256]{1,0:T(8,128)(2,1)S(1)}) custom-call(bf16[256,256]{1,0:T(8,128)(2,1)S(1)} %copy-done.1, bf16[1,256]{1,0:T(2,128)(2,1)S(1)} %reshape.14.b_ref, bf16[256,256]{1,0:T(8,128)(2,1)S(1)} %shard_map.104.refs_0_, ...), custom_call_target="tpu_custom_call" | custom-call | tf_op jit(solution)/shard_map/pallas_call | solution.py:250
  19.5 0.1 collective-permute-start.6
  19.6 1.4 %collective-permute-done.6.got_ref = bf16[400,256]{1,0:T(8,128)(2,1)S(1)} collective-permute-done((bf16[400,256]{1,0:T(8,128)(2,1)S(1)}, bf16[400,256]{1,0:T(8,128)(2,1)S(1)}, u32[]{:S(2)}, u32[]{:S(2)}) %collective-permute-start.6) | collective-permute-done | bytes 204832 | tf_op jit(solution)/shard_map/ppermute | solution.py:206
  21.0 1.1 %collective-permute-start.9 = (bf16[128,256]{1,0:T(8,128)(2,1)S(1)}, bf16[128,256]{1,0:T(8,128)(2,1)S(1)}, u32[]{:S(2)}, u32[]{:S(2)}) collective-permute-start(bf16[128,256]{1,0:T(8,128)(2,1)S(1)} %shard_map.109.part_ref), channel_id=1, source_target_pairs={{0,4},{1,9},{2,6},{3,11},{4,0},{5,13},{6,2},{7,15},{8,12},{9,1},{1... | collective-permute-start | bytes 196616 | tf_op jit(solution)/shard_map/ppermute | solution.py:215
  22.2 0.3 shard_map.107
  22.5 1.0 %collective-permute-start.7 = (bf16[144,256]{1,0:T(8,128)(2,1)S(1)}, bf16[144,256]{1,0:T(8,128)(2,1)S(1)}, u32[]{:S(2)}, u32[]{:S(2)}) collective-permute-start(bf16[144,256]{1,0:T(8,128)(2,1)S(1)} %get-tuple-element.24.sent_ref), channel_id=1, source_target_pairs={{0,4},{1,9},{2,6},{3,11},{4,0},{5,13},{6,2},{7,15},{8,12},{9,1},{1... | collective-permute-start | bytes 221192 | tf_op jit(solution)/shard_map/ppermute | solution.py:215
  23.5 2.6 %collective-permute-done.9.got_ref = bf16[128,256]{1,0:T(8,128)(2,1)S(1)} collective-permute-done((bf16[128,256]{1,0:T(8,128)(2,1)S(1)}, bf16[128,256]{1,0:T(8,128)(2,1)S(1)}, u32[]{:S(2)}, u32[]{:S(2)}) %collective-permute-start.9) | collective-permute-done | bytes 65568 | tf_op jit(solution)/shard_map/ppermute | solution.py:215
  26.1 1.2 %collective-permute-start.10 = (bf16[128,256]{1,0:T(8,128)(2,1)S(1)}, bf16[128,256]{1,0:T(8,128)(2,1)S(1)}, u32[]{:S(2)}, u32[]{:S(2)}) collective-permute-start(bf16[128,256]{1,0:T(8,128)(2,1)S(1)} %shard_map.110.part_ref), channel_id=1, source_target_pairs={{0,8},{1,5},{2,10},{3,7},{4,12},{5,1},{6,14},{7,3},{8,0},{9,13},{1... | collective-permute-start | bytes 196616 | tf_op jit(solution)/shard_map/ppermute | solution.py:215
  27.3 0.4 %collective-permute-done.7.got_ref.refs_1_ = bf16[144,256]{1,0:T(8,128)(2,1)S(1)} collective-permute-done((bf16[144,256]{1,0:T(8,128)(2,1)S(1)}, bf16[144,256]{1,0:T(8,128)(2,1)S(1)}, u32[]{:S(2)}, u32[]{:S(2)}) %collective-permute-start.7) | collective-permute-done | bytes 73760 | tf_op jit(solution)/shard_map/ppermute | solution.py:215
  27.7 2.4 %collective-permute-start.8 = (bf16[144,256]{1,0:T(8,128)(2,1)S(1)}, bf16[144,256]{1,0:T(8,128)(2,1)S(1)}, u32[]{:S(2)}, u32[]{:S(2)}) collective-permute-start(bf16[144,256]{1,0:T(8,128)(2,1)S(1)} %shard_map.108.sent_ref), channel_id=1, source_target_pairs={{0,8},{1,5},{2,10},{3,7},{4,12},{5,1},{6,14},{7,3},{8,0},{9,13},{1... | collective-permute-start | bytes 221192 | tf_op jit(solution)/shard_map/ppermute | solution.py:215
  30.1 1.2 %collective-permute-start.12 = (bf16[128,256]{1,0:T(8,128)(2,1)S(1)}, bf16[128,256]{1,0:T(8,128)(2,1)S(1)}, u32[]{:S(2)}, u32[]{:S(2)}) collective-permute-start(bf16[128,256]{1,0:T(8,128)(2,1)S(1)} %get-tuple-element.27), channel_id=1, source_target_pairs={{0,4},{1,9},{2,6},{3,11},{4,0},{5,13},{6,2},{7,15},{8,12},{9,1},{1... | collective-permute-start | bytes 196616 | tf_op jit(solution)/shard_map/ppermute | solution.py:215
  31.4 0.7 %collective-permute-done.10.got_ref = bf16[128,256]{1,0:T(8,128)(2,1)S(1)} collective-permute-done((bf16[128,256]{1,0:T(8,128)(2,1)S(1)}, bf16[128,256]{1,0:T(8,128)(2,1)S(1)}, u32[]{:S(2)}, u32[]{:S(2)}) %collective-permute-start.10) | collective-permute-done | bytes 65568 | tf_op jit(solution)/shard_map/ppermute | solution.py:215
  32.1 0.1 collective-permute-start.11
  32.1 2.4 %collective-permute-done.12.refs_1_ = bf16[128,256]{1,0:T(8,128)(2,1)S(1)} collective-permute-done((bf16[128,256]{1,0:T(8,128)(2,1)S(1)}, bf16[128,256]{1,0:T(8,128)(2,1)S(1)}, u32[]{:S(2)}, u32[]{:S(2)}) %collective-permute-start.12) | collective-permute-done | bytes 65568 | tf_op jit(solution)/shard_map/ppermute | solution.py:215
  34.6 0.3 collective-permute-done.8.line_ref.refs_2_
  34.8 0.0 collective-permute-done.11.got_ref
  34.8 0.8 %shard_map.112 = (bf16[128,256]{1,0:T(8,128)(2,1)}, bf16[128,256]{1,0:T(8,128)(2,1)}, f32[256,256]{1,0:T(8,128)}, f32[1,256]{1,0:T(1,128)}) custom-call(bf16[128,256]{1,0:T(8,128)(2,1)S(1)} %get-tuple-element.21.act_ref, bf16[144,256]{1,0:T(8,128)(2,1)S(1)} %shard_map.108.sent_ref, bf16[144,256]{1,0:T(8,128)(2,1)S(1)} %collective-permute-done.8.line_ref.refs_2_, ...), custom_call_target="tpu_custom_call" | custom-call | tf_op jit(solution)/shard_map/pallas_call | solution.py:297
  (6 shorter events, 0.1 us)
Async XLA Ops:
  0.6 9.8 %collective-permute-start = (bf16[128,256]{1,0:T(8,128)(2,1)}, bf16[128,256]{1,0:T(8,128)(2,1)S(1)}, u32[]{:S(2)}, u32[]{:S(2)}) collective-permute-start(bf16[128,256]{1,0:T(8,128)(2,1)} %refs_3_.1), channel_id=1, source_target_pairs={{0,12},{4,8},{8,4},{12,0},{1,13},{5,9},{9,5},{13,1},{2,14},{6,10},... | collective-permute-start | bytes 196616 | tf_op jit(solution)/shard_map/ppermute | solution.py:206
  5.7 5.8 %collective-permute-start.1 = (bf16[128,256]{1,0:T(8,128)(2,1)}, bf16[128,256]{1,0:T(8,128)(2,1)S(1)}, u32[]{:S(2)}, u32[]{:S(2)}) collective-permute-start(bf16[128,256]{1,0:T(8,128)(2,1)} %refs_3_.1), channel_id=1, source_target_pairs={{0,8},{4,12},{8,0},{12,4},{1,9},{5,13},{9,1},{13,5},{2,10},{6,14},... | collective-permute-start | bytes 196616 | tf_op jit(solution)/shard_map/ppermute | solution.py:206
  5.7 5.8 %collective-permute-start.2 = (bf16[128,256]{1,0:T(8,128)(2,1)}, bf16[128,256]{1,0:T(8,128)(2,1)S(1)}, u32[]{:S(2)}, u32[]{:S(2)}) collective-permute-start(bf16[128,256]{1,0:T(8,128)(2,1)} %refs_3_.1), channel_id=1, source_target_pairs={{0,4},{4,0},{8,12},{12,8},{1,5},{5,1},{9,13},{13,9},{2,6},{6,2},{1... | collective-permute-start | bytes 196616 | tf_op jit(solution)/shard_map/ppermute | solution.py:206
  6.4 5.2 %collective-permute-start.3 = (bf16[128,256]{1,0:T(8,128)(2,1)}, bf16[128,256]{1,0:T(8,128)(2,1)S(1)}, u32[]{:S(2)}, u32[]{:S(2)}) collective-permute-start(bf16[128,256]{1,0:T(8,128)(2,1)} %refs_2_.1), channel_id=1, source_target_pairs={{0,2},{1,3},{2,0},{3,1},{4,6},{5,7},{6,4},{7,5},{8,10},{9,11},{10,... | collective-permute-start | bytes 196616 | tf_op jit(solution)/shard_map/ppermute | solution.py:206
  8.0 0.7 %copy-start.4 = (s32[4,1,2]{0,2,1:T(2,128)S(1)}, s32[4,1,2]{0,2,1:T(2,128)}, u32[]{:S(2)}) copy-start(s32[4,1,2]{0,2,1:T(2,128)} %param.9) | copy-start | bytes 100
  8.0 0.7 %copy-start.5 = (s32[4,1]{0,1:T(1,128)S(1)}, s32[4,1]{0,1:T(1,128)}, u32[]{:S(2)}) copy-start(s32[4,1]{0,1:T(1,128)} %param.10) | copy-start | bytes 52
  8.7 1.0 %copy-start = (bf16[4,1,2,128,128]{4,3,2,1,0:T(8,128)(2,1)S(1)}, bf16[4,1,2,128,128]{4,3,2,1,0:T(8,128)(2,1)}, u32[]{:S(2)}) copy-start(bf16[4,1,2,128,128]{4,3,2,1,0:T(8,128)(2,1)} %tiles_ref.1) | copy-start | bytes 786436
  9.7 1.9 %copy-start.3 = (bf16[128,256]{1,0:T(8,128)(2,1)S(1)}, bf16[128,256]{1,0:T(8,128)(2,1)}, u32[]{:S(2)}) copy-start(bf16[128,256]{1,0:T(8,128)(2,1)} %refs_3_.1) | copy-start | bytes 196612
  11.9 1.4 %collective-permute-start.4 = (bf16[256,256]{1,0:T(8,128)(2,1)S(1)}, bf16[256,256]{1,0:T(8,128)(2,1)S(1)}, u32[]{:S(2)}, u32[]{:S(2)}) collective-permute-start(bf16[256,256]{1,0:T(8,128)(2,1)S(1)} %get-tuple-element.19), channel_id=1, source_target_pairs={{0,1},{1,0},{2,3},{3,2},{4,5},{5,4},{6,7},{7,6},{8,9},{9,8},{10,11... | collective-permute-start | bytes 393224 | tf_op jit(solution)/shard_map/ppermute | solution.py:206
  13.3 1.9 %copy-start.6 = (bf16[256]{0:T(256)(128)(2,1)S(1)}, bf16[256]{0:T(256)(128)(2,1)}, u32[]{:S(2)}) copy-start(bf16[256]{0:T(256)(128)(2,1)} %param.12) | copy-start | bytes 1540
  13.3 5.6 %copy-start.1 = (bf16[256,256]{1,0:T(8,128)(2,1)S(1)}, bf16[256,256]{1,0:T(8,128)(2,1)}, u32[]{:S(2)}) copy-start(bf16[256,256]{1,0:T(8,128)(2,1)} %w_ref.1) | copy-start | bytes 393220
  13.3 5.6 %copy-start.2 = (bf16[128,256]{1,0:T(8,128)(2,1)S(1)}, bf16[128,256]{1,0:T(8,128)(2,1)}, u32[]{:S(2)}) copy-start(bf16[128,256]{1,0:T(8,128)(2,1)} %refs_2_.1) | copy-start | bytes 196612
  13.4 5.6 %collective-permute-start.5 = (bf16[256,256]{1,0:T(8,128)(2,1)S(1)}, bf16[256,256]{1,0:T(8,128)(2,1)S(1)}, u32[]{:S(2)}, u32[]{:S(2)}) collective-permute-start(bf16[256,256]{1,0:T(8,128)(2,1)S(1)} %shard_map.104.refs_0_), channel_id=1, source_target_pairs={{0,2},{1,3},{2,0},{3,1},{4,6},{5,7},{6,4},{7,5},{8,10},{9,11},{10,... | collective-permute-start | bytes 393224 | tf_op jit(solution)/shard_map/ppermute | solution.py:206
  19.5 1.5 %collective-permute-start.6 = (bf16[400,256]{1,0:T(8,128)(2,1)S(1)}, bf16[400,256]{1,0:T(8,128)(2,1)S(1)}, u32[]{:S(2)}, u32[]{:S(2)}) collective-permute-start(bf16[400,256]{1,0:T(8,128)(2,1)S(1)} %get-tuple-element.23), channel_id=1, source_target_pairs={{0,1},{1,0},{2,3},{3,2},{4,5},{5,4},{6,7},{7,6},{8,9},{9,8},{10,11... | collective-permute-start | bytes 614408 | tf_op jit(solution)/shard_map/ppermute | solution.py:206
  21.0 5.0 %collective-permute-start.9 = (bf16[128,256]{1,0:T(8,128)(2,1)S(1)}, bf16[128,256]{1,0:T(8,128)(2,1)S(1)}, u32[]{:S(2)}, u32[]{:S(2)}) collective-permute-start(bf16[128,256]{1,0:T(8,128)(2,1)S(1)} %shard_map.109.part_ref), channel_id=1, source_target_pairs={{0,4},{1,9},{2,6},{3,11},{4,0},{5,13},{6,2},{7,15},{8,12},{9,1},{1... | collective-permute-start | bytes 196616 | tf_op jit(solution)/shard_map/ppermute | solution.py:215
  22.5 5.2 %collective-permute-start.7 = (bf16[144,256]{1,0:T(8,128)(2,1)S(1)}, bf16[144,256]{1,0:T(8,128)(2,1)S(1)}, u32[]{:S(2)}, u32[]{:S(2)}) collective-permute-start(bf16[144,256]{1,0:T(8,128)(2,1)S(1)} %get-tuple-element.24.sent_ref), channel_id=1, source_target_pairs={{0,4},{1,9},{2,6},{3,11},{4,0},{5,13},{6,2},{7,15},{8,12},{9,1},{1... | collective-permute-start | bytes 221192 | tf_op jit(solution)/shard_map/ppermute | solution.py:215
  26.1 5.9 %collective-permute-start.10 = (bf16[128,256]{1,0:T(8,128)(2,1)S(1)}, bf16[128,256]{1,0:T(8,128)(2,1)S(1)}, u32[]{:S(2)}, u32[]{:S(2)}) collective-permute-start(bf16[128,256]{1,0:T(8,128)(2,1)S(1)} %shard_map.110.part_ref), channel_id=1, source_target_pairs={{0,8},{1,5},{2,10},{3,7},{4,12},{5,1},{6,14},{7,3},{8,0},{9,13},{1... | collective-permute-start | bytes 196616 | tf_op jit(solution)/shard_map/ppermute | solution.py:215
  27.7 7.1 %collective-permute-start.8 = (bf16[144,256]{1,0:T(8,128)(2,1)S(1)}, bf16[144,256]{1,0:T(8,128)(2,1)S(1)}, u32[]{:S(2)}, u32[]{:S(2)}) collective-permute-start(bf16[144,256]{1,0:T(8,128)(2,1)S(1)} %shard_map.108.sent_ref), channel_id=1, source_target_pairs={{0,8},{1,5},{2,10},{3,7},{4,12},{5,1},{6,14},{7,3},{8,0},{9,13},{1... | collective-permute-start | bytes 221192 | tf_op jit(solution)/shard_map/ppermute | solution.py:215
  30.1 4.4 %collective-permute-start.12 = (bf16[128,256]{1,0:T(8,128)(2,1)S(1)}, bf16[128,256]{1,0:T(8,128)(2,1)S(1)}, u32[]{:S(2)}, u32[]{:S(2)}) collective-permute-start(bf16[128,256]{1,0:T(8,128)(2,1)S(1)} %get-tuple-element.27), channel_id=1, source_target_pairs={{0,4},{1,9},{2,6},{3,11},{4,0},{5,13},{6,2},{7,15},{8,12},{9,1},{1... | collective-permute-start | bytes 196616 | tf_op jit(solution)/shard_map/ppermute | solution.py:215
  32.1 2.8 %collective-permute-start.11 = (bf16[128,256]{1,0:T(8,128)(2,1)S(1)}, bf16[128,256]{1,0:T(8,128)(2,1)S(1)}, u32[]{:S(2)}, u32[]{:S(2)}) collective-permute-start(bf16[128,256]{1,0:T(8,128)(2,1)S(1)} %shard_map.111.mine_ref), channel_id=1, source_target_pairs={{0,1},{1,0},{2,3},{3,2},{4,5},{5,4},{6,7},{7,6},{8,9},{9,8},{10,11... | collective-permute-start | bytes 196616 | tf_op jit(solution)/shard_map/ppermute | solution.py:206

commit v12 on v11

--- a/solution.py
+++ b/solution.py
@@ -179,7 +179,7 @@
 
 
 def range_kernel(firsts, with_line):
-    def body(sent_ref, got_ref, *refs):
+    def body(_, sent_ref, got_ref, *refs):
         out_ref = refs[-1]
         size = out_ref.shape[0] - PAD * with_line
         out_ref[:size, :] = sum_of(refs[:-1], firsts, size).astype(BF)
@@ -290,8 +290,8 @@
                 call(
                     range_kernel([at for _, at in over], last),
                     shape(size + PAD * last, width),
-                    count=2 + len(over),
-                )(sent, gots[-1], *[x for x, _ in over])
+                    count=3 + len(over),
+                )(gots[0], sent, gots[-1], *[x for x, _ in over])
             )
         terms = [(x, at, rows) for x, at, rows in terms if at < live]
     act, grad_features, grad_weight, grad_bias = call(

time: 35.8 us -> 36.6 us (1.022)
  waiting for transfers between devices: 13.8 us -> 15.1 us
  starting transfers between devices: 16.2 us -> 15.8 us
    ppermute x5, waiting for transfers between devices: 6.29 us -> 7.55 us  [step(): return lax.ppermute(x, ('row', 'col'), pairs)]
    ppermute x5, starting transfers between devices: 7.02 us -> 6.62 us  [step(): return lax.ppermute(x, ('row', 'col'), pairs)]
  transfers between devices with their start and end apart: 13 -> 13, of which waited for: 9 -> 7; matrix products, arithmetic and copies ran while one was open for 0% -> 0% of each run, Pallas kernels for 4% -> 4%
where the time goes in v12:
time: 36.6 us; the launch traced here: 36.5 us
  starting transfers between devices  15.8 us (43%)
  waiting for transfers between devices  15.1 us (41%)
  Pallas kernels  3.14 us (9%)
  local copies, waits for them, and re-layouts  1.66 us (5%)
  between operations  0.77 us (2%)
    ppermute x8, starting transfers between devices, swap(): return lax.ppermute(x, axis, [(i, i ^ by) for i in range(n)])  9.16 us
    ppermute x8, waiting for transfers between devices, swap(): return lax.ppermute(x, axis, [(i, i ^ by) for i in range(n)])  7.56 us
    ppermute x5, waiting for transfers between devices, step(): return lax.ppermute(x, ('row', 'col'), pairs)  7.55 us
    ppermute x5, starting transfers between devices, step(): return lax.ppermute(x, ('row', 'col'), pairs)  6.62 us
    unnamed x14, local copies, waits for them, and re-layouts  1.65 us
    pallas_call x1, Pallas kernels, shards(): call(dense_kernel(n_chip), shape(n_col * tile, n_row * tile), count=3, sm...  0.79 us
    pallas_call x1, Pallas kernels, shards(): call(last_kernel, (shape(tile, width), shape(tile, width), shape(width, w...  0.77 us
  transfers between devices with their start and end apart: 13, of which 7 were waited for; matrix products, arithmetic and copies ran while one was open for 0% of the time, Pallas kernels for 4%

profile of v12, /device:TPU:0, one launch (start us, length us, event | category | flops | bytes accessed | tf_op | source)
XLA Modules:
  0.0 36.5 jit_solution(7676785616624919957)
XLA Ops:
  0.6 5.1 %collective-permute-start = (bf16[128,256]{1,0:T(8,128)(2,1)}, bf16[128,256]{1,0:T(8,128)(2,1)S(1)}, u32[]{:S(2)}, u32[]{:S(2)}) collective-permute-start(bf16[128,256]{1,0:T(8,128)(2,1)} %refs_3_.1), channel_id=1, source_target_pairs={{0,12},{4,8},{8,4},{12,0},{1,13},{5,9},{9,5},{13,1},{2,14},{6,10},... | collective-permute-start | bytes 196616 | tf_op jit(solution)/shard_map/ppermute | solution.py:206
  5.7 0.0 collective-permute-start.1
  5.7 0.6 %collective-permute-start.2 = (bf16[128,256]{1,0:T(8,128)(2,1)}, bf16[128,256]{1,0:T(8,128)(2,1)S(1)}, u32[]{:S(2)}, u32[]{:S(2)}) collective-permute-start(bf16[128,256]{1,0:T(8,128)(2,1)} %refs_3_.1), channel_id=1, source_target_pairs={{0,4},{4,0},{8,12},{12,8},{1,5},{5,1},{9,13},{13,9},{2,6},{6,2},{1... | collective-permute-start | bytes 196616 | tf_op jit(solution)/shard_map/ppermute | solution.py:206
  6.4 1.6 %collective-permute-start.3 = (bf16[128,256]{1,0:T(8,128)(2,1)}, bf16[128,256]{1,0:T(8,128)(2,1)S(1)}, u32[]{:S(2)}, u32[]{:S(2)}) collective-permute-start(bf16[128,256]{1,0:T(8,128)(2,1)} %refs_2_.1), channel_id=1, source_target_pairs={{0,2},{1,3},{2,0},{3,1},{4,6},{5,7},{6,4},{7,5},{8,10},{9,11},{10,... | collective-permute-start | bytes 196616 | tf_op jit(solution)/shard_map/ppermute | solution.py:206
  8.0 0.0 copy-start.4
  8.0 0.0 copy-start.5
  8.0 0.7 %copy-done.4 = s32[4,1,2]{0,2,1:T(2,128)S(1)} copy-done((s32[4,1,2]{0,2,1:T(2,128)S(1)}, s32[4,1,2]{0,2,1:T(2,128)}, u32[]{:S(2)}) %copy-start.4) | copy-done | bytes 56
  8.7 0.0 copy-done.5
  8.7 0.0 copy-start
  8.7 0.9 %copy-done = bf16[4,1,2,128,128]{4,3,2,1,0:T(8,128)(2,1)S(1)} copy-done((bf16[4,1,2,128,128]{4,3,2,1,0:T(8,128)(2,1)S(1)}, bf16[4,1,2,128,128]{4,3,2,1,0:T(8,128)(2,1)}, u32[]{:S(2)}) %copy-start) | copy-done | bytes 262168
  9.7 0.0 copy-start.3
  9.7 0.8 %shard_map.102.a_ref = bf16[512,512]{1,0:T(8,128)(2,1)S(1)} custom-call(s32[1,2,4]{2,1,0:T(2,128)S(1)} %bitcast.3, s32[1,4]{1,0:T(1,128)S(1)} %bitcast.4, bf16[4,1,2,128,128]{4,3,2,1,0:T(8,128)(2,1)S(1)} %copy-done), custom_call_target="tpu_custom_call" | custom-call | tf_op jit(solution)/shard_map/pallas_call | solution.py:236
  10.5 0.0 collective-permute-done.refs_0_
  10.5 1.1 %collective-permute-done.1.refs_1_ = bf16[128,256]{1,0:T(8,128)(2,1)S(1)} collective-permute-done((bf16[128,256]{1,0:T(8,128)(2,1)}, bf16[128,256]{1,0:T(8,128)(2,1)S(1)}, u32[]{:S(2)}, u32[]{:S(2)}) %collective-permute-start.1) | collective-permute-done | bytes 65568 | tf_op jit(solution)/shard_map/ppermute | solution.py:206
  11.6 0.0 collective-permute-done.2.refs_2_
  11.6 0.0 collective-permute-done.3.refs_4_
  11.6 0.0 copy-done.3
  11.6 0.3 shard_map.103
  11.9 0.1 collective-permute-start.4
  12.0 1.3 %collective-permute-done.4.got_ref = bf16[256,256]{1,0:T(8,128)(2,1)S(1)} collective-permute-done((bf16[256,256]{1,0:T(8,128)(2,1)S(1)}, bf16[256,256]{1,0:T(8,128)(2,1)S(1)}, u32[]{:S(2)}, u32[]{:S(2)}) %collective-permute-start.4) | collective-permute-done | bytes 131104 | tf_op jit(solution)/shard_map/ppermute | solution.py:206
  13.3 0.0 copy-start.6
  13.3 0.0 copy-start.1
  13.3 0.0 copy-start.2
  13.4 1.6 %collective-permute-start.5 = (bf16[256,256]{1,0:T(8,128)(2,1)S(1)}, bf16[256,256]{1,0:T(8,128)(2,1)S(1)}, u32[]{:S(2)}, u32[]{:S(2)}) collective-permute-start(bf16[256,256]{1,0:T(8,128)(2,1)S(1)} %shard_map.104.refs_0_), channel_id=1, source_target_pairs={{0,2},{1,3},{2,0},{3,1},{4,6},{5,7},{6,4},{7,5},{8,10},{9,11},{10,... | collective-permute-start | bytes 393224 | tf_op jit(solution)/shard_map/ppermute | solution.py:206
  14.9 0.3 shard_map.105.refs_4_.at_ref
  15.3 0.0 copy-done.6
  15.3 3.7 %collective-permute-done.5.refs_1_ = bf16[256,256]{1,0:T(8,128)(2,1)S(1)} collective-permute-done((bf16[256,256]{1,0:T(8,128)(2,1)S(1)}, bf16[256,256]{1,0:T(8,128)(2,1)S(1)}, u32[]{:S(2)}, u32[]{:S(2)}) %collective-permute-start.5) | collective-permute-done | bytes 131104 | tf_op jit(solution)/shard_map/ppermute | solution.py:206
  19.0 0.0 copy-done.1
  19.0 0.0 copy-done.2
  19.0 0.5 %shard_map.106 = (bf16[128,256]{1,0:T(8,128)(2,1)S(1)}, bf16[272,256]{1,0:T(8,128)(2,1)S(1)}, bf16[128,256]{1,0:T(8,128)(2,1)S(1)}, bf16[400,256]{1,0:T(8,128)(2,1)S(1)}) custom-call(bf16[256,256]{1,0:T(8,128)(2,1)S(1)} %copy-done.1, bf16[1,256]{1,0:T(2,128)(2,1)S(1)} %reshape.14.b_ref, bf16[256,256]{1,0:T(8,128)(2,1)S(1)} %shard_map.104.refs_0_, ...), custom_call_target="tpu_custom_call" | custom-call | tf_op jit(solution)/shard_map/pallas_call | solution.py:250
  19.5 0.1 collective-permute-start.6
  19.6 1.4 %collective-permute-done.6.got_ref = bf16[400,256]{1,0:T(8,128)(2,1)S(1)} collective-permute-done((bf16[400,256]{1,0:T(8,128)(2,1)S(1)}, bf16[400,256]{1,0:T(8,128)(2,1)S(1)}, u32[]{:S(2)}, u32[]{:S(2)}) %collective-permute-start.6) | collective-permute-done | bytes 204832 | tf_op jit(solution)/shard_map/ppermute | solution.py:206
  21.0 1.1 %collective-permute-start.10 = (bf16[128,256]{1,0:T(8,128)(2,1)S(1)}, bf16[128,256]{1,0:T(8,128)(2,1)S(1)}, u32[]{:S(2)}, u32[]{:S(2)}) collective-permute-start(bf16[128,256]{1,0:T(8,128)(2,1)S(1)} %shard_map.109.part_ref), channel_id=1, source_target_pairs={{0,4},{1,9},{2,6},{3,11},{4,0},{5,13},{6,2},{7,15},{8,12},{9,1},{1... | collective-permute-start | bytes 196616 | tf_op jit(solution)/shard_map/ppermute | solution.py:215
  22.2 0.3 shard_map.107
  22.5 1.0 %collective-permute-start.8 = (bf16[144,256]{1,0:T(8,128)(2,1)S(1)}, bf16[144,256]{1,0:T(8,128)(2,1)S(1)}, u32[]{:S(2)}, u32[]{:S(2)}) collective-permute-start(bf16[144,256]{1,0:T(8,128)(2,1)S(1)} %get-tuple-element.25.sent_ref), channel_id=1, source_target_pairs={{0,4},{1,9},{2,6},{3,11},{4,0},{5,13},{6,2},{7,15},{8,12},{9,1},{1... | collective-permute-start | bytes 221192 | tf_op jit(solution)/shard_map/ppermute | solution.py:215
  23.5 1.1 %collective-permute-start.7 = (bf16[128,256]{1,0:T(8,128)(2,1)S(1)}, bf16[128,256]{1,0:T(8,128)(2,1)S(1)}, u32[]{:S(2)}, u32[]{:S(2)}) collective-permute-start(bf16[128,256]{1,0:T(8,128)(2,1)S(1)} %get-tuple-element.24), channel_id=1, source_target_pairs={{0,4},{1,9},{2,6},{3,11},{4,0},{5,13},{6,2},{7,15},{8,12},{9,1},{1... | collective-permute-start | bytes 196616 | tf_op jit(solution)/shard_map/ppermute | solution.py:215
  24.6 1.5 %collective-permute-done.10.got_ref = bf16[128,256]{1,0:T(8,128)(2,1)S(1)} collective-permute-done((bf16[128,256]{1,0:T(8,128)(2,1)S(1)}, bf16[128,256]{1,0:T(8,128)(2,1)S(1)}, u32[]{:S(2)}, u32[]{:S(2)}) %collective-permute-start.10) | collective-permute-done | bytes 65568 | tf_op jit(solution)/shard_map/ppermute | solution.py:215
  26.1 1.2 %collective-permute-start.11 = (bf16[128,256]{1,0:T(8,128)(2,1)S(1)}, bf16[128,256]{1,0:T(8,128)(2,1)S(1)}, u32[]{:S(2)}, u32[]{:S(2)}) collective-permute-start(bf16[128,256]{1,0:T(8,128)(2,1)S(1)} %shard_map.110.part_ref), channel_id=1, source_target_pairs={{0,8},{1,5},{2,10},{3,7},{4,12},{5,1},{6,14},{7,3},{8,0},{9,13},{1... | collective-permute-start | bytes 196616 | tf_op jit(solution)/shard_map/ppermute | solution.py:215
  27.3 2.2 %collective-permute-done.7._.refs_1_ = bf16[128,256]{1,0:T(8,128)(2,1)S(1)} collective-permute-done((bf16[128,256]{1,0:T(8,128)(2,1)S(1)}, bf16[128,256]{1,0:T(8,128)(2,1)S(1)}, u32[]{:S(2)}, u32[]{:S(2)}) %collective-permute-start.7) | collective-permute-done | bytes 65568 | tf_op jit(solution)/shard_map/ppermute | solution.py:215
  29.6 0.0 collective-permute-done.8.got_ref.refs_1_
  29.6 2.1 %collective-permute-start.9 = (bf16[144,256]{1,0:T(8,128)(2,1)S(1)}, bf16[144,256]{1,0:T(8,128)(2,1)S(1)}, u32[]{:S(2)}, u32[]{:S(2)}) collective-permute-start(bf16[144,256]{1,0:T(8,128)(2,1)S(1)} %shard_map.108.sent_ref), channel_id=1, source_target_pairs={{0,8},{1,5},{2,10},{3,7},{4,12},{5,1},{6,14},{7,3},{8,0},{9,13},{1... | collective-permute-start | bytes 221192 | tf_op jit(solution)/shard_map/ppermute | solution.py:215
  31.7 0.0 collective-permute-done.11.got_ref
  31.8 0.1 collective-permute-start.12
  31.8 3.8 %collective-permute-done.9.line_ref.refs_2_ = bf16[144,256]{1,0:T(8,128)(2,1)S(1)} collective-permute-done((bf16[144,256]{1,0:T(8,128)(2,1)S(1)}, bf16[144,256]{1,0:T(8,128)(2,1)S(1)}, u32[]{:S(2)}, u32[]{:S(2)}) %collective-permute-start.9) | collective-permute-done | bytes 73760 | tf_op jit(solution)/shard_map/ppermute | solution.py:215
  35.7 0.0 collective-permute-done.12.got_ref
  35.7 0.8 %shard_map.112 = (bf16[128,256]{1,0:T(8,128)(2,1)}, bf16[128,256]{1,0:T(8,128)(2,1)}, f32[256,256]{1,0:T(8,128)}, f32[1,256]{1,0:T(1,128)}) custom-call(bf16[128,256]{1,0:T(8,128)(2,1)S(1)} %get-tuple-element.21.act_ref, bf16[144,256]{1,0:T(8,128)(2,1)S(1)} %shard_map.108.sent_ref, bf16[144,256]{1,0:T(8,128)(2,1)S(1)} %collective-permute-done.9.line_ref.refs_2_, ...), custom_call_target="tpu_custom_call" | custom-call | tf_op jit(solution)/shard_map/pallas_call | solution.py:297
  (6 shorter events, 0.1 us)
Async XLA Ops:
  0.6 9.8 %collective-permute-start = (bf16[128,256]{1,0:T(8,128)(2,1)}, bf16[128,256]{1,0:T(8,128)(2,1)S(1)}, u32[]{:S(2)}, u32[]{:S(2)}) collective-permute-start(bf16[128,256]{1,0:T(8,128)(2,1)} %refs_3_.1), channel_id=1, source_target_pairs={{0,12},{4,8},{8,4},{12,0},{1,13},{5,9},{9,5},{13,1},{2,14},{6,10},... | collective-permute-start | bytes 196616 | tf_op jit(solution)/shard_map/ppermute | solution.py:206
  5.7 5.8 %collective-permute-start.1 = (bf16[128,256]{1,0:T(8,128)(2,1)}, bf16[128,256]{1,0:T(8,128)(2,1)S(1)}, u32[]{:S(2)}, u32[]{:S(2)}) collective-permute-start(bf16[128,256]{1,0:T(8,128)(2,1)} %refs_3_.1), channel_id=1, source_target_pairs={{0,8},{4,12},{8,0},{12,4},{1,9},{5,13},{9,1},{13,5},{2,10},{6,14},... | collective-permute-start | bytes 196616 | tf_op jit(solution)/shard_map/ppermute | solution.py:206
  5.7 5.8 %collective-permute-start.2 = (bf16[128,256]{1,0:T(8,128)(2,1)}, bf16[128,256]{1,0:T(8,128)(2,1)S(1)}, u32[]{:S(2)}, u32[]{:S(2)}) collective-permute-start(bf16[128,256]{1,0:T(8,128)(2,1)} %refs_3_.1), channel_id=1, source_target_pairs={{0,4},{4,0},{8,12},{12,8},{1,5},{5,1},{9,13},{13,9},{2,6},{6,2},{1... | collective-permute-start | bytes 196616 | tf_op jit(solution)/shard_map/ppermute | solution.py:206
  6.4 5.2 %collective-permute-start.3 = (bf16[128,256]{1,0:T(8,128)(2,1)}, bf16[128,256]{1,0:T(8,128)(2,1)S(1)}, u32[]{:S(2)}, u32[]{:S(2)}) collective-permute-start(bf16[128,256]{1,0:T(8,128)(2,1)} %refs_2_.1), channel_id=1, source_target_pairs={{0,2},{1,3},{2,0},{3,1},{4,6},{5,7},{6,4},{7,5},{8,10},{9,11},{10,... | collective-permute-start | bytes 196616 | tf_op jit(solution)/shard_map/ppermute | solution.py:206
  8.0 0.7 %copy-start.4 = (s32[4,1,2]{0,2,1:T(2,128)S(1)}, s32[4,1,2]{0,2,1:T(2,128)}, u32[]{:S(2)}) copy-start(s32[4,1,2]{0,2,1:T(2,128)} %param.9) | copy-start | bytes 100
  8.0 0.7 %copy-start.5 = (s32[4,1]{0,1:T(1,128)S(1)}, s32[4,1]{0,1:T(1,128)}, u32[]{:S(2)}) copy-start(s32[4,1]{0,1:T(1,128)} %param.10) | copy-start | bytes 52
  8.7 1.0 %copy-start = (bf16[4,1,2,128,128]{4,3,2,1,0:T(8,128)(2,1)S(1)}, bf16[4,1,2,128,128]{4,3,2,1,0:T(8,128)(2,1)}, u32[]{:S(2)}) copy-start(bf16[4,1,2,128,128]{4,3,2,1,0:T(8,128)(2,1)} %tiles_ref.1) | copy-start | bytes 786436
  9.7 1.9 %copy-start.3 = (bf16[128,256]{1,0:T(8,128)(2,1)S(1)}, bf16[128,256]{1,0:T(8,128)(2,1)}, u32[]{:S(2)}) copy-start(bf16[128,256]{1,0:T(8,128)(2,1)} %refs_3_.1) | copy-start | bytes 196612
  11.9 1.4 %collective-permute-start.4 = (bf16[256,256]{1,0:T(8,128)(2,1)S(1)}, bf16[256,256]{1,0:T(8,128)(2,1)S(1)}, u32[]{:S(2)}, u32[]{:S(2)}) collective-permute-start(bf16[256,256]{1,0:T(8,128)(2,1)S(1)} %get-tuple-element.19), channel_id=1, source_target_pairs={{0,1},{1,0},{2,3},{3,2},{4,5},{5,4},{6,7},{7,6},{8,9},{9,8},{10,11... | collective-permute-start | bytes 393224 | tf_op jit(solution)/shard_map/ppermute | solution.py:206
  13.3 1.9 %copy-start.6 = (bf16[256]{0:T(256)(128)(2,1)S(1)}, bf16[256]{0:T(256)(128)(2,1)}, u32[]{:S(2)}) copy-start(bf16[256]{0:T(256)(128)(2,1)} %param.12) | copy-start | bytes 1540
  13.3 5.6 %copy-start.1 = (bf16[256,256]{1,0:T(8,128)(2,1)S(1)}, bf16[256,256]{1,0:T(8,128)(2,1)}, u32[]{:S(2)}) copy-start(bf16[256,256]{1,0:T(8,128)(2,1)} %w_ref.1) | copy-start | bytes 393220
  13.3 5.6 %copy-start.2 = (bf16[128,256]{1,0:T(8,128)(2,1)S(1)}, bf16[128,256]{1,0:T(8,128)(2,1)}, u32[]{:S(2)}) copy-start(bf16[128,256]{1,0:T(8,128)(2,1)} %refs_2_.1) | copy-start | bytes 196612
  13.4 5.6 %collective-permute-start.5 = (bf16[256,256]{1,0:T(8,128)(2,1)S(1)}, bf16[256,256]{1,0:T(8,128)(2,1)S(1)}, u32[]{:S(2)}, u32[]{:S(2)}) collective-permute-start(bf16[256,256]{1,0:T(8,128)(2,1)S(1)} %shard_map.104.refs_0_), channel_id=1, source_target_pairs={{0,2},{1,3},{2,0},{3,1},{4,6},{5,7},{6,4},{7,5},{8,10},{9,11},{10,... | collective-permute-start | bytes 393224 | tf_op jit(solution)/shard_map/ppermute | solution.py:206
  19.5 1.5 %collective-permute-start.6 = (bf16[400,256]{1,0:T(8,128)(2,1)S(1)}, bf16[400,256]{1,0:T(8,128)(2,1)S(1)}, u32[]{:S(2)}, u32[]{:S(2)}) collective-permute-start(bf16[400,256]{1,0:T(8,128)(2,1)S(1)} %get-tuple-element.23), channel_id=1, source_target_pairs={{0,1},{1,0},{2,3},{3,2},{4,5},{5,4},{6,7},{7,6},{8,9},{9,8},{10,11... | collective-permute-start | bytes 614408 | tf_op jit(solution)/shard_map/ppermute | solution.py:206
  21.0 5.0 %collective-permute-start.10 = (bf16[128,256]{1,0:T(8,128)(2,1)S(1)}, bf16[128,256]{1,0:T(8,128)(2,1)S(1)}, u32[]{:S(2)}, u32[]{:S(2)}) collective-permute-start(bf16[128,256]{1,0:T(8,128)(2,1)S(1)} %shard_map.109.part_ref), channel_id=1, source_target_pairs={{0,4},{1,9},{2,6},{3,11},{4,0},{5,13},{6,2},{7,15},{8,12},{9,1},{1... | collective-permute-start | bytes 196616 | tf_op jit(solution)/shard_map/ppermute | solution.py:215
  22.5 7.1 %collective-permute-start.8 = (bf16[144,256]{1,0:T(8,128)(2,1)S(1)}, bf16[144,256]{1,0:T(8,128)(2,1)S(1)}, u32[]{:S(2)}, u32[]{:S(2)}) collective-permute-start(bf16[144,256]{1,0:T(8,128)(2,1)S(1)} %get-tuple-element.25.sent_ref), channel_id=1, source_target_pairs={{0,4},{1,9},{2,6},{3,11},{4,0},{5,13},{6,2},{7,15},{8,12},{9,1},{1... | collective-permute-start | bytes 221192 | tf_op jit(solution)/shard_map/ppermute | solution.py:215
  23.5 6.0 %collective-permute-start.7 = (bf16[128,256]{1,0:T(8,128)(2,1)S(1)}, bf16[128,256]{1,0:T(8,128)(2,1)S(1)}, u32[]{:S(2)}, u32[]{:S(2)}) collective-permute-start(bf16[128,256]{1,0:T(8,128)(2,1)S(1)} %get-tuple-element.24), channel_id=1, source_target_pairs={{0,4},{1,9},{2,6},{3,11},{4,0},{5,13},{6,2},{7,15},{8,12},{9,1},{1... | collective-permute-start | bytes 196616 | tf_op jit(solution)/shard_map/ppermute | solution.py:215
  26.1 5.6 %collective-permute-start.11 = (bf16[128,256]{1,0:T(8,128)(2,1)S(1)}, bf16[128,256]{1,0:T(8,128)(2,1)S(1)}, u32[]{:S(2)}, u32[]{:S(2)}) collective-permute-start(bf16[128,256]{1,0:T(8,128)(2,1)S(1)} %shard_map.110.part_ref), channel_id=1, source_target_pairs={{0,8},{1,5},{2,10},{3,7},{4,12},{5,1},{6,14},{7,3},{8,0},{9,13},{1... | collective-permute-start | bytes 196616 | tf_op jit(solution)/shard_map/ppermute | solution.py:215
  29.6 6.1 %collective-permute-start.9 = (bf16[144,256]{1,0:T(8,128)(2,1)S(1)}, bf16[144,256]{1,0:T(8,128)(2,1)S(1)}, u32[]{:S(2)}, u32[]{:S(2)}) collective-permute-start(bf16[144,256]{1,0:T(8,128)(2,1)S(1)} %shard_map.108.sent_ref), channel_id=1, source_target_pairs={{0,8},{1,5},{2,10},{3,7},{4,12},{5,1},{6,14},{7,3},{8,0},{9,13},{1... | collective-permute-start | bytes 221192 | tf_op jit(solution)/shard_map/ppermute | solution.py:215
  31.8 3.9 %collective-permute-start.12 = (bf16[128,256]{1,0:T(8,128)(2,1)S(1)}, bf16[128,256]{1,0:T(8,128)(2,1)S(1)}, u32[]{:S(2)}, u32[]{:S(2)}) collective-permute-start(bf16[128,256]{1,0:T(8,128)(2,1)S(1)} %shard_map.111.mine_ref), channel_id=1, source_target_pairs={{0,1},{1,0},{2,3},{3,2},{4,5},{5,4},{6,7},{7,6},{8,9},{9,8},{10,11... | collective-permute-start | bytes 196616 | tf_op jit(solution)/shard_map/ppermute | solution.py:206

commit v13 on v11

--- a/solution.py
+++ b/solution.py
@@ -206,11 +206,11 @@
     return lax.ppermute(x, axis, [(i, i ^ by) for i in range(n)])
 
 
-def step(x, n_row, n_col, by):
+def step(x, n_row, n_col, by, first=0):
     pairs = []
     for i in range(n_row):
         for j in range(n_col):
-            bit = by if j % 2 == 0 else n_row // 2 // by
+            bit = by if j % 2 == first else n_row // 2 // by
             pairs.append((i * n_col + j, (i ^ bit) * n_col + j))
     return lax.ppermute(x, ("row", "col"), pairs)
 
@@ -273,7 +273,7 @@
     )(at, keep, got)
     terms, by = [(keep, 0, live)], 1
     while True:
-        other = step(part, n_row, n_col, by)
+        other = step(part, n_row, n_col, by, 1)
         sent, gots = sends[-1], [step(x, n_row, n_col, by) for x in reversed(sends)][::-1]
         terms += [(x, i * size, size) for i, x in enumerate(gots)]
         part = call(part_kernel, shape(piece, width), count=2)(part, other)

time: 35.8 us -> 37.4 us (1.045)
  waiting for transfers between devices: 13.8 us -> 14.9 us
  starting transfers between devices: 16.2 us -> 16.7 us
    ppermute x5, waiting for transfers between devices: 6.29 us -> 7.37 us  [step(): return lax.ppermute(x, ('row', 'col'), pairs)]
    ppermute x5, starting transfers between devices: 7.02 us -> 7.56 us  [step(): return lax.ppermute(x, ('row', 'col'), pairs)]
  transfers between devices with their start and end apart: 13 -> 13, of which waited for: 9 -> 7; matrix products, arithmetic and copies ran while one was open for 0% -> 0% of each run, Pallas kernels for 4% -> 4%
where the time goes in v13:
time: 37.4 us; the launch traced here: 37.2 us
  starting transfers between devices  16.7 us (45%)
  waiting for transfers between devices  14.9 us (40%)
  Pallas kernels  3.15 us (8%)
  local copies, waits for them, and re-layouts  1.66 us (4%)
  between operations  0.78 us (2%)
    ppermute x8, starting transfers between devices, swap(): return lax.ppermute(x, axis, [(i, i ^ by) for i in range(n)])  9.16 us
    ppermute x5, starting transfers between devices, step(): return lax.ppermute(x, ('row', 'col'), pairs)  7.56 us
    ppermute x8, waiting for transfers between devices, swap(): return lax.ppermute(x, axis, [(i, i ^ by) for i in range(n)])  7.56 us
    ppermute x5, waiting for transfers between devices, step(): return lax.ppermute(x, ('row', 'col'), pairs)  7.37 us
    unnamed x14, local copies, waits for them, and re-layouts  1.65 us
    pallas_call x1, Pallas kernels, shards(): call(dense_kernel(n_chip), shape(n_col * tile, n_row * tile), count=3, sm...  0.79 us
    pallas_call x1, Pallas kernels, shards(): call(last_kernel, (shape(tile, width), shape(tile, width), shape(width, w...  0.78 us
  transfers between devices with their start and end apart: 13, of which 7 were waited for; matrix products, arithmetic and copies ran while one was open for 0% of the time, Pallas kernels for 4%

profile of v13, /device:TPU:0, one launch (start us, length us, event | category | flops | bytes accessed | tf_op | source)
XLA Modules:
  0.0 37.2 jit_solution(5228733960791851166)
XLA Ops:
  0.6 5.1 %collective-permute-start = (bf16[128,256]{1,0:T(8,128)(2,1)}, bf16[128,256]{1,0:T(8,128)(2,1)S(1)}, u32[]{:S(2)}, u32[]{:S(2)}) collective-permute-start(bf16[128,256]{1,0:T(8,128)(2,1)} %refs_3_.1), channel_id=1, source_target_pairs={{0,12},{4,8},{8,4},{12,0},{1,13},{5,9},{9,5},{13,1},{2,14},{6,10},... | collective-permute-start | bytes 196616 | tf_op jit(solution)/shard_map/ppermute | solution.py:206
  5.7 0.0 collective-permute-start.1
  5.7 0.6 %collective-permute-start.2 = (bf16[128,256]{1,0:T(8,128)(2,1)}, bf16[128,256]{1,0:T(8,128)(2,1)S(1)}, u32[]{:S(2)}, u32[]{:S(2)}) collective-permute-start(bf16[128,256]{1,0:T(8,128)(2,1)} %refs_3_.1), channel_id=1, source_target_pairs={{0,4},{4,0},{8,12},{12,8},{1,5},{5,1},{9,13},{13,9},{2,6},{6,2},{1... | collective-permute-start | bytes 196616 | tf_op jit(solution)/shard_map/ppermute | solution.py:206
  6.4 1.6 %collective-permute-start.3 = (bf16[128,256]{1,0:T(8,128)(2,1)}, bf16[128,256]{1,0:T(8,128)(2,1)S(1)}, u32[]{:S(2)}, u32[]{:S(2)}) collective-permute-start(bf16[128,256]{1,0:T(8,128)(2,1)} %refs_2_.1), channel_id=1, source_target_pairs={{0,2},{1,3},{2,0},{3,1},{4,6},{5,7},{6,4},{7,5},{8,10},{9,11},{10,... | collective-permute-start | bytes 196616 | tf_op jit(solution)/shard_map/ppermute | solution.py:206
  8.0 0.0 copy-start.4
  8.0 0.0 copy-start.5
  8.0 0.7 %copy-done.4 = s32[4,1,2]{0,2,1:T(2,128)S(1)} copy-done((s32[4,1,2]{0,2,1:T(2,128)S(1)}, s32[4,1,2]{0,2,1:T(2,128)}, u32[]{:S(2)}) %copy-start.4) | copy-done | bytes 56
  8.7 0.0 copy-done.5
  8.7 0.0 copy-start
  8.7 0.9 %copy-done = bf16[4,1,2,128,128]{4,3,2,1,0:T(8,128)(2,1)S(1)} copy-done((bf16[4,1,2,128,128]{4,3,2,1,0:T(8,128)(2,1)S(1)}, bf16[4,1,2,128,128]{4,3,2,1,0:T(8,128)(2,1)}, u32[]{:S(2)}) %copy-start) | copy-done | bytes 262168
  9.7 0.0 copy-start.3
  9.7 0.8 %shard_map.102.a_ref = bf16[512,512]{1,0:T(8,128)(2,1)S(1)} custom-call(s32[1,2,4]{2,1,0:T(2,128)S(1)} %bitcast.3, s32[1,4]{1,0:T(1,128)S(1)} %bitcast.4, bf16[4,1,2,128,128]{4,3,2,1,0:T(8,128)(2,1)S(1)} %copy-done), custom_call_target="tpu_custom_call" | custom-call | tf_op jit(solution)/shard_map/pallas_call | solution.py:236
  10.5 0.0 collective-permute-done.refs_0_
  10.5 1.1 %collective-permute-done.1.refs_1_ = bf16[128,256]{1,0:T(8,128)(2,1)S(1)} collective-permute-done((bf16[128,256]{1,0:T(8,128)(2,1)}, bf16[128,256]{1,0:T(8,128)(2,1)S(1)}, u32[]{:S(2)}, u32[]{:S(2)}) %collective-permute-start.1) | collective-permute-done | bytes 65568 | tf_op jit(solution)/shard_map/ppermute | solution.py:206
  11.6 0.0 collective-permute-done.2.refs_2_
  11.6 0.0 collective-permute-done.3.refs_4_
  11.6 0.0 copy-done.3
  11.6 0.3 shard_map.103
  11.9 0.1 collective-permute-start.4
  12.0 1.3 %collective-permute-done.4.got_ref = bf16[256,256]{1,0:T(8,128)(2,1)S(1)} collective-permute-done((bf16[256,256]{1,0:T(8,128)(2,1)S(1)}, bf16[256,256]{1,0:T(8,128)(2,1)S(1)}, u32[]{:S(2)}, u32[]{:S(2)}) %collective-permute-start.4) | collective-permute-done | bytes 131104 | tf_op jit(solution)/shard_map/ppermute | solution.py:206
  13.3 0.0 copy-start.6
  13.3 0.0 copy-start.1
  13.3 0.0 copy-start.2
  13.4 1.6 %collective-permute-start.5 = (bf16[256,256]{1,0:T(8,128)(2,1)S(1)}, bf16[256,256]{1,0:T(8,128)(2,1)S(1)}, u32[]{:S(2)}, u32[]{:S(2)}) collective-permute-start(bf16[256,256]{1,0:T(8,128)(2,1)S(1)} %shard_map.104.refs_0_), channel_id=1, source_target_pairs={{0,2},{1,3},{2,0},{3,1},{4,6},{5,7},{6,4},{7,5},{8,10},{9,11},{10,... | collective-permute-start | bytes 393224 | tf_op jit(solution)/shard_map/ppermute | solution.py:206
  14.9 0.3 shard_map.105.refs_4_.at_ref
  15.3 0.0 copy-done.6
  15.3 3.7 %collective-permute-done.5.refs_1_ = bf16[256,256]{1,0:T(8,128)(2,1)S(1)} collective-permute-done((bf16[256,256]{1,0:T(8,128)(2,1)S(1)}, bf16[256,256]{1,0:T(8,128)(2,1)S(1)}, u32[]{:S(2)}, u32[]{:S(2)}) %collective-permute-start.5) | collective-permute-done | bytes 131104 | tf_op jit(solution)/shard_map/ppermute | solution.py:206
  19.0 0.0 copy-done.1
  19.0 0.0 copy-done.2
  19.0 0.5 %shard_map.106 = (bf16[128,256]{1,0:T(8,128)(2,1)S(1)}, bf16[272,256]{1,0:T(8,128)(2,1)S(1)}, bf16[128,256]{1,0:T(8,128)(2,1)S(1)}, bf16[400,256]{1,0:T(8,128)(2,1)S(1)}) custom-call(bf16[256,256]{1,0:T(8,128)(2,1)S(1)} %copy-done.1, bf16[1,256]{1,0:T(2,128)(2,1)S(1)} %reshape.14.b_ref, bf16[256,256]{1,0:T(8,128)(2,1)S(1)} %shard_map.104.refs_0_, ...), custom_call_target="tpu_custom_call" | custom-call | tf_op jit(solution)/shard_map/pallas_call | solution.py:250
  19.5 0.1 collective-permute-start.6
  19.6 1.4 %collective-permute-done.6.got_ref = bf16[400,256]{1,0:T(8,128)(2,1)S(1)} collective-permute-done((bf16[400,256]{1,0:T(8,128)(2,1)S(1)}, bf16[400,256]{1,0:T(8,128)(2,1)S(1)}, u32[]{:S(2)}, u32[]{:S(2)}) %collective-permute-start.6) | collective-permute-done | bytes 204832 | tf_op jit(solution)/shard_map/ppermute | solution.py:206
  21.0 1.6 %collective-permute-start.9 = (bf16[128,256]{1,0:T(8,128)(2,1)S(1)}, bf16[128,256]{1,0:T(8,128)(2,1)S(1)}, u32[]{:S(2)}, u32[]{:S(2)}) collective-permute-start(bf16[128,256]{1,0:T(8,128)(2,1)S(1)} %shard_map.109.part_ref), channel_id=1, source_target_pairs={{0,8},{1,5},{2,10},{3,7},{4,12},{5,1},{6,14},{7,3},{8,0},{9,13},{1... | collective-permute-start | bytes 196616 | tf_op jit(solution)/shard_map/ppermute | solution.py:215
  22.7 0.3 shard_map.107
  23.0 2.1 %collective-permute-start.7 = (bf16[144,256]{1,0:T(8,128)(2,1)S(1)}, bf16[144,256]{1,0:T(8,128)(2,1)S(1)}, u32[]{:S(2)}, u32[]{:S(2)}) collective-permute-start(bf16[144,256]{1,0:T(8,128)(2,1)S(1)} %get-tuple-element.24.sent_ref), channel_id=1, source_target_pairs={{0,4},{1,9},{2,6},{3,11},{4,0},{5,13},{6,2},{7,15},{8,12},{9,1},{1... | collective-permute-start | bytes 221192 | tf_op jit(solution)/shard_map/ppermute | solution.py:215
  25.1 3.0 %collective-permute-done.9.got_ref = bf16[128,256]{1,0:T(8,128)(2,1)S(1)} collective-permute-done((bf16[128,256]{1,0:T(8,128)(2,1)S(1)}, bf16[128,256]{1,0:T(8,128)(2,1)S(1)}, u32[]{:S(2)}, u32[]{:S(2)}) %collective-permute-start.9) | collective-permute-done | bytes 65568 | tf_op jit(solution)/shard_map/ppermute | solution.py:215
  28.1 0.1 collective-permute-start.10
  28.2 0.0 collective-permute-done.7.got_ref.refs_1_
  28.3 3.7 %collective-permute-start.8 = (bf16[144,256]{1,0:T(8,128)(2,1)S(1)}, bf16[144,256]{1,0:T(8,128)(2,1)S(1)}, u32[]{:S(2)}, u32[]{:S(2)}) collective-permute-start(bf16[144,256]{1,0:T(8,128)(2,1)S(1)} %shard_map.108.sent_ref), channel_id=1, source_target_pairs={{0,8},{1,5},{2,10},{3,7},{4,12},{5,1},{6,14},{7,3},{8,0},{9,13},{1... | collective-permute-start | bytes 221192 | tf_op jit(solution)/shard_map/ppermute | solution.py:215
  32.0 0.0 collective-permute-start.12
  32.0 0.5 %collective-permute-done.10.got_ref = bf16[128,256]{1,0:T(8,128)(2,1)S(1)} collective-permute-done((bf16[128,256]{1,0:T(8,128)(2,1)S(1)}, bf16[128,256]{1,0:T(8,128)(2,1)S(1)}, u32[]{:S(2)}, u32[]{:S(2)}) %collective-permute-start.10) | collective-permute-done | bytes 65568 | tf_op jit(solution)/shard_map/ppermute | solution.py:215
  32.6 0.1 collective-permute-start.11
  32.7 3.8 %collective-permute-done.12.refs_1_ = bf16[128,256]{1,0:T(8,128)(2,1)S(1)} collective-permute-done((bf16[128,256]{1,0:T(8,128)(2,1)S(1)}, bf16[128,256]{1,0:T(8,128)(2,1)S(1)}, u32[]{:S(2)}, u32[]{:S(2)}) %collective-permute-start.12) | collective-permute-done | bytes 65568 | tf_op jit(solution)/shard_map/ppermute | solution.py:215
  36.5 0.0 collective-permute-done.8.line_ref.refs_2_
  36.5 0.0 collective-permute-done.11.got_ref
  36.5 0.8 %shard_map.112 = (bf16[128,256]{1,0:T(8,128)(2,1)}, bf16[128,256]{1,0:T(8,128)(2,1)}, f32[256,256]{1,0:T(8,128)}, f32[1,256]{1,0:T(1,128)}) custom-call(bf16[128,256]{1,0:T(8,128)(2,1)S(1)} %get-tuple-element.21.act_ref, bf16[144,256]{1,0:T(8,128)(2,1)S(1)} %shard_map.108.sent_ref, bf16[144,256]{1,0:T(8,128)(2,1)S(1)} %collective-permute-done.8.line_ref.refs_2_, ...), custom_call_target="tpu_custom_call" | custom-call | tf_op jit(solution)/shard_map/pallas_call | solution.py:297
  (6 shorter events, 0.1 us)
Async XLA Ops:
  0.6 9.8 %collective-permute-start = (bf16[128,256]{1,0:T(8,128)(2,1)}, bf16[128,256]{1,0:T(8,128)(2,1)S(1)}, u32[]{:S(2)}, u32[]{:S(2)}) collective-permute-start(bf16[128,256]{1,0:T(8,128)(2,1)} %refs_3_.1), channel_id=1, source_target_pairs={{0,12},{4,8},{8,4},{12,0},{1,13},{5,9},{9,5},{13,1},{2,14},{6,10},... | collective-permute-start | bytes 196616 | tf_op jit(solution)/shard_map/ppermute | solution.py:206
  5.7 5.8 %collective-permute-start.1 = (bf16[128,256]{1,0:T(8,128)(2,1)}, bf16[128,256]{1,0:T(8,128)(2,1)S(1)}, u32[]{:S(2)}, u32[]{:S(2)}) collective-permute-start(bf16[128,256]{1,0:T(8,128)(2,1)} %refs_3_.1), channel_id=1, source_target_pairs={{0,8},{4,12},{8,0},{12,4},{1,9},{5,13},{9,1},{13,5},{2,10},{6,14},... | collective-permute-start | bytes 196616 | tf_op jit(solution)/shard_map/ppermute | solution.py:206
  5.7 5.8 %collective-permute-start.2 = (bf16[128,256]{1,0:T(8,128)(2,1)}, bf16[128,256]{1,0:T(8,128)(2,1)S(1)}, u32[]{:S(2)}, u32[]{:S(2)}) collective-permute-start(bf16[128,256]{1,0:T(8,128)(2,1)} %refs_3_.1), channel_id=1, source_target_pairs={{0,4},{4,0},{8,12},{12,8},{1,5},{5,1},{9,13},{13,9},{2,6},{6,2},{1... | collective-permute-start | bytes 196616 | tf_op jit(solution)/shard_map/ppermute | solution.py:206
  6.4 5.2 %collective-permute-start.3 = (bf16[128,256]{1,0:T(8,128)(2,1)}, bf16[128,256]{1,0:T(8,128)(2,1)S(1)}, u32[]{:S(2)}, u32[]{:S(2)}) collective-permute-start(bf16[128,256]{1,0:T(8,128)(2,1)} %refs_2_.1), channel_id=1, source_target_pairs={{0,2},{1,3},{2,0},{3,1},{4,6},{5,7},{6,4},{7,5},{8,10},{9,11},{10,... | collective-permute-start | bytes 196616 | tf_op jit(solution)/shard_map/ppermute | solution.py:206
  8.0 0.7 %copy-start.4 = (s32[4,1,2]{0,2,1:T(2,128)S(1)}, s32[4,1,2]{0,2,1:T(2,128)}, u32[]{:S(2)}) copy-start(s32[4,1,2]{0,2,1:T(2,128)} %param.9) | copy-start | bytes 100
  8.0 0.7 %copy-start.5 = (s32[4,1]{0,1:T(1,128)S(1)}, s32[4,1]{0,1:T(1,128)}, u32[]{:S(2)}) copy-start(s32[4,1]{0,1:T(1,128)} %param.10) | copy-start | bytes 52
  8.7 1.0 %copy-start = (bf16[4,1,2,128,128]{4,3,2,1,0:T(8,128)(2,1)S(1)}, bf16[4,1,2,128,128]{4,3,2,1,0:T(8,128)(2,1)}, u32[]{:S(2)}) copy-start(bf16[4,1,2,128,128]{4,3,2,1,0:T(8,128)(2,1)} %tiles_ref.1) | copy-start | bytes 786436
  9.7 1.9 %copy-start.3 = (bf16[128,256]{1,0:T(8,128)(2,1)S(1)}, bf16[128,256]{1,0:T(8,128)(2,1)}, u32[]{:S(2)}) copy-start(bf16[128,256]{1,0:T(8,128)(2,1)} %refs_3_.1) | copy-start | bytes 196612
  11.9 1.4 %collective-permute-start.4 = (bf16[256,256]{1,0:T(8,128)(2,1)S(1)}, bf16[256,256]{1,0:T(8,128)(2,1)S(1)}, u32[]{:S(2)}, u32[]{:S(2)}) collective-permute-start(bf16[256,256]{1,0:T(8,128)(2,1)S(1)} %get-tuple-element.19), channel_id=1, source_target_pairs={{0,1},{1,0},{2,3},{3,2},{4,5},{5,4},{6,7},{7,6},{8,9},{9,8},{10,11... | collective-permute-start | bytes 393224 | tf_op jit(solution)/shard_map/ppermute | solution.py:206
  13.3 1.9 %copy-start.6 = (bf16[256]{0:T(256)(128)(2,1)S(1)}, bf16[256]{0:T(256)(128)(2,1)}, u32[]{:S(2)}) copy-start(bf16[256]{0:T(256)(128)(2,1)} %param.12) | copy-start | bytes 1540
  13.3 5.6 %copy-start.1 = (bf16[256,256]{1,0:T(8,128)(2,1)S(1)}, bf16[256,256]{1,0:T(8,128)(2,1)}, u32[]{:S(2)}) copy-start(bf16[256,256]{1,0:T(8,128)(2,1)} %w_ref.1) | copy-start | bytes 393220
  13.3 5.6 %copy-start.2 = (bf16[128,256]{1,0:T(8,128)(2,1)S(1)}, bf16[128,256]{1,0:T(8,128)(2,1)}, u32[]{:S(2)}) copy-start(bf16[128,256]{1,0:T(8,128)(2,1)} %refs_2_.1) | copy-start | bytes 196612
  13.4 5.6 %collective-permute-start.5 = (bf16[256,256]{1,0:T(8,128)(2,1)S(1)}, bf16[256,256]{1,0:T(8,128)(2,1)S(1)}, u32[]{:S(2)}, u32[]{:S(2)}) collective-permute-start(bf16[256,256]{1,0:T(8,128)(2,1)S(1)} %shard_map.104.refs_0_), channel_id=1, source_target_pairs={{0,2},{1,3},{2,0},{3,1},{4,6},{5,7},{6,4},{7,5},{8,10},{9,11},{10,... | collective-permute-start | bytes 393224 | tf_op jit(solution)/shard_map/ppermute | solution.py:206
  19.5 1.5 %collective-permute-start.6 = (bf16[400,256]{1,0:T(8,128)(2,1)S(1)}, bf16[400,256]{1,0:T(8,128)(2,1)S(1)}, u32[]{:S(2)}, u32[]{:S(2)}) collective-permute-start(bf16[400,256]{1,0:T(8,128)(2,1)S(1)} %get-tuple-element.23), channel_id=1, source_target_pairs={{0,1},{1,0},{2,3},{3,2},{4,5},{5,4},{6,7},{7,6},{8,9},{9,8},{10,11... | collective-permute-start | bytes 614408 | tf_op jit(solution)/shard_map/ppermute | solution.py:206
  21.0 7.1 %collective-permute-start.9 = (bf16[128,256]{1,0:T(8,128)(2,1)S(1)}, bf16[128,256]{1,0:T(8,128)(2,1)S(1)}, u32[]{:S(2)}, u32[]{:S(2)}) collective-permute-start(bf16[128,256]{1,0:T(8,128)(2,1)S(1)} %shard_map.109.part_ref), channel_id=1, source_target_pairs={{0,8},{1,5},{2,10},{3,7},{4,12},{5,1},{6,14},{7,3},{8,0},{9,13},{1... | collective-permute-start | bytes 196616 | tf_op jit(solution)/shard_map/ppermute | solution.py:215
  23.0 5.2 %collective-permute-start.7 = (bf16[144,256]{1,0:T(8,128)(2,1)S(1)}, bf16[144,256]{1,0:T(8,128)(2,1)S(1)}, u32[]{:S(2)}, u32[]{:S(2)}) collective-permute-start(bf16[144,256]{1,0:T(8,128)(2,1)S(1)} %get-tuple-element.24.sent_ref), channel_id=1, source_target_pairs={{0,4},{1,9},{2,6},{3,11},{4,0},{5,13},{6,2},{7,15},{8,12},{9,1},{1... | collective-permute-start | bytes 221192 | tf_op jit(solution)/shard_map/ppermute | solution.py:215
  28.1 4.4 %collective-permute-start.10 = (bf16[128,256]{1,0:T(8,128)(2,1)S(1)}, bf16[128,256]{1,0:T(8,128)(2,1)S(1)}, u32[]{:S(2)}, u32[]{:S(2)}) collective-permute-start(bf16[128,256]{1,0:T(8,128)(2,1)S(1)} %shard_map.110.part_ref), channel_id=1, source_target_pairs={{0,4},{1,9},{2,6},{3,11},{4,0},{5,13},{6,2},{7,15},{8,12},{9,1},{1... | collective-permute-start | bytes 196616 | tf_op jit(solution)/shard_map/ppermute | solution.py:215
  28.3 8.2 %collective-permute-start.8 = (bf16[144,256]{1,0:T(8,128)(2,1)S(1)}, bf16[144,256]{1,0:T(8,128)(2,1)S(1)}, u32[]{:S(2)}, u32[]{:S(2)}) collective-permute-start(bf16[144,256]{1,0:T(8,128)(2,1)S(1)} %shard_map.108.sent_ref), channel_id=1, source_target_pairs={{0,8},{1,5},{2,10},{3,7},{4,12},{5,1},{6,14},{7,3},{8,0},{9,13},{1... | collective-permute-start | bytes 221192 | tf_op jit(solution)/shard_map/ppermute | solution.py:215
  32.0 4.5 %collective-permute-start.12 = (bf16[128,256]{1,0:T(8,128)(2,1)S(1)}, bf16[128,256]{1,0:T(8,128)(2,1)S(1)}, u32[]{:S(2)}, u32[]{:S(2)}) collective-permute-start(bf16[128,256]{1,0:T(8,128)(2,1)S(1)} %get-tuple-element.27), channel_id=1, source_target_pairs={{0,4},{1,9},{2,6},{3,11},{4,0},{5,13},{6,2},{7,15},{8,12},{9,1},{1... | collective-permute-start | bytes 196616 | tf_op jit(solution)/shard_map/ppermute | solution.py:215
  32.6 3.9 %collective-permute-start.11 = (bf16[128,256]{1,0:T(8,128)(2,1)S(1)}, bf16[128,256]{1,0:T(8,128)(2,1)S(1)}, u32[]{:S(2)}, u32[]{:S(2)}) collective-permute-start(bf16[128,256]{1,0:T(8,128)(2,1)S(1)} %shard_map.111.mine_ref), channel_id=1, source_target_pairs={{0,1},{1,0},{2,3},{3,2},{4,5},{5,4},{6,7},{7,6},{8,9},{9,8},{10,11... | collective-permute-start | bytes 196616 | tf_op jit(solution)/shard_map/ppermute | solution.py:206

commit v14 on v13

--- a/solution.py
+++ b/solution.py
@@ -73,10 +73,9 @@
 def transpose_kernel(n_row):
     def body(a_ref, at_ref):
         tile = at_ref.shape[0] // n_row
-        core = lax.rem(lax.axis_index("col"), 2)
 
         def turn(p, carry):
-            place = jnp.where(core == 0, reversed_bits(p, n_row), p)
+            place = reversed_bits(p, n_row)
             here = a_ref[:, pl.ds(pl.multiple_of(p * tile, tile), tile)]
             at_ref[pl.ds(pl.multiple_of(place * tile, tile), tile), :] = here.T
             return carry
@@ -204,15 +203,6 @@
 
 def swap(x, axis, n, by):
     return lax.ppermute(x, axis, [(i, i ^ by) for i in range(n)])
-
-
-def step(x, n_row, n_col, by, first=0):
-    pairs = []
-    for i in range(n_row):
-        for j in range(n_col):
-            bit = by if j % 2 == first else n_row // 2 // by
-            pairs.append((i * n_col + j, (i ^ bit) * n_col + j))
-    return lax.ppermute(x, ("row", "col"), pairs)
 
 
 def deal(xs, axis):
@@ -273,8 +263,8 @@
     )(at, keep, got)
     terms, by = [(keep, 0, live)], 1
     while True:
-        other = step(part, n_row, n_col, by, 1)
-        sent, gots = sends[-1], [step(x, n_row, n_col, by) for x in reversed(sends)][::-1]
+        other = swap(part, "row", n_row, n_row // 2 // by)
+        sent, gots = sends[-1], [swap(x, "row", n_row, by) for x in reversed(sends)][::-1]
         terms += [(x, i * size, size) for i, x in enumerate(gots)]
         part = call(part_kernel, shape(piece, width), count=2)(part, other)
         by *= 2

time: 37.4 us -> 36.1 us (0.965)
  waiting for transfers between devices: 14.9 us -> 14.1 us
  starting transfers between devices: 16.7 us -> 16.2 us
    ppermute x5 -> x0, starting transfers between devices: 7.56 us -> none  [step(): return lax.ppermute(x, ('row', 'col'), pairs)]
    ppermute x5 -> x0, waiting for transfers between devices: 7.37 us -> none  [step(): return lax.ppermute(x, ('row', 'col'), pairs)]
    ppermute x8 -> x13, starting transfers between devices: 9.16 us -> 16.2 us  [swap(): return lax.ppermute(x, axis, [(i, i ^ by) for i in range(n)])]
    ppermute x8 -> x13, waiting for transfers between devices: 7.56 us -> 14.1 us  [swap(): return lax.ppermute(x, axis, [(i, i ^ by) for i in range(n)])]
  transfers between devices with their start and end apart: 13 -> 13, of which waited for: 7 -> 8; matrix products, arithmetic and copies ran while one was open for 0% -> 0% of each run, Pallas kernels for 4% -> 4%
where the time goes in v14:
time: 36.1 us; the launch traced here: 35.9 us
  starting transfers between devices  16.2 us (45%)
  waiting for transfers between devices  14.1 us (39%)
  Pallas kernels  3.17 us (9%)
  local copies, waits for them, and re-layouts  1.66 us (5%)
  between operations  0.77 us (2%)
    ppermute x13, starting transfers between devices, swap(): return lax.ppermute(x, axis, [(i, i ^ by) for i in range(n)])  16.2 us
    ppermute x13, waiting for transfers between devices, swap(): return lax.ppermute(x, axis, [(i, i ^ by) for i in range(n)])  14.1 us
    unnamed x14, local copies, waits for them, and re-layouts  1.65 us
    pallas_call x1, Pallas kernels, shards(): call(dense_kernel(n_chip), shape(n_col * tile, n_row * tile), count=3, sm...  0.81 us
    pallas_call x1, Pallas kernels, shards(): call(last_kernel, (shape(tile, width), shape(tile, width), shape(width, w...  0.78 us
  transfers between devices with their start and end apart: 13, of which 8 were waited for; matrix products, arithmetic and copies ran while one was open for 0% of the time, Pallas kernels for 4%

profile of v14, /device:TPU:0, one launch (start us, length us, event | category | flops | bytes accessed | tf_op | source)
XLA Modules:
  0.0 35.9 jit_solution(1663669193612182603)
XLA Ops:
  0.6 5.1 %collective-permute-start = (bf16[128,256]{1,0:T(8,128)(2,1)}, bf16[128,256]{1,0:T(8,128)(2,1)S(1)}, u32[]{:S(2)}, u32[]{:S(2)}) collective-permute-start(bf16[128,256]{1,0:T(8,128)(2,1)} %refs_3_.1), channel_id=1, source_target_pairs={{0,12},{4,8},{8,4},{12,0},{1,13},{5,9},{9,5},{13,1},{2,14},{6,10},... | collective-permute-start | bytes 196616 | tf_op jit(solution)/shard_map/ppermute | solution.py:205
  5.7 0.0 collective-permute-start.1
  5.7 0.6 %collective-permute-start.2 = (bf16[128,256]{1,0:T(8,128)(2,1)}, bf16[128,256]{1,0:T(8,128)(2,1)S(1)}, u32[]{:S(2)}, u32[]{:S(2)}) collective-permute-start(bf16[128,256]{1,0:T(8,128)(2,1)} %refs_3_.1), channel_id=1, source_target_pairs={{0,4},{4,0},{8,12},{12,8},{1,5},{5,1},{9,13},{13,9},{2,6},{6,2},{1... | collective-permute-start | bytes 196616 | tf_op jit(solution)/shard_map/ppermute | solution.py:205
  6.4 1.6 %collective-permute-start.3 = (bf16[128,256]{1,0:T(8,128)(2,1)}, bf16[128,256]{1,0:T(8,128)(2,1)S(1)}, u32[]{:S(2)}, u32[]{:S(2)}) collective-permute-start(bf16[128,256]{1,0:T(8,128)(2,1)} %refs_2_.1), channel_id=1, source_target_pairs={{0,2},{1,3},{2,0},{3,1},{4,6},{5,7},{6,4},{7,5},{8,10},{9,11},{10,... | collective-permute-start | bytes 196616 | tf_op jit(solution)/shard_map/ppermute | solution.py:205
  8.0 0.0 copy-start.4
  8.0 0.0 copy-start.5
  8.0 0.7 %copy-done.4 = s32[4,1,2]{0,2,1:T(2,128)S(1)} copy-done((s32[4,1,2]{0,2,1:T(2,128)S(1)}, s32[4,1,2]{0,2,1:T(2,128)}, u32[]{:S(2)}) %copy-start.4) | copy-done | bytes 56
  8.7 0.0 copy-done.5
  8.7 0.0 copy-start
  8.7 0.9 %copy-done = bf16[4,1,2,128,128]{4,3,2,1,0:T(8,128)(2,1)S(1)} copy-done((bf16[4,1,2,128,128]{4,3,2,1,0:T(8,128)(2,1)S(1)}, bf16[4,1,2,128,128]{4,3,2,1,0:T(8,128)(2,1)}, u32[]{:S(2)}) %copy-start) | copy-done | bytes 262168
  9.7 0.0 copy-start.3
  9.7 0.8 %shard_map.102.a_ref = bf16[512,512]{1,0:T(8,128)(2,1)S(1)} custom-call(s32[1,2,4]{2,1,0:T(2,128)S(1)} %bitcast.3, s32[1,4]{1,0:T(1,128)S(1)} %bitcast.4, bf16[4,1,2,128,128]{4,3,2,1,0:T(8,128)(2,1)S(1)} %copy-done), custom_call_target="tpu_custom_call" | custom-call | tf_op jit(solution)/shard_map/pallas_call | solution.py:226
  10.5 0.0 collective-permute-done.refs_0_
  10.5 1.1 %collective-permute-done.1.refs_1_ = bf16[128,256]{1,0:T(8,128)(2,1)S(1)} collective-permute-done((bf16[128,256]{1,0:T(8,128)(2,1)}, bf16[128,256]{1,0:T(8,128)(2,1)S(1)}, u32[]{:S(2)}, u32[]{:S(2)}) %collective-permute-start.1) | collective-permute-done | bytes 65568 | tf_op jit(solution)/shard_map/ppermute | solution.py:205
  11.6 0.0 collective-permute-done.2.refs_2_
  11.6 0.0 collective-permute-done.3.refs_4_
  11.6 0.0 copy-done.3
  11.6 0.3 shard_map.103
  11.9 0.1 collective-permute-start.4
  12.0 1.3 %collective-permute-done.4.got_ref = bf16[256,256]{1,0:T(8,128)(2,1)S(1)} collective-permute-done((bf16[256,256]{1,0:T(8,128)(2,1)S(1)}, bf16[256,256]{1,0:T(8,128)(2,1)S(1)}, u32[]{:S(2)}, u32[]{:S(2)}) %collective-permute-start.4) | collective-permute-done | bytes 131104 | tf_op jit(solution)/shard_map/ppermute | solution.py:205
  13.3 0.0 copy-start.6
  13.3 0.0 copy-start.1
  13.3 0.0 copy-start.2
  13.4 1.6 %collective-permute-start.5 = (bf16[256,256]{1,0:T(8,128)(2,1)S(1)}, bf16[256,256]{1,0:T(8,128)(2,1)S(1)}, u32[]{:S(2)}, u32[]{:S(2)}) collective-permute-start(bf16[256,256]{1,0:T(8,128)(2,1)S(1)} %shard_map.104.refs_0_), channel_id=1, source_target_pairs={{0,2},{1,3},{2,0},{3,1},{4,6},{5,7},{6,4},{7,5},{8,10},{9,11},{10,... | collective-permute-start | bytes 393224 | tf_op jit(solution)/shard_map/ppermute | solution.py:205
  14.9 0.3 shard_map.105.refs_4_.at_ref
  15.3 0.0 copy-done.6
  15.3 3.7 %collective-permute-done.5.refs_1_ = bf16[256,256]{1,0:T(8,128)(2,1)S(1)} collective-permute-done((bf16[256,256]{1,0:T(8,128)(2,1)S(1)}, bf16[256,256]{1,0:T(8,128)(2,1)S(1)}, u32[]{:S(2)}, u32[]{:S(2)}) %collective-permute-start.5) | collective-permute-done | bytes 131104 | tf_op jit(solution)/shard_map/ppermute | solution.py:205
  19.0 0.0 copy-done.1
  19.0 0.0 copy-done.2
  19.0 0.5 %shard_map.106 = (bf16[128,256]{1,0:T(8,128)(2,1)S(1)}, bf16[272,256]{1,0:T(8,128)(2,1)S(1)}, bf16[128,256]{1,0:T(8,128)(2,1)S(1)}, bf16[400,256]{1,0:T(8,128)(2,1)S(1)}) custom-call(bf16[256,256]{1,0:T(8,128)(2,1)S(1)} %copy-done.1, bf16[1,256]{1,0:T(2,128)(2,1)S(1)} %reshape.14.b_ref, bf16[256,256]{1,0:T(8,128)(2,1)S(1)} %shard_map.104.refs_0_, ...), custom_call_target="tpu_custom_call" | custom-call | tf_op jit(solution)/shard_map/pallas_call | solution.py:240
  19.5 0.1 collective-permute-start.6
  19.6 1.4 %collective-permute-done.6.got_ref = bf16[400,256]{1,0:T(8,128)(2,1)S(1)} collective-permute-done((bf16[400,256]{1,0:T(8,128)(2,1)S(1)}, bf16[400,256]{1,0:T(8,128)(2,1)S(1)}, u32[]{:S(2)}, u32[]{:S(2)}) %collective-permute-start.6) | collective-permute-done | bytes 204832 | tf_op jit(solution)/shard_map/ppermute | solution.py:205
  21.0 1.6 %collective-permute-start.9 = (bf16[128,256]{1,0:T(8,128)(2,1)S(1)}, bf16[128,256]{1,0:T(8,128)(2,1)S(1)}, u32[]{:S(2)}, u32[]{:S(2)}) collective-permute-start(bf16[128,256]{1,0:T(8,128)(2,1)S(1)} %shard_map.109.part_ref), channel_id=1, source_target_pairs={{0,8},{4,12},{8,0},{12,4},{1,9},{5,13},{9,1},{13,5},{2,10},{6,14},... | collective-permute-start | bytes 196616 | tf_op jit(solution)/shard_map/ppermute | solution.py:205
  22.7 0.3 shard_map.107
  23.0 2.1 %collective-permute-start.7 = (bf16[144,256]{1,0:T(8,128)(2,1)S(1)}, bf16[144,256]{1,0:T(8,128)(2,1)S(1)}, u32[]{:S(2)}, u32[]{:S(2)}) collective-permute-start(bf16[144,256]{1,0:T(8,128)(2,1)S(1)} %get-tuple-element.24.sent_ref), channel_id=1, source_target_pairs={{0,4},{4,0},{8,12},{12,8},{1,5},{5,1},{9,13},{13,9},{2,6},{6,2},{1... | collective-permute-start | bytes 221192 | tf_op jit(solution)/shard_map/ppermute | solution.py:205
  25.1 2.5 %collective-permute-done.9.got_ref = bf16[128,256]{1,0:T(8,128)(2,1)S(1)} collective-permute-done((bf16[128,256]{1,0:T(8,128)(2,1)S(1)}, bf16[128,256]{1,0:T(8,128)(2,1)S(1)}, u32[]{:S(2)}, u32[]{:S(2)}) %collective-permute-start.9) | collective-permute-done | bytes 65568 | tf_op jit(solution)/shard_map/ppermute | solution.py:205
  27.6 0.3 collective-permute-start.10
  27.9 0.2 collective-permute-done.7.got_ref.refs_1_
  28.2 2.7 %collective-permute-start.8 = (bf16[144,256]{1,0:T(8,128)(2,1)S(1)}, bf16[144,256]{1,0:T(8,128)(2,1)S(1)}, u32[]{:S(2)}, u32[]{:S(2)}) collective-permute-start(bf16[144,256]{1,0:T(8,128)(2,1)S(1)} %shard_map.108.sent_ref), channel_id=1, source_target_pairs={{0,8},{4,12},{8,0},{12,4},{1,9},{5,13},{9,1},{13,5},{2,10},{6,14},... | collective-permute-start | bytes 221192 | tf_op jit(solution)/shard_map/ppermute | solution.py:205
  30.9 0.3 collective-permute-start.12
  31.2 1.5 %collective-permute-done.10.got_ref = bf16[128,256]{1,0:T(8,128)(2,1)S(1)} collective-permute-done((bf16[128,256]{1,0:T(8,128)(2,1)S(1)}, bf16[128,256]{1,0:T(8,128)(2,1)S(1)}, u32[]{:S(2)}, u32[]{:S(2)}) %collective-permute-start.10) | collective-permute-done | bytes 65568 | tf_op jit(solution)/shard_map/ppermute | solution.py:205
  32.7 0.1 collective-permute-start.11
  32.8 2.3 %collective-permute-done.12.refs_1_ = bf16[128,256]{1,0:T(8,128)(2,1)S(1)} collective-permute-done((bf16[128,256]{1,0:T(8,128)(2,1)S(1)}, bf16[128,256]{1,0:T(8,128)(2,1)S(1)}, u32[]{:S(2)}, u32[]{:S(2)}) %collective-permute-start.12) | collective-permute-done | bytes 65568 | tf_op jit(solution)/shard_map/ppermute | solution.py:205
  35.2 0.0 collective-permute-done.8.line_ref.refs_2_
  35.2 0.0 collective-permute-done.11.got_ref
  35.2 0.8 %shard_map.112 = (bf16[128,256]{1,0:T(8,128)(2,1)}, bf16[128,256]{1,0:T(8,128)(2,1)}, f32[256,256]{1,0:T(8,128)}, f32[1,256]{1,0:T(1,128)}) custom-call(bf16[128,256]{1,0:T(8,128)(2,1)S(1)} %get-tuple-element.21.act_ref, bf16[144,256]{1,0:T(8,128)(2,1)S(1)} %shard_map.108.sent_ref, bf16[144,256]{1,0:T(8,128)(2,1)S(1)} %collective-permute-done.8.line_ref.refs_2_, ...), custom_call_target="tpu_custom_call" | custom-call | tf_op jit(solution)/shard_map/pallas_call | solution.py:287
  (6 shorter events, 0.1 us)
Async XLA Ops:
  0.6 9.8 %collective-permute-start = (bf16[128,256]{1,0:T(8,128)(2,1)}, bf16[128,256]{1,0:T(8,128)(2,1)S(1)}, u32[]{:S(2)}, u32[]{:S(2)}) collective-permute-start(bf16[128,256]{1,0:T(8,128)(2,1)} %refs_3_.1), channel_id=1, source_target_pairs={{0,12},{4,8},{8,4},{12,0},{1,13},{5,9},{9,5},{13,1},{2,14},{6,10},... | collective-permute-start | bytes 196616 | tf_op jit(solution)/shard_map/ppermute | solution.py:205
  5.7 5.8 %collective-permute-start.1 = (bf16[128,256]{1,0:T(8,128)(2,1)}, bf16[128,256]{1,0:T(8,128)(2,1)S(1)}, u32[]{:S(2)}, u32[]{:S(2)}) collective-permute-start(bf16[128,256]{1,0:T(8,128)(2,1)} %refs_3_.1), channel_id=1, source_target_pairs={{0,8},{4,12},{8,0},{12,4},{1,9},{5,13},{9,1},{13,5},{2,10},{6,14},... | collective-permute-start | bytes 196616 | tf_op jit(solution)/shard_map/ppermute | solution.py:205
  5.7 5.8 %collective-permute-start.2 = (bf16[128,256]{1,0:T(8,128)(2,1)}, bf16[128,256]{1,0:T(8,128)(2,1)S(1)}, u32[]{:S(2)}, u32[]{:S(2)}) collective-permute-start(bf16[128,256]{1,0:T(8,128)(2,1)} %refs_3_.1), channel_id=1, source_target_pairs={{0,4},{4,0},{8,12},{12,8},{1,5},{5,1},{9,13},{13,9},{2,6},{6,2},{1... | collective-permute-start | bytes 196616 | tf_op jit(solution)/shard_map/ppermute | solution.py:205
  6.4 5.2 %collective-permute-start.3 = (bf16[128,256]{1,0:T(8,128)(2,1)}, bf16[128,256]{1,0:T(8,128)(2,1)S(1)}, u32[]{:S(2)}, u32[]{:S(2)}) collective-permute-start(bf16[128,256]{1,0:T(8,128)(2,1)} %refs_2_.1), channel_id=1, source_target_pairs={{0,2},{1,3},{2,0},{3,1},{4,6},{5,7},{6,4},{7,5},{8,10},{9,11},{10,... | collective-permute-start | bytes 196616 | tf_op jit(solution)/shard_map/ppermute | solution.py:205
  8.0 0.7 %copy-start.4 = (s32[4,1,2]{0,2,1:T(2,128)S(1)}, s32[4,1,2]{0,2,1:T(2,128)}, u32[]{:S(2)}) copy-start(s32[4,1,2]{0,2,1:T(2,128)} %param.9) | copy-start | bytes 100
  8.0 0.7 %copy-start.5 = (s32[4,1]{0,1:T(1,128)S(1)}, s32[4,1]{0,1:T(1,128)}, u32[]{:S(2)}) copy-start(s32[4,1]{0,1:T(1,128)} %param.10) | copy-start | bytes 52
  8.7 1.0 %copy-start = (bf16[4,1,2,128,128]{4,3,2,1,0:T(8,128)(2,1)S(1)}, bf16[4,1,2,128,128]{4,3,2,1,0:T(8,128)(2,1)}, u32[]{:S(2)}) copy-start(bf16[4,1,2,128,128]{4,3,2,1,0:T(8,128)(2,1)} %tiles_ref.1) | copy-start | bytes 786436
  9.7 1.9 %copy-start.3 = (bf16[128,256]{1,0:T(8,128)(2,1)S(1)}, bf16[128,256]{1,0:T(8,128)(2,1)}, u32[]{:S(2)}) copy-start(bf16[128,256]{1,0:T(8,128)(2,1)} %refs_3_.1) | copy-start | bytes 196612
  11.9 1.4 %collective-permute-start.4 = (bf16[256,256]{1,0:T(8,128)(2,1)S(1)}, bf16[256,256]{1,0:T(8,128)(2,1)S(1)}, u32[]{:S(2)}, u32[]{:S(2)}) collective-permute-start(bf16[256,256]{1,0:T(8,128)(2,1)S(1)} %get-tuple-element.19), channel_id=1, source_target_pairs={{0,1},{1,0},{2,3},{3,2},{4,5},{5,4},{6,7},{7,6},{8,9},{9,8},{10,11... | collective-permute-start | bytes 393224 | tf_op jit(solution)/shard_map/ppermute | solution.py:205
  13.3 1.9 %copy-start.6 = (bf16[256]{0:T(256)(128)(2,1)S(1)}, bf16[256]{0:T(256)(128)(2,1)}, u32[]{:S(2)}) copy-start(bf16[256]{0:T(256)(128)(2,1)} %param.12) | copy-start | bytes 1540
  13.3 5.6 %copy-start.1 = (bf16[256,256]{1,0:T(8,128)(2,1)S(1)}, bf16[256,256]{1,0:T(8,128)(2,1)}, u32[]{:S(2)}) copy-start(bf16[256,256]{1,0:T(8,128)(2,1)} %w_ref.1) | copy-start | bytes 393220
  13.3 5.6 %copy-start.2 = (bf16[128,256]{1,0:T(8,128)(2,1)S(1)}, bf16[128,256]{1,0:T(8,128)(2,1)}, u32[]{:S(2)}) copy-start(bf16[128,256]{1,0:T(8,128)(2,1)} %refs_2_.1) | copy-start | bytes 196612
  13.4 5.6 %collective-permute-start.5 = (bf16[256,256]{1,0:T(8,128)(2,1)S(1)}, bf16[256,256]{1,0:T(8,128)(2,1)S(1)}, u32[]{:S(2)}, u32[]{:S(2)}) collective-permute-start(bf16[256,256]{1,0:T(8,128)(2,1)S(1)} %shard_map.104.refs_0_), channel_id=1, source_target_pairs={{0,2},{1,3},{2,0},{3,1},{4,6},{5,7},{6,4},{7,5},{8,10},{9,11},{10,... | collective-permute-start | bytes 393224 | tf_op jit(solution)/shard_map/ppermute | solution.py:205
  19.5 1.5 %collective-permute-start.6 = (bf16[400,256]{1,0:T(8,128)(2,1)S(1)}, bf16[400,256]{1,0:T(8,128)(2,1)S(1)}, u32[]{:S(2)}, u32[]{:S(2)}) collective-permute-start(bf16[400,256]{1,0:T(8,128)(2,1)S(1)} %get-tuple-element.23), channel_id=1, source_target_pairs={{0,1},{1,0},{2,3},{3,2},{4,5},{5,4},{6,7},{7,6},{8,9},{9,8},{10,11... | collective-permute-start | bytes 614408 | tf_op jit(solution)/shard_map/ppermute | solution.py:205
  21.0 6.5 %collective-permute-start.9 = (bf16[128,256]{1,0:T(8,128)(2,1)S(1)}, bf16[128,256]{1,0:T(8,128)(2,1)S(1)}, u32[]{:S(2)}, u32[]{:S(2)}) collective-permute-start(bf16[128,256]{1,0:T(8,128)(2,1)S(1)} %shard_map.109.part_ref), channel_id=1, source_target_pairs={{0,8},{4,12},{8,0},{12,4},{1,9},{5,13},{9,1},{13,5},{2,10},{6,14},... | collective-permute-start | bytes 196616 | tf_op jit(solution)/shard_map/ppermute | solution.py:205
  23.0 5.2 %collective-permute-start.7 = (bf16[144,256]{1,0:T(8,128)(2,1)S(1)}, bf16[144,256]{1,0:T(8,128)(2,1)S(1)}, u32[]{:S(2)}, u32[]{:S(2)}) collective-permute-start(bf16[144,256]{1,0:T(8,128)(2,1)S(1)} %get-tuple-element.24.sent_ref), channel_id=1, source_target_pairs={{0,4},{4,0},{8,12},{12,8},{1,5},{5,1},{9,13},{13,9},{2,6},{6,2},{1... | collective-permute-start | bytes 221192 | tf_op jit(solution)/shard_map/ppermute | solution.py:205
  27.6 5.1 %collective-permute-start.10 = (bf16[128,256]{1,0:T(8,128)(2,1)S(1)}, bf16[128,256]{1,0:T(8,128)(2,1)S(1)}, u32[]{:S(2)}, u32[]{:S(2)}) collective-permute-start(bf16[128,256]{1,0:T(8,128)(2,1)S(1)} %shard_map.110.part_ref), channel_id=1, source_target_pairs={{0,4},{4,0},{8,12},{12,8},{1,5},{5,1},{9,13},{13,9},{2,6},{6,2},{1... | collective-permute-start | bytes 196616 | tf_op jit(solution)/shard_map/ppermute | solution.py:205
  28.2 7.0 %collective-permute-start.8 = (bf16[144,256]{1,0:T(8,128)(2,1)S(1)}, bf16[144,256]{1,0:T(8,128)(2,1)S(1)}, u32[]{:S(2)}, u32[]{:S(2)}) collective-permute-start(bf16[144,256]{1,0:T(8,128)(2,1)S(1)} %shard_map.108.sent_ref), channel_id=1, source_target_pairs={{0,8},{4,12},{8,0},{12,4},{1,9},{5,13},{9,1},{13,5},{2,10},{6,14},... | collective-permute-start | bytes 221192 | tf_op jit(solution)/shard_map/ppermute | solution.py:205
  30.9 4.3 %collective-permute-start.12 = (bf16[128,256]{1,0:T(8,128)(2,1)S(1)}, bf16[128,256]{1,0:T(8,128)(2,1)S(1)}, u32[]{:S(2)}, u32[]{:S(2)}) collective-permute-start(bf16[128,256]{1,0:T(8,128)(2,1)S(1)} %get-tuple-element.27), channel_id=1, source_target_pairs={{0,4},{4,0},{8,12},{12,8},{1,5},{5,1},{9,13},{13,9},{2,6},{6,2},{1... | collective-permute-start | bytes 196616 | tf_op jit(solution)/shard_map/ppermute | solution.py:205
  32.7 2.4 %collective-permute-start.11 = (bf16[128,256]{1,0:T(8,128)(2,1)S(1)}, bf16[128,256]{1,0:T(8,128)(2,1)S(1)}, u32[]{:S(2)}, u32[]{:S(2)}) collective-permute-start(bf16[128,256]{1,0:T(8,128)(2,1)S(1)} %shard_map.111.mine_ref), channel_id=1, source_target_pairs={{0,1},{1,0},{2,3},{3,2},{4,5},{5,4},{6,7},{7,6},{8,9},{9,8},{10,11... | collective-permute-start | bytes 196616 | tf_op jit(solution)/shard_map/ppermute | solution.py:205

commit v15 on v14

--- a/solution.py
+++ b/solution.py
@@ -263,7 +263,7 @@
     )(at, keep, got)
     terms, by = [(keep, 0, live)], 1
     while True:
-        other = swap(part, "row", n_row, n_row // 2 // by)
+        other = swap(part, "row", n_row, by)
         sent, gots = sends[-1], [swap(x, "row", n_row, by) for x in reversed(sends)][::-1]
         terms += [(x, i * size, size) for i, x in enumerate(gots)]
         part = call(part_kernel, shape(piece, width), count=2)(part, other)

time: 36.1 us -> 35.7 us (0.989)
  no operation moved by 1% of the time
where the time goes in v15:
time: 35.7 us; the launch traced here: 35.5 us
  starting transfers between devices  16 us (45%)
  waiting for transfers between devices  13.9 us (39%)
  Pallas kernels  3.14 us (9%)
  local copies, waits for them, and re-layouts  1.66 us (5%)
  between operations  0.77 us (2%)
    ppermute x13, starting transfers between devices, swap(): return lax.ppermute(x, axis, [(i, i ^ by) for i in range(n)])  16 us
    ppermute x13, waiting for transfers between devices, swap(): return lax.ppermute(x, axis, [(i, i ^ by) for i in range(n)])  13.9 us
    unnamed x14, local copies, waits for them, and re-layouts  1.65 us
    pallas_call x1, Pallas kernels, shards(): call(dense_kernel(n_chip), shape(n_col * tile, n_row * tile), count=3, sm...  0.79 us
    pallas_call x1, Pallas kernels, shards(): call(last_kernel, (shape(tile, width), shape(tile, width), shape(width, w...  0.77 us
  transfers between devices with their start and end apart: 13, of which 8 were waited for; matrix products, arithmetic and copies ran while one was open for 0% of the time, Pallas kernels for 4%

profile of v15, /device:TPU:0, one launch (start us, length us, event | category | flops | bytes accessed | tf_op | source)
XLA Modules:
  0.0 35.5 jit_solution(1171485111477452306)
XLA Ops:
  0.6 5.1 %collective-permute-start = (bf16[128,256]{1,0:T(8,128)(2,1)}, bf16[128,256]{1,0:T(8,128)(2,1)S(1)}, u32[]{:S(2)}, u32[]{:S(2)}) collective-permute-start(bf16[128,256]{1,0:T(8,128)(2,1)} %refs_3_.1), channel_id=1, source_target_pairs={{0,12},{4,8},{8,4},{12,0},{1,13},{5,9},{9,5},{13,1},{2,14},{6,10},... | collective-permute-start | bytes 196616 | tf_op jit(solution)/shard_map/ppermute | solution.py:205
  5.7 0.0 collective-permute-start.1
  5.7 0.6 %collective-permute-start.2 = (bf16[128,256]{1,0:T(8,128)(2,1)}, bf16[128,256]{1,0:T(8,128)(2,1)S(1)}, u32[]{:S(2)}, u32[]{:S(2)}) collective-permute-start(bf16[128,256]{1,0:T(8,128)(2,1)} %refs_3_.1), channel_id=1, source_target_pairs={{0,4},{4,0},{8,12},{12,8},{1,5},{5,1},{9,13},{13,9},{2,6},{6,2},{1... | collective-permute-start | bytes 196616 | tf_op jit(solution)/shard_map/ppermute | solution.py:205
  6.4 1.6 %collective-permute-start.3 = (bf16[128,256]{1,0:T(8,128)(2,1)}, bf16[128,256]{1,0:T(8,128)(2,1)S(1)}, u32[]{:S(2)}, u32[]{:S(2)}) collective-permute-start(bf16[128,256]{1,0:T(8,128)(2,1)} %refs_2_.1), channel_id=1, source_target_pairs={{0,2},{1,3},{2,0},{3,1},{4,6},{5,7},{6,4},{7,5},{8,10},{9,11},{10,... | collective-permute-start | bytes 196616 | tf_op jit(solution)/shard_map/ppermute | solution.py:205
  8.0 0.0 copy-start.4
  8.0 0.0 copy-start.5
  8.0 0.7 %copy-done.4 = s32[4,1,2]{0,2,1:T(2,128)S(1)} copy-done((s32[4,1,2]{0,2,1:T(2,128)S(1)}, s32[4,1,2]{0,2,1:T(2,128)}, u32[]{:S(2)}) %copy-start.4) | copy-done | bytes 56
  8.7 0.0 copy-done.5
  8.7 0.0 copy-start
  8.7 0.9 %copy-done = bf16[4,1,2,128,128]{4,3,2,1,0:T(8,128)(2,1)S(1)} copy-done((bf16[4,1,2,128,128]{4,3,2,1,0:T(8,128)(2,1)S(1)}, bf16[4,1,2,128,128]{4,3,2,1,0:T(8,128)(2,1)}, u32[]{:S(2)}) %copy-start) | copy-done | bytes 262168
  9.7 0.0 copy-start.3
  9.7 0.8 %shard_map.102.a_ref = bf16[512,512]{1,0:T(8,128)(2,1)S(1)} custom-call(s32[1,2,4]{2,1,0:T(2,128)S(1)} %bitcast.3, s32[1,4]{1,0:T(1,128)S(1)} %bitcast.4, bf16[4,1,2,128,128]{4,3,2,1,0:T(8,128)(2,1)S(1)} %copy-done), custom_call_target="tpu_custom_call" | custom-call | tf_op jit(solution)/shard_map/pallas_call | solution.py:226
  10.5 0.0 collective-permute-done.refs_0_
  10.5 1.1 %collective-permute-done.1.refs_1_ = bf16[128,256]{1,0:T(8,128)(2,1)S(1)} collective-permute-done((bf16[128,256]{1,0:T(8,128)(2,1)}, bf16[128,256]{1,0:T(8,128)(2,1)S(1)}, u32[]{:S(2)}, u32[]{:S(2)}) %collective-permute-start.1) | collective-permute-done | bytes 65568 | tf_op jit(solution)/shard_map/ppermute | solution.py:205
  11.6 0.0 collective-permute-done.2.refs_2_
  11.6 0.0 collective-permute-done.3.refs_4_
  11.6 0.0 copy-done.3
  11.6 0.3 shard_map.103
  11.9 0.1 collective-permute-start.4
  12.0 1.3 %collective-permute-done.4.got_ref = bf16[256,256]{1,0:T(8,128)(2,1)S(1)} collective-permute-done((bf16[256,256]{1,0:T(8,128)(2,1)S(1)}, bf16[256,256]{1,0:T(8,128)(2,1)S(1)}, u32[]{:S(2)}, u32[]{:S(2)}) %collective-permute-start.4) | collective-permute-done | bytes 131104 | tf_op jit(solution)/shard_map/ppermute | solution.py:205
  13.3 0.0 copy-start.6
  13.3 0.0 copy-start.1
  13.3 0.0 copy-start.2
  13.4 1.6 %collective-permute-start.5 = (bf16[256,256]{1,0:T(8,128)(2,1)S(1)}, bf16[256,256]{1,0:T(8,128)(2,1)S(1)}, u32[]{:S(2)}, u32[]{:S(2)}) collective-permute-start(bf16[256,256]{1,0:T(8,128)(2,1)S(1)} %shard_map.104.refs_0_), channel_id=1, source_target_pairs={{0,2},{1,3},{2,0},{3,1},{4,6},{5,7},{6,4},{7,5},{8,10},{9,11},{10,... | collective-permute-start | bytes 393224 | tf_op jit(solution)/shard_map/ppermute | solution.py:205
  14.9 0.3 shard_map.105.refs_4_.at_ref
  15.3 0.0 copy-done.6
  15.3 3.7 %collective-permute-done.5.refs_1_ = bf16[256,256]{1,0:T(8,128)(2,1)S(1)} collective-permute-done((bf16[256,256]{1,0:T(8,128)(2,1)S(1)}, bf16[256,256]{1,0:T(8,128)(2,1)S(1)}, u32[]{:S(2)}, u32[]{:S(2)}) %collective-permute-start.5) | collective-permute-done | bytes 131104 | tf_op jit(solution)/shard_map/ppermute | solution.py:205
  19.0 0.0 copy-done.1
  19.0 0.0 copy-done.2
  19.0 0.5 %shard_map.106 = (bf16[128,256]{1,0:T(8,128)(2,1)S(1)}, bf16[272,256]{1,0:T(8,128)(2,1)S(1)}, bf16[128,256]{1,0:T(8,128)(2,1)S(1)}, bf16[400,256]{1,0:T(8,128)(2,1)S(1)}) custom-call(bf16[256,256]{1,0:T(8,128)(2,1)S(1)} %copy-done.1, bf16[1,256]{1,0:T(2,128)(2,1)S(1)} %reshape.14.b_ref, bf16[256,256]{1,0:T(8,128)(2,1)S(1)} %shard_map.104.refs_0_, ...), custom_call_target="tpu_custom_call" | custom-call | tf_op jit(solution)/shard_map/pallas_call | solution.py:240
  19.5 0.1 collective-permute-start.6
  19.6 1.4 %collective-permute-done.6.got_ref = bf16[400,256]{1,0:T(8,128)(2,1)S(1)} collective-permute-done((bf16[400,256]{1,0:T(8,128)(2,1)S(1)}, bf16[400,256]{1,0:T(8,128)(2,1)S(1)}, u32[]{:S(2)}, u32[]{:S(2)}) %collective-permute-start.6) | collective-permute-done | bytes 204832 | tf_op jit(solution)/shard_map/ppermute | solution.py:205
  21.0 1.1 %collective-permute-start.9 = (bf16[128,256]{1,0:T(8,128)(2,1)S(1)}, bf16[128,256]{1,0:T(8,128)(2,1)S(1)}, u32[]{:S(2)}, u32[]{:S(2)}) collective-permute-start(bf16[128,256]{1,0:T(8,128)(2,1)S(1)} %shard_map.109.part_ref), channel_id=1, source_target_pairs={{0,4},{4,0},{8,12},{12,8},{1,5},{5,1},{9,13},{13,9},{2,6},{6,2},{1... | collective-permute-start | bytes 196616 | tf_op jit(solution)/shard_map/ppermute | solution.py:205
  22.2 0.3 shard_map.107
  22.5 1.0 %collective-permute-start.7 = (bf16[144,256]{1,0:T(8,128)(2,1)S(1)}, bf16[144,256]{1,0:T(8,128)(2,1)S(1)}, u32[]{:S(2)}, u32[]{:S(2)}) collective-permute-start(bf16[144,256]{1,0:T(8,128)(2,1)S(1)} %get-tuple-element.24.sent_ref), channel_id=1, source_target_pairs={{0,4},{4,0},{8,12},{12,8},{1,5},{5,1},{9,13},{13,9},{2,6},{6,2},{1... | collective-permute-start | bytes 221192 | tf_op jit(solution)/shard_map/ppermute | solution.py:205
  23.5 2.2 %collective-permute-done.9.got_ref = bf16[128,256]{1,0:T(8,128)(2,1)S(1)} collective-permute-done((bf16[128,256]{1,0:T(8,128)(2,1)S(1)}, bf16[128,256]{1,0:T(8,128)(2,1)S(1)}, u32[]{:S(2)}, u32[]{:S(2)}) %collective-permute-start.9) | collective-permute-done | bytes 65568 | tf_op jit(solution)/shard_map/ppermute | solution.py:205
  25.8 1.5 %collective-permute-start.10 = (bf16[128,256]{1,0:T(8,128)(2,1)S(1)}, bf16[128,256]{1,0:T(8,128)(2,1)S(1)}, u32[]{:S(2)}, u32[]{:S(2)}) collective-permute-start(bf16[128,256]{1,0:T(8,128)(2,1)S(1)} %shard_map.110.part_ref), channel_id=1, source_target_pairs={{0,8},{4,12},{8,0},{12,4},{1,9},{5,13},{9,1},{13,5},{2,10},{6,14},... | collective-permute-start | bytes 196616 | tf_op jit(solution)/shard_map/ppermute | solution.py:205
  27.3 0.0 collective-permute-done.7.got_ref.refs_1_
  27.3 2.8 %collective-permute-start.8 = (bf16[144,256]{1,0:T(8,128)(2,1)S(1)}, bf16[144,256]{1,0:T(8,128)(2,1)S(1)}, u32[]{:S(2)}, u32[]{:S(2)}) collective-permute-start(bf16[144,256]{1,0:T(8,128)(2,1)S(1)} %shard_map.108.sent_ref), channel_id=1, source_target_pairs={{0,8},{4,12},{8,0},{12,4},{1,9},{5,13},{9,1},{13,5},{2,10},{6,14},... | collective-permute-start | bytes 221192 | tf_op jit(solution)/shard_map/ppermute | solution.py:205
  30.1 0.5 %collective-permute-start.12 = (bf16[128,256]{1,0:T(8,128)(2,1)S(1)}, bf16[128,256]{1,0:T(8,128)(2,1)S(1)}, u32[]{:S(2)}, u32[]{:S(2)}) collective-permute-start(bf16[128,256]{1,0:T(8,128)(2,1)S(1)} %get-tuple-element.27), channel_id=1, source_target_pairs={{0,4},{4,0},{8,12},{12,8},{1,5},{5,1},{9,13},{13,9},{2,6},{6,2},{1... | collective-permute-start | bytes 196616 | tf_op jit(solution)/shard_map/ppermute | solution.py:205
  30.5 2.6 %collective-permute-done.10.got_ref = bf16[128,256]{1,0:T(8,128)(2,1)S(1)} collective-permute-done((bf16[128,256]{1,0:T(8,128)(2,1)S(1)}, bf16[128,256]{1,0:T(8,128)(2,1)S(1)}, u32[]{:S(2)}, u32[]{:S(2)}) %collective-permute-start.10) | collective-permute-done | bytes 65568 | tf_op jit(solution)/shard_map/ppermute | solution.py:205
  33.1 0.1 collective-permute-start.11
  33.2 1.3 %collective-permute-done.12.refs_1_ = bf16[128,256]{1,0:T(8,128)(2,1)S(1)} collective-permute-done((bf16[128,256]{1,0:T(8,128)(2,1)S(1)}, bf16[128,256]{1,0:T(8,128)(2,1)S(1)}, u32[]{:S(2)}, u32[]{:S(2)}) %collective-permute-start.12) | collective-permute-done | bytes 65568 | tf_op jit(solution)/shard_map/ppermute | solution.py:205
  34.5 0.2 collective-permute-done.8.line_ref.refs_2_
  34.7 0.0 collective-permute-done.11.got_ref
  34.7 0.8 %shard_map.112 = (bf16[128,256]{1,0:T(8,128)(2,1)}, bf16[128,256]{1,0:T(8,128)(2,1)}, f32[256,256]{1,0:T(8,128)}, f32[1,256]{1,0:T(1,128)}) custom-call(bf16[128,256]{1,0:T(8,128)(2,1)S(1)} %get-tuple-element.21.act_ref, bf16[144,256]{1,0:T(8,128)(2,1)S(1)} %shard_map.108.sent_ref, bf16[144,256]{1,0:T(8,128)(2,1)S(1)} %collective-permute-done.8.line_ref.refs_2_, ...), custom_call_target="tpu_custom_call" | custom-call | tf_op jit(solution)/shard_map/pallas_call | solution.py:287
  (6 shorter events, 0.1 us)
Async XLA Ops:
  0.6 9.8 %collective-permute-start = (bf16[128,256]{1,0:T(8,128)(2,1)}, bf16[128,256]{1,0:T(8,128)(2,1)S(1)}, u32[]{:S(2)}, u32[]{:S(2)}) collective-permute-start(bf16[128,256]{1,0:T(8,128)(2,1)} %refs_3_.1), channel_id=1, source_target_pairs={{0,12},{4,8},{8,4},{12,0},{1,13},{5,9},{9,5},{13,1},{2,14},{6,10},... | collective-permute-start | bytes 196616 | tf_op jit(solution)/shard_map/ppermute | solution.py:205
  5.7 5.8 %collective-permute-start.1 = (bf16[128,256]{1,0:T(8,128)(2,1)}, bf16[128,256]{1,0:T(8,128)(2,1)S(1)}, u32[]{:S(2)}, u32[]{:S(2)}) collective-permute-start(bf16[128,256]{1,0:T(8,128)(2,1)} %refs_3_.1), channel_id=1, source_target_pairs={{0,8},{4,12},{8,0},{12,4},{1,9},{5,13},{9,1},{13,5},{2,10},{6,14},... | collective-permute-start | bytes 196616 | tf_op jit(solution)/shard_map/ppermute | solution.py:205
  5.7 5.8 %collective-permute-start.2 = (bf16[128,256]{1,0:T(8,128)(2,1)}, bf16[128,256]{1,0:T(8,128)(2,1)S(1)}, u32[]{:S(2)}, u32[]{:S(2)}) collective-permute-start(bf16[128,256]{1,0:T(8,128)(2,1)} %refs_3_.1), channel_id=1, source_target_pairs={{0,4},{4,0},{8,12},{12,8},{1,5},{5,1},{9,13},{13,9},{2,6},{6,2},{1... | collective-permute-start | bytes 196616 | tf_op jit(solution)/shard_map/ppermute | solution.py:205
  6.4 5.2 %collective-permute-start.3 = (bf16[128,256]{1,0:T(8,128)(2,1)}, bf16[128,256]{1,0:T(8,128)(2,1)S(1)}, u32[]{:S(2)}, u32[]{:S(2)}) collective-permute-start(bf16[128,256]{1,0:T(8,128)(2,1)} %refs_2_.1), channel_id=1, source_target_pairs={{0,2},{1,3},{2,0},{3,1},{4,6},{5,7},{6,4},{7,5},{8,10},{9,11},{10,... | collective-permute-start | bytes 196616 | tf_op jit(solution)/shard_map/ppermute | solution.py:205
  8.0 0.7 %copy-start.4 = (s32[4,1,2]{0,2,1:T(2,128)S(1)}, s32[4,1,2]{0,2,1:T(2,128)}, u32[]{:S(2)}) copy-start(s32[4,1,2]{0,2,1:T(2,128)} %param.9) | copy-start | bytes 100
  8.0 0.7 %copy-start.5 = (s32[4,1]{0,1:T(1,128)S(1)}, s32[4,1]{0,1:T(1,128)}, u32[]{:S(2)}) copy-start(s32[4,1]{0,1:T(1,128)} %param.10) | copy-start | bytes 52
  8.7 1.0 %copy-start = (bf16[4,1,2,128,128]{4,3,2,1,0:T(8,128)(2,1)S(1)}, bf16[4,1,2,128,128]{4,3,2,1,0:T(8,128)(2,1)}, u32[]{:S(2)}) copy-start(bf16[4,1,2,128,128]{4,3,2,1,0:T(8,128)(2,1)} %tiles_ref.1) | copy-start | bytes 786436
  9.7 1.9 %copy-start.3 = (bf16[128,256]{1,0:T(8,128)(2,1)S(1)}, bf16[128,256]{1,0:T(8,128)(2,1)}, u32[]{:S(2)}) copy-start(bf16[128,256]{1,0:T(8,128)(2,1)} %refs_3_.1) | copy-start | bytes 196612
  11.9 1.4 %collective-permute-start.4 = (bf16[256,256]{1,0:T(8,128)(2,1)S(1)}, bf16[256,256]{1,0:T(8,128)(2,1)S(1)}, u32[]{:S(2)}, u32[]{:S(2)}) collective-permute-start(bf16[256,256]{1,0:T(8,128)(2,1)S(1)} %get-tuple-element.19), channel_id=1, source_target_pairs={{0,1},{1,0},{2,3},{3,2},{4,5},{5,4},{6,7},{7,6},{8,9},{9,8},{10,11... | collective-permute-start | bytes 393224 | tf_op jit(solution)/shard_map/ppermute | solution.py:205
  13.3 1.9 %copy-start.6 = (bf16[256]{0:T(256)(128)(2,1)S(1)}, bf16[256]{0:T(256)(128)(2,1)}, u32[]{:S(2)}) copy-start(bf16[256]{0:T(256)(128)(2,1)} %param.12) | copy-start | bytes 1540
  13.3 5.6 %copy-start.1 = (bf16[256,256]{1,0:T(8,128)(2,1)S(1)}, bf16[256,256]{1,0:T(8,128)(2,1)}, u32[]{:S(2)}) copy-start(bf16[256,256]{1,0:T(8,128)(2,1)} %w_ref.1) | copy-start | bytes 393220
  13.3 5.6 %copy-start.2 = (bf16[128,256]{1,0:T(8,128)(2,1)S(1)}, bf16[128,256]{1,0:T(8,128)(2,1)}, u32[]{:S(2)}) copy-start(bf16[128,256]{1,0:T(8,128)(2,1)} %refs_2_.1) | copy-start | bytes 196612
  13.4 5.6 %collective-permute-start.5 = (bf16[256,256]{1,0:T(8,128)(2,1)S(1)}, bf16[256,256]{1,0:T(8,128)(2,1)S(1)}, u32[]{:S(2)}, u32[]{:S(2)}) collective-permute-start(bf16[256,256]{1,0:T(8,128)(2,1)S(1)} %shard_map.104.refs_0_), channel_id=1, source_target_pairs={{0,2},{1,3},{2,0},{3,1},{4,6},{5,7},{6,4},{7,5},{8,10},{9,11},{10,... | collective-permute-start | bytes 393224 | tf_op jit(solution)/shard_map/ppermute | solution.py:205
  19.5 1.5 %collective-permute-start.6 = (bf16[400,256]{1,0:T(8,128)(2,1)S(1)}, bf16[400,256]{1,0:T(8,128)(2,1)S(1)}, u32[]{:S(2)}, u32[]{:S(2)}) collective-permute-start(bf16[400,256]{1,0:T(8,128)(2,1)S(1)} %get-tuple-element.23), channel_id=1, source_target_pairs={{0,1},{1,0},{2,3},{3,2},{4,5},{5,4},{6,7},{7,6},{8,9},{9,8},{10,11... | collective-permute-start | bytes 614408 | tf_op jit(solution)/shard_map/ppermute | solution.py:205
  21.0 4.7 %collective-permute-start.9 = (bf16[128,256]{1,0:T(8,128)(2,1)S(1)}, bf16[128,256]{1,0:T(8,128)(2,1)S(1)}, u32[]{:S(2)}, u32[]{:S(2)}) collective-permute-start(bf16[128,256]{1,0:T(8,128)(2,1)S(1)} %shard_map.109.part_ref), channel_id=1, source_target_pairs={{0,4},{4,0},{8,12},{12,8},{1,5},{5,1},{9,13},{13,9},{2,6},{6,2},{1... | collective-permute-start | bytes 196616 | tf_op jit(solution)/shard_map/ppermute | solution.py:205
  22.5 4.8 %collective-permute-start.7 = (bf16[144,256]{1,0:T(8,128)(2,1)S(1)}, bf16[144,256]{1,0:T(8,128)(2,1)S(1)}, u32[]{:S(2)}, u32[]{:S(2)}) collective-permute-start(bf16[144,256]{1,0:T(8,128)(2,1)S(1)} %get-tuple-element.24.sent_ref), channel_id=1, source_target_pairs={{0,4},{4,0},{8,12},{12,8},{1,5},{5,1},{9,13},{13,9},{2,6},{6,2},{1... | collective-permute-start | bytes 221192 | tf_op jit(solution)/shard_map/ppermute | solution.py:205
  25.8 7.4 %collective-permute-start.10 = (bf16[128,256]{1,0:T(8,128)(2,1)S(1)}, bf16[128,256]{1,0:T(8,128)(2,1)S(1)}, u32[]{:S(2)}, u32[]{:S(2)}) collective-permute-start(bf16[128,256]{1,0:T(8,128)(2,1)S(1)} %shard_map.110.part_ref), channel_id=1, source_target_pairs={{0,8},{4,12},{8,0},{12,4},{1,9},{5,13},{9,1},{13,5},{2,10},{6,14},... | collective-permute-start | bytes 196616 | tf_op jit(solution)/shard_map/ppermute | solution.py:205
  27.3 7.4 %collective-permute-start.8 = (bf16[144,256]{1,0:T(8,128)(2,1)S(1)}, bf16[144,256]{1,0:T(8,128)(2,1)S(1)}, u32[]{:S(2)}, u32[]{:S(2)}) collective-permute-start(bf16[144,256]{1,0:T(8,128)(2,1)S(1)} %shard_map.108.sent_ref), channel_id=1, source_target_pairs={{0,8},{4,12},{8,0},{12,4},{1,9},{5,13},{9,1},{13,5},{2,10},{6,14},... | collective-permute-start | bytes 221192 | tf_op jit(solution)/shard_map/ppermute | solution.py:205
  30.1 4.5 %collective-permute-start.12 = (bf16[128,256]{1,0:T(8,128)(2,1)S(1)}, bf16[128,256]{1,0:T(8,128)(2,1)S(1)}, u32[]{:S(2)}, u32[]{:S(2)}) collective-permute-start(bf16[128,256]{1,0:T(8,128)(2,1)S(1)} %get-tuple-element.27), channel_id=1, source_target_pairs={{0,4},{4,0},{8,12},{12,8},{1,5},{5,1},{9,13},{13,9},{2,6},{6,2},{1... | collective-permute-start | bytes 196616 | tf_op jit(solution)/shard_map/ppermute | solution.py:205
  33.1 1.6 %collective-permute-start.11 = (bf16[128,256]{1,0:T(8,128)(2,1)S(1)}, bf16[128,256]{1,0:T(8,128)(2,1)S(1)}, u32[]{:S(2)}, u32[]{:S(2)}) collective-permute-start(bf16[128,256]{1,0:T(8,128)(2,1)S(1)} %shard_map.111.mine_ref), channel_id=1, source_target_pairs={{0,1},{1,0},{2,3},{3,2},{4,5},{5,4},{6,7},{7,6},{8,9},{9,8},{10,11... | collective-permute-start | bytes 196616 | tf_op jit(solution)/shard_map/ppermute | solution.py:205

commit v16 on v15

--- a/solution.py
+++ b/solution.py
@@ -85,13 +85,22 @@
     return body
 
 
+def meeting(n_row):
+    half = n_row // 2
+    return [half] + [p for p in range(n_row - 1, -1, -1) if p != half]
+
+
+def places(n_row):
+    return [meeting(n_row).index(p) for p in range(n_row)]
+
+
 def forward_kernel(n_row, n_cot):
     def body(a_ref, *refs):
         ins, (keep_ref, send_ref, *outs) = refs[:n_row], refs[n_row + n_cot :]
         for ref, out in zip(refs[n_row:], outs):
             out[...] = ref[...]
         half = keep_ref.shape[0]
-        x = jnp.concatenate([ref[...] for ref in ins[::-1]], axis=0)
+        x = jnp.concatenate([ins[i][...] for i in places(n_row)], axis=0)
         send_ref[...] = dot(a_ref[half:, :], x).astype(BF)
         keep_ref[...] = dot(a_ref[:half, :], x)
 
@@ -234,7 +243,7 @@
         forward_kernel(n_row, n_chip - 1),
         (shape(half, width, dtype=F32), shape(half, width)) + (shape(tile, width),) * (n_chip - 1),
         count=n_row + n_chip,
-    )(a, *xs[::-1], *cots[1:])
+    )(a, *[xs[p] for p in meeting(n_row)], *cots[1:])
     chip = call(chip_kernel, shape(half, width), count=2)(keep, swap(send, "col", n_col, 1))
     sums = [chip] + [swap(chip, "col", n_col, 2 * v) for v in range(1, n_chip)]
     act, keep, part, send = call(

time: 35.7 us -> 35.5 us (level)
  transfers between devices with their start and end apart: 13 -> 13, of which waited for: 8 -> 9; matrix products, arithmetic and copies ran while one was open for 0% -> 0% of each run, Pallas kernels for 4% -> 4%
where the time goes in v16:
time: 35.5 us; the launch traced here: 35.3 us
  starting transfers between devices  16.1 us (45%)
  waiting for transfers between devices  13.6 us (38%)
  Pallas kernels  3.14 us (9%)
  local copies, waits for them, and re-layouts  1.66 us (5%)
  between operations  0.77 us (2%)
    ppermute x13, starting transfers between devices, swap(): return lax.ppermute(x, axis, [(i, i ^ by) for i in range(n)])  16.1 us
    ppermute x13, waiting for transfers between devices, swap(): return lax.ppermute(x, axis, [(i, i ^ by) for i in range(n)])  13.6 us
    unnamed x14, local copies, waits for them, and re-layouts  1.65 us
    pallas_call x1, Pallas kernels, shards(): call(dense_kernel(n_chip), shape(n_col * tile, n_row * tile), count=3, sm...  0.79 us
    pallas_call x1, Pallas kernels, shards(): call(last_kernel, (shape(tile, width), shape(tile, width), shape(width, w...  0.77 us
  transfers between devices with their start and end apart: 13, of which 9 were waited for; matrix products, arithmetic and copies ran while one was open for 0% of the time, Pallas kernels for 4%

profile of v16, /device:TPU:0, one launch (start us, length us, event | category | flops | bytes accessed | tf_op | source)
XLA Modules:
  0.0 35.3 jit_solution(12332225657464039742)
XLA Ops:
  0.6 4.1 %collective-permute-start = (bf16[128,256]{1,0:T(8,128)(2,1)}, bf16[128,256]{1,0:T(8,128)(2,1)S(1)}, u32[]{:S(2)}, u32[]{:S(2)}) collective-permute-start(bf16[128,256]{1,0:T(8,128)(2,1)} %refs_3_.1), channel_id=1, source_target_pairs={{0,8},{4,12},{8,0},{12,4},{1,9},{5,13},{9,1},{13,5},{2,10},{6,14},... | collective-permute-start | bytes 196616 | tf_op jit(solution)/shard_map/ppermute | solution.py:214
  4.7 1.3 %collective-permute-start.1 = (bf16[128,256]{1,0:T(8,128)(2,1)}, bf16[128,256]{1,0:T(8,128)(2,1)S(1)}, u32[]{:S(2)}, u32[]{:S(2)}) collective-permute-start(bf16[128,256]{1,0:T(8,128)(2,1)} %refs_3_.1), channel_id=1, source_target_pairs={{0,12},{4,8},{8,4},{12,0},{1,13},{5,9},{9,5},{13,1},{2,14},{6,10},... | collective-permute-start | bytes 196616 | tf_op jit(solution)/shard_map/ppermute | solution.py:214
  6.1 0.2 collective-permute-start.2
  6.3 1.5 %collective-permute-start.3 = (bf16[128,256]{1,0:T(8,128)(2,1)}, bf16[128,256]{1,0:T(8,128)(2,1)S(1)}, u32[]{:S(2)}, u32[]{:S(2)}) collective-permute-start(bf16[128,256]{1,0:T(8,128)(2,1)} %refs_2_.1), channel_id=1, source_target_pairs={{0,2},{1,3},{2,0},{3,1},{4,6},{5,7},{6,4},{7,5},{8,10},{9,11},{10,... | collective-permute-start | bytes 196616 | tf_op jit(solution)/shard_map/ppermute | solution.py:214
  7.8 0.0 copy-start.4
  7.8 0.0 copy-start.5
  7.8 0.7 %copy-done.4 = s32[4,1,2]{0,2,1:T(2,128)S(1)} copy-done((s32[4,1,2]{0,2,1:T(2,128)S(1)}, s32[4,1,2]{0,2,1:T(2,128)}, u32[]{:S(2)}) %copy-start.4) | copy-done | bytes 56
  8.5 0.0 copy-done.5
  8.5 0.0 copy-start
  8.5 0.9 %copy-done = bf16[4,1,2,128,128]{4,3,2,1,0:T(8,128)(2,1)S(1)} copy-done((bf16[4,1,2,128,128]{4,3,2,1,0:T(8,128)(2,1)S(1)}, bf16[4,1,2,128,128]{4,3,2,1,0:T(8,128)(2,1)}, u32[]{:S(2)}) %copy-start) | copy-done | bytes 262168
  9.4 0.0 copy-start.3
  9.4 0.8 %shard_map.102.a_ref = bf16[512,512]{1,0:T(8,128)(2,1)S(1)} custom-call(s32[1,2,4]{2,1,0:T(2,128)S(1)} %bitcast.3, s32[1,4]{1,0:T(1,128)S(1)} %bitcast.4, bf16[4,1,2,128,128]{4,3,2,1,0:T(8,128)(2,1)S(1)} %copy-done), custom_call_target="tpu_custom_call" | custom-call | tf_op jit(solution)/shard_map/pallas_call | solution.py:235
  10.2 0.0 collective-permute-done.refs_0_
  10.2 0.9 %collective-permute-done.1.refs_1_ = bf16[128,256]{1,0:T(8,128)(2,1)S(1)} collective-permute-done((bf16[128,256]{1,0:T(8,128)(2,1)}, bf16[128,256]{1,0:T(8,128)(2,1)S(1)}, u32[]{:S(2)}, u32[]{:S(2)}) %collective-permute-start.1) | collective-permute-done | bytes 65568 | tf_op jit(solution)/shard_map/ppermute | solution.py:214
  11.2 0.1 collective-permute-done.2.refs_2_
  11.3 0.0 collective-permute-done.3.refs_4_
  11.3 0.0 copy-done.3
  11.3 0.3 shard_map.103
  11.6 0.1 collective-permute-start.4
  11.7 1.3 %collective-permute-done.4.got_ref = bf16[256,256]{1,0:T(8,128)(2,1)S(1)} collective-permute-done((bf16[256,256]{1,0:T(8,128)(2,1)S(1)}, bf16[256,256]{1,0:T(8,128)(2,1)S(1)}, u32[]{:S(2)}, u32[]{:S(2)}) %collective-permute-start.4) | collective-permute-done | bytes 131104 | tf_op jit(solution)/shard_map/ppermute | solution.py:214
  13.0 0.0 copy-start.6
  13.0 0.0 copy-start.1
  13.0 0.0 copy-start.2
  13.1 1.6 %collective-permute-start.5 = (bf16[256,256]{1,0:T(8,128)(2,1)S(1)}, bf16[256,256]{1,0:T(8,128)(2,1)S(1)}, u32[]{:S(2)}, u32[]{:S(2)}) collective-permute-start(bf16[256,256]{1,0:T(8,128)(2,1)S(1)} %shard_map.104.refs_0_), channel_id=1, source_target_pairs={{0,2},{1,3},{2,0},{3,1},{4,6},{5,7},{6,4},{7,5},{8,10},{9,11},{10,... | collective-permute-start | bytes 393224 | tf_op jit(solution)/shard_map/ppermute | solution.py:214
  14.6 0.3 shard_map.105.refs_4_.at_ref
  15.0 0.0 copy-done.6
  15.0 3.7 %collective-permute-done.5.refs_1_ = bf16[256,256]{1,0:T(8,128)(2,1)S(1)} collective-permute-done((bf16[256,256]{1,0:T(8,128)(2,1)S(1)}, bf16[256,256]{1,0:T(8,128)(2,1)S(1)}, u32[]{:S(2)}, u32[]{:S(2)}) %collective-permute-start.5) | collective-permute-done | bytes 131104 | tf_op jit(solution)/shard_map/ppermute | solution.py:214
  18.7 0.0 copy-done.1
  18.7 0.0 copy-done.2
  18.7 0.5 %shard_map.106 = (bf16[128,256]{1,0:T(8,128)(2,1)S(1)}, bf16[272,256]{1,0:T(8,128)(2,1)S(1)}, bf16[128,256]{1,0:T(8,128)(2,1)S(1)}, bf16[400,256]{1,0:T(8,128)(2,1)S(1)}) custom-call(bf16[256,256]{1,0:T(8,128)(2,1)S(1)} %copy-done.1, bf16[1,256]{1,0:T(2,128)(2,1)S(1)} %reshape.14.b_ref, bf16[256,256]{1,0:T(8,128)(2,1)S(1)} %shard_map.104.refs_0_, ...), custom_call_target="tpu_custom_call" | custom-call | tf_op jit(solution)/shard_map/pallas_call | solution.py:249
  19.2 0.1 collective-permute-start.6
  19.3 1.4 %collective-permute-done.6.got_ref = bf16[400,256]{1,0:T(8,128)(2,1)S(1)} collective-permute-done((bf16[400,256]{1,0:T(8,128)(2,1)S(1)}, bf16[400,256]{1,0:T(8,128)(2,1)S(1)}, u32[]{:S(2)}, u32[]{:S(2)}) %collective-permute-start.6) | collective-permute-done | bytes 204832 | tf_op jit(solution)/shard_map/ppermute | solution.py:214
  20.7 1.4 %collective-permute-start.9 = (bf16[128,256]{1,0:T(8,128)(2,1)S(1)}, bf16[128,256]{1,0:T(8,128)(2,1)S(1)}, u32[]{:S(2)}, u32[]{:S(2)}) collective-permute-start(bf16[128,256]{1,0:T(8,128)(2,1)S(1)} %shard_map.109.part_ref), channel_id=1, source_target_pairs={{0,4},{4,0},{8,12},{12,8},{1,5},{5,1},{9,13},{13,9},{2,6},{6,2},{1... | collective-permute-start | bytes 196616 | tf_op jit(solution)/shard_map/ppermute | solution.py:214
  22.1 0.3 shard_map.107
  22.4 0.8 %collective-permute-start.7 = (bf16[144,256]{1,0:T(8,128)(2,1)S(1)}, bf16[144,256]{1,0:T(8,128)(2,1)S(1)}, u32[]{:S(2)}, u32[]{:S(2)}) collective-permute-start(bf16[144,256]{1,0:T(8,128)(2,1)S(1)} %get-tuple-element.24.sent_ref), channel_id=1, source_target_pairs={{0,4},{4,0},{8,12},{12,8},{1,5},{5,1},{9,13},{13,9},{2,6},{6,2},{1... | collective-permute-start | bytes 221192 | tf_op jit(solution)/shard_map/ppermute | solution.py:214
  23.2 2.0 %collective-permute-done.9.got_ref = bf16[128,256]{1,0:T(8,128)(2,1)S(1)} collective-permute-done((bf16[128,256]{1,0:T(8,128)(2,1)S(1)}, bf16[128,256]{1,0:T(8,128)(2,1)S(1)}, u32[]{:S(2)}, u32[]{:S(2)}) %collective-permute-start.9) | collective-permute-done | bytes 65568 | tf_op jit(solution)/shard_map/ppermute | solution.py:214
  25.3 3.1 %collective-permute-start.10 = (bf16[128,256]{1,0:T(8,128)(2,1)S(1)}, bf16[128,256]{1,0:T(8,128)(2,1)S(1)}, u32[]{:S(2)}, u32[]{:S(2)}) collective-permute-start(bf16[128,256]{1,0:T(8,128)(2,1)S(1)} %shard_map.110.part_ref), channel_id=1, source_target_pairs={{0,8},{4,12},{8,0},{12,4},{1,9},{5,13},{9,1},{13,5},{2,10},{6,14},... | collective-permute-start | bytes 196616 | tf_op jit(solution)/shard_map/ppermute | solution.py:214
  28.4 0.0 collective-permute-done.7.got_ref.refs_1_
  28.4 1.3 %collective-permute-start.8 = (bf16[144,256]{1,0:T(8,128)(2,1)S(1)}, bf16[144,256]{1,0:T(8,128)(2,1)S(1)}, u32[]{:S(2)}, u32[]{:S(2)}) collective-permute-start(bf16[144,256]{1,0:T(8,128)(2,1)S(1)} %shard_map.108.sent_ref), channel_id=1, source_target_pairs={{0,8},{4,12},{8,0},{12,4},{1,9},{5,13},{9,1},{13,5},{2,10},{6,14},... | collective-permute-start | bytes 221192 | tf_op jit(solution)/shard_map/ppermute | solution.py:214
  29.7 0.6 %collective-permute-start.12 = (bf16[128,256]{1,0:T(8,128)(2,1)S(1)}, bf16[128,256]{1,0:T(8,128)(2,1)S(1)}, u32[]{:S(2)}, u32[]{:S(2)}) collective-permute-start(bf16[128,256]{1,0:T(8,128)(2,1)S(1)} %get-tuple-element.27), channel_id=1, source_target_pairs={{0,4},{4,0},{8,12},{12,8},{1,5},{5,1},{9,13},{13,9},{2,6},{6,2},{1... | collective-permute-start | bytes 196616 | tf_op jit(solution)/shard_map/ppermute | solution.py:214
  30.3 2.3 %collective-permute-done.10.got_ref = bf16[128,256]{1,0:T(8,128)(2,1)S(1)} collective-permute-done((bf16[128,256]{1,0:T(8,128)(2,1)S(1)}, bf16[128,256]{1,0:T(8,128)(2,1)S(1)}, u32[]{:S(2)}, u32[]{:S(2)}) %collective-permute-start.10) | collective-permute-done | bytes 65568 | tf_op jit(solution)/shard_map/ppermute | solution.py:214
  32.7 0.1 collective-permute-start.11
  32.7 1.3 %collective-permute-done.12.refs_1_ = bf16[128,256]{1,0:T(8,128)(2,1)S(1)} collective-permute-done((bf16[128,256]{1,0:T(8,128)(2,1)S(1)}, bf16[128,256]{1,0:T(8,128)(2,1)S(1)}, u32[]{:S(2)}, u32[]{:S(2)}) %collective-permute-start.12) | collective-permute-done | bytes 65568 | tf_op jit(solution)/shard_map/ppermute | solution.py:214
  34.0 0.6 %collective-permute-done.8.line_ref.refs_2_ = bf16[144,256]{1,0:T(8,128)(2,1)S(1)} collective-permute-done((bf16[144,256]{1,0:T(8,128)(2,1)S(1)}, bf16[144,256]{1,0:T(8,128)(2,1)S(1)}, u32[]{:S(2)}, u32[]{:S(2)}) %collective-permute-start.8) | collective-permute-done | bytes 73760 | tf_op jit(solution)/shard_map/ppermute | solution.py:214
  34.6 0.0 collective-permute-done.11.got_ref
  34.6 0.8 %shard_map.112 = (bf16[128,256]{1,0:T(8,128)(2,1)}, bf16[128,256]{1,0:T(8,128)(2,1)}, f32[256,256]{1,0:T(8,128)}, f32[1,256]{1,0:T(1,128)}) custom-call(bf16[128,256]{1,0:T(8,128)(2,1)S(1)} %get-tuple-element.21.act_ref, bf16[144,256]{1,0:T(8,128)(2,1)S(1)} %shard_map.108.sent_ref, bf16[144,256]{1,0:T(8,128)(2,1)S(1)} %collective-permute-done.8.line_ref.refs_2_, ...), custom_call_target="tpu_custom_call" | custom-call | tf_op jit(solution)/shard_map/pallas_call | solution.py:296
  (6 shorter events, 0.1 us)
Async XLA Ops:
  0.6 9.6 %collective-permute-start = (bf16[128,256]{1,0:T(8,128)(2,1)}, bf16[128,256]{1,0:T(8,128)(2,1)S(1)}, u32[]{:S(2)}, u32[]{:S(2)}) collective-permute-start(bf16[128,256]{1,0:T(8,128)(2,1)} %refs_3_.1), channel_id=1, source_target_pairs={{0,8},{4,12},{8,0},{12,4},{1,9},{5,13},{9,1},{13,5},{2,10},{6,14},... | collective-permute-start | bytes 196616 | tf_op jit(solution)/shard_map/ppermute | solution.py:214
  4.7 6.4 %collective-permute-start.1 = (bf16[128,256]{1,0:T(8,128)(2,1)}, bf16[128,256]{1,0:T(8,128)(2,1)S(1)}, u32[]{:S(2)}, u32[]{:S(2)}) collective-permute-start(bf16[128,256]{1,0:T(8,128)(2,1)} %refs_3_.1), channel_id=1, source_target_pairs={{0,12},{4,8},{8,4},{12,0},{1,13},{5,9},{9,5},{13,1},{2,14},{6,10},... | collective-permute-start | bytes 196616 | tf_op jit(solution)/shard_map/ppermute | solution.py:214
  6.1 5.2 %collective-permute-start.2 = (bf16[128,256]{1,0:T(8,128)(2,1)}, bf16[128,256]{1,0:T(8,128)(2,1)S(1)}, u32[]{:S(2)}, u32[]{:S(2)}) collective-permute-start(bf16[128,256]{1,0:T(8,128)(2,1)} %refs_3_.1), channel_id=1, source_target_pairs={{0,4},{4,0},{8,12},{12,8},{1,5},{5,1},{9,13},{13,9},{2,6},{6,2},{1... | collective-permute-start | bytes 196616 | tf_op jit(solution)/shard_map/ppermute | solution.py:214
  6.3 5.0 %collective-permute-start.3 = (bf16[128,256]{1,0:T(8,128)(2,1)}, bf16[128,256]{1,0:T(8,128)(2,1)S(1)}, u32[]{:S(2)}, u32[]{:S(2)}) collective-permute-start(bf16[128,256]{1,0:T(8,128)(2,1)} %refs_2_.1), channel_id=1, source_target_pairs={{0,2},{1,3},{2,0},{3,1},{4,6},{5,7},{6,4},{7,5},{8,10},{9,11},{10,... | collective-permute-start | bytes 196616 | tf_op jit(solution)/shard_map/ppermute | solution.py:214
  7.8 0.7 %copy-start.4 = (s32[4,1,2]{0,2,1:T(2,128)S(1)}, s32[4,1,2]{0,2,1:T(2,128)}, u32[]{:S(2)}) copy-start(s32[4,1,2]{0,2,1:T(2,128)} %param.9) | copy-start | bytes 100
  7.8 0.7 %copy-start.5 = (s32[4,1]{0,1:T(1,128)S(1)}, s32[4,1]{0,1:T(1,128)}, u32[]{:S(2)}) copy-start(s32[4,1]{0,1:T(1,128)} %param.10) | copy-start | bytes 52
  8.5 1.0 %copy-start = (bf16[4,1,2,128,128]{4,3,2,1,0:T(8,128)(2,1)S(1)}, bf16[4,1,2,128,128]{4,3,2,1,0:T(8,128)(2,1)}, u32[]{:S(2)}) copy-start(bf16[4,1,2,128,128]{4,3,2,1,0:T(8,128)(2,1)} %tiles_ref.1) | copy-start | bytes 786436
  9.4 1.8 %copy-start.3 = (bf16[128,256]{1,0:T(8,128)(2,1)S(1)}, bf16[128,256]{1,0:T(8,128)(2,1)}, u32[]{:S(2)}) copy-start(bf16[128,256]{1,0:T(8,128)(2,1)} %refs_3_.1) | copy-start | bytes 196612
  11.6 1.4 %collective-permute-start.4 = (bf16[256,256]{1,0:T(8,128)(2,1)S(1)}, bf16[256,256]{1,0:T(8,128)(2,1)S(1)}, u32[]{:S(2)}, u32[]{:S(2)}) collective-permute-start(bf16[256,256]{1,0:T(8,128)(2,1)S(1)} %get-tuple-element.19), channel_id=1, source_target_pairs={{0,1},{1,0},{2,3},{3,2},{4,5},{5,4},{6,7},{7,6},{8,9},{9,8},{10,11... | collective-permute-start | bytes 393224 | tf_op jit(solution)/shard_map/ppermute | solution.py:214
  13.0 1.9 %copy-start.6 = (bf16[256]{0:T(256)(128)(2,1)S(1)}, bf16[256]{0:T(256)(128)(2,1)}, u32[]{:S(2)}) copy-start(bf16[256]{0:T(256)(128)(2,1)} %param.12) | copy-start | bytes 1540
  13.0 5.6 %copy-start.1 = (bf16[256,256]{1,0:T(8,128)(2,1)S(1)}, bf16[256,256]{1,0:T(8,128)(2,1)}, u32[]{:S(2)}) copy-start(bf16[256,256]{1,0:T(8,128)(2,1)} %w_ref.1) | copy-start | bytes 393220
  13.0 5.6 %copy-start.2 = (bf16[128,256]{1,0:T(8,128)(2,1)S(1)}, bf16[128,256]{1,0:T(8,128)(2,1)}, u32[]{:S(2)}) copy-start(bf16[128,256]{1,0:T(8,128)(2,1)} %refs_2_.1) | copy-start | bytes 196612
  13.1 5.6 %collective-permute-start.5 = (bf16[256,256]{1,0:T(8,128)(2,1)S(1)}, bf16[256,256]{1,0:T(8,128)(2,1)S(1)}, u32[]{:S(2)}, u32[]{:S(2)}) collective-permute-start(bf16[256,256]{1,0:T(8,128)(2,1)S(1)} %shard_map.104.refs_0_), channel_id=1, source_target_pairs={{0,2},{1,3},{2,0},{3,1},{4,6},{5,7},{6,4},{7,5},{8,10},{9,11},{10,... | collective-permute-start | bytes 393224 | tf_op jit(solution)/shard_map/ppermute | solution.py:214
  19.2 1.5 %collective-permute-start.6 = (bf16[400,256]{1,0:T(8,128)(2,1)S(1)}, bf16[400,256]{1,0:T(8,128)(2,1)S(1)}, u32[]{:S(2)}, u32[]{:S(2)}) collective-permute-start(bf16[400,256]{1,0:T(8,128)(2,1)S(1)} %get-tuple-element.23), channel_id=1, source_target_pairs={{0,1},{1,0},{2,3},{3,2},{4,5},{5,4},{6,7},{7,6},{8,9},{9,8},{10,11... | collective-permute-start | bytes 614408 | tf_op jit(solution)/shard_map/ppermute | solution.py:214
  20.7 4.5 %collective-permute-start.9 = (bf16[128,256]{1,0:T(8,128)(2,1)S(1)}, bf16[128,256]{1,0:T(8,128)(2,1)S(1)}, u32[]{:S(2)}, u32[]{:S(2)}) collective-permute-start(bf16[128,256]{1,0:T(8,128)(2,1)S(1)} %shard_map.109.part_ref), channel_id=1, source_target_pairs={{0,4},{4,0},{8,12},{12,8},{1,5},{5,1},{9,13},{13,9},{2,6},{6,2},{1... | collective-permute-start | bytes 196616 | tf_op jit(solution)/shard_map/ppermute | solution.py:214
  22.4 6.0 %collective-permute-start.7 = (bf16[144,256]{1,0:T(8,128)(2,1)S(1)}, bf16[144,256]{1,0:T(8,128)(2,1)S(1)}, u32[]{:S(2)}, u32[]{:S(2)}) collective-permute-start(bf16[144,256]{1,0:T(8,128)(2,1)S(1)} %get-tuple-element.24.sent_ref), channel_id=1, source_target_pairs={{0,4},{4,0},{8,12},{12,8},{1,5},{5,1},{9,13},{13,9},{2,6},{6,2},{1... | collective-permute-start | bytes 221192 | tf_op jit(solution)/shard_map/ppermute | solution.py:214
  25.3 7.4 %collective-permute-start.10 = (bf16[128,256]{1,0:T(8,128)(2,1)S(1)}, bf16[128,256]{1,0:T(8,128)(2,1)S(1)}, u32[]{:S(2)}, u32[]{:S(2)}) collective-permute-start(bf16[128,256]{1,0:T(8,128)(2,1)S(1)} %shard_map.110.part_ref), channel_id=1, source_target_pairs={{0,8},{4,12},{8,0},{12,4},{1,9},{5,13},{9,1},{13,5},{2,10},{6,14},... | collective-permute-start | bytes 196616 | tf_op jit(solution)/shard_map/ppermute | solution.py:214
  28.4 6.1 %collective-permute-start.8 = (bf16[144,256]{1,0:T(8,128)(2,1)S(1)}, bf16[144,256]{1,0:T(8,128)(2,1)S(1)}, u32[]{:S(2)}, u32[]{:S(2)}) collective-permute-start(bf16[144,256]{1,0:T(8,128)(2,1)S(1)} %shard_map.108.sent_ref), channel_id=1, source_target_pairs={{0,8},{4,12},{8,0},{12,4},{1,9},{5,13},{9,1},{13,5},{2,10},{6,14},... | collective-permute-start | bytes 221192 | tf_op jit(solution)/shard_map/ppermute | solution.py:214
  29.7 4.3 %collective-permute-start.12 = (bf16[128,256]{1,0:T(8,128)(2,1)S(1)}, bf16[128,256]{1,0:T(8,128)(2,1)S(1)}, u32[]{:S(2)}, u32[]{:S(2)}) collective-permute-start(bf16[128,256]{1,0:T(8,128)(2,1)S(1)} %get-tuple-element.27), channel_id=1, source_target_pairs={{0,4},{4,0},{8,12},{12,8},{1,5},{5,1},{9,13},{13,9},{2,6},{6,2},{1... | collective-permute-start | bytes 196616 | tf_op jit(solution)/shard_map/ppermute | solution.py:214
  32.7 1.9 %collective-permute-start.11 = (bf16[128,256]{1,0:T(8,128)(2,1)S(1)}, bf16[128,256]{1,0:T(8,128)(2,1)S(1)}, u32[]{:S(2)}, u32[]{:S(2)}) collective-permute-start(bf16[128,256]{1,0:T(8,128)(2,1)S(1)} %shard_map.111.mine_ref), channel_id=1, source_target_pairs={{0,1},{1,0},{2,3},{3,2},{4,5},{5,4},{6,7},{7,6},{8,9},{9,8},{10,11... | collective-permute-start | bytes 196616 | tf_op jit(solution)/shard_map/ppermute | solution.py:214

commit v17 on v16

--- a/solution.py
+++ b/solution.py
@@ -96,8 +96,10 @@
 
 def forward_kernel(n_row, n_cot):
     def body(a_ref, *refs):
-        ins, (keep_ref, send_ref, *outs) = refs[:n_row], refs[n_row + n_cot :]
-        for ref, out in zip(refs[n_row:], outs):
+        far = n_row - 2
+        ins = refs[:far] + refs[far + n_cot : n_row + n_cot]
+        keep_ref, send_ref, *outs = refs[n_row + n_cot :]
+        for ref, out in zip(refs[far:], outs):
             out[...] = ref[...]
         half = keep_ref.shape[0]
         x = jnp.concatenate([ins[i][...] for i in places(n_row)], axis=0)
@@ -239,11 +241,12 @@
         smem=2,
     )(columns, counts, adj_tiles)
     at = call(transpose_kernel(n_row), shape(n_row * tile, n_col * tile), count=1)(a)
+    met = [xs[p] for p in meeting(n_row)]
     keep, send, *cots[1:] = call(
         forward_kernel(n_row, n_chip - 1),
         (shape(half, width, dtype=F32), shape(half, width)) + (shape(tile, width),) * (n_chip - 1),
         count=n_row + n_chip,
-    )(a, *[xs[p] for p in meeting(n_row)], *cots[1:])
+    )(a, *met[:-2], *cots[1:], *met[-2:])
     chip = call(chip_kernel, shape(half, width), count=2)(keep, swap(send, "col", n_col, 1))
     sums = [chip] + [swap(chip, "col", n_col, 2 * v) for v in range(1, n_chip)]
     act, keep, part, send = call(

time: 35.5 us -> 35.8 us (level)
  waiting for transfers between devices: 13.6 us -> 15.3 us
  starting transfers between devices: 16.1 us -> 14.8 us
    ppermute x13, waiting for transfers between devices: 13.6 us -> 15.3 us  [swap(): return lax.ppermute(x, axis, [(i, i ^ by) for i in range(n)])]
    ppermute x13, starting transfers between devices: 16.1 us -> 14.8 us  [swap(): return lax.ppermute(x, axis, [(i, i ^ by) for i in range(n)])]
where the time goes in v17:
time: 35.8 us; the launch traced here: 35.6 us
  waiting for transfers between devices  15.3 us (43%)
  starting transfers between devices  14.8 us (41%)
  Pallas kernels  3.14 us (9%)
  local copies, waits for them, and re-layouts  1.66 us (5%)
  between operations  0.77 us (2%)
    ppermute x13, waiting for transfers between devices, swap(): return lax.ppermute(x, axis, [(i, i ^ by) for i in range(n)])  15.3 us
    ppermute x13, starting transfers between devices, swap(): return lax.ppermute(x, axis, [(i, i ^ by) for i in range(n)])  14.8 us
    unnamed x14, local copies, waits for them, and re-layouts  1.65 us
    pallas_call x1, Pallas kernels, shards(): call(dense_kernel(n_chip), shape(n_col * tile, n_row * tile), count=3, sm...  0.79 us
    pallas_call x1, Pallas kernels, shards(): call(last_kernel, (shape(tile, width), shape(tile, width), shape(width, w...  0.77 us
  transfers between devices with their start and end apart: 13, of which 9 were waited for; matrix products, arithmetic and copies ran while one was open for 0% of the time, Pallas kernels for 4%

profile of v17, /device:TPU:0, one launch (start us, length us, event | category | flops | bytes accessed | tf_op | source)
XLA Modules:
  0.0 35.6 jit_solution(1782672942706320924)
XLA Ops:
  0.6 4.1 %collective-permute-start = (bf16[128,256]{1,0:T(8,128)(2,1)}, bf16[128,256]{1,0:T(8,128)(2,1)S(1)}, u32[]{:S(2)}, u32[]{:S(2)}) collective-permute-start(bf16[128,256]{1,0:T(8,128)(2,1)} %refs_4_.1), channel_id=1, source_target_pairs={{0,8},{4,12},{8,0},{12,4},{1,9},{5,13},{9,1},{13,5},{2,10},{6,14},... | collective-permute-start | bytes 196616 | tf_op jit(solution)/shard_map/ppermute | solution.py:216
  4.7 1.3 %collective-permute-start.1 = (bf16[128,256]{1,0:T(8,128)(2,1)}, bf16[128,256]{1,0:T(8,128)(2,1)S(1)}, u32[]{:S(2)}, u32[]{:S(2)}) collective-permute-start(bf16[128,256]{1,0:T(8,128)(2,1)} %refs_4_.1), channel_id=1, source_target_pairs={{0,12},{4,8},{8,4},{12,0},{1,13},{5,9},{9,5},{13,1},{2,14},{6,10},... | collective-permute-start | bytes 196616 | tf_op jit(solution)/shard_map/ppermute | solution.py:216
  6.1 1.5 %collective-permute-start.2 = (bf16[128,256]{1,0:T(8,128)(2,1)}, bf16[128,256]{1,0:T(8,128)(2,1)S(1)}, u32[]{:S(2)}, u32[]{:S(2)}) collective-permute-start(bf16[128,256]{1,0:T(8,128)(2,1)} %refs_2_.1), channel_id=1, source_target_pairs={{0,2},{1,3},{2,0},{3,1},{4,6},{5,7},{6,4},{7,5},{8,10},{9,11},{10,... | collective-permute-start | bytes 196616 | tf_op jit(solution)/shard_map/ppermute | solution.py:216
  7.6 0.2 collective-permute-start.3
  7.8 0.0 copy-start.4
  7.8 0.0 copy-start.5
  7.8 0.7 %copy-done.4 = s32[4,1,2]{0,2,1:T(2,128)S(1)} copy-done((s32[4,1,2]{0,2,1:T(2,128)S(1)}, s32[4,1,2]{0,2,1:T(2,128)}, u32[]{:S(2)}) %copy-start.4) | copy-done | bytes 56
  8.5 0.0 copy-done.5
  8.5 0.0 copy-start
  8.5 0.9 %copy-done = bf16[4,1,2,128,128]{4,3,2,1,0:T(8,128)(2,1)S(1)} copy-done((bf16[4,1,2,128,128]{4,3,2,1,0:T(8,128)(2,1)S(1)}, bf16[4,1,2,128,128]{4,3,2,1,0:T(8,128)(2,1)}, u32[]{:S(2)}) %copy-start) | copy-done | bytes 262168
  9.4 0.0 copy-start.3
  9.4 0.8 %shard_map.102.a_ref = bf16[512,512]{1,0:T(8,128)(2,1)S(1)} custom-call(s32[1,2,4]{2,1,0:T(2,128)S(1)} %bitcast.3, s32[1,4]{1,0:T(1,128)S(1)} %bitcast.4, bf16[4,1,2,128,128]{4,3,2,1,0:T(8,128)(2,1)S(1)} %copy-done), custom_call_target="tpu_custom_call" | custom-call | tf_op jit(solution)/shard_map/pallas_call | solution.py:237
  10.2 0.0 collective-permute-done.refs_0_
  10.2 1.3 %collective-permute-done.1.refs_1_ = bf16[128,256]{1,0:T(8,128)(2,1)S(1)} collective-permute-done((bf16[128,256]{1,0:T(8,128)(2,1)}, bf16[128,256]{1,0:T(8,128)(2,1)S(1)}, u32[]{:S(2)}, u32[]{:S(2)}) %collective-permute-start.1) | collective-permute-done | bytes 65568 | tf_op jit(solution)/shard_map/ppermute | solution.py:216
  11.5 0.0 collective-permute-done.2.refs_2_
  11.5 0.6 %collective-permute-done.3.refs_3_ = bf16[128,256]{1,0:T(8,128)(2,1)S(1)} collective-permute-done((bf16[128,256]{1,0:T(8,128)(2,1)}, bf16[128,256]{1,0:T(8,128)(2,1)S(1)}, u32[]{:S(2)}, u32[]{:S(2)}) %collective-permute-start.3) | collective-permute-done | bytes 65568 | tf_op jit(solution)/shard_map/ppermute | solution.py:216
  12.1 0.0 copy-done.3
  12.1 0.3 shard_map.103
  12.4 0.1 collective-permute-start.4
  12.5 1.3 %collective-permute-done.4.got_ref = bf16[256,256]{1,0:T(8,128)(2,1)S(1)} collective-permute-done((bf16[256,256]{1,0:T(8,128)(2,1)S(1)}, bf16[256,256]{1,0:T(8,128)(2,1)S(1)}, u32[]{:S(2)}, u32[]{:S(2)}) %collective-permute-start.4) | collective-permute-done | bytes 131104 | tf_op jit(solution)/shard_map/ppermute | solution.py:216
  13.9 0.0 copy-start.6
  13.9 0.0 copy-start.1
  13.9 0.0 copy-start.2
  13.9 1.2 %collective-permute-start.5 = (bf16[256,256]{1,0:T(8,128)(2,1)S(1)}, bf16[256,256]{1,0:T(8,128)(2,1)S(1)}, u32[]{:S(2)}, u32[]{:S(2)}) collective-permute-start(bf16[256,256]{1,0:T(8,128)(2,1)S(1)} %shard_map.104.refs_0_), channel_id=1, source_target_pairs={{0,2},{1,3},{2,0},{3,1},{4,6},{5,7},{6,4},{7,5},{8,10},{9,11},{10,... | collective-permute-start | bytes 393224 | tf_op jit(solution)/shard_map/ppermute | solution.py:216
  15.1 0.3 shard_map.105.refs_4_.at_ref
  15.5 0.0 copy-done.6
  15.5 4.0 %collective-permute-done.5.refs_1_ = bf16[256,256]{1,0:T(8,128)(2,1)S(1)} collective-permute-done((bf16[256,256]{1,0:T(8,128)(2,1)S(1)}, bf16[256,256]{1,0:T(8,128)(2,1)S(1)}, u32[]{:S(2)}, u32[]{:S(2)}) %collective-permute-start.5) | collective-permute-done | bytes 131104 | tf_op jit(solution)/shard_map/ppermute | solution.py:216
  19.5 0.0 copy-done.1
  19.5 0.0 copy-done.2
  19.5 0.5 %shard_map.106 = (bf16[128,256]{1,0:T(8,128)(2,1)S(1)}, bf16[272,256]{1,0:T(8,128)(2,1)S(1)}, bf16[128,256]{1,0:T(8,128)(2,1)S(1)}, bf16[400,256]{1,0:T(8,128)(2,1)S(1)}) custom-call(bf16[256,256]{1,0:T(8,128)(2,1)S(1)} %copy-done.1, bf16[1,256]{1,0:T(2,128)(2,1)S(1)} %reshape.14.b_ref, bf16[256,256]{1,0:T(8,128)(2,1)S(1)} %shard_map.104.refs_0_, ...), custom_call_target="tpu_custom_call" | custom-call | tf_op jit(solution)/shard_map/pallas_call | solution.py:252
  20.1 0.1 collective-permute-start.6
  20.1 1.4 %collective-permute-done.6.got_ref = bf16[400,256]{1,0:T(8,128)(2,1)S(1)} collective-permute-done((bf16[400,256]{1,0:T(8,128)(2,1)S(1)}, bf16[400,256]{1,0:T(8,128)(2,1)S(1)}, u32[]{:S(2)}, u32[]{:S(2)}) %collective-permute-start.6) | collective-permute-done | bytes 204832 | tf_op jit(solution)/shard_map/ppermute | solution.py:216
  21.6 0.2 collective-permute-start.9
  21.8 0.3 shard_map.107
  22.1 1.9 %collective-permute-start.7 = (bf16[144,256]{1,0:T(8,128)(2,1)S(1)}, bf16[144,256]{1,0:T(8,128)(2,1)S(1)}, u32[]{:S(2)}, u32[]{:S(2)}) collective-permute-start(bf16[144,256]{1,0:T(8,128)(2,1)S(1)} %get-tuple-element.24.sent_ref), channel_id=1, source_target_pairs={{0,4},{4,0},{8,12},{12,8},{1,5},{5,1},{9,13},{13,9},{2,6},{6,2},{1... | collective-permute-start | bytes 221192 | tf_op jit(solution)/shard_map/ppermute | solution.py:216
  24.1 2.5 %collective-permute-done.9.got_ref = bf16[128,256]{1,0:T(8,128)(2,1)S(1)} collective-permute-done((bf16[128,256]{1,0:T(8,128)(2,1)S(1)}, bf16[128,256]{1,0:T(8,128)(2,1)S(1)}, u32[]{:S(2)}, u32[]{:S(2)}) %collective-permute-start.9) | collective-permute-done | bytes 65568 | tf_op jit(solution)/shard_map/ppermute | solution.py:216
  26.6 1.2 %collective-permute-start.10 = (bf16[128,256]{1,0:T(8,128)(2,1)S(1)}, bf16[128,256]{1,0:T(8,128)(2,1)S(1)}, u32[]{:S(2)}, u32[]{:S(2)}) collective-permute-start(bf16[128,256]{1,0:T(8,128)(2,1)S(1)} %shard_map.110.part_ref), channel_id=1, source_target_pairs={{0,8},{4,12},{8,0},{12,4},{1,9},{5,13},{9,1},{13,5},{2,10},{6,14},... | collective-permute-start | bytes 196616 | tf_op jit(solution)/shard_map/ppermute | solution.py:216
  27.8 0.0 collective-permute-done.7.got_ref.refs_1_
  27.8 2.4 %collective-permute-start.8 = (bf16[144,256]{1,0:T(8,128)(2,1)S(1)}, bf16[144,256]{1,0:T(8,128)(2,1)S(1)}, u32[]{:S(2)}, u32[]{:S(2)}) collective-permute-start(bf16[144,256]{1,0:T(8,128)(2,1)S(1)} %shard_map.108.sent_ref), channel_id=1, source_target_pairs={{0,8},{4,12},{8,0},{12,4},{1,9},{5,13},{9,1},{13,5},{2,10},{6,14},... | collective-permute-start | bytes 221192 | tf_op jit(solution)/shard_map/ppermute | solution.py:216
  30.2 0.5 %collective-permute-start.12 = (bf16[128,256]{1,0:T(8,128)(2,1)S(1)}, bf16[128,256]{1,0:T(8,128)(2,1)S(1)}, u32[]{:S(2)}, u32[]{:S(2)}) collective-permute-start(bf16[128,256]{1,0:T(8,128)(2,1)S(1)} %get-tuple-element.27), channel_id=1, source_target_pairs={{0,4},{4,0},{8,12},{12,8},{1,5},{5,1},{9,13},{13,9},{2,6},{6,2},{1... | collective-permute-start | bytes 196616 | tf_op jit(solution)/shard_map/ppermute | solution.py:216
  30.7 2.6 %collective-permute-done.10.got_ref = bf16[128,256]{1,0:T(8,128)(2,1)S(1)} collective-permute-done((bf16[128,256]{1,0:T(8,128)(2,1)S(1)}, bf16[128,256]{1,0:T(8,128)(2,1)S(1)}, u32[]{:S(2)}, u32[]{:S(2)}) %collective-permute-start.10) | collective-permute-done | bytes 65568 | tf_op jit(solution)/shard_map/ppermute | solution.py:216
  33.3 0.1 collective-permute-start.11
  33.4 1.3 %collective-permute-done.12.refs_1_ = bf16[128,256]{1,0:T(8,128)(2,1)S(1)} collective-permute-done((bf16[128,256]{1,0:T(8,128)(2,1)S(1)}, bf16[128,256]{1,0:T(8,128)(2,1)S(1)}, u32[]{:S(2)}, u32[]{:S(2)}) %collective-permute-start.12) | collective-permute-done | bytes 65568 | tf_op jit(solution)/shard_map/ppermute | solution.py:216
  34.7 0.1 collective-permute-done.8.line_ref.refs_2_
  34.8 0.0 collective-permute-done.11.got_ref
  34.9 0.8 %shard_map.112 = (bf16[128,256]{1,0:T(8,128)(2,1)}, bf16[128,256]{1,0:T(8,128)(2,1)}, f32[256,256]{1,0:T(8,128)}, f32[1,256]{1,0:T(1,128)}) custom-call(bf16[128,256]{1,0:T(8,128)(2,1)S(1)} %get-tuple-element.21.act_ref, bf16[144,256]{1,0:T(8,128)(2,1)S(1)} %shard_map.108.sent_ref, bf16[144,256]{1,0:T(8,128)(2,1)S(1)} %collective-permute-done.8.line_ref.refs_2_, ...), custom_call_target="tpu_custom_call" | custom-call | tf_op jit(solution)/shard_map/pallas_call | solution.py:299
  (6 shorter events, 0.1 us)
Async XLA Ops:
  0.6 9.6 %collective-permute-start = (bf16[128,256]{1,0:T(8,128)(2,1)}, bf16[128,256]{1,0:T(8,128)(2,1)S(1)}, u32[]{:S(2)}, u32[]{:S(2)}) collective-permute-start(bf16[128,256]{1,0:T(8,128)(2,1)} %refs_4_.1), channel_id=1, source_target_pairs={{0,8},{4,12},{8,0},{12,4},{1,9},{5,13},{9,1},{13,5},{2,10},{6,14},... | collective-permute-start | bytes 196616 | tf_op jit(solution)/shard_map/ppermute | solution.py:216
  4.7 6.8 %collective-permute-start.1 = (bf16[128,256]{1,0:T(8,128)(2,1)}, bf16[128,256]{1,0:T(8,128)(2,1)S(1)}, u32[]{:S(2)}, u32[]{:S(2)}) collective-permute-start(bf16[128,256]{1,0:T(8,128)(2,1)} %refs_4_.1), channel_id=1, source_target_pairs={{0,12},{4,8},{8,4},{12,0},{1,13},{5,9},{9,5},{13,1},{2,14},{6,10},... | collective-permute-start | bytes 196616 | tf_op jit(solution)/shard_map/ppermute | solution.py:216
  6.1 5.4 %collective-permute-start.2 = (bf16[128,256]{1,0:T(8,128)(2,1)}, bf16[128,256]{1,0:T(8,128)(2,1)S(1)}, u32[]{:S(2)}, u32[]{:S(2)}) collective-permute-start(bf16[128,256]{1,0:T(8,128)(2,1)} %refs_2_.1), channel_id=1, source_target_pairs={{0,2},{1,3},{2,0},{3,1},{4,6},{5,7},{6,4},{7,5},{8,10},{9,11},{10,... | collective-permute-start | bytes 196616 | tf_op jit(solution)/shard_map/ppermute | solution.py:216
  7.6 4.6 %collective-permute-start.3 = (bf16[128,256]{1,0:T(8,128)(2,1)}, bf16[128,256]{1,0:T(8,128)(2,1)S(1)}, u32[]{:S(2)}, u32[]{:S(2)}) collective-permute-start(bf16[128,256]{1,0:T(8,128)(2,1)} %refs_4_.1), channel_id=1, source_target_pairs={{0,4},{4,0},{8,12},{12,8},{1,5},{5,1},{9,13},{13,9},{2,6},{6,2},{1... | collective-permute-start | bytes 196616 | tf_op jit(solution)/shard_map/ppermute | solution.py:216
  7.8 0.7 %copy-start.4 = (s32[4,1,2]{0,2,1:T(2,128)S(1)}, s32[4,1,2]{0,2,1:T(2,128)}, u32[]{:S(2)}) copy-start(s32[4,1,2]{0,2,1:T(2,128)} %param.9) | copy-start | bytes 100
  7.8 0.7 %copy-start.5 = (s32[4,1]{0,1:T(1,128)S(1)}, s32[4,1]{0,1:T(1,128)}, u32[]{:S(2)}) copy-start(s32[4,1]{0,1:T(1,128)} %param.10) | copy-start | bytes 52
  8.5 1.0 %copy-start = (bf16[4,1,2,128,128]{4,3,2,1,0:T(8,128)(2,1)S(1)}, bf16[4,1,2,128,128]{4,3,2,1,0:T(8,128)(2,1)}, u32[]{:S(2)}) copy-start(bf16[4,1,2,128,128]{4,3,2,1,0:T(8,128)(2,1)} %tiles_ref.1) | copy-start | bytes 786436
  9.4 2.7 %copy-start.3 = (bf16[128,256]{1,0:T(8,128)(2,1)S(1)}, bf16[128,256]{1,0:T(8,128)(2,1)}, u32[]{:S(2)}) copy-start(bf16[128,256]{1,0:T(8,128)(2,1)} %refs_4_.1) | copy-start | bytes 196612
  12.4 1.4 %collective-permute-start.4 = (bf16[256,256]{1,0:T(8,128)(2,1)S(1)}, bf16[256,256]{1,0:T(8,128)(2,1)S(1)}, u32[]{:S(2)}, u32[]{:S(2)}) collective-permute-start(bf16[256,256]{1,0:T(8,128)(2,1)S(1)} %get-tuple-element.19), channel_id=1, source_target_pairs={{0,1},{1,0},{2,3},{3,2},{4,5},{5,4},{6,7},{7,6},{8,9},{9,8},{10,11... | collective-permute-start | bytes 393224 | tf_op jit(solution)/shard_map/ppermute | solution.py:216
  13.9 1.6 %copy-start.6 = (bf16[256]{0:T(256)(128)(2,1)S(1)}, bf16[256]{0:T(256)(128)(2,1)}, u32[]{:S(2)}) copy-start(bf16[256]{0:T(256)(128)(2,1)} %param.12) | copy-start | bytes 1540
  13.9 5.6 %copy-start.1 = (bf16[256,256]{1,0:T(8,128)(2,1)S(1)}, bf16[256,256]{1,0:T(8,128)(2,1)}, u32[]{:S(2)}) copy-start(bf16[256,256]{1,0:T(8,128)(2,1)} %w_ref.1) | copy-start | bytes 393220
  13.9 5.6 %copy-start.2 = (bf16[128,256]{1,0:T(8,128)(2,1)S(1)}, bf16[128,256]{1,0:T(8,128)(2,1)}, u32[]{:S(2)}) copy-start(bf16[128,256]{1,0:T(8,128)(2,1)} %refs_2_.1) | copy-start | bytes 196612
  13.9 5.6 %collective-permute-start.5 = (bf16[256,256]{1,0:T(8,128)(2,1)S(1)}, bf16[256,256]{1,0:T(8,128)(2,1)S(1)}, u32[]{:S(2)}, u32[]{:S(2)}) collective-permute-start(bf16[256,256]{1,0:T(8,128)(2,1)S(1)} %shard_map.104.refs_0_), channel_id=1, source_target_pairs={{0,2},{1,3},{2,0},{3,1},{4,6},{5,7},{6,4},{7,5},{8,10},{9,11},{10,... | collective-permute-start | bytes 393224 | tf_op jit(solution)/shard_map/ppermute | solution.py:216
  20.1 1.5 %collective-permute-start.6 = (bf16[400,256]{1,0:T(8,128)(2,1)S(1)}, bf16[400,256]{1,0:T(8,128)(2,1)S(1)}, u32[]{:S(2)}, u32[]{:S(2)}) collective-permute-start(bf16[400,256]{1,0:T(8,128)(2,1)S(1)} %get-tuple-element.23), channel_id=1, source_target_pairs={{0,1},{1,0},{2,3},{3,2},{4,5},{5,4},{6,7},{7,6},{8,9},{9,8},{10,11... | collective-permute-start | bytes 614408 | tf_op jit(solution)/shard_map/ppermute | solution.py:216
  21.6 5.0 %collective-permute-start.9 = (bf16[128,256]{1,0:T(8,128)(2,1)S(1)}, bf16[128,256]{1,0:T(8,128)(2,1)S(1)}, u32[]{:S(2)}, u32[]{:S(2)}) collective-permute-start(bf16[128,256]{1,0:T(8,128)(2,1)S(1)} %shard_map.109.part_ref), channel_id=1, source_target_pairs={{0,4},{4,0},{8,12},{12,8},{1,5},{5,1},{9,13},{13,9},{2,6},{6,2},{1... | collective-permute-start | bytes 196616 | tf_op jit(solution)/shard_map/ppermute | solution.py:216
  22.1 5.7 %collective-permute-start.7 = (bf16[144,256]{1,0:T(8,128)(2,1)S(1)}, bf16[144,256]{1,0:T(8,128)(2,1)S(1)}, u32[]{:S(2)}, u32[]{:S(2)}) collective-permute-start(bf16[144,256]{1,0:T(8,128)(2,1)S(1)} %get-tuple-element.24.sent_ref), channel_id=1, source_target_pairs={{0,4},{4,0},{8,12},{12,8},{1,5},{5,1},{9,13},{13,9},{2,6},{6,2},{1... | collective-permute-start | bytes 221192 | tf_op jit(solution)/shard_map/ppermute | solution.py:216
  26.6 6.7 %collective-permute-start.10 = (bf16[128,256]{1,0:T(8,128)(2,1)S(1)}, bf16[128,256]{1,0:T(8,128)(2,1)S(1)}, u32[]{:S(2)}, u32[]{:S(2)}) collective-permute-start(bf16[128,256]{1,0:T(8,128)(2,1)S(1)} %shard_map.110.part_ref), channel_id=1, source_target_pairs={{0,8},{4,12},{8,0},{12,4},{1,9},{5,13},{9,1},{13,5},{2,10},{6,14},... | collective-permute-start | bytes 196616 | tf_op jit(solution)/shard_map/ppermute | solution.py:216
  27.8 7.0 %collective-permute-start.8 = (bf16[144,256]{1,0:T(8,128)(2,1)S(1)}, bf16[144,256]{1,0:T(8,128)(2,1)S(1)}, u32[]{:S(2)}, u32[]{:S(2)}) collective-permute-start(bf16[144,256]{1,0:T(8,128)(2,1)S(1)} %shard_map.108.sent_ref), channel_id=1, source_target_pairs={{0,8},{4,12},{8,0},{12,4},{1,9},{5,13},{9,1},{13,5},{2,10},{6,14},... | collective-permute-start | bytes 221192 | tf_op jit(solution)/shard_map/ppermute | solution.py:216
  30.2 4.5 %collective-permute-start.12 = (bf16[128,256]{1,0:T(8,128)(2,1)S(1)}, bf16[128,256]{1,0:T(8,128)(2,1)S(1)}, u32[]{:S(2)}, u32[]{:S(2)}) collective-permute-start(bf16[128,256]{1,0:T(8,128)(2,1)S(1)} %get-tuple-element.27), channel_id=1, source_target_pairs={{0,4},{4,0},{8,12},{12,8},{1,5},{5,1},{9,13},{13,9},{2,6},{6,2},{1... | collective-permute-start | bytes 196616 | tf_op jit(solution)/shard_map/ppermute | solution.py:216
  33.3 1.6 %collective-permute-start.11 = (bf16[128,256]{1,0:T(8,128)(2,1)S(1)}, bf16[128,256]{1,0:T(8,128)(2,1)S(1)}, u32[]{:S(2)}, u32[]{:S(2)}) collective-permute-start(bf16[128,256]{1,0:T(8,128)(2,1)S(1)} %shard_map.111.mine_ref), channel_id=1, source_target_pairs={{0,1},{1,0},{2,3},{3,2},{4,5},{5,4},{6,7},{7,6},{8,9},{9,8},{10,11... | collective-permute-start | bytes 196616 | tf_op jit(solution)/shard_map/ppermute | solution.py:216
